TPU v7x, 32 devices: a whole 2x2x4 slice. The times are simulated.
32 devices in a mesh: comp: 2 (over x), tx: 4 (over z), ty: 4 (over y, core).
Axes of the slice: x: 2, y: 2, z: 4, core: 2. Of those that a mesh axis runs over, the one named last changes fastest.
Arguments:
- state: float32 [2, 16, 512, 2048], P('comp', None, 'tx', 'ty'), may hold values from -6 to 6
- coefs: float32 [2, 3, 512, 2048], P('comp', None, 'tx', 'ty'), may hold values from -0.2 to 0.2
- land_sea: int32 [512, 2048], P('tx', 'ty'), may hold values 0 or 1
- gamma: float32 [2, 8], P('comp'), may hold values from 0.1 to 0.4
- pair_src: int32 [2, 8192], P('comp', ('tx', 'ty')), may hold values from 0 to 511
- pair_dev: int32 [2, 8192, 1], P('comp', ('tx', 'ty')), may hold values from 0 to 15; in each aligned block of 512 rows (0 to 511, 512 to 1023, ..., all dimensions but the last counted through in order) at most 64 rows name the same one
- pair_blk: int32 [2, 8192], P('comp', ('tx', 'ty')), may hold values from 0 to 511
- weights: bfloat16 [2, 8192, 128, 128], P('comp', ('tx', 'ty')), may hold values from -0.375 to 0.375
Outputs:
- new_state: float32 [2, 16, 512, 2048], P('comp', None, 'tx', 'ty')
- remapped: float32 [2, 8, 512, 2048], P('comp', None, 'tx', 'ty')
Inputs may be any that keep to these rules, and one draw needn't show every extreme that they name: `pair_dev`: among the 512 weight blocks of one tile of one component, at most 64 name the same target tile, a bound that some block reaches.
All inputs are finite; a program needn't handle non-finite values. No bound on the sum of `land_sea` on one device may be relied on, other than what follows from the above.
Results may differ from a plain program's by a relative error of at most 0.0029.
Values sent between devices are 32-bit elements; how exact they have to be, the bound alone decides.
No kernel may reach another device: no remote copies, remote signals or barrier semaphores. Data moves between devices by JAX's collectives and lax.ppermute only.
A program may use at most 128 MiB of HBM per device.

v0:
```python
import jax
import jax.numpy as jnp
from jax import lax
from jax.sharding import PartitionSpec as P


def swapped(block, axis, bit):
    count = lax.axis_size(axis)
    route = []
    for low in range(count):
        high = low | 1 << bit
        if high != low and high < count:
            route += [(low, high), (high, low)]
    return lax.ppermute(block, axis, route)


def extended(cells, sides, width):
    for axis, dim in sides:
        count = lax.axis_size(axis)
        ends = count - 1
        head = lax.slice_in_dim(cells, 0, width, axis=dim)
        tail = lax.slice_in_dim(cells, cells.shape[dim] - width, cells.shape[dim], axis=dim)
        cells = jnp.concatenate(
            [
                lax.ppermute(tail, axis, [(i, (i + 1) % count) for i in range(ends)]),
                cells,
                lax.ppermute(head, axis, [((i + 1) % count, i) for i in range(ends)]),
            ],
            axis=dim,
        )
    return cells


def tendency(padded, coefs, recv, gamma, keep):
    center = padded[:, 1:-1, 1:-1]
    xminus = padded[:, :-2, 1:-1]
    xplus = padded[:, 2:, 1:-1]
    yminus = padded[:, 1:-1, :-2]
    yplus = padded[:, 1:-1, 2:]
    speed_x = coefs[0]
    speed_y = coefs[1]
    kappa = coefs[2]
    advect = -(
        jnp.maximum(speed_x, 0.0) * (center - xminus) + jnp.minimum(speed_x, 0.0) * (xplus - center)
    )
    advect = advect - (
        jnp.maximum(speed_y, 0.0) * (center - yminus) + jnp.minimum(speed_y, 0.0) * (yplus - center)
    )
    diffuse = kappa * (xplus + xminus + yplus + yminus - 4.0 * center)
    chan = recv.shape[0]
    couple = gamma[:, None, None] * (recv - center[:chan])
    couple = jnp.concatenate([couple, jnp.zeros_like(center[chan:])], axis=0)
    return keep * (advect + diffuse + couple)


def partner(buffers):
    return swapped((buffers[0], buffers[1]), "comp", 0)


def shallow_rims(field):
    return extended(field, (("tx", 1), ("ty", 2)), 1)


def body(state, coefs, land_sea, gamma, pair_src, pair_dev, pair_blk, weights):
    comp_index = lax.axis_index("comp")
    rows_tx = lax.axis_size("tx")
    rows_ty = lax.axis_size("ty")
    tiles = rows_tx * rows_ty
    nfield, cells_x, cells_y = (state.shape[1], state.shape[2], state.shape[3])
    chan = gamma.shape[1]
    pairs = weights.shape[1]
    width = weights.shape[2]
    nblock = cells_x * cells_y // width
    capacity = max(2, 2 * pairs // tiles)
    surface = state[0, :chan].reshape(chan, nblock, width).astype(jnp.bfloat16)
    picked = jnp.take(surface, pair_src[0], axis=1)
    contrib = jnp.einsum("pts,cps->pct", weights[0], picked, preferred_element_type=jnp.float32)
    target_tile = pair_dev[0, :, 0]
    member = (target_tile[:, None] == jnp.arange(tiles, dtype=jnp.int32)[None, :]).astype(jnp.int32)
    rank = jnp.sum(jnp.cumsum(member, axis=0) * member, axis=1) - 1
    slot = target_tile * capacity + rank
    outgoing = jnp.zeros((tiles * capacity, chan, width), jnp.float32).at[slot].set(contrib)
    out_ids = jnp.zeros((tiles * capacity,), jnp.int32).at[slot].set(pair_blk[0])
    outgoing, out_ids = partner((outgoing, out_ids))
    incoming, in_ids = (
        lax.all_to_all(
            outgoing.reshape(tiles, capacity, chan, width),
            ("tx", "ty"),
            split_axis=0,
            concat_axis=0,
            tiled=True,
        ),
        lax.all_to_all(
            out_ids.reshape(tiles, capacity), ("tx", "ty"), split_axis=0, concat_axis=0, tiled=True
        ),
    )
    incoming = incoming.reshape(tiles * capacity, chan, width)
    in_ids = in_ids.reshape(tiles * capacity)
    selector = (in_ids[:, None] == jnp.arange(nblock, dtype=jnp.int32)[None, :]).astype(jnp.float32)
    summed = jnp.einsum("sn,scb->cnb", selector, incoming, precision=lax.Precision.HIGHEST)
    recv = summed.reshape(chan, cells_x, cells_y)
    is_atmos = comp_index == 0
    keep = jnp.where(
        is_atmos, jnp.ones((cells_x, cells_y), jnp.float32), land_sea.astype(jnp.float32)
    )
    mix_a = jnp.where(is_atmos, 0.0, 0.5).astype(jnp.float32)
    mix_b = jnp.where(is_atmos, 1.0, 0.5).astype(jnp.float32)
    start = state[0]
    local_coefs = coefs[0]
    rates = gamma[0]
    first = tendency(shallow_rims(start), local_coefs, recv, rates, keep)
    section = start + first
    second = tendency(shallow_rims(section), local_coefs, recv, rates, keep)
    result = mix_a * start + (1.0 - mix_a) * section + mix_b * second
    return (result[None], recv[None])


def solution(mesh):
    placed = (
        P("comp", None, "tx", "ty"),
        P("comp", None, "tx", "ty"),
        P("tx", "ty"),
        P("comp", None),
        P("comp", ("tx", "ty")),
        P("comp", ("tx", "ty"), None),
        P("comp", ("tx", "ty")),
        P("comp", ("tx", "ty"), None, None),
    )
    return jax.shard_map(
        body,
        mesh=mesh,
        in_specs=placed,
        out_specs=(P("comp", None, "tx", "ty"), P("comp", None, "tx", "ty")),
        check_vma=False,
    )
```

profile of v0, /device:TPU:1, one launch (start us, length us, event | category | flops | bytes accessed | tf_op | source)
XLA Modules:
  0.0 363.1 jit_solution(11803040187424477803)
XLA Ops:
  0.6 0.7 compare_select_fusion
  1.3 0.7 compare_and_fusion
  2.0 0.7 fusion.54
  2.7 1.1 reduce-window.6
  4.1 0.8 fusion.53
  4.9 0.7 compare_select_fusion.1
  5.6 1.7 slice.130
  7.3 0.7 convert_element_type.18
  8.0 0.7 copy.24
  8.7 1.8 gather_fusion
  10.5 11.8 %fusion = f32[512,8,128]{2,1,0:T(8,128)S(1)} fusion(bf16[1,512,128,128]{3,2,1,0:T(8,128)(2,1)} %param.15, bf16[512,8,128]{2,1,0:T(8,128)(2,1)S(1)} %gather_fusion, pred[512]{0:T(512)(128)(4,1)S(1)} %compare_and_fusion), kind=kOutput, calls=%fused_computation.3 | convolution fusion | flops 134742016 | bytes 19923456 | tf_op jit(solution)/shard_map/pts,cps->pct/dot_general | solution.py:77
  22.2 2.3 broadcast_in_dim.19
  24.6 50.5 %scatter_fusion = f32[1024,8,128]{2,1,0:T(8,128)} fusion(f32[1024,8,128]{2,1,0:T(8,128)} %broadcast_in_dim.19, s32[512]{0:T(512)S(1)} %bitcast.71, f32[512,8,128]{2,1,0:T(8,128)S(1)} %fusion), kind=kCustom, calls=%fused_computation.1 | custom fusion | bytes 6293504 | tf_op jit(solution)/shard_map/scatter | solution.py:82
  75.1 2.0 collective-permute-start.4
  77.1 2.6 scatter_custom_fusion.1
  79.8 88.0 %collective-permute-done.5 = s32[1024]{0:T(1024)S(1)} collective-permute-done((s32[1024]{0:T(1024)S(1)}, s32[1024]{0:T(1024)S(1)}, u32[]{:S(2)}, u32[]{:S(2)}) %collective-permute-start.5) | collective-permute-done | bytes 4128 | tf_op jit(solution)/shard_map/ppermute | solution.py:14
  167.9 12.8 %all_to_all.14 = s32[16,1,64]{2,1,0:T(1,128)S(1)} all-to-all(s32[16,1,64]{2,1,0:T(1,128)S(1)} %all_to_all.10), channel_id=1, replica_groups=mesh['comp'=2,'tx'=4,'ty'=4] {'tx','ty'}, dimensions={0} | all-to-all | bytes 8192 | tf_op jit(solution)/shard_map/all_to_all | solution.py:93
  180.7 5.1 %all-to-all-start = ((f32[16,64,8,128]{3,2,1,0:T(8,128)}), f32[16,64,8,128]{3,2,1,0:T(8,128)}, u32[]{:S(2)}, u32[]{:S(2)}) async-start(f32[16,64,8,128]{3,2,1,0:T(8,128)} %bitcast.18), calls=%async_computation | async-start | bytes 8388608 | tf_op jit(solution)/shard_map/all_to_all | solution.py:86
  185.9 1.1 fusion.59
  186.9 3.3 collective-permute-start
  190.3 1.3 collective-permute-start.1
  191.6 1.1 maximum_bitcast_fusion.1
  192.7 61.9 %collective-permute-done = f32[16,1,512]{2,1,0:T(1,128)S(1)} collective-permute-done((f32[16,1,512]{2,1,0:T(1,128)S(1)}, f32[16,1,512]{2,1,0:T(1,128)S(1)}, u32[]{:S(2)}, u32[]{:S(2)}) %collective-permute-start) | collective-permute-done | bytes 32800 | tf_op jit(solution)/shard_map/ppermute | solution.py:25
  254.6 2.0 pad_maximum_fusion.21
  256.6 0.6 copy.19
  257.2 0.6 copy.21
  257.8 2.6 collective-permute-start.3
  260.4 4.3 %collective-permute-start.2 = (f32[16,130,1]{1,0,2:T(8,128)S(1)}, f32[16,130,1]{1,0,2:T(8,128)S(1)}, u32[]{:S(2)}, u32[]{:S(2)}) collective-permute-start(f32[16,130,1]{1,0,2:T(8,128)S(1)} %copy.19), channel_id=1, source_target_pairs={{0,1},{1,2},{2,3},{4,5},{5,6},{6,7},{8,9},{9,10},{10,11},{12,13},{... | collective-permute-start | bytes 24968 | tf_op jit(solution)/shard_map/ppermute | solution.py:25
  265.3 0.7 reduce.5
  266.5 1.4 copy.22
  267.9 6.1 %fusion.42 = f32[8,512,128]{1,2,0:T(8,128)S(1)} fusion(f32[1024,8,128]{2,1,0:T(8,128)} %bitcast.19, s32[1024]{0:T(1024)S(1)} %eq.52), kind=kOutput, calls=%fused_computation.64 | convolution fusion | flops 6442975232 | bytes 6295552 | tf_op jit(solution)/shard_map/sn,scb->cnb/dot_general | solution.py:100
  274.1 1.8 copy.26
  275.9 1.7 reshape.144
  277.7 2.4 fusion.39
  280.9 10.0 %fusion.29 = f32[16,128,512]{2,1,0:T(8,128)S(1)} fusion(f32[16,128,512]{2,1,0:T(8,128)S(1)} %bitcast.68, f32[16,1,512]{2,1,0:T(1,128)S(1)} %collective-permute-done.1, f32[16,1,512]{2,1,0:T(1,128)S(1)} %collective-permute-done, f32[8,128,512]{2,1,0:T(8,128)S(1)} %fusion.39, f32[16,130,1]{2,1,0:T(8,128)S(1)} %copy-done.3, f32[16,130,1]{2,1,0:T(8,128)S(1)} %copy.20, ...), kind=kLoop, calls=%fused_computation.47 | loop fusion | flops 31457280 | bytes 12140800 | tf_op jit(solution)/shard_map/add | solution.py:112
  291.0 1.9 copy-done.1
  293.0 26.5 %collective-permute-start.6 = (f32[16,1,512]{2,1,0:T(1,128)S(1)}, f32[16,1,512]{2,1,0:T(1,128)S(1)}, u32[]{:S(2)}, u32[]{:S(2)}) collective-permute-start(f32[16,1,512]{2,1,0:T(1,128)S(1)} %get-tuple-element.6), channel_id=1, source_target_pairs={{0,4},{4,8},{8,12},{1,5},{5,9},{9,13},{2,6},{6,10},{10,14},{3,7},{... | collective-permute-start | bytes 98312 | tf_op jit(solution)/shard_map/ppermute | solution.py:25
  319.5 1.3 collective-permute-start.7
  320.8 3.8 %collective-permute-done.7 = f32[16,1,512]{2,1,0:T(1,128)S(1)} collective-permute-done((f32[16,1,512]{2,1,0:T(1,128)S(1)}, f32[16,1,512]{2,1,0:T(1,128)S(1)}, u32[]{:S(2)}, u32[]{:S(2)}) %collective-permute-start.7) | collective-permute-done | bytes 32800 | tf_op jit(solution)/shard_map/ppermute | solution.py:27
  324.6 3.0 pad_maximum_fusion.18
  327.6 2.4 copy.27
  330.6 2.5 collective-permute-start.9
  333.1 4.2 %collective-permute-start.8 = (f32[16,130,1]{1,0,2:T(8,128)}, f32[16,130,1]{1,0,2:T(8,128)}, u32[]{:S(2)}, u32[]{:S(2)}) collective-permute-start(f32[16,130,1]{1,0,2:T(8,128)} %copy.27), channel_id=1, source_target_pairs={{0,1},{1,2},{2,3},{4,5},{5,6},{6,7},{8,9},{9,10},{10,11},{12,13},{... | collective-permute-start | bytes 24968 | tf_op jit(solution)/shard_map/ppermute | solution.py:25
  337.3 3.5 fusion.38
  340.8 2.9 broadcast_in_dim_reshape.4
  343.7 1.1 copy.28
  344.9 2.2 copy.30
  347.0 16.1 %fusion.13 = f32[1,16,128,512]{3,2,1,0:T(8,128)} fusion(f32[16,1,512]{2,1,0:T(1,128)S(1)} %collective-permute-done.7, f32[16,128,512]{2,1,0:T(8,128)} %copy-done.1, f32[16,1,512]{2,1,0:T(1,128)S(1)} %collective-permute-done.6, f32[8,128,512]{2,1,0:T(8,128)S(1)} %copy-done.2, f32[16,130,1]{2,1,0:T(8,128)} %copy.30, f32[16,130,1]{2,1,0:T(8,128)S(1)} %copy.28, ...), kind=kLoop, calls=%fused_computation.23 | loop fusion | flops 35651584 | bytes 16335116 | tf_op jit(solution)/shard_map/broadcast_in_dim | solution.py:115
  (40 shorter events, 3.1 us)
Async XLA Ops:
  75.1 105.7 %collective-permute-start.4 = (f32[1024,8,128]{2,1,0:T(8,128)}, f32[1024,8,128]{2,1,0:T(8,128)}, u32[]{:S(2)}, u32[]{:S(2)}) collective-permute-start(f32[1024,8,128]{2,1,0:T(8,128)} %scatter_fusion), channel_id=1, source_target_pairs={{0,16},{16,0},{1,17},{17,1},{2,18},{18,2},{3,19},{19,3},{4,20},{20... | collective-permute-start | bytes 12582920 | tf_op jit(solution)/shard_map/ppermute | solution.py:14
  79.7 88.1 %collective-permute-start.5 = (s32[1024]{0:T(1024)S(1)}, s32[1024]{0:T(1024)S(1)}, u32[]{:S(2)}, u32[]{:S(2)}) collective-permute-start(s32[1024]{0:T(1024)S(1)} %scatter_custom_fusion.1), channel_id=1, source_target_pairs={{0,16},{16,0},{1,17},{17,1},{2,18},{18,2},{3,19},{19,3},{4,20},{20... | collective-permute-start | bytes 12296 | tf_op jit(solution)/shard_map/ppermute | solution.py:14
  180.7 10.8 %copy-start.7 = (f32[1,3,128,512]{3,2,1,0:T(8,128)S(1)}, f32[1,3,128,512]{3,2,1,0:T(8,128)}, u32[]{:S(2)}) copy-start(f32[1,3,128,512]{3,2,1,0:T(8,128)} %param.9) | copy-start | bytes 2359300
  180.7 87.2 %all-to-all-start = ((f32[16,64,8,128]{3,2,1,0:T(8,128)}), f32[16,64,8,128]{3,2,1,0:T(8,128)}, u32[]{:S(2)}, u32[]{:S(2)}) async-start(f32[16,64,8,128]{3,2,1,0:T(8,128)} %bitcast.18), calls=%async_computation | async-start | bytes 8388608 | tf_op jit(solution)/shard_map/all_to_all | solution.py:86
  186.9 67.6 %collective-permute-start = (f32[16,1,512]{2,1,0:T(1,128)S(1)}, f32[16,1,512]{2,1,0:T(1,128)S(1)}, u32[]{:S(2)}, u32[]{:S(2)}) collective-permute-start(f32[16,1,512]{2,1,0:T(1,128)S(1)} %get-tuple-element.8), channel_id=1, source_target_pairs={{0,4},{4,8},{8,12},{1,5},{5,9},{9,13},{2,6},{6,10},{10,14},{3,7},{... | collective-permute-start | bytes 98312 | tf_op jit(solution)/shard_map/ppermute | solution.py:25
  190.3 64.3 %collective-permute-start.1 = (f32[16,1,512]{2,1,0:T(1,128)S(1)}, f32[16,1,512]{2,1,0:T(1,128)S(1)}, u32[]{:S(2)}, u32[]{:S(2)}) collective-permute-start(f32[16,1,512]{2,1,0:T(1,128)S(1)} %get-tuple-element.9), channel_id=1, source_target_pairs={{4,0},{8,4},{12,8},{5,1},{9,5},{13,9},{6,2},{10,6},{14,10},{7,3},{... | collective-permute-start | bytes 98312 | tf_op jit(solution)/shard_map/ppermute | solution.py:27
  192.7 72.1 %copy-start.8 = (s32[128,512]{1,0:T(8,128)S(1)}, s32[128,512]{1,0:T(8,128)}, u32[]{:S(2)}) copy-start(s32[128,512]{1,0:T(8,128)} %param.10) | copy-start | bytes 786436
  257.8 8.7 %collective-permute-start.3 = (f32[16,130,1]{1,0,2:T(8,128)S(1)}, f32[16,130,1]{1,0,2:T(8,128)S(1)}, u32[]{:S(2)}, u32[]{:S(2)}) collective-permute-start(f32[16,130,1]{1,0,2:T(8,128)S(1)} %copy.21), channel_id=1, source_target_pairs={{1,0},{2,1},{3,2},{5,4},{6,5},{7,6},{9,8},{10,9},{11,10},{13,12},{... | collective-permute-start | bytes 24968 | tf_op jit(solution)/shard_map/ppermute | solution.py:27
  260.4 5.7 %collective-permute-start.2 = (f32[16,130,1]{1,0,2:T(8,128)S(1)}, f32[16,130,1]{1,0,2:T(8,128)S(1)}, u32[]{:S(2)}, u32[]{:S(2)}) collective-permute-start(f32[16,130,1]{1,0,2:T(8,128)S(1)} %copy.19), channel_id=1, source_target_pairs={{0,1},{1,2},{2,3},{4,5},{5,6},{6,7},{8,9},{9,10},{10,11},{12,13},{... | collective-permute-start | bytes 24968 | tf_op jit(solution)/shard_map/ppermute | solution.py:25
  274.0 3.6 copy-start.9
  277.6 2.8 copy-start
  277.6 3.1 copy-start.3
  277.6 3.1 copy-start.4
  277.6 3.2 copy-start.5
  277.7 3.3 copy-start.6
  291.0 1.9 copy-start.1
  293.0 27.8 %collective-permute-start.6 = (f32[16,1,512]{2,1,0:T(1,128)S(1)}, f32[16,1,512]{2,1,0:T(1,128)S(1)}, u32[]{:S(2)}, u32[]{:S(2)}) collective-permute-start(f32[16,1,512]{2,1,0:T(1,128)S(1)} %get-tuple-element.6), channel_id=1, source_target_pairs={{0,4},{4,8},{8,12},{1,5},{5,9},{9,13},{2,6},{6,10},{10,14},{3,7},{... | collective-permute-start | bytes 98312 | tf_op jit(solution)/shard_map/ppermute | solution.py:25
  319.5 5.1 %collective-permute-start.7 = (f32[16,1,512]{2,1,0:T(1,128)S(1)}, f32[16,1,512]{2,1,0:T(1,128)S(1)}, u32[]{:S(2)}, u32[]{:S(2)}) collective-permute-start(f32[16,1,512]{2,1,0:T(1,128)S(1)} %get-tuple-element.7), channel_id=1, source_target_pairs={{4,0},{8,4},{12,8},{5,1},{9,5},{13,9},{6,2},{10,6},{14,10},{7,3},{... | collective-permute-start | bytes 98312 | tf_op jit(solution)/shard_map/ppermute | solution.py:27
  330.6 14.2 %collective-permute-start.9 = (f32[16,130,1]{1,0,2:T(8,128)S(1)}, f32[16,130,1]{1,0,2:T(8,128)}, u32[]{:S(2)}, u32[]{:S(2)}) collective-permute-start(f32[16,130,1]{1,0,2:T(8,128)S(1)} %copy.29), channel_id=1, source_target_pairs={{1,0},{2,1},{3,2},{5,4},{6,5},{7,6},{9,8},{10,9},{11,10},{13,12},{... | collective-permute-start | bytes 24968 | tf_op jit(solution)/shard_map/ppermute | solution.py:27
  333.1 10.6 %collective-permute-start.8 = (f32[16,130,1]{1,0,2:T(8,128)}, f32[16,130,1]{1,0,2:T(8,128)}, u32[]{:S(2)}, u32[]{:S(2)}) collective-permute-start(f32[16,130,1]{1,0,2:T(8,128)} %copy.27), channel_id=1, source_target_pairs={{0,1},{1,2},{2,3},{4,5},{5,6},{6,7},{8,9},{9,10},{10,11},{12,13},{... | collective-permute-start | bytes 24968 | tf_op jit(solution)/shard_map/ppermute | solution.py:25
  340.8 6.2 %copy-start.2 = (f32[8,128,512]{2,1,0:T(8,128)S(1)}, f32[8,128,512]{2,1,0:T(8,128)}, u32[]{:S(2)}) copy-start(f32[8,128,512]{2,1,0:T(8,128)} %fusion.38) | copy-start | bytes 6291460
where the time goes:
time: 365 us; the launch traced here: 363 us
  waiting for transfers between devices  154 us (42%)
  local copies, waits for them, and re-layouts  81 us (22%)
  starting transfers between devices  53.2 us (15%)
  other arithmetic  43.5 us (12%)
  matrix products  17.9 us (5%)
  blocking collectives  12.8 us (4%)
    ppermute x2, waiting for transfers between devices, swapped(): return lax.ppermute(block, axis, route)  88 us
    ppermute x4, waiting for transfers between devices, extended(): lax.ppermute(tail, axis, [(i, (i + 1) % count) for i in range(ends)])  61.9 us
    scatter x1, local copies, waits for them, and re-layouts, body(): jnp.zeros((tiles * capacity, chan, width), jnp.float32).at[slot]  50.5 us
    ppermute x4, starting transfers between devices, extended(): lax.ppermute(tail, axis, [(i, (i + 1) % count) for i in range(ends)])  38.4 us
    broadcast_in_dim x1, other arithmetic, body(): return (result[None], recv[None])  16.1 us
    all_to_all x1, blocking collectives, body(): lax.all_to_all(out_ids.reshape(tiles, capacity), ('tx', 'ty'), split_axis...  12.8 us
    dot_general x1, matrix products, body(): jnp.einsum('pts,cps->pct', weights[0], picked, preferred_element_type=jnp...  11.8 us
    add x1, other arithmetic, body(): section = start + first  10 us
  transfers between devices with their start and end apart: 11, of which 3 were waited for; matrix products, arithmetic and copies ran while one was open for 5% of the time, Pallas kernels for 0%

commit v1 on v0

v1 whole, which is shorter than its diff:
```python
import functools

import jax
import jax.numpy as jnp
from jax import lax
from jax.experimental import pallas as pl
from jax.experimental.pallas import tpu as pltpu
from jax.sharding import PartitionSpec as P

LANES = 128
STEP_PAIRS = 64
NT = (((1,), (1,)), ((), ()))


def shift_pairs(count, by):
    return [(i, i + by) for i in range(count) if 0 <= i + by < count]


def crossed(axis, by):
    count = lax.axis_size(axis)
    return [
        (c * count + i, (1 - c) * count + j) for c in range(2) for i, j in shift_pairs(count, by)
    ]


def contribution_kernel(dims, src_ref, dev_ref, blk_ref, state_ref, weights_ref, *rest):
    tiles, capacity, pairs, fields, cells_x, cells_y, width, chunks = dims
    outs = rest[: len(chunks)]
    cells, left_ref, product, w_ref, place_v, place_s = rest[len(chunks) : len(chunks) + 6]
    field_sems, weight_sems, place_sem = rest[len(chunks) + 6 :]
    parts = cells_y // width
    steps = pairs // STEP_PAIRS

    field_copies = [
        pltpu.make_async_copy(
            state_ref.at[0, f, :, pl.ds(q * width, width)],
            cells.at[pl.ds((q * fields + f) * cells_x, cells_x), :],
            field_sems.at[f * parts + q],
        )
        for f in range(fields)
        for q in range(parts)
    ]

    def weight_copy(step):
        some = pl.ds(step * STEP_PAIRS, STEP_PAIRS)
        return pltpu.make_async_copy(
            weights_ref.at[0, some], w_ref.at[some], weight_sems.at[step]
        )

    for copy in field_copies:
        copy.start()
    for step in range(steps):
        weight_copy(step).start()

    dev = dev_ref[...]
    tile_of = lax.broadcasted_iota(jnp.int32, (tiles, pairs), 0)
    lane_of = lax.broadcasted_iota(jnp.int32, (tiles, pairs), 1)
    member = (tile_of == dev).astype(jnp.float32)
    total = member
    shift = 1
    while shift < pairs:
        total = total + jnp.where(lane_of >= shift, pltpu.roll(total, shift, 1), 0.0)
        shift *= 2
    rank = (jnp.sum(member * total, axis=0, keepdims=True) - 1.0).astype(jnp.int32)
    src = src_ref[...]
    place_v[0:1, :] = dev * (capacity + 1) + rank
    place_v[1:2, :] = (src % parts) * (fields * cells_x) + src // parts
    to_scalars = pltpu.make_async_copy(place_v, place_s, place_sem)
    to_scalars.start()

    for out in outs:
        out[...] = jnp.zeros_like(out)
    slot_of = lax.broadcasted_iota(jnp.int32, (LANES, pairs), 0) % capacity
    chosen = (slot_of == rank).astype(jnp.bfloat16)
    blk = blk_ref[...]

    def spread(values):
        return lax.dot_general(
            (member * values).astype(jnp.bfloat16), chosen, NT, preferred_element_type=jnp.float32
        )

    ids = spread((blk // 256).astype(jnp.float32)) * 256.0
    ids = ids + spread((blk % 256).astype(jnp.float32))
    ids = jnp.where(spread(jnp.ones(dev.shape, jnp.float32)) > 0.5, ids, -1.0)
    for t in range(tiles):
        row = jnp.broadcast_to(ids[t : t + 1, :], (fields, LANES))
        for out in outs:
            out[t * (capacity + 1) + capacity] = row[: out.shape[1]]
    to_scalars.wait()
    for copy in field_copies:
        copy.wait()

    zeros = jnp.zeros((fields, width), jnp.float32)

    def cells_of(p):
        return cells[pl.ds(place_s[1, p], fields, stride=cells_x), :]

    def gather(step, carry):
        for i in range(0, STEP_PAIRS, 2):
            p = step * STEP_PAIRS + i
            one = jnp.concatenate([cells_of(p), zeros], axis=1)
            two = jnp.concatenate([zeros, cells_of(p + 1)], axis=1)
            rows = pl.ds(pl.multiple_of(p * fields, 2 * fields), 2 * fields)
            left_ref[rows, :] = jnp.concatenate([one, two], axis=0).astype(jnp.bfloat16)
        return carry

    def multiply(step, carry):
        weight_copy(step).wait()
        for i in range(0, STEP_PAIRS, 4):
            p = step * STEP_PAIRS + i
            rows = pl.ds(pl.multiple_of(p * fields, 4 * fields), 4 * fields)
            w = [w_ref[p + j] for j in range(4)]
            right = jnp.concatenate(
                [jnp.concatenate(w[0:2], axis=1), jnp.concatenate(w[2:4], axis=1)], axis=0
            )
            four = lax.dot_general(
                left_ref[rows, :], right, NT, preferred_element_type=jnp.float32
            )
            low = pl.ds(pl.multiple_of(p * fields, 2 * fields), 2 * fields)
            high = pl.ds(pl.multiple_of((p + 2) * fields, 2 * fields), 2 * fields)
            product[low, :] = four[: 2 * fields, :width]
            product[high, :] = four[2 * fields :, width:]
        return carry

    def scatter(step, carry):
        for i in range(STEP_PAIRS):
            p = step * STEP_PAIRS + i
            slot = place_s[0, p]
            one = product[pl.ds(pl.multiple_of(p * fields, fields), fields), :]
            for out, (first, last) in zip(outs, chunks):
                out[slot] = one[first:last]
        return carry

    lax.fori_loop(0, steps, gather, 0)
    lax.fori_loop(0, steps, multiply, 0)
    lax.fori_loop(0, steps, scatter, 0)


def contributions(state, pair_src, pair_dev, pair_blk, weights, tiles, capacity, chunks):
    _, _, cells_x, cells_y = state.shape
    fields = chunks[-1][1]
    pairs, width = weights.shape[1], weights.shape[2]
    rows = tiles * (capacity + 1)
    dims = (tiles, capacity, pairs, fields, cells_x, cells_y, width, chunks)
    parts = cells_y // width
    shapes = [(rows, last - first, width) for first, last in chunks]
    return pl.pallas_call(
        functools.partial(contribution_kernel, dims),
        in_specs=[pl.BlockSpec(memory_space=pltpu.VMEM)] * 3
        + [pl.BlockSpec(memory_space=pltpu.HBM)] * 2,
        out_specs=[pl.BlockSpec(memory_space=pltpu.VMEM) for _ in shapes],
        out_shape=[jax.ShapeDtypeStruct(shape, jnp.float32) for shape in shapes],
        scratch_shapes=[
            pltpu.VMEM((parts * fields * cells_x, width), jnp.float32),
            pltpu.VMEM((pairs * fields, 2 * width), jnp.bfloat16),
            pltpu.VMEM((pairs * fields, width), jnp.float32),
            pltpu.VMEM((pairs, width, width), jnp.bfloat16),
            pltpu.VMEM((8, pairs), jnp.int32),
            pltpu.SMEM((8, pairs), jnp.int32),
            pltpu.SemaphoreType.DMA((parts * fields,)),
            pltpu.SemaphoreType.DMA((pairs // STEP_PAIRS,)),
            pltpu.SemaphoreType.DMA,
        ],
        compiler_params=pltpu.CompilerParams(vmem_limit_bytes=56 * 1024 * 1024),
        cost_estimate=pl.CostEstimate(
            flops=2 * pairs * fields * width * width,
            bytes_accessed=2 * pairs * width * width + 8 * rows * fields * width,
            transcendentals=0,
        ),
        name="contributions",
    )(pair_src, pair_dev.reshape(1, pairs), pair_blk, state, weights)


def sum_kernel(dims, in_ref, out_ref, top_ref, bottom_ref, left_ref, right_ref, pick, high, low):
    tiles, capacity, fields, cells_x, cells_y, width = dims
    parts = cells_y // width
    group = LANES // capacity
    stride = (capacity + 1) * fields
    block_of = lax.broadcasted_iota(jnp.int32, (cells_x * parts, LANES), 0)
    block_of = (block_of % cells_x) * parts + block_of // cells_x
    block_of = block_of.astype(jnp.float32)
    lane = lax.broadcasted_iota(jnp.int32, (1, LANES), 1)
    for k in range(tiles // group):
        columns = pl.ds(k * LANES, LANES)
        ids = None
        for i in range(group):
            source = k * group + i
            row = in_ref[pl.ds(source * stride + capacity * fields, 1), :]
            ids = row if ids is None else jnp.where(lane // capacity == i, row, ids)
            for f in range(fields):
                x = in_ref[pl.ds(source * stride + f, capacity, stride=fields), :]
                rounded = x.astype(jnp.bfloat16)
                place = (
                    pl.ds(source * capacity, capacity),
                    pl.ds(f * width, width),
                )
                high[place] = rounded
                low[place] = (x - rounded.astype(jnp.float32)).astype(jnp.bfloat16)
        pick[:, columns] = (block_of == ids).astype(jnp.bfloat16)
    for q in range(parts):
        chosen = pick[pl.ds(q * cells_x, cells_x), :]
        total = jnp.dot(chosen, high[...], preferred_element_type=jnp.float32)
        total = total + jnp.dot(chosen, low[...], preferred_element_type=jnp.float32)
        for f in range(fields):
            tile = total[:, f * width : (f + 1) * width]
            out_ref[f, :, pl.ds(q * width, width)] = tile
            top_ref[pl.ds(f, 1), pl.ds(q * width, width)] = tile[:1]
            bottom_ref[pl.ds(f, 1), pl.ds(q * width, width)] = tile[cells_x - 1 :]
            if q == 0:
                left_ref[pl.ds(f, 1), :] = tile.T[:1]
            if q == parts - 1:
                right_ref[pl.ds(f, 1), :] = tile.T[width - 1 :]


def summed(rows, tiles, capacity, fields, cells_x, cells_y, width):
    dims = (tiles, capacity, fields, cells_x, cells_y, width)
    slots = tiles * capacity
    blocks = cells_x * cells_y // width
    shapes = [
        (fields, cells_x, cells_y),
        (fields, cells_y),
        (fields, cells_y),
        (fields, cells_x),
        (fields, cells_x),
    ]
    return pl.pallas_call(
        functools.partial(sum_kernel, dims),
        out_shape=[jax.ShapeDtypeStruct(shape, jnp.float32) for shape in shapes],
        scratch_shapes=[
            pltpu.VMEM((blocks, slots), jnp.bfloat16),
            pltpu.VMEM((slots, fields * width), jnp.bfloat16),
            pltpu.VMEM((slots, fields * width), jnp.bfloat16),
        ],
        compiler_params=pltpu.CompilerParams(vmem_limit_bytes=40 * 1024 * 1024),
        cost_estimate=pl.CostEstimate(
            flops=4 * blocks * slots * fields * width,
            bytes_accessed=4 * fields * width * (slots + blocks),
            transcendentals=0,
        ),
        name="sum_by_block",
    )(rows.reshape(tiles * (capacity + 1) * fields, width))


def stencil_factors(coefs, keep):
    u, v, kappa = coefs
    return [
        keep,
        keep * (jnp.maximum(u, 0.0) + kappa),
        keep * (kappa - jnp.minimum(u, 0.0)),
        keep * (jnp.maximum(v, 0.0) + kappa),
        keep * (kappa - jnp.minimum(v, 0.0)),
        -keep * (jnp.abs(u) + jnp.abs(v) + 4.0 * kappa),
    ]


def tendency(s, rate, factors, top, bottom, left, right):
    cells_x, cells_y = s.shape
    x_of = lax.broadcasted_iota(jnp.int32, s.shape, 0)
    y_of = lax.broadcasted_iota(jnp.int32, s.shape, 1)
    out = (factors[5] - rate * factors[0]) * s
    out += factors[1] * jnp.where(x_of == 0, top, pltpu.roll(s, 1, 0))
    out += factors[2] * jnp.where(x_of == cells_x - 1, bottom, pltpu.roll(s, cells_x - 1, 0))
    out += factors[3] * jnp.where(y_of == 0, left, pltpu.roll(s, 1, 1))
    out += factors[4] * jnp.where(y_of == cells_y - 1, right, pltpu.roll(s, cells_y - 1, 1))
    return out


def columns_of(rows):
    spare = 8 - rows.shape[0]
    if spare:
        rows = jnp.concatenate([rows, jnp.zeros((spare, rows.shape[1]), rows.dtype)], axis=0)
    return rows.T


def line_count(nfield):
    return 2 * nfield + 8


def edge_kernel(mix_ref, state_tops, state_ends, state_lefts, state_rights, coefs_tops, coefs_ends,
                coefs_lefts, coefs_rights, land_tops, land_ends, land_lefts, land_rights,
                x_low, x_high, y_low, y_high):
    nfield = state_tops.shape[1]
    last_row, last_lane = state_tops.shape[2] - 1, state_lefts.shape[3] - 1
    atmos = mix_ref[0, 1] == 1.0

    def kept(land):
        return jnp.where(atmos, 1.0, land.astype(jnp.float32))

    for out, state, coefs, land, lines in (
        (x_low, state_tops, coefs_tops, land_tops, (0, 1)),
        (x_high, state_ends, coefs_ends, land_ends, (last_row - 1, last_row)),
    ):
        outer = lines[0] if lines[0] == 0 else lines[1]
        out[2 * nfield :, :] = jnp.zeros((8, out.shape[1]), jnp.float32)
        for j, line in enumerate(lines):
            for f in range(nfield):
                out[j * nfield + f : j * nfield + f + 1, :] = state[0, f, line : line + 1, :]
        for c in range(3):
            out[2 * nfield + c : 2 * nfield + c + 1, :] = coefs[0, c, outer : outer + 1, :]
        out[2 * nfield + 3 : 2 * nfield + 4, :] = kept(land[outer : outer + 1, :])

    for out, state, coefs, land, lines in (
        (y_low, state_lefts, coefs_lefts, land_lefts, (0, 1)),
        (y_high, state_rights, coefs_rights, land_rights, (last_lane - 1, last_lane)),
    ):
        outer = lines[0] if lines[0] == 0 else lines[1]
        lane = lax.broadcasted_iota(jnp.int32, land.shape, 1)
        packed = jnp.zeros(land.shape, jnp.float32)

        def put(packed, tile, at, to):
            moved = (to - at) % LANES
            tile = pltpu.roll(tile, moved, 1) if moved else tile
            return jnp.where(lane == to, tile, packed)

        for j, line in enumerate(lines):
            for f in range(nfield):
                packed = put(packed, state[0, f], line, j * nfield + f)
        for c in range(3):
            packed = put(packed, coefs[0, c], outer, 2 * nfield + c)
        packed = put(packed, kept(land[...]), outer, 2 * nfield + 3)
        out[...] = packed.T[: out.shape[0]]


def edges_of(state, coefs, land_sea, mix):
    _, nfield, cells_x, cells_y = state.shape
    lines = line_count(nfield)
    ends = [
        ((8, cells_y), (0, 0)),
        ((8, cells_y), (cells_x // 8 - 1, 0)),
        ((cells_x, LANES), (0, 0)),
        ((cells_x, LANES), (0, cells_y // LANES - 1)),
    ]
    at = lambda lead, place: lambda i: (0,) * len(lead) + place
    specs = [pl.BlockSpec(memory_space=pltpu.SMEM)]
    for lead in ((1, nfield), (1, 3), ()):
        specs += [pl.BlockSpec(lead + shape, at(lead, place)) for shape, place in ends]
    shapes = [(lines, cells_y)] * 2 + [(lines, cells_x)] * 2
    return pl.pallas_call(
        edge_kernel,
        grid=(1,),
        in_specs=specs,
        out_specs=[pl.BlockSpec(shape, lambda i: (0, 0)) for shape in shapes],
        out_shape=[jax.ShapeDtypeStruct(shape, jnp.float32) for shape in shapes],
        compiler_params=pltpu.CompilerParams(vmem_limit_bytes=40 * 1024 * 1024),
        cost_estimate=pl.CostEstimate(
            flops=state.size, bytes_accessed=4 * 1024 * 1024, transcendentals=0
        ),
        name="edges",
    )(mix, *[state] * 4, *[coefs] * 4, *[land_sea] * 4)


def outer_section(center, across, along, factors, rate):
    lane = lax.broadcasted_iota(jnp.int32, center.shape, 1)
    count = center.shape[1]
    before = jnp.where(lane == 0, along[0], pltpu.roll(center, 1, 1))
    after = jnp.where(lane == count - 1, along[1], pltpu.roll(center, count - 1, 1))
    keep, low, high, back, ahead, middle = factors
    out = center + low * across[0] + high * across[1] + back * before + ahead * after
    return out + (middle - rate * keep) * center


def base_kernel(rate_ref, mix_ref, rates_ref, coefs_ref, land_ref, x_low, x_high, y_low, y_high,
                above, below, left, right, corners_left, corners_right, state_ref,
                out_ref, factors, rows, cols):
    f = pl.program_id(0)
    nfield = rates_ref.shape[0]
    lines = line_count(nfield)

    @pl.when(f == 0)
    def _():
        keep = jnp.where(mix_ref[0, 1] == 1.0, 1.0, land_ref[...].astype(jnp.float32))
        for i, factor in enumerate(stencil_factors([coefs_ref[0, c] for c in range(3)], keep)):
            factors[i] = factor
        rate = rates_ref[:, 0:1]
        near, far = pl.ds(0, nfield), pl.ds(nfield, nfield)
        last = corners_left.shape[1] - 1
        corner = (
            (corners_left[nfield : 2 * nfield, last:], corners_left[lines : lines + nfield, last:]),
            (corners_right[nfield : 2 * nfield, 0:1], corners_right[lines : lines + nfield, 0:1]),
        )
        for i, (ref, center, across, along, is_column) in enumerate(
            (
                (above, above[far, :], (above[near, :], x_low[near, :]), (corner[0][0], corner[1][0]), False),
                (below, below[near, :], (x_high[far, :], below[far, :]), (corner[0][1], corner[1][1]), False),
                (left, left[far, :], (left[near, :], y_low[near, :]), corner[0], True),
                (right, right[near, :], (y_high[far, :], right[far, :]), corner[1], True),
            )
        ):
            first = 2 * nfield
            of_line = stencil_factors(
                [ref[first + c : first + c + 1, :] for c in range(3)],
                ref[first + 3 : first + 4, :],
            )
            if is_column:
                of_line = [of_line[j] for j in (0, 3, 4, 1, 2, 5)]
            section = outer_section(center, across, along, of_line, rate)
            kept = cols if is_column else rows
            kept[pl.ds(i % 2 * nfield, nfield), :] = center
            kept[pl.ds((2 + i % 2) * nfield, nfield), :] = section

    rate = rate_ref[0, f]
    mix_a, mix_b = mix_ref[0, 0], mix_ref[0, 1]
    s = state_ref[0, 0]
    row = [rows[pl.ds(i * nfield + f, 1), :] for i in range(4)]
    col = columns_of(
        jnp.concatenate([cols[pl.ds(i * nfield + f, 1), :] for i in range(4)], axis=0)
    )
    s1 = s + tendency(s, rate, factors, row[0], row[1], col[:, 0:1], col[:, 1:2])
    more = tendency(s1, rate, factors, row[2], row[3], col[:, 2:3], col[:, 3:4])
    out_ref[0, 0] = mix_a * s + (1.0 - mix_a) * s1 + mix_b * more


def base_of(state, coefs, land_sea, rates, mix, edges, received, corners):
    _, nfield, cells_x, cells_y = state.shape
    field = pl.BlockSpec((1, 1, cells_x, cells_y), lambda f: (0, f, 0, 0))
    whole = lambda a: pl.BlockSpec(a.shape, lambda f: (0,) * a.ndim)
    rates_wide = jnp.broadcast_to(rates.T, (nfield, LANES))
    operands = [rates_wide, coefs, land_sea, *edges, *received, *corners]
    return pl.pallas_call(
        base_kernel,
        grid=(nfield,),
        in_specs=[
            pl.BlockSpec(memory_space=pltpu.SMEM),
            pl.BlockSpec(memory_space=pltpu.SMEM),
            *[whole(a) for a in operands],
            field,
        ],
        out_specs=[field, pl.BlockSpec((6, cells_x, cells_y), lambda f: (0, 0, 0))],
        out_shape=[
            jax.ShapeDtypeStruct(state.shape, jnp.float32),
            jax.ShapeDtypeStruct((6, cells_x, cells_y), jnp.float32),
        ],
        scratch_shapes=[
            pltpu.VMEM((4 * nfield, cells_y), jnp.float32),
            pltpu.VMEM((4 * nfield, cells_x), jnp.float32),
        ],
        compiler_params=pltpu.CompilerParams(vmem_limit_bytes=40 * 1024 * 1024),
        cost_estimate=pl.CostEstimate(
            flops=40 * state.size, bytes_accessed=8 * state.size, transcendentals=0
        ),
        name="base",
    )(rates, mix, *operands, state)


def finish_kernel(
    first, gamma_ref, mix_ref, factors, above, below, before, after, base_ref, recv_ref,
    top_ref, bottom_ref, left_ref, right_ref, *rest
):
    new_ref, out_ref = rest[-2:]
    f = pl.program_id(0)
    rate = gamma_ref[0, first + f]
    mix_b = mix_ref[0, 1]
    recv = recv_ref[0]
    g = factors[0] * recv * rate
    row = pl.ds(f, 1)
    keep_row = above.shape[0] - 5
    keep = slice(keep_row, keep_row + 1)
    top = above[keep, :] * top_ref[row, :] * rate
    bottom = below[keep, :] * bottom_ref[row, :] * rate
    left = before[keep, :] * left_ref[row, :] * rate
    right = after[keep, :] * right_ref[row, :] * rate
    cols = columns_of(jnp.concatenate([left, right], axis=0))
    more = tendency(g, rate, factors, top, bottom, cols[:, 0:1], cols[:, 1:2])
    new_ref[0, 0] = base_ref[0, 0] + mix_b * (2.0 * g + more)
    out_ref[0, 0] = recv


def finished(first, new_state, remapped, recv, rims, gamma, mix, factors, received):
    fields, cells_x, cells_y = recv.shape
    chan = gamma.shape[1]
    whole = lambda a: pl.BlockSpec(a.shape, lambda f: (0,) * a.ndim)
    field = pl.BlockSpec((1, 1, cells_x, cells_y), lambda f: (0, first + f, 0, 0))
    operands = [gamma, mix, factors, *received, new_state, recv, *rims]
    specs = [
        pl.BlockSpec(memory_space=pltpu.SMEM),
        pl.BlockSpec(memory_space=pltpu.SMEM),
        whole(factors),
        *[whole(lines) for lines in received],
        field,
        pl.BlockSpec((1, cells_x, cells_y), lambda f: (f, 0, 0)),
        *[whole(rim) for rim in rims],
    ]
    aliases = {7: 0}
    if remapped is not None:
        aliases[len(operands)] = 1
        operands.append(remapped)
        specs.append(pl.BlockSpec(memory_space=pl.ANY))
    return pl.pallas_call(
        functools.partial(finish_kernel, first),
        grid=(fields,),
        in_specs=specs,
        out_specs=[field, field],
        out_shape=[
            jax.ShapeDtypeStruct(new_state.shape, jnp.float32),
            jax.ShapeDtypeStruct((1, chan, cells_x, cells_y), jnp.float32),
        ],
        input_output_aliases=aliases,
        compiler_params=pltpu.CompilerParams(vmem_limit_bytes=40 * 1024 * 1024),
        cost_estimate=pl.CostEstimate(
            flops=20 * recv.size, bytes_accessed=20 * recv.size, transcendentals=0
        ),
        name="finish",
    )(*operands)


def body(state, coefs, land_sea, gamma, pair_src, pair_dev, pair_blk, weights):
    tx, ty = lax.axis_size("tx"), lax.axis_size("ty")
    tiles = tx * ty
    nfield, cells_x, cells_y = state.shape[1:]
    chan = gamma.shape[1]
    pairs, width = weights.shape[1], weights.shape[2]
    capacity = max(2, 2 * pairs // tiles)
    half = chan // 2
    chunks = ((0, half), (half, chan))
    early, late = contributions(
        state, pair_src, pair_dev, pair_blk, weights, tiles, capacity, chunks
    )
    swap = [(0, 1), (1, 0)]

    def exchanged(rows):
        rows = rows.reshape(tiles, capacity + 1, rows.shape[1], width)
        return lax.all_to_all(rows, ("tx", "ty"), split_axis=0, concat_axis=0, tiled=True)

    def add_up(rows):
        return summed(rows, tiles, capacity, half, cells_x, cells_y, width)

    late_in = exchanged(late)
    early_in = lax.ppermute(early, "comp", swap)

    land_after, _ = lax.optimization_barrier((land_sea, late))
    is_atmos = lax.axis_index("comp") == 0
    mix = jnp.where(is_atmos, jnp.array([[0.0, 1.0]]), jnp.array([[0.5, 0.5]]))
    mix = mix.astype(jnp.float32)
    rates = jnp.concatenate([gamma, jnp.zeros((1, nfield - chan), jnp.float32)], axis=1)
    x_low, x_high, y_low, y_high = edges_of(state, coefs, land_after, mix)
    left = lax.ppermute(y_high, "ty", shift_pairs(ty, 1))
    right = lax.ppermute(y_low, "ty", shift_pairs(ty, -1))
    above = lax.ppermute(x_high, "tx", shift_pairs(tx, 1))
    below = lax.ppermute(x_low, "tx", shift_pairs(tx, -1))
    received = (above, below, left, right)

    early_in = exchanged(early_in)

    ends = jnp.concatenate([above[:, cells_y - LANES :], below[:, cells_y - LANES :]], axis=0)
    starts = jnp.concatenate([above[:, :LANES], below[:, :LANES]], axis=0)
    corners_left = lax.ppermute(ends, "ty", shift_pairs(ty, 1))
    corners_right = lax.ppermute(starts, "ty", shift_pairs(ty, -1))
    base, factors = base_of(
        state, coefs, land_after, rates, mix, (x_low, x_high, y_low, y_high), received,
        (corners_left, corners_right),
    )

    recv_late, top, bottom, left, right = add_up(late_in)
    recv_late = lax.ppermute(recv_late, "comp", swap)
    rims_late = (
        lax.ppermute(bottom, ("comp", "tx"), crossed("tx", 1)),
        lax.ppermute(top, ("comp", "tx"), crossed("tx", -1)),
        lax.ppermute(right, ("comp", "ty"), crossed("ty", 1)),
        lax.ppermute(left, ("comp", "ty"), crossed("ty", -1)),
    )
    recv_early, top, bottom, left, right = add_up(early_in)
    rims_early = (
        lax.ppermute(bottom, "tx", shift_pairs(tx, 1)),
        lax.ppermute(top, "tx", shift_pairs(tx, -1)),
        lax.ppermute(right, "ty", shift_pairs(ty, 1)),
        lax.ppermute(left, "ty", shift_pairs(ty, -1)),
    )
    rest = (gamma, mix, factors, received)
    new_state, remapped = finished(half, base, None, recv_late, rims_late, *rest)
    new_state, remapped = finished(0, new_state, remapped, recv_early, rims_early, *rest)
    return new_state, remapped


def solution(mesh):
    placed = (
        P("comp", None, "tx", "ty"),
        P("comp", None, "tx", "ty"),
        P("tx", "ty"),
        P("comp", None),
        P("comp", ("tx", "ty")),
        P("comp", ("tx", "ty"), None),
        P("comp", ("tx", "ty")),
        P("comp", ("tx", "ty"), None, None),
    )
    return jax.shard_map(
        body,
        mesh=mesh,
        in_specs=placed,
        out_specs=(P("comp", None, "tx", "ty"), P("comp", None, "tx", "ty")),
        check_vma=False,
    )
```

time: 365 us -> 191 us (0.52)
  waiting for transfers between devices: 154 us -> 61.2 us
  local copies, waits for them, and re-layouts: 81 us -> 8.69 us
  Pallas kernels: 0 us -> 47.1 us
  other arithmetic: 43.5 us -> 1.24 us
  matrix products: 17.9 us -> 0 us
  starting transfers between devices: 53.2 us -> 70.2 us
  blocking collectives: 12.8 us -> 0 us
    ppermute x10 -> x16, waiting for transfers between devices: 154 us -> 61.2 us  [the longest x1 46.9 us: body(): early_in = lax.ppermute(early, 'comp', swap)]
    scatter x2 -> x0, local copies, waits for them, and re-layouts: 53.1 us -> none  [the longest x1 50.5 us: body(): jnp.zeros((tiles * capacity, chan, width), jnp.float32).at[slot]]
    pallas_call x0 -> x7, Pallas kernels: none -> 47.1 us  [the longest x1 18.9 us: contributions(): pl.pallas_call(functools.partial(contribution_kernel, dims), in_specs=[pl...]
    dot_general x2 -> x0, matrix products: 17.9 us -> none  [the longest x1 11.8 us: body(): jnp.einsum('pts,cps->pct', weights[0], picked, preferred_element_type=jnp...]
    broadcast_in_dim x1 -> x0, other arithmetic: 16.1 us -> none  [body(): return (result[None], recv[None])]
    all_to_all x1 -> x0, blocking collectives: 12.8 us -> none  [body(): lax.all_to_all(out_ids.reshape(tiles, capacity), ('tx', 'ty'), split_axis...]
    add x1 -> x0, other arithmetic: 10 us -> none  [body(): section = start + first]
    all_to_all x1 -> x2, starting transfers between devices: 5.12 us -> 14.1 us  [exchanged(): lax.all_to_all(rows, ('tx', 'ty'), split_axis=0, concat_axis=0, tiled=True)]
  transfers between devices with their start and end apart: 11 -> 18, of which waited for: 3 -> 3; matrix products, arithmetic and copies ran while one was open for 5% -> 1% of each run, Pallas kernels for 0% -> 13%
where the time goes in v1:
time: 191 us; the launch traced here: 190 us
  starting transfers between devices  70.2 us (37%)
  waiting for transfers between devices  61.2 us (32%)
  Pallas kernels  47.1 us (25%)
  local copies, waits for them, and re-layouts  8.69 us (5%)
    ppermute x1, waiting for transfers between devices, body(): early_in = lax.ppermute(early, 'comp', swap)  46.9 us
    pallas_call x1, Pallas kernels, contributions(): pl.pallas_call(functools.partial(contribution_kernel, dims), in_specs=[pl...  18.9 us
    ppermute x1, starting transfers between devices, body(): lax.ppermute(bottom, ('comp', 'tx'), crossed('tx', 1))  16.5 us
    all_to_all x2, starting transfers between devices, exchanged(): lax.all_to_all(rows, ('tx', 'ty'), split_axis=0, concat_axis=0, tiled=True)  14.1 us
    pallas_call x1, Pallas kernels, base_of(): pl.pallas_call(base_kernel, grid=(nfield,), in_specs=[pl.BlockSpec(memory...  13.2 us
    ppermute x1, waiting for transfers between devices, body(): below = lax.ppermute(x_low, 'tx', shift_pairs(tx, -1))  10.3 us
    unnamed x32, local copies, waits for them, and re-layouts  8.61 us
    pallas_call x2, Pallas kernels, finished(): pl.pallas_call(functools.partial(finish_kernel, first), grid=(fields,), i...  8.5 us
  transfers between devices with their start and end apart: 18, of which 3 were waited for; matrix products, arithmetic and copies ran while one was open for 1% of the time, Pallas kernels for 13%

profile of v1, /device:TPU:1, one launch (start us, length us, event | category | flops | bytes accessed | tf_op | source)
XLA Modules:
  0.0 189.5 jit_solution(1504099492434275357)
XLA Ops:
  0.6 18.9 %contributions.1 = (f32[1040,4,128]{2,1,0:T(4,128)}, f32[1040,4,128]{2,1,0:T(4,128)}) custom-call(s32[1,512]{1,0:T(1,128)} %src_ref.1, s32[1,512]{1,0:T(1,128)} %bitcast.10, s32[1,512]{1,0:T(1,128)} %blk_ref.1, f32[1,16,128,512]{3,2,1,0:T(8,128)} %state_ref.3, bf16[1,512,128,128]{3,2,1,0:T(8,128)(2,1)} %weights_ref.1), custom_call_target="tpu_custom_call" | custom-call | flops 134217728 | bytes 25296896 | tf_op jit(solution)/shard_map/contributions/pallas_call | solution.py:147
  19.5 7.4 %all-to-all-start = ((f32[16,65,4,128]{3,2,1,0:T(4,128)}), f32[16,65,4,128]{3,2,1,0:T(4,128)S(1)}, u32[]{:S(2)}, u32[]{:S(2)}) async-start(f32[16,65,4,128]{3,2,1,0:T(4,128)} %bitcast.9), calls=%async_computation | async-start | bytes 4259840 | tf_op jit(solution)/shard_map/all_to_all | solution.py:522
  26.9 1.2 collective-permute-start.11
  28.1 46.9 %collective-permute-done.11 = f32[1040,4,128]{2,1,0:T(4,128)} collective-permute-done((f32[1040,4,128]{2,1,0:T(4,128)}, f32[1040,4,128]{2,1,0:T(4,128)}, u32[]{:S(2)}, u32[]{:S(2)}) %collective-permute-start.11) | collective-permute-done | bytes 2129952 | tf_op jit(solution)/shard_map/ppermute | solution.py:528
  75.0 0.0 all-to-all-done
  75.0 1.3 copy-done.4
  76.3 6.8 %all-to-all-start.1 = ((f32[16,65,4,128]{3,2,1,0:T(4,128)}), f32[16,65,4,128]{3,2,1,0:T(4,128)S(1)}, u32[]{:S(2)}, u32[]{:S(2)}) async-start(f32[16,65,4,128]{3,2,1,0:T(4,128)} %bitcast.4), calls=%async_computation.1 | async-start | bytes 4259840 | tf_op jit(solution)/shard_map/all_to_all | solution.py:522
  83.1 0.0 copy-start.3
  83.1 0.0 copy-start.5
  83.1 1.7 copy-done.5
  84.8 2.7 %sum_by_block.2 = (f32[4,128,512]{2,1,0:T(8,128)}, f32[4,512]{1,0:T(4,128)S(1)}, f32[4,512]{1,0:T(4,128)S(1)}, f32[4,128]{1,0:T(4,128)}, f32[4,128]{1,0:T(4,128)}) custom-call(f32[4160,128]{1,0:T(8,128)S(1)} %bitcast.8), custom_call_target="tpu_custom_call" | custom-call | flops 1073741824 | bytes 3145728 | tf_op jit(solution)/shard_map/sum_by_block/pallas_call | solution.py:226
  87.5 0.6 copy-done.11
  88.1 0.6 copy-done.13
  88.7 1.2 collective-permute-start.6
  89.9 0.0 copy-start
  89.9 2.2 %copy-done = f32[1,16,128,512]{3,2,1,0:T(8,128)S(1)} copy-done((f32[1,16,128,512]{3,2,1,0:T(8,128)S(1)}, f32[1,16,128,512]{3,2,1,0:T(8,128)}, u32[]{:S(2)}) %copy-start) | copy-done | bytes 4194328
  92.1 2.0 %edges.1 = (f32[40,512]{1,0:T(8,128)S(1)}, f32[40,512]{1,0:T(8,128)S(1)}, f32[40,128]{1,0:T(8,128)S(1)}, f32[40,128]{1,0:T(8,128)S(1)}) custom-call(f32[1,2]{1,0:T(1,128)S(1)} %broadcast_select_fusion.mix_ref, f32[1,16,128,512]{3,2,1,0:T(8,128)S(1)} %copy-done, f32[1,16,128,512]{3,2,1,0:T(8,128)S(1)} %copy-done, f32[1,16,128,512]{3,2,1,0:T(8,128)S(1)} %copy-done, ...), custom_call_target="tpu_custom_call" | custom-call | flops 1048576 | bytes 4194304 | tf_op jit(solution)/shard_map/edges/pallas_call | solution.py:338
  94.1 1.3 collective-permute-start.1
  95.4 2.3 %collective-permute-start.3 = (f32[40,128]{1,0:T(8,128)S(1)}, f32[40,128]{1,0:T(8,128)S(1)}, u32[]{:S(2)}, u32[]{:S(2)}) collective-permute-start(f32[40,128]{1,0:T(8,128)S(1)} %get-tuple-element.27.y_low), channel_id=1, source_target_pairs={{1,0},{2,1},{3,2},{5,4},{6,5},{7,6},{9,8},{10,9},{11,10},{13,12},{... | collective-permute-start | bytes 61448 | tf_op jit(solution)/shard_map/ppermute | solution.py:537
  97.7 3.5 %collective-permute-start.2 = (f32[40,128]{1,0:T(8,128)S(1)}, f32[40,128]{1,0:T(8,128)S(1)}, u32[]{:S(2)}, u32[]{:S(2)}) collective-permute-start(f32[40,128]{1,0:T(8,128)S(1)} %get-tuple-element.28.y_high), channel_id=1, source_target_pairs={{0,1},{1,2},{2,3},{4,5},{5,6},{6,7},{8,9},{9,10},{10,11},{12,13},{... | collective-permute-start | bytes 61448 | tf_op jit(solution)/shard_map/ppermute | solution.py:536
  101.2 4.3 %collective-permute-start = (f32[40,512]{1,0:T(8,128)S(1)}, f32[40,512]{1,0:T(8,128)S(1)}, u32[]{:S(2)}, u32[]{:S(2)}) collective-permute-start(f32[40,512]{1,0:T(8,128)S(1)} %get-tuple-element.26.x_high), channel_id=1, source_target_pairs={{0,4},{4,8},{8,12},{1,5},{5,9},{9,13},{2,6},{6,10},{10,14},{3,7},{... | collective-permute-start | bytes 245768 | tf_op jit(solution)/shard_map/ppermute | solution.py:538
  105.4 10.3 %collective-permute-done.1.below = f32[40,512]{1,0:T(8,128)S(1)} collective-permute-done((f32[40,512]{1,0:T(8,128)S(1)}, f32[40,512]{1,0:T(8,128)S(1)}, u32[]{:S(2)}, u32[]{:S(2)}) %collective-permute-start.1) | collective-permute-done | bytes 81952 | tf_op jit(solution)/shard_map/ppermute | solution.py:539
  115.7 4.0 %collective-permute-done.above = f32[40,512]{1,0:T(8,128)S(1)} collective-permute-done((f32[40,512]{1,0:T(8,128)S(1)}, f32[40,512]{1,0:T(8,128)S(1)}, u32[]{:S(2)}, u32[]{:S(2)}) %collective-permute-start) | collective-permute-done | bytes 81952 | tf_op jit(solution)/shard_map/ppermute | solution.py:538
  119.8 0.6 pad_maximum_fusion
  120.4 4.1 %collective-permute-start.4 = (f32[80,128]{1,0:T(8,128)}, f32[80,128]{1,0:T(8,128)}, u32[]{:S(2)}, u32[]{:S(2)}) collective-permute-start(f32[80,128]{1,0:T(8,128)} %pad_maximum_fusion), channel_id=1, source_target_pairs={{0,1},{1,2},{2,3},{4,5},{5,6},{6,7},{8,9},{9,10},{10,11},{12,13},{... | collective-permute-start | bytes 122888 | tf_op jit(solution)/shard_map/ppermute | solution.py:546
  124.6 0.6 pad_maximum_fusion.1
  125.2 1.9 %collective-permute-start.5 = (f32[80,128]{1,0:T(8,128)}, f32[80,128]{1,0:T(8,128)}, u32[]{:S(2)}, u32[]{:S(2)}) collective-permute-start(f32[80,128]{1,0:T(8,128)} %pad_maximum_fusion.1), channel_id=1, source_target_pairs={{1,0},{2,1},{3,2},{5,4},{6,5},{7,6},{9,8},{10,9},{11,10},{13,12},{... | collective-permute-start | bytes 122888 | tf_op jit(solution)/shard_map/ppermute | solution.py:547
  127.1 0.0 collective-permute-done.3.right.after
  127.1 4.6 %collective-permute-start.9 = (f32[4,128]{1,0:T(4,128)}, f32[4,128]{1,0:T(4,128)}, u32[]{:S(2)}, u32[]{:S(2)}) collective-permute-start(f32[4,128]{1,0:T(4,128)} %get-tuple-element.34), channel_id=1, source_target_pairs={{0,17},{1,18},{2,19},{16,1},{17,2},{18,3},{4,21},{5,22},{6,23},{20... | collective-permute-start | bytes 6152 | tf_op jit(solution)/shard_map/ppermute | solution.py:558
  131.8 0.0 collective-permute-done.2.left.before
  131.8 1.9 %collective-permute-start.10 = (f32[4,128]{1,0:T(4,128)}, f32[4,128]{1,0:T(4,128)}, u32[]{:S(2)}, u32[]{:S(2)}) collective-permute-start(f32[4,128]{1,0:T(4,128)} %get-tuple-element.35), channel_id=1, source_target_pairs={{1,16},{2,17},{3,18},{17,0},{18,1},{19,2},{5,20},{6,21},{7,22},{21... | collective-permute-start | bytes 6152 | tf_op jit(solution)/shard_map/ppermute | solution.py:559
  133.7 0.0 all-to-all-done.1
  133.8 1.8 sum_by_block.3
  135.6 0.0 collective-permute-done.4.corners_left
  135.6 16.5 %collective-permute-start.7 = (f32[4,512]{1,0:T(4,128)S(1)}, f32[4,512]{1,0:T(4,128)S(1)}, u32[]{:S(2)}, u32[]{:S(2)}) collective-permute-start(f32[4,512]{1,0:T(4,128)S(1)} %copy-done.14), channel_id=1, source_target_pairs={{0,20},{4,24},{8,28},{16,4},{20,8},{24,12},{1,21},{5,25},{9,29},{1... | collective-permute-start | bytes 24584 | tf_op jit(solution)/shard_map/ppermute | solution.py:556
  152.1 1.3 collective-permute-start.8
  153.4 0.0 collective-permute-done.9.left_ref
  153.4 4.4 %collective-permute-start.12 = (f32[4,512]{1,0:T(4,128)S(1)}, f32[4,512]{1,0:T(4,128)S(1)}, u32[]{:S(2)}, u32[]{:S(2)}) collective-permute-start(f32[4,512]{1,0:T(4,128)S(1)} %get-tuple-element.39), channel_id=1, source_target_pairs={{0,4},{4,8},{8,12},{1,5},{5,9},{9,13},{2,6},{6,10},{10,14},{3,7},{... | collective-permute-start | bytes 24584 | tf_op jit(solution)/shard_map/ppermute | solution.py:563
  157.8 1.3 collective-permute-start.13
  159.1 4.4 %collective-permute-start.14 = (f32[4,128]{1,0:T(4,128)S(1)}, f32[4,128]{1,0:T(4,128)S(1)}, u32[]{:S(2)}, u32[]{:S(2)}) collective-permute-start(f32[4,128]{1,0:T(4,128)S(1)} %get-tuple-element.41), channel_id=1, source_target_pairs={{0,1},{1,2},{2,3},{4,5},{5,6},{6,7},{8,9},{9,10},{10,11},{12,13},{... | collective-permute-start | bytes 6152 | tf_op jit(solution)/shard_map/ppermute | solution.py:565
  163.6 1.9 %collective-permute-start.15 = (f32[4,128]{1,0:T(4,128)S(1)}, f32[4,128]{1,0:T(4,128)S(1)}, u32[]{:S(2)}, u32[]{:S(2)}) collective-permute-start(f32[4,128]{1,0:T(4,128)S(1)} %get-tuple-element.42), channel_id=1, source_target_pairs={{1,0},{2,1},{3,2},{5,4},{6,5},{7,6},{9,8},{10,9},{11,10},{13,12},{... | collective-permute-start | bytes 6152 | tf_op jit(solution)/shard_map/ppermute | solution.py:566
  165.5 0.1 broadcast_in_dim.8.rates_ref
  165.6 2.2 %copy-done.1 = f32[1,16,128,512]{3,2,1,0:T(8,128)S(1)} copy-done((f32[1,16,128,512]{3,2,1,0:T(8,128)S(1)}, f32[1,16,128,512]{3,2,1,0:T(8,128)}, u32[]{:S(2)}) %copy-start.1) | copy-done | bytes 4194328
  167.8 13.2 %base.1 = (f32[1,16,128,512]{3,2,1,0:T(8,128)}, f32[6,128,512]{2,1,0:T(8,128)S(1)}) custom-call(f32[1,16]{1,0:T(1,128)S(1)} %get-tuple-element.49.rate_ref, f32[1,2]{1,0:T(1,128)S(1)} %broadcast_select_fusion.mix_ref, f32[16,128]{1,0:T(8,128)S(1)} %broadcast_in_dim.8.rates_ref, f32[1,3,128,512]{3,2,1,0:T(8,128)S(1)} %copy-done.2, s32[128,512]{1,0:T(8,128)S(1)} %copy-done.3, ...), custom_call_target="tpu_custom_call" | custom-call | flops 41943040 | bytes 8388608 | tf_op jit(solution)/shard_map/base/pallas_call | solution.py:419
  181.0 0.0 collective-permute-done.6.recv_ref
  181.0 4.4 %finish.2 = (f32[1,16,128,512]{3,2,1,0:T(8,128)}, f32[1,8,128,512]{3,2,1,0:T(8,128)}) custom-call(f32[1,8]{1,0:T(1,128)S(1)} %copy-done.10, f32[1,2]{1,0:T(1,128)S(1)} %broadcast_select_fusion.mix_ref, f32[6,128,512]{2,1,0:T(8,128)S(1)} %get-tuple-element.29.factors, f32[40,512]{1,0:T(8,128)S(1)} %collective-permute-done.above, ...), custom_call_target="tpu_custom_call", output_to_operand_aliasing={{0}: (7, {})} | custom-call | flops 5242880 | bytes 5242880 | tf_op jit(solution)/shard_map/finish/pallas_call | solution.py:488
  185.3 0.0 collective-permute-done.13.bottom_ref
  185.3 4.2 %finish.3 = (f32[1,16,128,512]{3,2,1,0:T(8,128)}, f32[1,8,128,512]{3,2,1,0:T(8,128)}) custom-call(f32[1,8]{1,0:T(1,128)S(1)} %copy-done.10, f32[1,2]{1,0:T(1,128)S(1)} %broadcast_select_fusion.mix_ref, f32[6,128,512]{2,1,0:T(8,128)S(1)} %get-tuple-element.29.factors, ...), custom_call_target="tpu_custom_call", output_to_operand_aliasing={{0}: (7, {}), {1}: (13, {})} | custom-call | flops 5242880 | bytes 5242880 | tf_op jit(solution)/shard_map/finish/pallas_call | solution.py:488
  (34 shorter events, 0.1 us)
Async XLA Ops:
  19.5 55.5 %all-to-all-start = ((f32[16,65,4,128]{3,2,1,0:T(4,128)}), f32[16,65,4,128]{3,2,1,0:T(4,128)S(1)}, u32[]{:S(2)}, u32[]{:S(2)}) async-start(f32[16,65,4,128]{3,2,1,0:T(4,128)} %bitcast.9), calls=%async_computation | async-start | bytes 4259840 | tf_op jit(solution)/shard_map/all_to_all | solution.py:522
  26.9 48.1 %collective-permute-start.11 = (f32[1040,4,128]{2,1,0:T(4,128)}, f32[1040,4,128]{2,1,0:T(4,128)}, u32[]{:S(2)}, u32[]{:S(2)}) collective-permute-start(f32[1040,4,128]{2,1,0:T(4,128)} %get-tuple-element.37), channel_id=1, source_target_pairs={{0,16},{16,0},{1,17},{17,1},{2,18},{18,2},{3,19},{19,3},{4,20},{20... | collective-permute-start | bytes 6389768 | tf_op jit(solution)/shard_map/ppermute | solution.py:528
  75.0 1.3 copy-start.4
  76.3 13.6 %copy-start.15 = (f32[1,2]{1,0:T(1,128)S(1)}, f32[1,2]{1,0:T(1,128)}, u32[]{:S(2)}) copy-start(f32[1,2]{1,0:T(1,128)} %constant.14.clone) | copy-start | bytes 28
  76.3 57.4 %all-to-all-start.1 = ((f32[16,65,4,128]{3,2,1,0:T(4,128)}), f32[16,65,4,128]{3,2,1,0:T(4,128)S(1)}, u32[]{:S(2)}, u32[]{:S(2)}) async-start(f32[16,65,4,128]{3,2,1,0:T(4,128)} %bitcast.4), calls=%async_computation.1 | async-start | bytes 4259840 | tf_op jit(solution)/shard_map/all_to_all | solution.py:522
  83.1 6.8 %copy-start.2 = (f32[1,3,128,512]{3,2,1,0:T(8,128)S(1)}, f32[1,3,128,512]{3,2,1,0:T(8,128)}, u32[]{:S(2)}) copy-start(f32[1,3,128,512]{3,2,1,0:T(8,128)} %coefs_ref.1) | copy-start | bytes 2359300
  83.1 6.8 %copy-start.3 = (s32[128,512]{1,0:T(8,128)S(1)}, s32[128,512]{1,0:T(8,128)}, u32[]{:S(2)}) copy-start(s32[128,512]{1,0:T(8,128)} %land_ref) | copy-start | bytes 786436
  83.1 1.7 copy-start.5
  87.5 0.6 copy-start.11
  88.1 0.6 copy-start.13
  88.7 92.3 %collective-permute-start.6 = (f32[4,128,512]{2,1,0:T(8,128)}, f32[4,128,512]{2,1,0:T(8,128)}, u32[]{:S(2)}, u32[]{:S(2)}) collective-permute-start(f32[4,128,512]{2,1,0:T(8,128)} %get-tuple-element.31), channel_id=1, source_target_pairs={{0,16},{16,0},{1,17},{17,1},{2,18},{18,2},{3,19},{19,3},{4,20},{20... | collective-permute-start | bytes 3145736 | tf_op jit(solution)/shard_map/ppermute | solution.py:554
  89.9 2.2 %copy-start = (f32[1,16,128,512]{3,2,1,0:T(8,128)S(1)}, f32[1,16,128,512]{3,2,1,0:T(8,128)}, u32[]{:S(2)}) copy-start(f32[1,16,128,512]{3,2,1,0:T(8,128)} %state_ref.3) | copy-start | bytes 12582916
  94.1 37.6 %copy-start.6 = (f32[40,128]{1,0:T(8,128)}, f32[40,128]{1,0:T(8,128)S(1)}, u32[]{:S(2)}) copy-start(f32[40,128]{1,0:T(8,128)S(1)} %get-tuple-element.27.y_low) | copy-start | bytes 61444
  94.1 37.7 %copy-start.8 = (f32[40,128]{1,0:T(8,128)}, f32[40,128]{1,0:T(8,128)S(1)}, u32[]{:S(2)}) copy-start(f32[40,128]{1,0:T(8,128)S(1)} %get-tuple-element.28.y_high) | copy-start | bytes 61444
  94.1 21.6 %collective-permute-start.1 = (f32[40,512]{1,0:T(8,128)S(1)}, f32[40,512]{1,0:T(8,128)S(1)}, u32[]{:S(2)}, u32[]{:S(2)}) collective-permute-start(f32[40,512]{1,0:T(8,128)S(1)} %get-tuple-element.25.x_low), channel_id=1, source_target_pairs={{4,0},{8,4},{12,8},{5,1},{9,5},{13,9},{6,2},{10,6},{14,10},{7,3},{... | collective-permute-start | bytes 245768 | tf_op jit(solution)/shard_map/ppermute | solution.py:539
  95.4 31.7 %collective-permute-start.3 = (f32[40,128]{1,0:T(8,128)S(1)}, f32[40,128]{1,0:T(8,128)S(1)}, u32[]{:S(2)}, u32[]{:S(2)}) collective-permute-start(f32[40,128]{1,0:T(8,128)S(1)} %get-tuple-element.27.y_low), channel_id=1, source_target_pairs={{1,0},{2,1},{3,2},{5,4},{6,5},{7,6},{9,8},{10,9},{11,10},{13,12},{... | collective-permute-start | bytes 61448 | tf_op jit(solution)/shard_map/ppermute | solution.py:537
  97.7 34.0 %collective-permute-start.2 = (f32[40,128]{1,0:T(8,128)S(1)}, f32[40,128]{1,0:T(8,128)S(1)}, u32[]{:S(2)}, u32[]{:S(2)}) collective-permute-start(f32[40,128]{1,0:T(8,128)S(1)} %get-tuple-element.28.y_high), channel_id=1, source_target_pairs={{0,1},{1,2},{2,3},{4,5},{5,6},{6,7},{8,9},{9,10},{10,11},{12,13},{... | collective-permute-start | bytes 61448 | tf_op jit(solution)/shard_map/ppermute | solution.py:536
  101.2 18.6 %collective-permute-start = (f32[40,512]{1,0:T(8,128)S(1)}, f32[40,512]{1,0:T(8,128)S(1)}, u32[]{:S(2)}, u32[]{:S(2)}) collective-permute-start(f32[40,512]{1,0:T(8,128)S(1)} %get-tuple-element.26.x_high), channel_id=1, source_target_pairs={{0,4},{4,8},{8,12},{1,5},{5,9},{9,13},{2,6},{6,10},{10,14},{3,7},{... | collective-permute-start | bytes 245768 | tf_op jit(solution)/shard_map/ppermute | solution.py:538
  115.7 43.4 %copy-start.10 = (f32[1,8]{1,0:T(1,128)S(1)}, f32[1,8]{1,0:T(1,128)}, u32[]{:S(2)}) copy-start(f32[1,8]{1,0:T(1,128)} %gamma_ref.3) | copy-start | bytes 100
  120.4 15.2 %collective-permute-start.4 = (f32[80,128]{1,0:T(8,128)}, f32[80,128]{1,0:T(8,128)}, u32[]{:S(2)}, u32[]{:S(2)}) collective-permute-start(f32[80,128]{1,0:T(8,128)} %pad_maximum_fusion), channel_id=1, source_target_pairs={{0,1},{1,2},{2,3},{4,5},{5,6},{6,7},{8,9},{9,10},{10,11},{12,13},{... | collective-permute-start | bytes 122888 | tf_op jit(solution)/shard_map/ppermute | solution.py:546
  125.2 26.9 %collective-permute-start.5 = (f32[80,128]{1,0:T(8,128)}, f32[80,128]{1,0:T(8,128)}, u32[]{:S(2)}, u32[]{:S(2)}) collective-permute-start(f32[80,128]{1,0:T(8,128)} %pad_maximum_fusion.1), channel_id=1, source_target_pairs={{1,0},{2,1},{3,2},{5,4},{6,5},{7,6},{9,8},{10,9},{11,10},{13,12},{... | collective-permute-start | bytes 122888 | tf_op jit(solution)/shard_map/ppermute | solution.py:547
  127.1 26.3 %collective-permute-start.9 = (f32[4,128]{1,0:T(4,128)}, f32[4,128]{1,0:T(4,128)}, u32[]{:S(2)}, u32[]{:S(2)}) collective-permute-start(f32[4,128]{1,0:T(4,128)} %get-tuple-element.34), channel_id=1, source_target_pairs={{0,17},{1,18},{2,19},{16,1},{17,2},{18,3},{4,21},{5,22},{6,23},{20... | collective-permute-start | bytes 6152 | tf_op jit(solution)/shard_map/ppermute | solution.py:558
  131.8 26.0 %collective-permute-start.10 = (f32[4,128]{1,0:T(4,128)}, f32[4,128]{1,0:T(4,128)}, u32[]{:S(2)}, u32[]{:S(2)}) collective-permute-start(f32[4,128]{1,0:T(4,128)} %get-tuple-element.35), channel_id=1, source_target_pairs={{1,16},{2,17},{3,18},{17,0},{18,1},{19,2},{5,20},{6,21},{7,22},{21... | collective-permute-start | bytes 6152 | tf_op jit(solution)/shard_map/ppermute | solution.py:559
  133.7 1.9 copy-start.14
  133.7 18.4 %copy-start.12 = (f32[4,512]{1,0:T(4,128)S(1)}, f32[4,512]{1,0:T(4,128)}, u32[]{:S(2)}) copy-start(f32[4,512]{1,0:T(4,128)} %copy-done.11) | copy-start | bytes 24580
  133.7 31.8 %copy-start.7 = (f32[40,128]{1,0:T(8,128)S(1)}, f32[40,128]{1,0:T(8,128)}, u32[]{:S(2)}) copy-start(f32[40,128]{1,0:T(8,128)} %copy-done.6) | copy-start | bytes 61444
  133.8 31.8 %copy-start.9 = (f32[40,128]{1,0:T(8,128)S(1)}, f32[40,128]{1,0:T(8,128)}, u32[]{:S(2)}) copy-start(f32[40,128]{1,0:T(8,128)} %copy-done.8) | copy-start | bytes 61444
  135.6 23.5 %collective-permute-start.7 = (f32[4,512]{1,0:T(4,128)S(1)}, f32[4,512]{1,0:T(4,128)S(1)}, u32[]{:S(2)}, u32[]{:S(2)}) collective-permute-start(f32[4,512]{1,0:T(4,128)S(1)} %copy-done.14), channel_id=1, source_target_pairs={{0,20},{4,24},{8,28},{16,4},{20,8},{24,12},{1,21},{5,25},{9,29},{1... | collective-permute-start | bytes 24584 | tf_op jit(solution)/shard_map/ppermute | solution.py:556
  152.1 11.5 %collective-permute-start.8 = (f32[4,512]{1,0:T(4,128)S(1)}, f32[4,512]{1,0:T(4,128)S(1)}, u32[]{:S(2)}, u32[]{:S(2)}) collective-permute-start(f32[4,512]{1,0:T(4,128)S(1)} %copy-done.12), channel_id=1, source_target_pairs={{4,16},{8,20},{12,24},{20,0},{24,4},{28,8},{5,17},{9,21},{13,25},{... | collective-permute-start | bytes 24584 | tf_op jit(solution)/shard_map/ppermute | solution.py:557
  153.4 31.9 %collective-permute-start.12 = (f32[4,512]{1,0:T(4,128)S(1)}, f32[4,512]{1,0:T(4,128)S(1)}, u32[]{:S(2)}, u32[]{:S(2)}) collective-permute-start(f32[4,512]{1,0:T(4,128)S(1)} %get-tuple-element.39), channel_id=1, source_target_pairs={{0,4},{4,8},{8,12},{1,5},{5,9},{9,13},{2,6},{6,10},{10,14},{3,7},{... | collective-permute-start | bytes 24584 | tf_op jit(solution)/shard_map/ppermute | solution.py:563
  157.8 27.6 %collective-permute-start.13 = (f32[4,512]{1,0:T(4,128)S(1)}, f32[4,512]{1,0:T(4,128)S(1)}, u32[]{:S(2)}, u32[]{:S(2)}) collective-permute-start(f32[4,512]{1,0:T(4,128)S(1)} %get-tuple-element.40), channel_id=1, source_target_pairs={{4,0},{8,4},{12,8},{5,1},{9,5},{13,9},{6,2},{10,6},{14,10},{7,3},{... | collective-permute-start | bytes 24584 | tf_op jit(solution)/shard_map/ppermute | solution.py:564
  159.1 26.2 %collective-permute-start.14 = (f32[4,128]{1,0:T(4,128)S(1)}, f32[4,128]{1,0:T(4,128)S(1)}, u32[]{:S(2)}, u32[]{:S(2)}) collective-permute-start(f32[4,128]{1,0:T(4,128)S(1)} %get-tuple-element.41), channel_id=1, source_target_pairs={{0,1},{1,2},{2,3},{4,5},{5,6},{6,7},{8,9},{9,10},{10,11},{12,13},{... | collective-permute-start | bytes 6152 | tf_op jit(solution)/shard_map/ppermute | solution.py:565
  163.6 21.7 %collective-permute-start.15 = (f32[4,128]{1,0:T(4,128)S(1)}, f32[4,128]{1,0:T(4,128)S(1)}, u32[]{:S(2)}, u32[]{:S(2)}) collective-permute-start(f32[4,128]{1,0:T(4,128)S(1)} %get-tuple-element.42), channel_id=1, source_target_pairs={{1,0},{2,1},{3,2},{5,4},{6,5},{7,6},{9,8},{10,9},{11,10},{13,12},{... | collective-permute-start | bytes 6152 | tf_op jit(solution)/shard_map/ppermute | solution.py:566
  165.6 2.2 %copy-start.1 = (f32[1,16,128,512]{3,2,1,0:T(8,128)S(1)}, f32[1,16,128,512]{3,2,1,0:T(8,128)}, u32[]{:S(2)}) copy-start(f32[1,16,128,512]{3,2,1,0:T(8,128)} %state_ref.3) | copy-start | bytes 12582916

commit v2 on v1

--- a/solution.py
+++ b/solution.py
@@ -26,8 +26,8 @@
 def contribution_kernel(dims, src_ref, dev_ref, blk_ref, state_ref, weights_ref, *rest):
     tiles, capacity, pairs, fields, cells_x, cells_y, width, chunks = dims
     outs = rest[: len(chunks)]
-    cells, left_ref, product, w_ref, place_v, place_s = rest[len(chunks) : len(chunks) + 6]
-    field_sems, weight_sems, place_sem = rest[len(chunks) + 6 :]
+    cells, left_ref, w_ref, pair_v, place_v, place_s = rest[len(chunks) : len(chunks) + 6]
+    field_sems, weight_sems, pair_sems, place_sem = rest[len(chunks) + 6 :]
     parts = cells_y // width
     steps = pairs // STEP_PAIRS
 
@@ -47,12 +47,18 @@
             weights_ref.at[0, some], w_ref.at[some], weight_sems.at[step]
         )
 
-    for copy in field_copies:
+    pair_copies = [
+        pltpu.make_async_copy(ref, pair_v.at[i], pair_sems.at[i])
+        for i, ref in enumerate((src_ref, dev_ref, blk_ref))
+    ]
+    for copy in pair_copies + field_copies:
         copy.start()
     for step in range(steps):
         weight_copy(step).start()
-
-    dev = dev_ref[...]
+    for copy in pair_copies:
+        copy.wait()
+
+    src, dev, blk = pair_v[0], pair_v[1], pair_v[2]
     tile_of = lax.broadcasted_iota(jnp.int32, (tiles, pairs), 0)
     lane_of = lax.broadcasted_iota(jnp.int32, (tiles, pairs), 1)
     member = (tile_of == dev).astype(jnp.float32)
@@ -62,7 +68,6 @@
         total = total + jnp.where(lane_of >= shift, pltpu.roll(total, shift, 1), 0.0)
         shift *= 2
     rank = (jnp.sum(member * total, axis=0, keepdims=True) - 1.0).astype(jnp.int32)
-    src = src_ref[...]
     place_v[0:1, :] = dev * (capacity + 1) + rank
     place_v[1:2, :] = (src % parts) * (fields * cells_x) + src // parts
     to_scalars = pltpu.make_async_copy(place_v, place_s, place_sem)
@@ -72,7 +77,6 @@
         out[...] = jnp.zeros_like(out)
     slot_of = lax.broadcasted_iota(jnp.int32, (LANES, pairs), 0) % capacity
     chosen = (slot_of == rank).astype(jnp.bfloat16)
-    blk = blk_ref[...]
 
     def spread(values):
         return lax.dot_general(
@@ -90,50 +94,35 @@
     for copy in field_copies:
         copy.wait()
 
-    zeros = jnp.zeros((fields, width), jnp.float32)
-
-    def cells_of(p):
-        return cells[pl.ds(place_s[1, p], fields, stride=cells_x), :]
+    group = LANES // fields
+    lane = lax.broadcasted_iota(jnp.int32, (width, LANES), 1) // fields
 
     def gather(step, carry):
-        for i in range(0, STEP_PAIRS, 2):
+        for i in range(STEP_PAIRS):
             p = step * STEP_PAIRS + i
-            one = jnp.concatenate([cells_of(p), zeros], axis=1)
-            two = jnp.concatenate([zeros, cells_of(p + 1)], axis=1)
-            rows = pl.ds(pl.multiple_of(p * fields, 2 * fields), 2 * fields)
-            left_ref[rows, :] = jnp.concatenate([one, two], axis=0).astype(jnp.bfloat16)
+            rows = pl.ds(pl.multiple_of(p * fields, fields), fields)
+            left_ref[rows, :] = cells[pl.ds(place_s[1, p], fields, stride=cells_x), :]
         return carry
 
     def multiply(step, carry):
         weight_copy(step).wait()
-        for i in range(0, STEP_PAIRS, 4):
-            p = step * STEP_PAIRS + i
-            rows = pl.ds(pl.multiple_of(p * fields, 4 * fields), 4 * fields)
-            w = [w_ref[p + j] for j in range(4)]
-            right = jnp.concatenate(
-                [jnp.concatenate(w[0:2], axis=1), jnp.concatenate(w[2:4], axis=1)], axis=0
-            )
-            four = lax.dot_general(
-                left_ref[rows, :], right, NT, preferred_element_type=jnp.float32
-            )
-            low = pl.ds(pl.multiple_of(p * fields, 2 * fields), 2 * fields)
-            high = pl.ds(pl.multiple_of((p + 2) * fields, 2 * fields), 2 * fields)
-            product[low, :] = four[: 2 * fields, :width]
-            product[high, :] = four[2 * fields :, width:]
-        return carry
-
-    def scatter(step, carry):
-        for i in range(STEP_PAIRS):
-            p = step * STEP_PAIRS + i
-            slot = place_s[0, p]
-            one = product[pl.ds(pl.multiple_of(p * fields, fields), fields), :]
-            for out, (first, last) in zip(outs, chunks):
-                out[slot] = one[first:last]
+        for first_pair in range(0, STEP_PAIRS, group):
+            p = step * STEP_PAIRS + first_pair
+            rows = pl.ds(pl.multiple_of(p * fields, LANES), LANES)
+            right = left_ref[rows, :].T.astype(jnp.bfloat16)
+            kept = None
+            for j in range(group):
+                one = jnp.dot(w_ref[p + j], right, preferred_element_type=jnp.float32)
+                kept = one if kept is None else jnp.where(lane == j, one, kept)
+            kept = kept.T
+            for j in range(group):
+                slot = place_s[0, p + j]
+                for out, (first, last) in zip(outs, chunks):
+                    out[slot] = kept[j * fields + first : j * fields + last]
         return carry
 
     lax.fori_loop(0, steps, gather, 0)
     lax.fori_loop(0, steps, multiply, 0)
-    lax.fori_loop(0, steps, scatter, 0)
 
 
 def contributions(state, pair_src, pair_dev, pair_blk, weights, tiles, capacity, chunks):
@@ -146,19 +135,19 @@
     shapes = [(rows, last - first, width) for first, last in chunks]
     return pl.pallas_call(
         functools.partial(contribution_kernel, dims),
-        in_specs=[pl.BlockSpec(memory_space=pltpu.VMEM)] * 3
-        + [pl.BlockSpec(memory_space=pltpu.HBM)] * 2,
+        in_specs=[pl.BlockSpec(memory_space=pltpu.HBM)] * 5,
         out_specs=[pl.BlockSpec(memory_space=pltpu.VMEM) for _ in shapes],
         out_shape=[jax.ShapeDtypeStruct(shape, jnp.float32) for shape in shapes],
         scratch_shapes=[
             pltpu.VMEM((parts * fields * cells_x, width), jnp.float32),
-            pltpu.VMEM((pairs * fields, 2 * width), jnp.bfloat16),
             pltpu.VMEM((pairs * fields, width), jnp.float32),
             pltpu.VMEM((pairs, width, width), jnp.bfloat16),
+            pltpu.VMEM((3, 1, pairs), jnp.int32),
             pltpu.VMEM((8, pairs), jnp.int32),
             pltpu.SMEM((8, pairs), jnp.int32),
             pltpu.SemaphoreType.DMA((parts * fields,)),
             pltpu.SemaphoreType.DMA((pairs // STEP_PAIRS,)),
+            pltpu.SemaphoreType.DMA((3,)),
             pltpu.SemaphoreType.DMA,
         ],
         compiler_params=pltpu.CompilerParams(vmem_limit_bytes=56 * 1024 * 1024),
@@ -537,8 +526,10 @@
     right = lax.ppermute(y_low, "ty", shift_pairs(ty, -1))
     above = lax.ppermute(x_high, "tx", shift_pairs(tx, 1))
     below = lax.ppermute(x_low, "tx", shift_pairs(tx, -1))
+    early_in, above, below, left, right = lax.optimization_barrier(
+        (early_in, above, below, left, right)
+    )
     received = (above, below, left, right)
-
     early_in = exchanged(early_in)
 
     ends = jnp.concatenate([above[:, cells_y - LANES :], below[:, cells_y - LANES :]], axis=0)
@@ -558,6 +549,7 @@
         lax.ppermute(right, ("comp", "ty"), crossed("ty", 1)),
         lax.ppermute(left, ("comp", "ty"), crossed("ty", -1)),
     )
+    early_in, factors = lax.optimization_barrier((early_in, factors))
     recv_early, top, bottom, left, right = add_up(early_in)
     rims_early = (
         lax.ppermute(bottom, "tx", shift_pairs(tx, 1)),

time: 191 us -> 153 us (0.80)
  waiting for transfers between devices: 61.2 us -> 42 us
  starting transfers between devices: 70.2 us -> 58.1 us
  local copies, waits for them, and re-layouts: 8.69 us -> 3.49 us
    ppermute x1, waiting for transfers between devices: 46.9 us -> 11.4 us  [body(): early_in = lax.ppermute(early, 'comp', swap)]
    ppermute x1, starting transfers between devices: 16.5 us -> 2.61 us  [body(): lax.ppermute(bottom, ('comp', 'tx'), crossed('tx', 1))]
    ppermute x1, waiting for transfers between devices: 10.3 us -> 0.01 us  [body(): below = lax.ppermute(x_low, 'tx', shift_pairs(tx, -1))]
    ppermute x1, waiting for transfers between devices: 4.04 us -> 13.7 us  [body(): above = lax.ppermute(x_high, 'tx', shift_pairs(tx, 1))]
    all_to_all x2, waiting for transfers between devices: 0.01 us -> 6.71 us  [exchanged(): lax.all_to_all(rows, ('tx', 'ty'), split_axis=0, concat_axis=0, tiled=True)]
    ppermute x1, waiting for transfers between devices: 0.01 us -> 5.91 us  [body(): right = lax.ppermute(y_low, 'ty', shift_pairs(ty, -1))]
    unnamed x32 -> x20, local copies, waits for them, and re-layouts: 8.61 us -> 3.41 us
    ppermute x1, waiting for transfers between devices: 0.01 us -> 4.13 us  [body(): corners_right = lax.ppermute(starts, 'ty', shift_pairs(ty, -1))]
  transfers between devices with their start and end apart: 18 -> 18, of which waited for: 3 -> 6; matrix products, arithmetic and copies ran while one was open for 1% -> 0% of each run, Pallas kernels for 13% -> 16%
where the time goes in v2:
time: 153 us; the launch traced here: 152 us
  starting transfers between devices  58.1 us (38%)
  Pallas kernels  47.7 us (31%)
  waiting for transfers between devices  42 us (27%)
  local copies, waits for them, and re-layouts  3.49 us (2%)
    pallas_call x1, Pallas kernels, contributions(): pl.pallas_call(functools.partial(contribution_kernel, dims), in_specs=[pl...  19.2 us
    all_to_all x2, starting transfers between devices, exchanged(): lax.all_to_all(rows, ('tx', 'ty'), split_axis=0, concat_axis=0, tiled=True)  14.1 us
    ppermute x1, waiting for transfers between devices, body(): above = lax.ppermute(x_high, 'tx', shift_pairs(tx, 1))  13.7 us
    pallas_call x1, Pallas kernels, base_of(): pl.pallas_call(base_kernel, grid=(nfield,), in_specs=[pl.BlockSpec(memory...  12 us
    ppermute x1, waiting for transfers between devices, body(): early_in = lax.ppermute(early, 'comp', swap)  11.4 us
    pallas_call x2, Pallas kernels, finished(): pl.pallas_call(functools.partial(finish_kernel, first), grid=(fields,), i...  8.35 us
    ppermute x1, starting transfers between devices, body(): lax.ppermute(bottom, 'tx', shift_pairs(tx, 1))  7.83 us
    all_to_all x2, waiting for transfers between devices, exchanged(): lax.all_to_all(rows, ('tx', 'ty'), split_axis=0, concat_axis=0, tiled=True)  6.71 us
  transfers between devices with their start and end apart: 18, of which 6 were waited for; matrix products, arithmetic and copies ran while one was open for 0% of the time, Pallas kernels for 16%

profile of v2, /device:TPU:1, one launch (start us, length us, event | category | flops | bytes accessed | tf_op | source)
XLA Modules:
  0.0 152.3 jit_solution(13771118809436348460)
XLA Ops:
  0.6 19.2 %contributions.1 = (f32[1040,4,128]{2,1,0:T(4,128)}, f32[1040,4,128]{2,1,0:T(4,128)}) custom-call(s32[1,512]{1,0:T(1,128)} %src_ref.1, s32[1,512]{1,0:T(1,128)} %bitcast.9, s32[1,512]{1,0:T(1,128)} %blk_ref.1, f32[1,16,128,512]{3,2,1,0:T(8,128)} %state_ref.3, bf16[1,512,128,128]{3,2,1,0:T(8,128)(2,1)} %weights_ref.1), custom_call_target="tpu_custom_call" | custom-call | flops 134217728 | bytes 25296896 | tf_op jit(solution)/shard_map/contributions/pallas_call | solution.py:136
  19.9 0.0 copy-start.9
  19.9 0.0 copy-start.2
  19.9 0.0 copy-start.3
  19.9 7.5 %all-to-all-start.1 = ((f32[16,65,4,128]{3,2,1,0:T(4,128)}), f32[16,65,4,128]{3,2,1,0:T(4,128)S(1)}, u32[]{:S(2)}, u32[]{:S(2)}) async-start(f32[16,65,4,128]{3,2,1,0:T(4,128)} %bitcast.8), calls=%async_computation.1 | async-start | bytes 4259840 | tf_op jit(solution)/shard_map/all_to_all | solution.py:511
  27.4 1.2 collective-permute-start
  28.6 0.0 copy-start
  28.6 2.2 %copy-done = f32[1,16,128,512]{3,2,1,0:T(8,128)S(1)} copy-done((f32[1,16,128,512]{3,2,1,0:T(8,128)S(1)}, f32[1,16,128,512]{3,2,1,0:T(8,128)}, u32[]{:S(2)}) %copy-start) | copy-done | bytes 4194328
  30.8 2.0 %edges.1 = (f32[40,512]{1,0:T(8,128)S(1)}, f32[40,512]{1,0:T(8,128)S(1)}, f32[40,128]{1,0:T(8,128)S(1)}, f32[40,128]{1,0:T(8,128)S(1)}) custom-call(f32[1,2]{1,0:T(1,128)S(1)} %broadcast_select_fusion.mix_ref, f32[1,16,128,512]{3,2,1,0:T(8,128)S(1)} %copy-done, f32[1,16,128,512]{3,2,1,0:T(8,128)S(1)} %copy-done, f32[1,16,128,512]{3,2,1,0:T(8,128)S(1)} %copy-done, ...), custom_call_target="tpu_custom_call" | custom-call | flops 1048576 | bytes 4194304 | tf_op jit(solution)/shard_map/edges/pallas_call | solution.py:327
  32.8 3.3 %collective-permute-start.1 = (f32[40,512]{1,0:T(8,128)S(1)}, f32[40,512]{1,0:T(8,128)S(1)}, u32[]{:S(2)}, u32[]{:S(2)}) collective-permute-start(f32[40,512]{1,0:T(8,128)S(1)} %get-tuple-element.33.x_high), channel_id=1, source_target_pairs={{0,4},{4,8},{8,12},{1,5},{5,9},{9,13},{2,6},{6,10},{10,14},{3,7},{... | collective-permute-start | bytes 245768 | tf_op jit(solution)/shard_map/ppermute | solution.py:527
  36.1 1.3 collective-permute-start.2
  37.4 3.9 %collective-permute-start.3 = (f32[40,128]{1,0:T(8,128)S(1)}, f32[40,128]{1,0:T(8,128)S(1)}, u32[]{:S(2)}, u32[]{:S(2)}) collective-permute-start(f32[40,128]{1,0:T(8,128)S(1)} %get-tuple-element.35.y_high), channel_id=1, source_target_pairs={{0,1},{1,2},{2,3},{4,5},{5,6},{6,7},{8,9},{9,10},{10,11},{12,13},{... | collective-permute-start | bytes 61448 | tf_op jit(solution)/shard_map/ppermute | solution.py:525
  41.3 0.6 copy-done.6
  41.9 1.9 %collective-permute-start.4 = (f32[40,128]{1,0:T(8,128)S(1)}, f32[40,128]{1,0:T(8,128)S(1)}, u32[]{:S(2)}, u32[]{:S(2)}) collective-permute-start(f32[40,128]{1,0:T(8,128)S(1)} %get-tuple-element.36.y_low), channel_id=1, source_target_pairs={{1,0},{2,1},{3,2},{5,4},{6,5},{7,6},{9,8},{10,9},{11,10},{13,12},{... | collective-permute-start | bytes 61448 | tf_op jit(solution)/shard_map/ppermute | solution.py:526
  43.8 0.6 copy-done.4
  44.4 0.0 collective-permute-done.3.left.before
  44.4 5.9 %collective-permute-done.4.right.after = f32[40,128]{1,0:T(8,128)S(1)} collective-permute-done((f32[40,128]{1,0:T(8,128)S(1)}, f32[40,128]{1,0:T(8,128)S(1)}, u32[]{:S(2)}, u32[]{:S(2)}) %collective-permute-start.4) | collective-permute-done | bytes 20512 | tf_op jit(solution)/shard_map/ppermute | solution.py:526
  50.3 13.7 %collective-permute-done.1.above = f32[40,512]{1,0:T(8,128)S(1)} collective-permute-done((f32[40,512]{1,0:T(8,128)S(1)}, f32[40,512]{1,0:T(8,128)S(1)}, u32[]{:S(2)}, u32[]{:S(2)}) %collective-permute-start.1) | collective-permute-done | bytes 81952 | tf_op jit(solution)/shard_map/ppermute | solution.py:527
  64.1 0.0 collective-permute-done.2.below
  64.1 11.4 %collective-permute-done = f32[1040,4,128]{2,1,0:T(4,128)} collective-permute-done((f32[1040,4,128]{2,1,0:T(4,128)}, f32[1040,4,128]{2,1,0:T(4,128)}, u32[]{:S(2)}, u32[]{:S(2)}) %collective-permute-start) | collective-permute-done | bytes 2129952 | tf_op jit(solution)/shard_map/ppermute | solution.py:517
  75.5 0.0 all-to-all-done.1
  75.5 6.6 %all-to-all-start = ((f32[16,65,4,128]{3,2,1,0:T(4,128)}), f32[16,65,4,128]{3,2,1,0:T(4,128)}, u32[]{:S(2)}, u32[]{:S(2)}) async-start(f32[16,65,4,128]{3,2,1,0:T(4,128)} %bitcast.1), calls=%async_computation | async-start | bytes 4259840 | tf_op jit(solution)/shard_map/all_to_all | solution.py:511
  82.1 0.0 copy-start.1
  82.1 2.7 %sum_by_block.2 = (f32[4,128,512]{2,1,0:T(8,128)}, f32[4,512]{1,0:T(4,128)}, f32[4,512]{1,0:T(4,128)}, f32[4,128]{1,0:T(4,128)}, f32[4,128]{1,0:T(4,128)}) custom-call(f32[4160,128]{1,0:T(8,128)S(1)} %bitcast.7), custom_call_target="tpu_custom_call" | custom-call | flops 1073741824 | bytes 3145728 | tf_op jit(solution)/shard_map/sum_by_block/pallas_call | solution.py:215
  84.8 1.2 collective-permute-start.7
  86.1 3.8 %collective-permute-start.5 = (f32[80,128]{1,0:T(8,128)S(1)}, f32[80,128]{1,0:T(8,128)S(1)}, u32[]{:S(2)}, u32[]{:S(2)}) collective-permute-start(f32[80,128]{1,0:T(8,128)S(1)} %pad_maximum_fusion), channel_id=1, source_target_pairs={{0,1},{1,2},{2,3},{4,5},{5,6},{6,7},{8,9},{9,10},{10,11},{12,13},{... | collective-permute-start | bytes 122888 | tf_op jit(solution)/shard_map/ppermute | solution.py:537
  89.9 1.9 %collective-permute-start.6 = (f32[80,128]{1,0:T(8,128)S(1)}, f32[80,128]{1,0:T(8,128)S(1)}, u32[]{:S(2)}, u32[]{:S(2)}) collective-permute-start(f32[80,128]{1,0:T(8,128)S(1)} %pad_maximum_fusion.1), channel_id=1, source_target_pairs={{1,0},{2,1},{3,2},{5,4},{6,5},{7,6},{9,8},{10,9},{11,10},{13,12},{... | collective-permute-start | bytes 122888 | tf_op jit(solution)/shard_map/ppermute | solution.py:538
  91.9 0.1 collective-permute-done.5.corners_left
  91.9 4.1 %collective-permute-done.6.corners_right = f32[80,128]{1,0:T(8,128)S(1)} collective-permute-done((f32[80,128]{1,0:T(8,128)S(1)}, f32[80,128]{1,0:T(8,128)S(1)}, u32[]{:S(2)}, u32[]{:S(2)}) %collective-permute-start.6) | collective-permute-done | bytes 40992 | tf_op jit(solution)/shard_map/ppermute | solution.py:538
  96.1 0.1 broadcast_in_dim.8.rates_ref
  96.2 12.0 %base.1 = (f32[1,16,128,512]{3,2,1,0:T(8,128)}, f32[6,128,512]{2,1,0:T(8,128)S(1)}) custom-call(f32[1,16]{1,0:T(1,128)S(1)} %get-tuple-element.63.rate_ref, f32[1,2]{1,0:T(1,128)S(1)} %broadcast_select_fusion.mix_ref, f32[16,128]{1,0:T(8,128)S(1)} %broadcast_in_dim.8.rates_ref, f32[1,3,128,512]{3,2,1,0:T(8,128)S(1)} %copy-done.2, s32[128,512]{1,0:T(8,128)S(1)} %copy-done.3, ...), custom_call_target="tpu_custom_call" | custom-call | flops 41943040 | bytes 8388608 | tf_op jit(solution)/shard_map/base/pallas_call | solution.py:408
  108.2 1.9 %collective-permute-start.10 = (f32[4,128]{1,0:T(4,128)}, f32[4,128]{1,0:T(4,128)S(1)}, u32[]{:S(2)}, u32[]{:S(2)}) collective-permute-start(f32[4,128]{1,0:T(4,128)} %get-tuple-element.48), channel_id=1, source_target_pairs={{0,17},{1,18},{2,19},{16,1},{17,2},{18,3},{4,21},{5,22},{6,23},{20... | collective-permute-start | bytes 6152 | tf_op jit(solution)/shard_map/ppermute | solution.py:549
  110.1 3.6 %collective-permute-start.11 = (f32[4,128]{1,0:T(4,128)}, f32[4,128]{1,0:T(4,128)S(1)}, u32[]{:S(2)}, u32[]{:S(2)}) collective-permute-start(f32[4,128]{1,0:T(4,128)} %get-tuple-element.49), channel_id=1, source_target_pairs={{1,16},{2,17},{3,18},{17,0},{18,1},{19,2},{5,20},{6,21},{7,22},{21... | collective-permute-start | bytes 6152 | tf_op jit(solution)/shard_map/ppermute | solution.py:550
  113.7 2.6 %collective-permute-start.8 = (f32[4,512]{1,0:T(4,128)}, f32[4,512]{1,0:T(4,128)S(1)}, u32[]{:S(2)}, u32[]{:S(2)}) collective-permute-start(f32[4,512]{1,0:T(4,128)} %get-tuple-element.46), channel_id=1, source_target_pairs={{0,20},{4,24},{8,28},{16,4},{20,8},{24,12},{1,21},{5,25},{9,29},{1... | collective-permute-start | bytes 24584 | tf_op jit(solution)/shard_map/ppermute | solution.py:547
  116.3 1.3 collective-permute-start.9
  117.6 6.7 %all-to-all-done = f32[16,65,4,128]{3,2,1,0:T(4,128)} async-done(((f32[16,65,4,128]{3,2,1,0:T(4,128)}), f32[16,65,4,128]{3,2,1,0:T(4,128)}, u32[]{:S(2)}, u32[]{:S(2)}) %all-to-all-start) | async-done | bytes 2129952 | tf_op jit(solution)/shard_map/all_to_all | solution.py:511
  124.3 3.4 %sum_by_block.3 = (f32[4,128,512]{2,1,0:T(8,128)S(1)}, f32[4,512]{1,0:T(4,128)S(1)}, f32[4,512]{1,0:T(4,128)S(1)}, f32[4,128]{1,0:T(4,128)S(1)}, f32[4,128]{1,0:T(4,128)S(1)}) custom-call(f32[4160,128]{1,0:T(8,128)} %bitcast.5.in_ref), custom_call_target="tpu_custom_call" | custom-call | flops 1073741824 | bytes 3145728 | tf_op jit(solution)/shard_map/sum_by_block/pallas_call | solution.py:215
  127.8 7.8 %collective-permute-start.12 = (f32[4,512]{1,0:T(4,128)S(1)}, f32[4,512]{1,0:T(4,128)S(1)}, u32[]{:S(2)}, u32[]{:S(2)}) collective-permute-start(f32[4,512]{1,0:T(4,128)S(1)} %get-tuple-element.53), channel_id=1, source_target_pairs={{0,4},{4,8},{8,12},{1,5},{5,9},{9,13},{2,6},{6,10},{10,14},{3,7},{... | collective-permute-start | bytes 24584 | tf_op jit(solution)/shard_map/ppermute | solution.py:555
  135.6 0.0 collective-permute-done.11.right_ref
  135.6 1.3 collective-permute-start.13
  136.9 5.0 %collective-permute-start.14 = (f32[4,128]{1,0:T(4,128)S(1)}, f32[4,128]{1,0:T(4,128)S(1)}, u32[]{:S(2)}, u32[]{:S(2)}) collective-permute-start(f32[4,128]{1,0:T(4,128)S(1)} %get-tuple-element.55), channel_id=1, source_target_pairs={{0,1},{1,2},{2,3},{4,5},{5,6},{6,7},{8,9},{9,10},{10,11},{12,13},{... | collective-permute-start | bytes 6152 | tf_op jit(solution)/shard_map/ppermute | solution.py:557
  141.9 1.9 %collective-permute-start.15 = (f32[4,128]{1,0:T(4,128)S(1)}, f32[4,128]{1,0:T(4,128)S(1)}, u32[]{:S(2)}, u32[]{:S(2)}) collective-permute-start(f32[4,128]{1,0:T(4,128)S(1)} %get-tuple-element.56), channel_id=1, source_target_pairs={{1,0},{2,1},{3,2},{5,4},{6,5},{7,6},{9,8},{10,9},{11,10},{13,12},{... | collective-permute-start | bytes 6152 | tf_op jit(solution)/shard_map/ppermute | solution.py:558
  143.9 0.0 collective-permute-done.7.recv_ref
  143.9 4.3 %finish.2 = (f32[1,16,128,512]{3,2,1,0:T(8,128)}, f32[1,8,128,512]{3,2,1,0:T(8,128)}) custom-call(f32[1,8]{1,0:T(1,128)S(1)} %copy-done.8, f32[1,2]{1,0:T(1,128)S(1)} %broadcast_select_fusion.mix_ref, f32[6,128,512]{2,1,0:T(8,128)S(1)} %get-tuple-element.43.factors, f32[40,512]{1,0:T(8,128)S(1)} %collective-permute-done.1.above, ...), custom_call_target="tpu_custom_call", output_to_operand_aliasing={{0}: (7, {})} | custom-call | flops 5242880 | bytes 5242880 | tf_op jit(solution)/shard_map/finish/pallas_call | solution.py:477
  148.1 0.0 collective-permute-done.14.left_ref
  148.2 0.0 collective-permute-done.12.top_ref
  148.2 0.0 collective-permute-done.13.bottom_ref
  148.2 4.1 %finish.3 = (f32[1,16,128,512]{3,2,1,0:T(8,128)}, f32[1,8,128,512]{3,2,1,0:T(8,128)}) custom-call(f32[1,8]{1,0:T(1,128)S(1)} %copy-done.8, f32[1,2]{1,0:T(1,128)S(1)} %broadcast_select_fusion.mix_ref, f32[6,128,512]{2,1,0:T(8,128)S(1)} %get-tuple-element.43.factors, ...), custom_call_target="tpu_custom_call", output_to_operand_aliasing={{0}: (7, {}), {1}: (13, {})} | custom-call | flops 5242880 | bytes 5242880 | tf_op jit(solution)/shard_map/finish/pallas_call | solution.py:477
  (21 shorter events, 0.1 us)
Async XLA Ops:
  19.9 8.7 %copy-start.9 = (f32[1,2]{1,0:T(1,128)S(1)}, f32[1,2]{1,0:T(1,128)}, u32[]{:S(2)}) copy-start(f32[1,2]{1,0:T(1,128)} %constant.14.clone) | copy-start | bytes 28
  19.9 8.7 %copy-start.2 = (f32[1,3,128,512]{3,2,1,0:T(8,128)S(1)}, f32[1,3,128,512]{3,2,1,0:T(8,128)}, u32[]{:S(2)}) copy-start(f32[1,3,128,512]{3,2,1,0:T(8,128)} %coefs_ref.1) | copy-start | bytes 2359300
  19.9 8.7 %copy-start.3 = (s32[128,512]{1,0:T(8,128)S(1)}, s32[128,512]{1,0:T(8,128)}, u32[]{:S(2)}) copy-start(s32[128,512]{1,0:T(8,128)} %land_ref) | copy-start | bytes 786436
  19.9 55.6 %all-to-all-start.1 = ((f32[16,65,4,128]{3,2,1,0:T(4,128)}), f32[16,65,4,128]{3,2,1,0:T(4,128)S(1)}, u32[]{:S(2)}, u32[]{:S(2)}) async-start(f32[16,65,4,128]{3,2,1,0:T(4,128)} %bitcast.8), calls=%async_computation.1 | async-start | bytes 4259840 | tf_op jit(solution)/shard_map/all_to_all | solution.py:511
  27.4 48.1 %collective-permute-start = (f32[1040,4,128]{2,1,0:T(4,128)}, f32[1040,4,128]{2,1,0:T(4,128)}, u32[]{:S(2)}, u32[]{:S(2)}) collective-permute-start(f32[1040,4,128]{2,1,0:T(4,128)} %get-tuple-element.30), channel_id=1, source_target_pairs={{0,16},{16,0},{1,17},{17,1},{2,18},{18,2},{3,19},{19,3},{4,20},{20... | collective-permute-start | bytes 6389768 | tf_op jit(solution)/shard_map/ppermute | solution.py:517
  28.6 2.2 %copy-start = (f32[1,16,128,512]{3,2,1,0:T(8,128)S(1)}, f32[1,16,128,512]{3,2,1,0:T(8,128)}, u32[]{:S(2)}) copy-start(f32[1,16,128,512]{3,2,1,0:T(8,128)} %state_ref.3) | copy-start | bytes 12582916
  32.8 31.3 %collective-permute-start.1 = (f32[40,512]{1,0:T(8,128)S(1)}, f32[40,512]{1,0:T(8,128)S(1)}, u32[]{:S(2)}, u32[]{:S(2)}) collective-permute-start(f32[40,512]{1,0:T(8,128)S(1)} %get-tuple-element.33.x_high), channel_id=1, source_target_pairs={{0,4},{4,8},{8,12},{1,5},{5,9},{9,13},{2,6},{6,10},{10,14},{3,7},{... | collective-permute-start | bytes 245768 | tf_op jit(solution)/shard_map/ppermute | solution.py:527
  36.1 28.0 %collective-permute-start.2 = (f32[40,512]{1,0:T(8,128)S(1)}, f32[40,512]{1,0:T(8,128)S(1)}, u32[]{:S(2)}, u32[]{:S(2)}) collective-permute-start(f32[40,512]{1,0:T(8,128)S(1)} %get-tuple-element.34.x_low), channel_id=1, source_target_pairs={{4,0},{8,4},{12,8},{5,1},{9,5},{13,9},{6,2},{10,6},{14,10},{7,3},{... | collective-permute-start | bytes 245768 | tf_op jit(solution)/shard_map/ppermute | solution.py:528
  37.4 7.0 %collective-permute-start.3 = (f32[40,128]{1,0:T(8,128)S(1)}, f32[40,128]{1,0:T(8,128)S(1)}, u32[]{:S(2)}, u32[]{:S(2)}) collective-permute-start(f32[40,128]{1,0:T(8,128)S(1)} %get-tuple-element.35.y_high), channel_id=1, source_target_pairs={{0,1},{1,2},{2,3},{4,5},{5,6},{6,7},{8,9},{9,10},{10,11},{12,13},{... | collective-permute-start | bytes 61448 | tf_op jit(solution)/shard_map/ppermute | solution.py:525
  41.3 0.6 copy-start.6
  41.9 8.4 %collective-permute-start.4 = (f32[40,128]{1,0:T(8,128)S(1)}, f32[40,128]{1,0:T(8,128)S(1)}, u32[]{:S(2)}, u32[]{:S(2)}) collective-permute-start(f32[40,128]{1,0:T(8,128)S(1)} %get-tuple-element.36.y_low), channel_id=1, source_target_pairs={{1,0},{2,1},{3,2},{5,4},{6,5},{7,6},{9,8},{10,9},{11,10},{13,12},{... | collective-permute-start | bytes 61448 | tf_op jit(solution)/shard_map/ppermute | solution.py:526
  43.8 0.6 copy-start.4
  75.5 48.9 %all-to-all-start = ((f32[16,65,4,128]{3,2,1,0:T(4,128)}), f32[16,65,4,128]{3,2,1,0:T(4,128)}, u32[]{:S(2)}, u32[]{:S(2)}) async-start(f32[16,65,4,128]{3,2,1,0:T(4,128)} %bitcast.1), calls=%async_computation | async-start | bytes 4259840 | tf_op jit(solution)/shard_map/all_to_all | solution.py:511
  82.1 9.7 %copy-start.8 = (f32[1,8]{1,0:T(1,128)S(1)}, f32[1,8]{1,0:T(1,128)}, u32[]{:S(2)}) copy-start(f32[1,8]{1,0:T(1,128)} %gamma_ref.3) | copy-start | bytes 100
  82.1 14.0 %copy-start.1 = (f32[1,16,128,512]{3,2,1,0:T(8,128)S(1)}, f32[1,16,128,512]{3,2,1,0:T(8,128)}, u32[]{:S(2)}) copy-start(f32[1,16,128,512]{3,2,1,0:T(8,128)} %state_ref.3) | copy-start | bytes 12582916
  82.1 14.0 %copy-start.5 = (f32[40,128]{1,0:T(8,128)S(1)}, f32[40,128]{1,0:T(8,128)}, u32[]{:S(2)}) copy-start(f32[40,128]{1,0:T(8,128)} %copy-done.4) | copy-start | bytes 61444
  82.1 14.0 %copy-start.7 = (f32[40,128]{1,0:T(8,128)S(1)}, f32[40,128]{1,0:T(8,128)}, u32[]{:S(2)}) copy-start(f32[40,128]{1,0:T(8,128)} %copy-done.6) | copy-start | bytes 61444
  84.8 59.0 %collective-permute-start.7 = (f32[4,128,512]{2,1,0:T(8,128)}, f32[4,128,512]{2,1,0:T(8,128)}, u32[]{:S(2)}, u32[]{:S(2)}) collective-permute-start(f32[4,128,512]{2,1,0:T(8,128)} %get-tuple-element.45), channel_id=1, source_target_pairs={{0,16},{16,0},{1,17},{17,1},{2,18},{18,2},{3,19},{19,3},{4,20},{20... | collective-permute-start | bytes 3145736 | tf_op jit(solution)/shard_map/ppermute | solution.py:545
  86.1 5.9 %collective-permute-start.5 = (f32[80,128]{1,0:T(8,128)S(1)}, f32[80,128]{1,0:T(8,128)S(1)}, u32[]{:S(2)}, u32[]{:S(2)}) collective-permute-start(f32[80,128]{1,0:T(8,128)S(1)} %pad_maximum_fusion), channel_id=1, source_target_pairs={{0,1},{1,2},{2,3},{4,5},{5,6},{6,7},{8,9},{9,10},{10,11},{12,13},{... | collective-permute-start | bytes 122888 | tf_op jit(solution)/shard_map/ppermute | solution.py:537
  89.9 6.2 %collective-permute-start.6 = (f32[80,128]{1,0:T(8,128)S(1)}, f32[80,128]{1,0:T(8,128)S(1)}, u32[]{:S(2)}, u32[]{:S(2)}) collective-permute-start(f32[80,128]{1,0:T(8,128)S(1)} %pad_maximum_fusion.1), channel_id=1, source_target_pairs={{1,0},{2,1},{3,2},{5,4},{6,5},{7,6},{9,8},{10,9},{11,10},{13,12},{... | collective-permute-start | bytes 122888 | tf_op jit(solution)/shard_map/ppermute | solution.py:538
  108.2 19.6 %collective-permute-start.10 = (f32[4,128]{1,0:T(4,128)}, f32[4,128]{1,0:T(4,128)S(1)}, u32[]{:S(2)}, u32[]{:S(2)}) collective-permute-start(f32[4,128]{1,0:T(4,128)} %get-tuple-element.48), channel_id=1, source_target_pairs={{0,17},{1,18},{2,19},{16,1},{17,2},{18,3},{4,21},{5,22},{6,23},{20... | collective-permute-start | bytes 6152 | tf_op jit(solution)/shard_map/ppermute | solution.py:549
  110.1 25.5 %collective-permute-start.11 = (f32[4,128]{1,0:T(4,128)}, f32[4,128]{1,0:T(4,128)S(1)}, u32[]{:S(2)}, u32[]{:S(2)}) collective-permute-start(f32[4,128]{1,0:T(4,128)} %get-tuple-element.49), channel_id=1, source_target_pairs={{1,16},{2,17},{3,18},{17,0},{18,1},{19,2},{5,20},{6,21},{7,22},{21... | collective-permute-start | bytes 6152 | tf_op jit(solution)/shard_map/ppermute | solution.py:550
  113.7 23.2 %collective-permute-start.8 = (f32[4,512]{1,0:T(4,128)}, f32[4,512]{1,0:T(4,128)S(1)}, u32[]{:S(2)}, u32[]{:S(2)}) collective-permute-start(f32[4,512]{1,0:T(4,128)} %get-tuple-element.46), channel_id=1, source_target_pairs={{0,20},{4,24},{8,28},{16,4},{20,8},{24,12},{1,21},{5,25},{9,29},{1... | collective-permute-start | bytes 24584 | tf_op jit(solution)/shard_map/ppermute | solution.py:547
  116.3 25.6 %collective-permute-start.9 = (f32[4,512]{1,0:T(4,128)}, f32[4,512]{1,0:T(4,128)S(1)}, u32[]{:S(2)}, u32[]{:S(2)}) collective-permute-start(f32[4,512]{1,0:T(4,128)} %get-tuple-element.47), channel_id=1, source_target_pairs={{4,16},{8,20},{12,24},{20,0},{24,4},{28,8},{5,17},{9,21},{13,25},{... | collective-permute-start | bytes 24584 | tf_op jit(solution)/shard_map/ppermute | solution.py:548
  127.8 20.4 %collective-permute-start.12 = (f32[4,512]{1,0:T(4,128)S(1)}, f32[4,512]{1,0:T(4,128)S(1)}, u32[]{:S(2)}, u32[]{:S(2)}) collective-permute-start(f32[4,512]{1,0:T(4,128)S(1)} %get-tuple-element.53), channel_id=1, source_target_pairs={{0,4},{4,8},{8,12},{1,5},{5,9},{9,13},{2,6},{6,10},{10,14},{3,7},{... | collective-permute-start | bytes 24584 | tf_op jit(solution)/shard_map/ppermute | solution.py:555
  135.6 12.5 %collective-permute-start.13 = (f32[4,512]{1,0:T(4,128)S(1)}, f32[4,512]{1,0:T(4,128)S(1)}, u32[]{:S(2)}, u32[]{:S(2)}) collective-permute-start(f32[4,512]{1,0:T(4,128)S(1)} %get-tuple-element.54), channel_id=1, source_target_pairs={{4,0},{8,4},{12,8},{5,1},{9,5},{13,9},{6,2},{10,6},{14,10},{7,3},{... | collective-permute-start | bytes 24584 | tf_op jit(solution)/shard_map/ppermute | solution.py:556
  136.9 11.2 %collective-permute-start.14 = (f32[4,128]{1,0:T(4,128)S(1)}, f32[4,128]{1,0:T(4,128)S(1)}, u32[]{:S(2)}, u32[]{:S(2)}) collective-permute-start(f32[4,128]{1,0:T(4,128)S(1)} %get-tuple-element.55), channel_id=1, source_target_pairs={{0,1},{1,2},{2,3},{4,5},{5,6},{6,7},{8,9},{9,10},{10,11},{12,13},{... | collective-permute-start | bytes 6152 | tf_op jit(solution)/shard_map/ppermute | solution.py:557
  141.9 6.2 %collective-permute-start.15 = (f32[4,128]{1,0:T(4,128)S(1)}, f32[4,128]{1,0:T(4,128)S(1)}, u32[]{:S(2)}, u32[]{:S(2)}) collective-permute-start(f32[4,128]{1,0:T(4,128)S(1)} %get-tuple-element.56), channel_id=1, source_target_pairs={{1,0},{2,1},{3,2},{5,4},{6,5},{7,6},{9,8},{10,9},{11,10},{13,12},{... | collective-permute-start | bytes 6152 | tf_op jit(solution)/shard_map/ppermute | solution.py:558

commit v3 on v2

--- a/solution.py
+++ b/solution.py
@@ -9,6 +9,7 @@
 
 LANES = 128
 STEP_PAIRS = 64
+STRIP = 8
 NT = (((1,), (1,)), ((), ()))
 
 
@@ -23,14 +24,28 @@
     ]
 
 
+def split(value, parts):
+    if parts & (parts - 1) == 0:
+        return lax.shift_right_logical(value, parts.bit_length() - 1), value & (parts - 1)
+    return lax.div(value, parts), lax.rem(value, parts)
+
+
 def contribution_kernel(dims, src_ref, dev_ref, blk_ref, state_ref, weights_ref, *rest):
     tiles, capacity, pairs, fields, cells_x, cells_y, width, chunks = dims
     outs = rest[: len(chunks)]
-    cells, left_ref, w_ref, pair_v, place_v, place_s = rest[len(chunks) : len(chunks) + 6]
-    field_sems, weight_sems, pair_sems, place_sem = rest[len(chunks) + 6 :]
+    cells, w_ref, pair_v, pair_s, taken = rest[len(chunks) : len(chunks) + 5]
+    field_sems, weight_sems, pair_sems = rest[len(chunks) + 5 :]
     parts = cells_y // width
     steps = pairs // STEP_PAIRS
 
+    scalar_copies = [
+        pltpu.make_async_copy(ref, pair_s.at[pl.ds(i, 1), :], pair_sems.at[i])
+        for i, ref in enumerate((src_ref, dev_ref))
+    ]
+    vector_copies = [
+        pltpu.make_async_copy(ref, pair_v.at[i], pair_sems.at[2 + i])
+        for i, ref in enumerate((dev_ref, blk_ref))
+    ]
     field_copies = [
         pltpu.make_async_copy(
             state_ref.at[0, f, :, pl.ds(q * width, width)],
@@ -47,18 +62,18 @@
             weights_ref.at[0, some], w_ref.at[some], weight_sems.at[step]
         )
 
-    pair_copies = [
-        pltpu.make_async_copy(ref, pair_v.at[i], pair_sems.at[i])
-        for i, ref in enumerate((src_ref, dev_ref, blk_ref))
-    ]
-    for copy in pair_copies + field_copies:
+    for copy in scalar_copies + vector_copies + field_copies:
         copy.start()
     for step in range(steps):
         weight_copy(step).start()
-    for copy in pair_copies:
+    for out in outs:
+        out[...] = jnp.zeros_like(out)
+    for t in range(tiles):
+        taken[t] = t * (capacity + 1)
+
+    for copy in vector_copies:
         copy.wait()
-
-    src, dev, blk = pair_v[0], pair_v[1], pair_v[2]
+    dev, blk = pair_v[0], pair_v[1]
     tile_of = lax.broadcasted_iota(jnp.int32, (tiles, pairs), 0)
     lane_of = lax.broadcasted_iota(jnp.int32, (tiles, pairs), 1)
     member = (tile_of == dev).astype(jnp.float32)
@@ -68,13 +83,6 @@
         total = total + jnp.where(lane_of >= shift, pltpu.roll(total, shift, 1), 0.0)
         shift *= 2
     rank = (jnp.sum(member * total, axis=0, keepdims=True) - 1.0).astype(jnp.int32)
-    place_v[0:1, :] = dev * (capacity + 1) + rank
-    place_v[1:2, :] = (src % parts) * (fields * cells_x) + src // parts
-    to_scalars = pltpu.make_async_copy(place_v, place_s, place_sem)
-    to_scalars.start()
-
-    for out in outs:
-        out[...] = jnp.zeros_like(out)
     slot_of = lax.broadcasted_iota(jnp.int32, (LANES, pairs), 0) % capacity
     chosen = (slot_of == rank).astype(jnp.bfloat16)
 
@@ -83,46 +91,37 @@
             (member * values).astype(jnp.bfloat16), chosen, NT, preferred_element_type=jnp.float32
         )
 
-    ids = spread((blk // 256).astype(jnp.float32)) * 256.0
-    ids = ids + spread((blk % 256).astype(jnp.float32))
+    high, low = split(blk, 256)
+    ids = spread(high.astype(jnp.float32)) * 256.0 + spread(low.astype(jnp.float32))
     ids = jnp.where(spread(jnp.ones(dev.shape, jnp.float32)) > 0.5, ids, -1.0)
     for t in range(tiles):
         row = jnp.broadcast_to(ids[t : t + 1, :], (fields, LANES))
         for out in outs:
             out[t * (capacity + 1) + capacity] = row[: out.shape[1]]
-    to_scalars.wait()
-    for copy in field_copies:
+    for copy in scalar_copies + field_copies:
         copy.wait()
 
-    group = LANES // fields
-    lane = lax.broadcasted_iota(jnp.int32, (width, LANES), 1) // fields
-
-    def gather(step, carry):
-        for i in range(STEP_PAIRS):
+    def cells_of(p):
+        x, part = split(pair_s[0, p], parts)
+        return cells[pl.ds(part * (fields * cells_x) + x, fields, stride=cells_x), :]
+
+    def some_pairs(step, carry):
+        weight_copy(step).wait()
+        for i in range(0, STEP_PAIRS, 2):
             p = step * STEP_PAIRS + i
-            rows = pl.ds(pl.multiple_of(p * fields, fields), fields)
-            left_ref[rows, :] = cells[pl.ds(place_s[1, p], fields, stride=cells_x), :]
+            left = jnp.concatenate([cells_of(p), cells_of(p + 1)], axis=0).astype(jnp.bfloat16)
+            right = w_ref[pl.ds(p, 2)].reshape(2 * width, width)
+            both = lax.dot_general(left, right, NT, preferred_element_type=jnp.float32)
+            for j in range(2):
+                tile = pair_s[1, p + j]
+                slot = taken[tile]
+                taken[tile] = slot + 1
+                one = both[j * fields : (j + 1) * fields, j * width : (j + 1) * width]
+                for out, (first, last) in zip(outs, chunks):
+                    out[slot] = one[first:last]
         return carry
 
-    def multiply(step, carry):
-        weight_copy(step).wait()
-        for first_pair in range(0, STEP_PAIRS, group):
-            p = step * STEP_PAIRS + first_pair
-            rows = pl.ds(pl.multiple_of(p * fields, LANES), LANES)
-            right = left_ref[rows, :].T.astype(jnp.bfloat16)
-            kept = None
-            for j in range(group):
-                one = jnp.dot(w_ref[p + j], right, preferred_element_type=jnp.float32)
-                kept = one if kept is None else jnp.where(lane == j, one, kept)
-            kept = kept.T
-            for j in range(group):
-                slot = place_s[0, p + j]
-                for out, (first, last) in zip(outs, chunks):
-                    out[slot] = kept[j * fields + first : j * fields + last]
-        return carry
-
-    lax.fori_loop(0, steps, gather, 0)
-    lax.fori_loop(0, steps, multiply, 0)
+    lax.fori_loop(0, steps, some_pairs, 0)
 
 
 def contributions(state, pair_src, pair_dev, pair_blk, weights, tiles, capacity, chunks):
@@ -140,17 +139,15 @@
         out_shape=[jax.ShapeDtypeStruct(shape, jnp.float32) for shape in shapes],
         scratch_shapes=[
             pltpu.VMEM((parts * fields * cells_x, width), jnp.float32),
-            pltpu.VMEM((pairs * fields, width), jnp.float32),
             pltpu.VMEM((pairs, width, width), jnp.bfloat16),
-            pltpu.VMEM((3, 1, pairs), jnp.int32),
-            pltpu.VMEM((8, pairs), jnp.int32),
-            pltpu.SMEM((8, pairs), jnp.int32),
+            pltpu.VMEM((2, 1, pairs), jnp.int32),
+            pltpu.SMEM((2, pairs), jnp.int32),
+            pltpu.SMEM((tiles,), jnp.int32),
             pltpu.SemaphoreType.DMA((parts * fields,)),
             pltpu.SemaphoreType.DMA((pairs // STEP_PAIRS,)),
-            pltpu.SemaphoreType.DMA((3,)),
-            pltpu.SemaphoreType.DMA,
+            pltpu.SemaphoreType.DMA((4,)),
         ],
-        compiler_params=pltpu.CompilerParams(vmem_limit_bytes=56 * 1024 * 1024),
+        compiler_params=pltpu.CompilerParams(vmem_limit_bytes=47 * 1024 * 1024),
         cost_estimate=pl.CostEstimate(
             flops=2 * pairs * fields * width * width,
             bytes_accessed=2 * pairs * width * width + 8 * rows * fields * width,
@@ -330,7 +327,7 @@
         in_specs=specs,
         out_specs=[pl.BlockSpec(shape, lambda i: (0, 0)) for shape in shapes],
         out_shape=[jax.ShapeDtypeStruct(shape, jnp.float32) for shape in shapes],
-        compiler_params=pltpu.CompilerParams(vmem_limit_bytes=40 * 1024 * 1024),
+        compiler_params=pltpu.CompilerParams(vmem_limit_bytes=56 * 1024 * 1024),
         cost_estimate=pl.CostEstimate(
             flops=state.size, bytes_accessed=4 * 1024 * 1024, transcendentals=0
         ),
@@ -435,7 +432,7 @@
     first, gamma_ref, mix_ref, factors, above, below, before, after, base_ref, recv_ref,
     top_ref, bottom_ref, left_ref, right_ref, *rest
 ):
-    new_ref, out_ref = rest[-2:]
+    new_ref, out_ref, wide = rest[-3:]
     f = pl.program_id(0)
     rate = gamma_ref[0, first + f]
     mix_b = mix_ref[0, 1]
@@ -444,14 +441,25 @@
     row = pl.ds(f, 1)
     keep_row = above.shape[0] - 5
     keep = slice(keep_row, keep_row + 1)
-    top = above[keep, :] * top_ref[row, :] * rate
-    bottom = below[keep, :] * bottom_ref[row, :] * rate
+    cells_x, cells_y = recv.shape
     left = before[keep, :] * left_ref[row, :] * rate
     right = after[keep, :] * right_ref[row, :] * rate
     cols = columns_of(jnp.concatenate([left, right], axis=0))
-    more = tendency(g, rate, factors, top, bottom, cols[:, 0:1], cols[:, 1:2])
-    new_ref[0, 0] = base_ref[0, 0] + mix_b * (2.0 * g + more)
+    wide[STRIP - 1 : STRIP, :] = above[keep, :] * top_ref[row, :] * rate
+    wide[STRIP + cells_x : STRIP + cells_x + 1, :] = below[keep, :] * bottom_ref[row, :] * rate
+    wide[STRIP : STRIP + cells_x, :] = g
     out_ref[0, 0] = recv
+    lane = lax.broadcasted_iota(jnp.int32, (STRIP, cells_y), 1)
+    for i in range(0, cells_x, STRIP):
+        rows = slice(i, i + STRIP)
+        mid = wide[STRIP + i : 2 * STRIP + i, :]
+        more = (factors[5, rows, :] - rate * factors[0, rows, :]) * mid
+        more += factors[1, rows, :] * wide[STRIP + i - 1 : 2 * STRIP + i - 1, :]
+        more += factors[2, rows, :] * wide[STRIP + i + 1 : 2 * STRIP + i + 1, :]
+        prior = jnp.where(lane == 0, cols[rows, 0:1], pltpu.roll(mid, 1, 1))
+        later = jnp.where(lane == cells_y - 1, cols[rows, 1:2], pltpu.roll(mid, cells_y - 1, 1))
+        more += factors[3, rows, :] * prior + factors[4, rows, :] * later
+        new_ref[0, 0, rows, :] = base_ref[0, 0, rows, :] + mix_b * (2.0 * mid + more)
 
 
 def finished(first, new_state, remapped, recv, rims, gamma, mix, factors, received):
@@ -484,6 +492,7 @@
             jax.ShapeDtypeStruct((1, chan, cells_x, cells_y), jnp.float32),
         ],
         input_output_aliases=aliases,
+        scratch_shapes=[pltpu.VMEM((cells_x + 2 * STRIP, cells_y), jnp.float32)],
         compiler_params=pltpu.CompilerParams(vmem_limit_bytes=40 * 1024 * 1024),
         cost_estimate=pl.CostEstimate(
             flops=20 * recv.size, bytes_accessed=20 * recv.size, transcendentals=0

time: 153 us -> 152 us (level)
  Pallas kernels: 47.7 us -> 43.7 us
    pallas_call x1, Pallas kernels: 19.2 us -> 13.3 us  [contributions(): pl.pallas_call(functools.partial(contribution_kernel, dims), in_specs=[pl...]
    pallas_call x1, Pallas kernels: 2 us -> 3.92 us  [edges_of(): pl.pallas_call(edge_kernel, grid=(1,), in_specs=specs, out_specs=[pl.Bloc...]
    unnamed x20 -> x30, local copies, waits for them, and re-layouts: 3.41 us -> 4.74 us
  transfers between devices with their start and end apart: 18 -> 18, of which waited for: 6 -> 6; matrix products, arithmetic and copies ran while one was open for 0% -> 0% of each run, Pallas kernels for 16% -> 17%
where the time goes in v3:
time: 152 us; the launch traced here: 151 us
  starting transfers between devices  58.3 us (38%)
  Pallas kernels  43.7 us (29%)
  waiting for transfers between devices  42.8 us (28%)
  local copies, waits for them, and re-layouts  4.82 us (3%)
    all_to_all x2, starting transfers between devices, exchanged(): lax.all_to_all(rows, ('tx', 'ty'), split_axis=0, concat_axis=0, tiled=True)  14.3 us
    ppermute x1, waiting for transfers between devices, body(): above = lax.ppermute(x_high, 'tx', shift_pairs(tx, 1))  13.8 us
    pallas_call x1, Pallas kernels, contributions(): pl.pallas_call(functools.partial(contribution_kernel, dims), in_specs=[pl...  13.3 us
    pallas_call x1, Pallas kernels, base_of(): pl.pallas_call(base_kernel, grid=(nfield,), in_specs=[pl.BlockSpec(memory...  12 us
    ppermute x1, waiting for transfers between devices, body(): early_in = lax.ppermute(early, 'comp', swap)  11.3 us
    pallas_call x2, Pallas kernels, finished(): pl.pallas_call(functools.partial(finish_kernel, first), grid=(fields,), i...  8.44 us
    ppermute x1, starting transfers between devices, body(): lax.ppermute(bottom, 'tx', shift_pairs(tx, 1))  7.84 us
    ppermute x1, waiting for transfers between devices, body(): right = lax.ppermute(y_low, 'ty', shift_pairs(ty, -1))  6.81 us
  transfers between devices with their start and end apart: 18, of which 6 were waited for; matrix products, arithmetic and copies ran while one was open for 0% of the time, Pallas kernels for 17%

profile of v3, /device:TPU:1, one launch (start us, length us, event | category | flops | bytes accessed | tf_op | source)
XLA Modules:
  0.0 151.3 jit_solution(16673776942869046083)
XLA Ops:
  0.6 0.7 copy-done.9
  1.3 0.7 copy-done.10
  2.0 0.7 copy-done.11
  2.7 13.3 %contributions.1 = (f32[1040,4,128]{2,1,0:T(4,128)S(1)}, f32[1040,4,128]{2,1,0:T(4,128)S(1)}) custom-call(s32[1,512]{1,0:T(1,128)S(1)} %copy-done.9, s32[1,512]{1,0:T(1,128)S(1)} %bitcast.9, s32[1,512]{1,0:T(1,128)S(1)} %copy-done.11, f32[1,16,128,512]{3,2,1,0:T(8,128)} %state_ref.3, bf16[1,512,128,128]{3,2,1,0:T(8,128)(2,1)} %weights_ref.1), custom_call_target="tpu_custom_call" | custom-call | flops 134217728 | bytes 25296896 | tf_op jit(solution)/shard_map/contributions/pallas_call | solution.py:135
  16.0 0.0 copy-start.3
  16.0 1.3 copy-done.3
  17.3 1.3 copy-done.13
  18.7 7.5 %all-to-all-start.1 = ((f32[16,65,4,128]{3,2,1,0:T(4,128)}), f32[16,65,4,128]{3,2,1,0:T(4,128)S(1)}, u32[]{:S(2)}, u32[]{:S(2)}) async-start(f32[16,65,4,128]{3,2,1,0:T(4,128)} %bitcast.8), calls=%async_computation.1 | async-start | bytes 4259840 | tf_op jit(solution)/shard_map/all_to_all | solution.py:520
  26.2 1.2 collective-permute-start
  27.4 0.6 broadcast_select_fusion.mix_ref
  28.0 3.9 %edges.1 = (f32[40,512]{1,0:T(8,128)}, f32[40,512]{1,0:T(8,128)}, f32[40,128]{1,0:T(8,128)}, f32[40,128]{1,0:T(8,128)}) custom-call(f32[1,2]{1,0:T(1,128)} %broadcast_select_fusion.mix_ref, f32[1,16,128,512]{3,2,1,0:T(8,128)} %state_ref.3, f32[1,16,128,512]{3,2,1,0:T(8,128)} %state_ref.3, f32[1,16,128,512]{3,2,1,0:T(8,128)} %state_ref.3, ...), custom_call_target="tpu_custom_call" | custom-call | flops 1048576 | bytes 4194304 | tf_op jit(solution)/shard_map/edges/pallas_call | solution.py:324
  31.9 3.3 %collective-permute-start.1 = (f32[40,512]{1,0:T(8,128)}, f32[40,512]{1,0:T(8,128)S(1)}, u32[]{:S(2)}, u32[]{:S(2)}) collective-permute-start(f32[40,512]{1,0:T(8,128)} %get-tuple-element.33.x_high), channel_id=1, source_target_pairs={{0,4},{4,8},{8,12},{1,5},{5,9},{9,13},{2,6},{6,10},{10,14},{3,7},{... | collective-permute-start | bytes 245768 | tf_op jit(solution)/shard_map/ppermute | solution.py:536
  35.2 1.3 collective-permute-start.2
  36.5 3.9 %collective-permute-start.3 = (f32[40,128]{1,0:T(8,128)}, f32[40,128]{1,0:T(8,128)S(1)}, u32[]{:S(2)}, u32[]{:S(2)}) collective-permute-start(f32[40,128]{1,0:T(8,128)} %get-tuple-element.35.y_high), channel_id=1, source_target_pairs={{0,1},{1,2},{2,3},{4,5},{5,6},{6,7},{8,9},{9,10},{10,11},{12,13},{... | collective-permute-start | bytes 61448 | tf_op jit(solution)/shard_map/ppermute | solution.py:534
  40.4 1.9 %collective-permute-start.4 = (f32[40,128]{1,0:T(8,128)}, f32[40,128]{1,0:T(8,128)S(1)}, u32[]{:S(2)}, u32[]{:S(2)}) collective-permute-start(f32[40,128]{1,0:T(8,128)} %get-tuple-element.36.y_low), channel_id=1, source_target_pairs={{1,0},{2,1},{3,2},{5,4},{6,5},{7,6},{9,8},{10,9},{11,10},{13,12},{... | collective-permute-start | bytes 61448 | tf_op jit(solution)/shard_map/ppermute | solution.py:535
  42.3 0.0 collective-permute-done.3.left.before
  42.3 6.8 %collective-permute-done.4.right.after = f32[40,128]{1,0:T(8,128)S(1)} collective-permute-done((f32[40,128]{1,0:T(8,128)}, f32[40,128]{1,0:T(8,128)S(1)}, u32[]{:S(2)}, u32[]{:S(2)}) %collective-permute-start.4) | collective-permute-done | bytes 20512 | tf_op jit(solution)/shard_map/ppermute | solution.py:535
  49.1 13.8 %collective-permute-done.1.above = f32[40,512]{1,0:T(8,128)S(1)} collective-permute-done((f32[40,512]{1,0:T(8,128)}, f32[40,512]{1,0:T(8,128)S(1)}, u32[]{:S(2)}, u32[]{:S(2)}) %collective-permute-start.1) | collective-permute-done | bytes 81952 | tf_op jit(solution)/shard_map/ppermute | solution.py:536
  62.9 0.0 collective-permute-done.2.below
  63.0 11.3 %collective-permute-done = f32[1040,4,128]{2,1,0:T(4,128)} collective-permute-done((f32[1040,4,128]{2,1,0:T(4,128)}, f32[1040,4,128]{2,1,0:T(4,128)}, u32[]{:S(2)}, u32[]{:S(2)}) %collective-permute-start) | collective-permute-done | bytes 2129952 | tf_op jit(solution)/shard_map/ppermute | solution.py:526
  74.3 0.0 all-to-all-done.1
  74.3 6.8 %all-to-all-start = ((f32[16,65,4,128]{3,2,1,0:T(4,128)}), f32[16,65,4,128]{3,2,1,0:T(4,128)}, u32[]{:S(2)}, u32[]{:S(2)}) async-start(f32[16,65,4,128]{3,2,1,0:T(4,128)} %bitcast.1), calls=%async_computation | async-start | bytes 4259840 | tf_op jit(solution)/shard_map/all_to_all | solution.py:520
  81.1 2.7 %sum_by_block.2 = (f32[4,128,512]{2,1,0:T(8,128)}, f32[4,512]{1,0:T(4,128)S(1)}, f32[4,512]{1,0:T(4,128)S(1)}, f32[4,128]{1,0:T(4,128)S(1)}, f32[4,128]{1,0:T(4,128)S(1)}) custom-call(f32[4160,128]{1,0:T(8,128)S(1)} %bitcast.7), custom_call_target="tpu_custom_call" | custom-call | flops 1073741824 | bytes 3145728 | tf_op jit(solution)/shard_map/sum_by_block/pallas_call | solution.py:212
  83.8 1.2 collective-permute-start.7
  85.0 3.8 %collective-permute-start.5 = (f32[80,128]{1,0:T(8,128)S(1)}, f32[80,128]{1,0:T(8,128)S(1)}, u32[]{:S(2)}, u32[]{:S(2)}) collective-permute-start(f32[80,128]{1,0:T(8,128)S(1)} %pad_maximum_fusion), channel_id=1, source_target_pairs={{0,1},{1,2},{2,3},{4,5},{5,6},{6,7},{8,9},{9,10},{10,11},{12,13},{... | collective-permute-start | bytes 122888 | tf_op jit(solution)/shard_map/ppermute | solution.py:546
  88.8 1.9 %collective-permute-start.6 = (f32[80,128]{1,0:T(8,128)S(1)}, f32[80,128]{1,0:T(8,128)S(1)}, u32[]{:S(2)}, u32[]{:S(2)}) collective-permute-start(f32[80,128]{1,0:T(8,128)S(1)} %pad_maximum_fusion.1), channel_id=1, source_target_pairs={{1,0},{2,1},{3,2},{5,4},{6,5},{7,6},{9,8},{10,9},{11,10},{13,12},{... | collective-permute-start | bytes 122888 | tf_op jit(solution)/shard_map/ppermute | solution.py:547
  90.8 0.1 collective-permute-done.5.corners_left
  90.9 4.1 %collective-permute-done.6.corners_right = f32[80,128]{1,0:T(8,128)S(1)} collective-permute-done((f32[80,128]{1,0:T(8,128)S(1)}, f32[80,128]{1,0:T(8,128)S(1)}, u32[]{:S(2)}, u32[]{:S(2)}) %collective-permute-start.6) | collective-permute-done | bytes 40992 | tf_op jit(solution)/shard_map/ppermute | solution.py:547
  95.0 0.1 broadcast_in_dim.8.rates_ref
  95.1 12.0 %base.1 = (f32[1,16,128,512]{3,2,1,0:T(8,128)}, f32[6,128,512]{2,1,0:T(8,128)S(1)}) custom-call(f32[1,16]{1,0:T(1,128)S(1)} %get-tuple-element.63.rate_ref, f32[1,2]{1,0:T(1,128)S(1)} %copy-done.8, f32[16,128]{1,0:T(8,128)S(1)} %broadcast_in_dim.8.rates_ref, f32[1,3,128,512]{3,2,1,0:T(8,128)S(1)} %copy-done.1, s32[128,512]{1,0:T(8,128)S(1)} %copy-done.2, ...), custom_call_target="tpu_custom_call" | custom-call | flops 41943040 | bytes 8388608 | tf_op jit(solution)/shard_map/base/pallas_call | solution.py:405
  107.1 1.9 %collective-permute-start.10 = (f32[4,128]{1,0:T(4,128)S(1)}, f32[4,128]{1,0:T(4,128)S(1)}, u32[]{:S(2)}, u32[]{:S(2)}) collective-permute-start(f32[4,128]{1,0:T(4,128)S(1)} %get-tuple-element.48), channel_id=1, source_target_pairs={{0,17},{1,18},{2,19},{16,1},{17,2},{18,3},{4,21},{5,22},{6,23},{20... | collective-permute-start | bytes 6152 | tf_op jit(solution)/shard_map/ppermute | solution.py:558
  109.1 3.6 %collective-permute-start.11 = (f32[4,128]{1,0:T(4,128)S(1)}, f32[4,128]{1,0:T(4,128)S(1)}, u32[]{:S(2)}, u32[]{:S(2)}) collective-permute-start(f32[4,128]{1,0:T(4,128)S(1)} %get-tuple-element.49), channel_id=1, source_target_pairs={{1,16},{2,17},{3,18},{17,0},{18,1},{19,2},{5,20},{6,21},{7,22},{21... | collective-permute-start | bytes 6152 | tf_op jit(solution)/shard_map/ppermute | solution.py:559
  112.7 2.6 %collective-permute-start.8 = (f32[4,512]{1,0:T(4,128)S(1)}, f32[4,512]{1,0:T(4,128)S(1)}, u32[]{:S(2)}, u32[]{:S(2)}) collective-permute-start(f32[4,512]{1,0:T(4,128)S(1)} %get-tuple-element.46), channel_id=1, source_target_pairs={{0,20},{4,24},{8,28},{16,4},{20,8},{24,12},{1,21},{5,25},{9,29},{1... | collective-permute-start | bytes 24584 | tf_op jit(solution)/shard_map/ppermute | solution.py:556
  115.3 1.3 collective-permute-start.9
  116.6 6.7 %all-to-all-done = f32[16,65,4,128]{3,2,1,0:T(4,128)} async-done(((f32[16,65,4,128]{3,2,1,0:T(4,128)}), f32[16,65,4,128]{3,2,1,0:T(4,128)}, u32[]{:S(2)}, u32[]{:S(2)}) %all-to-all-start) | async-done | bytes 2129952 | tf_op jit(solution)/shard_map/all_to_all | solution.py:520
  123.3 3.4 %sum_by_block.3 = (f32[4,128,512]{2,1,0:T(8,128)S(1)}, f32[4,512]{1,0:T(4,128)S(1)}, f32[4,512]{1,0:T(4,128)S(1)}, f32[4,128]{1,0:T(4,128)S(1)}, f32[4,128]{1,0:T(4,128)S(1)}) custom-call(f32[4160,128]{1,0:T(8,128)} %bitcast.5.in_ref), custom_call_target="tpu_custom_call" | custom-call | flops 1073741824 | bytes 3145728 | tf_op jit(solution)/shard_map/sum_by_block/pallas_call | solution.py:212
  126.7 0.0 collective-permute-done.10.left_ref
  126.7 7.8 %collective-permute-start.12 = (f32[4,512]{1,0:T(4,128)S(1)}, f32[4,512]{1,0:T(4,128)S(1)}, u32[]{:S(2)}, u32[]{:S(2)}) collective-permute-start(f32[4,512]{1,0:T(4,128)S(1)} %get-tuple-element.53), channel_id=1, source_target_pairs={{0,4},{4,8},{8,12},{1,5},{5,9},{9,13},{2,6},{6,10},{10,14},{3,7},{... | collective-permute-start | bytes 24584 | tf_op jit(solution)/shard_map/ppermute | solution.py:564
  134.6 0.0 collective-permute-done.11.right_ref
  134.6 1.3 collective-permute-start.13
  135.9 5.0 %collective-permute-start.14 = (f32[4,128]{1,0:T(4,128)S(1)}, f32[4,128]{1,0:T(4,128)S(1)}, u32[]{:S(2)}, u32[]{:S(2)}) collective-permute-start(f32[4,128]{1,0:T(4,128)S(1)} %get-tuple-element.55), channel_id=1, source_target_pairs={{0,1},{1,2},{2,3},{4,5},{5,6},{6,7},{8,9},{9,10},{10,11},{12,13},{... | collective-permute-start | bytes 6152 | tf_op jit(solution)/shard_map/ppermute | solution.py:566
  140.9 0.0 collective-permute-done.9.bottom_ref
  140.9 1.9 %collective-permute-start.15 = (f32[4,128]{1,0:T(4,128)S(1)}, f32[4,128]{1,0:T(4,128)S(1)}, u32[]{:S(2)}, u32[]{:S(2)}) collective-permute-start(f32[4,128]{1,0:T(4,128)S(1)} %get-tuple-element.56), channel_id=1, source_target_pairs={{1,0},{2,1},{3,2},{5,4},{6,5},{7,6},{9,8},{10,9},{11,10},{13,12},{... | collective-permute-start | bytes 6152 | tf_op jit(solution)/shard_map/ppermute | solution.py:567
  142.8 4.3 %finish.2 = (f32[1,16,128,512]{3,2,1,0:T(8,128)}, f32[1,8,128,512]{3,2,1,0:T(8,128)}) custom-call(f32[1,8]{1,0:T(1,128)S(1)} %copy-done.12, f32[1,2]{1,0:T(1,128)S(1)} %copy-done.8, f32[6,128,512]{2,1,0:T(8,128)S(1)} %get-tuple-element.43.factors, f32[40,512]{1,0:T(8,128)S(1)} %collective-permute-done.1.above, ...), custom_call_target="tpu_custom_call", output_to_operand_aliasing={{0}: (7, {})} | custom-call | flops 5242880 | bytes 5242880 | tf_op jit(solution)/shard_map/finish/pallas_call | solution.py:485
  147.1 0.0 collective-permute-done.14.left_ref
  147.1 0.0 collective-permute-done.15.right_ref
  147.2 0.0 collective-permute-done.13.bottom_ref
  147.2 4.1 %finish.3 = (f32[1,16,128,512]{3,2,1,0:T(8,128)}, f32[1,8,128,512]{3,2,1,0:T(8,128)}) custom-call(f32[1,8]{1,0:T(1,128)S(1)} %copy-done.12, f32[1,2]{1,0:T(1,128)S(1)} %copy-done.8, f32[6,128,512]{2,1,0:T(8,128)S(1)} %get-tuple-element.43.factors, f32[40,512]{1,0:T(8,128)S(1)} %collective-permute-done.1.above, ...), custom_call_target="tpu_custom_call", output_to_operand_aliasing={{0}: (7, {}), {1}: (13, {})} | custom-call | flops 5242880 | bytes 5242880 | tf_op jit(solution)/shard_map/finish/pallas_call | solution.py:485
  (31 shorter events, 0.1 us)
Async XLA Ops:
  0.6 0.7 copy-start.9
  1.3 0.7 copy-start.10
  2.0 0.7 copy-start.11
  16.0 1.3 copy-start.3
  17.3 1.3 copy-start.13
  18.7 8.7 %copy-start.14 = (f32[1,2]{1,0:T(1,128)S(1)}, f32[1,2]{1,0:T(1,128)}, u32[]{:S(2)}) copy-start(f32[1,2]{1,0:T(1,128)} %constant.14.clone) | copy-start | bytes 28
  18.7 55.6 %all-to-all-start.1 = ((f32[16,65,4,128]{3,2,1,0:T(4,128)}), f32[16,65,4,128]{3,2,1,0:T(4,128)S(1)}, u32[]{:S(2)}, u32[]{:S(2)}) async-start(f32[16,65,4,128]{3,2,1,0:T(4,128)} %bitcast.8), calls=%async_computation.1 | async-start | bytes 4259840 | tf_op jit(solution)/shard_map/all_to_all | solution.py:520
  26.2 48.1 %collective-permute-start = (f32[1040,4,128]{2,1,0:T(4,128)}, f32[1040,4,128]{2,1,0:T(4,128)}, u32[]{:S(2)}, u32[]{:S(2)}) collective-permute-start(f32[1040,4,128]{2,1,0:T(4,128)} %copy-done.13), channel_id=1, source_target_pairs={{0,16},{16,0},{1,17},{17,1},{2,18},{18,2},{3,19},{19,3},{4,20},{20... | collective-permute-start | bytes 6389768 | tf_op jit(solution)/shard_map/ppermute | solution.py:526
  31.9 31.1 %collective-permute-start.1 = (f32[40,512]{1,0:T(8,128)}, f32[40,512]{1,0:T(8,128)S(1)}, u32[]{:S(2)}, u32[]{:S(2)}) collective-permute-start(f32[40,512]{1,0:T(8,128)} %get-tuple-element.33.x_high), channel_id=1, source_target_pairs={{0,4},{4,8},{8,12},{1,5},{5,9},{9,13},{2,6},{6,10},{10,14},{3,7},{... | collective-permute-start | bytes 245768 | tf_op jit(solution)/shard_map/ppermute | solution.py:536
  35.2 27.8 %collective-permute-start.2 = (f32[40,512]{1,0:T(8,128)}, f32[40,512]{1,0:T(8,128)S(1)}, u32[]{:S(2)}, u32[]{:S(2)}) collective-permute-start(f32[40,512]{1,0:T(8,128)} %get-tuple-element.34.x_low), channel_id=1, source_target_pairs={{4,0},{8,4},{12,8},{5,1},{9,5},{13,9},{6,2},{10,6},{14,10},{7,3},{... | collective-permute-start | bytes 245768 | tf_op jit(solution)/shard_map/ppermute | solution.py:537
  36.5 5.8 %collective-permute-start.3 = (f32[40,128]{1,0:T(8,128)}, f32[40,128]{1,0:T(8,128)S(1)}, u32[]{:S(2)}, u32[]{:S(2)}) collective-permute-start(f32[40,128]{1,0:T(8,128)} %get-tuple-element.35.y_high), channel_id=1, source_target_pairs={{0,1},{1,2},{2,3},{4,5},{5,6},{6,7},{8,9},{9,10},{10,11},{12,13},{... | collective-permute-start | bytes 61448 | tf_op jit(solution)/shard_map/ppermute | solution.py:534
  40.4 8.7 %collective-permute-start.4 = (f32[40,128]{1,0:T(8,128)}, f32[40,128]{1,0:T(8,128)S(1)}, u32[]{:S(2)}, u32[]{:S(2)}) collective-permute-start(f32[40,128]{1,0:T(8,128)} %get-tuple-element.36.y_low), channel_id=1, source_target_pairs={{1,0},{2,1},{3,2},{5,4},{6,5},{7,6},{9,8},{10,9},{11,10},{13,12},{... | collective-permute-start | bytes 61448 | tf_op jit(solution)/shard_map/ppermute | solution.py:535
  74.3 16.5 %copy-start.12 = (f32[1,8]{1,0:T(1,128)S(1)}, f32[1,8]{1,0:T(1,128)}, u32[]{:S(2)}) copy-start(f32[1,8]{1,0:T(1,128)} %gamma_ref.3) | copy-start | bytes 100
  74.3 20.8 %copy-start.1 = (f32[1,3,128,512]{3,2,1,0:T(8,128)S(1)}, f32[1,3,128,512]{3,2,1,0:T(8,128)}, u32[]{:S(2)}) copy-start(f32[1,3,128,512]{3,2,1,0:T(8,128)} %coefs_ref.1) | copy-start | bytes 2359300
  74.3 20.8 %copy-start.2 = (s32[128,512]{1,0:T(8,128)S(1)}, s32[128,512]{1,0:T(8,128)}, u32[]{:S(2)}) copy-start(s32[128,512]{1,0:T(8,128)} %land_ref) | copy-start | bytes 786436
  74.3 20.8 %copy-start.5 = (f32[40,512]{1,0:T(8,128)S(1)}, f32[40,512]{1,0:T(8,128)}, u32[]{:S(2)}) copy-start(f32[40,512]{1,0:T(8,128)} %get-tuple-element.33.x_high) | copy-start | bytes 245764
  74.3 49.0 %all-to-all-start = ((f32[16,65,4,128]{3,2,1,0:T(4,128)}), f32[16,65,4,128]{3,2,1,0:T(4,128)}, u32[]{:S(2)}, u32[]{:S(2)}) async-start(f32[16,65,4,128]{3,2,1,0:T(4,128)} %bitcast.1), calls=%async_computation | async-start | bytes 4259840 | tf_op jit(solution)/shard_map/all_to_all | solution.py:520
  81.0 14.0 %copy-start = (f32[1,16,128,512]{3,2,1,0:T(8,128)S(1)}, f32[1,16,128,512]{3,2,1,0:T(8,128)}, u32[]{:S(2)}) copy-start(f32[1,16,128,512]{3,2,1,0:T(8,128)} %state_ref.3) | copy-start | bytes 12582916
  81.1 14.1 %copy-start.4 = (f32[40,512]{1,0:T(8,128)S(1)}, f32[40,512]{1,0:T(8,128)}, u32[]{:S(2)}) copy-start(f32[40,512]{1,0:T(8,128)} %get-tuple-element.34.x_low) | copy-start | bytes 245764
  81.1 14.1 %copy-start.6 = (f32[40,128]{1,0:T(8,128)S(1)}, f32[40,128]{1,0:T(8,128)}, u32[]{:S(2)}) copy-start(f32[40,128]{1,0:T(8,128)} %get-tuple-element.36.y_low) | copy-start | bytes 61444
  81.1 14.1 %copy-start.7 = (f32[40,128]{1,0:T(8,128)S(1)}, f32[40,128]{1,0:T(8,128)}, u32[]{:S(2)}) copy-start(f32[40,128]{1,0:T(8,128)} %get-tuple-element.35.y_high) | copy-start | bytes 61444
  81.1 14.1 %copy-start.8 = (f32[1,2]{1,0:T(1,128)S(1)}, f32[1,2]{1,0:T(1,128)}, u32[]{:S(2)}) copy-start(f32[1,2]{1,0:T(1,128)} %broadcast_select_fusion.mix_ref) | copy-start | bytes 28
  83.8 59.0 %collective-permute-start.7 = (f32[4,128,512]{2,1,0:T(8,128)}, f32[4,128,512]{2,1,0:T(8,128)}, u32[]{:S(2)}, u32[]{:S(2)}) collective-permute-start(f32[4,128,512]{2,1,0:T(8,128)} %get-tuple-element.45), channel_id=1, source_target_pairs={{0,16},{16,0},{1,17},{17,1},{2,18},{18,2},{3,19},{19,3},{4,20},{20... | collective-permute-start | bytes 3145736 | tf_op jit(solution)/shard_map/ppermute | solution.py:554
  85.0 5.9 %collective-permute-start.5 = (f32[80,128]{1,0:T(8,128)S(1)}, f32[80,128]{1,0:T(8,128)S(1)}, u32[]{:S(2)}, u32[]{:S(2)}) collective-permute-start(f32[80,128]{1,0:T(8,128)S(1)} %pad_maximum_fusion), channel_id=1, source_target_pairs={{0,1},{1,2},{2,3},{4,5},{5,6},{6,7},{8,9},{9,10},{10,11},{12,13},{... | collective-permute-start | bytes 122888 | tf_op jit(solution)/shard_map/ppermute | solution.py:546
  88.8 6.2 %collective-permute-start.6 = (f32[80,128]{1,0:T(8,128)S(1)}, f32[80,128]{1,0:T(8,128)S(1)}, u32[]{:S(2)}, u32[]{:S(2)}) collective-permute-start(f32[80,128]{1,0:T(8,128)S(1)} %pad_maximum_fusion.1), channel_id=1, source_target_pairs={{1,0},{2,1},{3,2},{5,4},{6,5},{7,6},{9,8},{10,9},{11,10},{13,12},{... | collective-permute-start | bytes 122888 | tf_op jit(solution)/shard_map/ppermute | solution.py:547
  107.1 19.6 %collective-permute-start.10 = (f32[4,128]{1,0:T(4,128)S(1)}, f32[4,128]{1,0:T(4,128)S(1)}, u32[]{:S(2)}, u32[]{:S(2)}) collective-permute-start(f32[4,128]{1,0:T(4,128)S(1)} %get-tuple-element.48), channel_id=1, source_target_pairs={{0,17},{1,18},{2,19},{16,1},{17,2},{18,3},{4,21},{5,22},{6,23},{20... | collective-permute-start | bytes 6152 | tf_op jit(solution)/shard_map/ppermute | solution.py:558
  109.1 25.5 %collective-permute-start.11 = (f32[4,128]{1,0:T(4,128)S(1)}, f32[4,128]{1,0:T(4,128)S(1)}, u32[]{:S(2)}, u32[]{:S(2)}) collective-permute-start(f32[4,128]{1,0:T(4,128)S(1)} %get-tuple-element.49), channel_id=1, source_target_pairs={{1,16},{2,17},{3,18},{17,0},{18,1},{19,2},{5,20},{6,21},{7,22},{21... | collective-permute-start | bytes 6152 | tf_op jit(solution)/shard_map/ppermute | solution.py:559
  112.7 23.2 %collective-permute-start.8 = (f32[4,512]{1,0:T(4,128)S(1)}, f32[4,512]{1,0:T(4,128)S(1)}, u32[]{:S(2)}, u32[]{:S(2)}) collective-permute-start(f32[4,512]{1,0:T(4,128)S(1)} %get-tuple-element.46), channel_id=1, source_target_pairs={{0,20},{4,24},{8,28},{16,4},{20,8},{24,12},{1,21},{5,25},{9,29},{1... | collective-permute-start | bytes 24584 | tf_op jit(solution)/shard_map/ppermute | solution.py:556
  115.3 25.5 %collective-permute-start.9 = (f32[4,512]{1,0:T(4,128)S(1)}, f32[4,512]{1,0:T(4,128)S(1)}, u32[]{:S(2)}, u32[]{:S(2)}) collective-permute-start(f32[4,512]{1,0:T(4,128)S(1)} %get-tuple-element.47), channel_id=1, source_target_pairs={{4,16},{8,20},{12,24},{20,0},{24,4},{28,8},{5,17},{9,21},{13,25},{... | collective-permute-start | bytes 24584 | tf_op jit(solution)/shard_map/ppermute | solution.py:557
  126.7 20.4 %collective-permute-start.12 = (f32[4,512]{1,0:T(4,128)S(1)}, f32[4,512]{1,0:T(4,128)S(1)}, u32[]{:S(2)}, u32[]{:S(2)}) collective-permute-start(f32[4,512]{1,0:T(4,128)S(1)} %get-tuple-element.53), channel_id=1, source_target_pairs={{0,4},{4,8},{8,12},{1,5},{5,9},{9,13},{2,6},{6,10},{10,14},{3,7},{... | collective-permute-start | bytes 24584 | tf_op jit(solution)/shard_map/ppermute | solution.py:564
  134.6 12.6 %collective-permute-start.13 = (f32[4,512]{1,0:T(4,128)S(1)}, f32[4,512]{1,0:T(4,128)S(1)}, u32[]{:S(2)}, u32[]{:S(2)}) collective-permute-start(f32[4,512]{1,0:T(4,128)S(1)} %get-tuple-element.54), channel_id=1, source_target_pairs={{4,0},{8,4},{12,8},{5,1},{9,5},{13,9},{6,2},{10,6},{14,10},{7,3},{... | collective-permute-start | bytes 24584 | tf_op jit(solution)/shard_map/ppermute | solution.py:565
  135.9 11.3 %collective-permute-start.14 = (f32[4,128]{1,0:T(4,128)S(1)}, f32[4,128]{1,0:T(4,128)S(1)}, u32[]{:S(2)}, u32[]{:S(2)}) collective-permute-start(f32[4,128]{1,0:T(4,128)S(1)} %get-tuple-element.55), channel_id=1, source_target_pairs={{0,1},{1,2},{2,3},{4,5},{5,6},{6,7},{8,9},{9,10},{10,11},{12,13},{... | collective-permute-start | bytes 6152 | tf_op jit(solution)/shard_map/ppermute | solution.py:566
  140.9 6.3 %collective-permute-start.15 = (f32[4,128]{1,0:T(4,128)S(1)}, f32[4,128]{1,0:T(4,128)S(1)}, u32[]{:S(2)}, u32[]{:S(2)}) collective-permute-start(f32[4,128]{1,0:T(4,128)S(1)} %get-tuple-element.56), channel_id=1, source_target_pairs={{1,0},{2,1},{3,2},{5,4},{6,5},{7,6},{9,8},{10,9},{11,10},{13,12},{... | collective-permute-start | bytes 6152 | tf_op jit(solution)/shard_map/ppermute | solution.py:567

commit v4 on v3

--- a/solution.py
+++ b/solution.py
@@ -30,11 +30,41 @@
     return lax.div(value, parts), lax.rem(value, parts)
 
 
-def contribution_kernel(dims, src_ref, dev_ref, blk_ref, state_ref, weights_ref, *rest):
-    tiles, capacity, pairs, fields, cells_x, cells_y, width, chunks = dims
-    outs = rest[: len(chunks)]
-    cells, w_ref, pair_v, pair_s, taken = rest[len(chunks) : len(chunks) + 5]
-    field_sems, weight_sems, pair_sems = rest[len(chunks) + 5 :]
+def slot_table(dev, blk, tiles, capacity):
+    pairs = dev.shape[1]
+    tile_of = lax.broadcasted_iota(jnp.int32, (tiles, pairs), 0)
+    lane_of = lax.broadcasted_iota(jnp.int32, (tiles, pairs), 1)
+    member = (tile_of == dev).astype(jnp.float32)
+    total = member
+    shift = 1
+    while shift < pairs:
+        total = total + jnp.where(lane_of >= shift, pltpu.roll(total, shift, 1), 0.0)
+        shift *= 2
+    rank = (jnp.sum(member * total, axis=0, keepdims=True) - 1.0).astype(jnp.int32)
+    slot_of = lax.broadcasted_iota(jnp.int32, (LANES, pairs), 0) % capacity
+    chosen = (slot_of == rank).astype(jnp.bfloat16)
+
+    def spread(values):
+        return lax.dot_general(
+            (member * values).astype(jnp.bfloat16), chosen, NT, preferred_element_type=jnp.float32
+        )
+
+    high, low = split(blk, 256)
+    ids = spread(high.astype(jnp.float32)) * 256.0 + spread(low.astype(jnp.float32))
+    return rank, jnp.where(spread(jnp.ones(dev.shape, jnp.float32)) > 0.5, ids, -1.0)
+
+
+def put_ids(out, ids, tiles, capacity):
+    for t in range(tiles):
+        out[t * (capacity + 1) + capacity] = jnp.broadcast_to(ids[t : t + 1, :], out.shape[1:])
+
+
+def contribution_kernel(
+    dims, src_ref, dev_ref, blk_ref, state_ref, weights_ref, early_ref, late_ref,
+    cells, w_ref, pair_v, pair_s, taken, field_sems, weight_sems, pair_sems,
+):
+    tiles, capacity, pairs, fields, cells_x, cells_y, width = dims
+    half = fields // 2
     parts = cells_y // width
     steps = pairs // STEP_PAIRS
 
@@ -66,38 +96,19 @@
         copy.start()
     for step in range(steps):
         weight_copy(step).start()
-    for out in outs:
-        out[...] = jnp.zeros_like(out)
+    late_ref[...] = jnp.zeros_like(late_ref)
     for t in range(tiles):
         taken[t] = t * (capacity + 1)
 
     for copy in vector_copies:
         copy.wait()
     dev, blk = pair_v[0], pair_v[1]
-    tile_of = lax.broadcasted_iota(jnp.int32, (tiles, pairs), 0)
-    lane_of = lax.broadcasted_iota(jnp.int32, (tiles, pairs), 1)
-    member = (tile_of == dev).astype(jnp.float32)
-    total = member
-    shift = 1
-    while shift < pairs:
-        total = total + jnp.where(lane_of >= shift, pltpu.roll(total, shift, 1), 0.0)
-        shift *= 2
-    rank = (jnp.sum(member * total, axis=0, keepdims=True) - 1.0).astype(jnp.int32)
-    slot_of = lax.broadcasted_iota(jnp.int32, (LANES, pairs), 0) % capacity
-    chosen = (slot_of == rank).astype(jnp.bfloat16)
-
-    def spread(values):
-        return lax.dot_general(
-            (member * values).astype(jnp.bfloat16), chosen, NT, preferred_element_type=jnp.float32
-        )
-
-    high, low = split(blk, 256)
-    ids = spread(high.astype(jnp.float32)) * 256.0 + spread(low.astype(jnp.float32))
-    ids = jnp.where(spread(jnp.ones(dev.shape, jnp.float32)) > 0.5, ids, -1.0)
-    for t in range(tiles):
-        row = jnp.broadcast_to(ids[t : t + 1, :], (fields, LANES))
-        for out in outs:
-            out[t * (capacity + 1) + capacity] = row[: out.shape[1]]
+    _, ids = slot_table(dev, blk, tiles, capacity)
+    put_ids(late_ref, ids, tiles, capacity)
+    code = (dev * (cells_x * parts) + blk).astype(jnp.float32)
+    for i in range(pairs // width):
+        place = (pairs + i // half, slice(i % half, i % half + 1), slice(None))
+        early_ref[place] = code[:, i * width : (i + 1) * width]
     for copy in scalar_copies + field_copies:
         copy.wait()
 
@@ -117,21 +128,21 @@
                 slot = taken[tile]
                 taken[tile] = slot + 1
                 one = both[j * fields : (j + 1) * fields, j * width : (j + 1) * width]
-                for out, (first, last) in zip(outs, chunks):
-                    out[slot] = one[first:last]
+                early_ref[p + j] = one[:half]
+                late_ref[slot] = one[half:]
         return carry
 
     lax.fori_loop(0, steps, some_pairs, 0)
 
 
-def contributions(state, pair_src, pair_dev, pair_blk, weights, tiles, capacity, chunks):
+def contributions(state, pair_src, pair_dev, pair_blk, weights, tiles, capacity, fields):
     _, _, cells_x, cells_y = state.shape
-    fields = chunks[-1][1]
+    half = fields // 2
     pairs, width = weights.shape[1], weights.shape[2]
     rows = tiles * (capacity + 1)
-    dims = (tiles, capacity, pairs, fields, cells_x, cells_y, width, chunks)
+    dims = (tiles, capacity, pairs, fields, cells_x, cells_y, width)
     parts = cells_y // width
-    shapes = [(rows, last - first, width) for first, last in chunks]
+    shapes = [(pairs + -(-pairs // (half * width)), half, width), (rows, half, width)]
     return pl.pallas_call(
         functools.partial(contribution_kernel, dims),
         in_specs=[pl.BlockSpec(memory_space=pltpu.HBM)] * 5,
@@ -147,7 +158,7 @@
             pltpu.SemaphoreType.DMA((pairs // STEP_PAIRS,)),
             pltpu.SemaphoreType.DMA((4,)),
         ],
-        compiler_params=pltpu.CompilerParams(vmem_limit_bytes=47 * 1024 * 1024),
+        compiler_params=pltpu.CompilerParams(vmem_limit_bytes=56 * 1024 * 1024),
         cost_estimate=pl.CostEstimate(
             flops=2 * pairs * fields * width * width,
             bytes_accessed=2 * pairs * width * width + 8 * rows * fields * width,
@@ -155,6 +166,49 @@
         ),
         name="contributions",
     )(pair_src, pair_dev.reshape(1, pairs), pair_blk, state, weights)
+
+
+def place_kernel(dims, in_ref, out_ref, place_v, place_s, place_sem):
+    tiles, capacity, pairs, blocks = dims
+    half, width = in_ref.shape[1:]
+    code = jnp.concatenate(
+        [in_ref[pairs + i // half][i % half : i % half + 1] for i in range(pairs // width)], axis=1
+    ).astype(jnp.int32)
+    dev, blk = split(code, blocks)
+    rank, ids = slot_table(dev, blk, tiles, capacity)
+    place_v[...] = jnp.broadcast_to(dev * (capacity + 1) + rank, place_v.shape)
+    copy = pltpu.make_async_copy(place_v, place_s, place_sem)
+    copy.start()
+    out_ref[...] = jnp.zeros_like(out_ref)
+    put_ids(out_ref, ids, tiles, capacity)
+    copy.wait()
+
+    def some_rows(step, carry):
+        for i in range(STEP_PAIRS):
+            p = step * STEP_PAIRS + i
+            out_ref[place_s[0, p]] = in_ref[p]
+        return carry
+
+    lax.fori_loop(0, pairs // STEP_PAIRS, some_rows, 0)
+
+
+def placed_rows(rows, tiles, capacity, pairs, blocks):
+    half, width = rows.shape[1:]
+    shape = (tiles * (capacity + 1), half, width)
+    return pl.pallas_call(
+        functools.partial(place_kernel, (tiles, capacity, pairs, blocks)),
+        out_shape=jax.ShapeDtypeStruct(shape, jnp.float32),
+        scratch_shapes=[
+            pltpu.VMEM((8, pairs), jnp.int32),
+            pltpu.SMEM((8, pairs), jnp.int32),
+            pltpu.SemaphoreType.DMA,
+        ],
+        compiler_params=pltpu.CompilerParams(vmem_limit_bytes=40 * 1024 * 1024),
+        cost_estimate=pl.CostEstimate(
+            flops=4 * rows.size, bytes_accessed=12 * rows.size, transcendentals=0
+        ),
+        name="place_in_slots",
+    )(rows)
 
 
 def sum_kernel(dims, in_ref, out_ref, top_ref, bottom_ref, left_ref, right_ref, pick, high, low):
@@ -327,7 +381,7 @@
         in_specs=specs,
         out_specs=[pl.BlockSpec(shape, lambda i: (0, 0)) for shape in shapes],
         out_shape=[jax.ShapeDtypeStruct(shape, jnp.float32) for shape in shapes],
-        compiler_params=pltpu.CompilerParams(vmem_limit_bytes=56 * 1024 * 1024),
+        compiler_params=pltpu.CompilerParams(vmem_limit_bytes=40 * 1024 * 1024),
         cost_estimate=pl.CostEstimate(
             flops=state.size, bytes_accessed=4 * 1024 * 1024, transcendentals=0
         ),
@@ -429,26 +483,36 @@
 
 
 def finish_kernel(
-    first, gamma_ref, mix_ref, factors, above, below, before, after, base_ref, recv_ref,
-    top_ref, bottom_ref, left_ref, right_ref, *rest
+    half, gamma_ref, mix_ref, factors, above, below, before, after, base_ref, early_ref, late_ref, *rest
 ):
-    new_ref, out_ref, wide = rest[-3:]
+    early_rims, late_rims = rest[:4], rest[4:8]
+    new_ref, out_ref, wide, cols = rest[8:]
     f = pl.program_id(0)
-    rate = gamma_ref[0, first + f]
+    rate = gamma_ref[0, f]
     mix_b = mix_ref[0, 1]
-    recv = recv_ref[0]
-    g = factors[0] * recv * rate
-    row = pl.ds(f, 1)
+    cells_x, cells_y = base_ref.shape[2:]
     keep_row = above.shape[0] - 5
     keep = slice(keep_row, keep_row + 1)
-    cells_x, cells_y = recv.shape
-    left = before[keep, :] * left_ref[row, :] * rate
-    right = after[keep, :] * right_ref[row, :] * rate
-    cols = columns_of(jnp.concatenate([left, right], axis=0))
-    wide[STRIP - 1 : STRIP, :] = above[keep, :] * top_ref[row, :] * rate
-    wide[STRIP + cells_x : STRIP + cells_x + 1, :] = below[keep, :] * bottom_ref[row, :] * rate
-    wide[STRIP : STRIP + cells_x, :] = g
-    out_ref[0, 0] = recv
+
+    def widen(recv_ref, rims, f):
+        top, bottom, left, right = (rim[pl.ds(f, 1), :] for rim in rims)
+        wide[STRIP - 1 : STRIP, :] = above[keep, :] * top * rate
+        wide[STRIP + cells_x : STRIP + cells_x + 1, :] = below[keep, :] * bottom * rate
+        sides = [before[keep, :] * left * rate, after[keep, :] * right * rate]
+        cols[...] = columns_of(jnp.concatenate(sides, axis=0))
+        for i in range(0, cells_x, STRIP):
+            recv = recv_ref[0, i : i + STRIP, :]
+            out_ref[0, 0, i : i + STRIP, :] = recv
+            wide[STRIP + i : 2 * STRIP + i, :] = factors[0, i : i + STRIP, :] * recv * rate
+
+    @pl.when(f < half)
+    def _():
+        widen(early_ref, early_rims, f)
+
+    @pl.when(f >= half)
+    def _():
+        widen(late_ref, late_rims, f - half)
+
     lane = lax.broadcasted_iota(jnp.int32, (STRIP, cells_y), 1)
     for i in range(0, cells_x, STRIP):
         rows = slice(i, i + STRIP)
@@ -462,43 +526,40 @@
         new_ref[0, 0, rows, :] = base_ref[0, 0, rows, :] + mix_b * (2.0 * mid + more)
 
 
-def finished(first, new_state, remapped, recv, rims, gamma, mix, factors, received):
-    fields, cells_x, cells_y = recv.shape
-    chan = gamma.shape[1]
+def finished(base, early, early_rims, late, late_rims, gamma, mix, factors, received):
+    half, cells_x, cells_y = early.shape
     whole = lambda a: pl.BlockSpec(a.shape, lambda f: (0,) * a.ndim)
-    field = pl.BlockSpec((1, 1, cells_x, cells_y), lambda f: (0, first + f, 0, 0))
-    operands = [gamma, mix, factors, *received, new_state, recv, *rims]
-    specs = [
-        pl.BlockSpec(memory_space=pltpu.SMEM),
-        pl.BlockSpec(memory_space=pltpu.SMEM),
-        whole(factors),
-        *[whole(lines) for lines in received],
-        field,
-        pl.BlockSpec((1, cells_x, cells_y), lambda f: (f, 0, 0)),
-        *[whole(rim) for rim in rims],
-    ]
-    aliases = {7: 0}
-    if remapped is not None:
-        aliases[len(operands)] = 1
-        operands.append(remapped)
-        specs.append(pl.BlockSpec(memory_space=pl.ANY))
+    field = pl.BlockSpec((1, 1, cells_x, cells_y), lambda f: (0, f, 0, 0))
+    recv = lambda at: pl.BlockSpec((1, cells_x, cells_y), lambda f: (at(f), 0, 0))
     return pl.pallas_call(
-        functools.partial(finish_kernel, first),
-        grid=(fields,),
-        in_specs=specs,
+        functools.partial(finish_kernel, half),
+        grid=(2 * half,),
+        in_specs=[
+            pl.BlockSpec(memory_space=pltpu.SMEM),
+            pl.BlockSpec(memory_space=pltpu.SMEM),
+            whole(factors),
+            *[whole(lines) for lines in received],
+            field,
+            recv(lambda f: jnp.minimum(f, half - 1)),
+            recv(lambda f: jnp.maximum(f - half, 0)),
+            *[whole(rim) for rim in (*early_rims, *late_rims)],
+        ],
         out_specs=[field, field],
         out_shape=[
-            jax.ShapeDtypeStruct(new_state.shape, jnp.float32),
-            jax.ShapeDtypeStruct((1, chan, cells_x, cells_y), jnp.float32),
-        ],
-        input_output_aliases=aliases,
-        scratch_shapes=[pltpu.VMEM((cells_x + 2 * STRIP, cells_y), jnp.float32)],
+            jax.ShapeDtypeStruct(base.shape, jnp.float32),
+            jax.ShapeDtypeStruct((1, 2 * half, cells_x, cells_y), jnp.float32),
+        ],
+        input_output_aliases={7: 0},
+        scratch_shapes=[
+            pltpu.VMEM((cells_x + 2 * STRIP, cells_y), jnp.float32),
+            pltpu.VMEM((cells_x, 8), jnp.float32),
+        ],
         compiler_params=pltpu.CompilerParams(vmem_limit_bytes=40 * 1024 * 1024),
         cost_estimate=pl.CostEstimate(
-            flops=20 * recv.size, bytes_accessed=20 * recv.size, transcendentals=0
+            flops=40 * early.size, bytes_accessed=40 * early.size, transcendentals=0
         ),
         name="finish",
-    )(*operands)
+    )(gamma, mix, factors, *received, base, early, late, *early_rims, *late_rims)
 
 
 def body(state, coefs, land_sea, gamma, pair_src, pair_dev, pair_blk, weights):
@@ -509,9 +570,8 @@
     pairs, width = weights.shape[1], weights.shape[2]
     capacity = max(2, 2 * pairs // tiles)
     half = chan // 2
-    chunks = ((0, half), (half, chan))
     early, late = contributions(
-        state, pair_src, pair_dev, pair_blk, weights, tiles, capacity, chunks
+        state, pair_src, pair_dev, pair_blk, weights, tiles, capacity, chan
     )
     swap = [(0, 1), (1, 0)]
 
@@ -523,7 +583,8 @@
         return summed(rows, tiles, capacity, half, cells_x, cells_y, width)
 
     late_in = exchanged(late)
-    early_in = lax.ppermute(early, "comp", swap)
+    early = lax.ppermute(early, "comp", swap)
+    early_in = placed_rows(early, tiles, capacity, pairs, cells_x * cells_y // width)
 
     land_after, _ = lax.optimization_barrier((land_sea, late))
     is_atmos = lax.axis_index("comp") == 0
@@ -566,10 +627,9 @@
         lax.ppermute(right, "ty", shift_pairs(ty, 1)),
         lax.ppermute(left, "ty", shift_pairs(ty, -1)),
     )
-    rest = (gamma, mix, factors, received)
-    new_state, remapped = finished(half, base, None, recv_late, rims_late, *rest)
-    new_state, remapped = finished(0, new_state, remapped, recv_early, rims_early, *rest)
-    return new_state, remapped
+    return finished(
+        base, recv_early, rims_early, recv_late, rims_late, gamma, mix, factors, received
+    )
 
 
 def solution(mesh):

time: 152 us -> 150 us (0.987)
  waiting for transfers between devices: 42.8 us -> 32.5 us
  starting transfers between devices: 58.3 us -> 62.8 us
  Pallas kernels: 43.7 us -> 46.7 us
  local copies, waits for them, and re-layouts: 4.82 us -> 6.37 us
    ppermute x1, waiting for transfers between devices: 13.8 us -> 6.43 us  [body(): above = lax.ppermute(x_high, 'tx', shift_pairs(tx, 1))]
    ppermute x1, waiting for transfers between devices: 6.81 us -> 0.01 us  [body(): right = lax.ppermute(y_low, 'ty', shift_pairs(ty, -1))]
    all_to_all x2, starting transfers between devices: 14.3 us -> 19.9 us  [exchanged(): lax.all_to_all(rows, ('tx', 'ty'), split_axis=0, concat_axis=0, tiled=True)]
    pallas_call x2, Pallas kernels: 8.44 us -> 12.7 us  [the longest x1 7.44 us: finished(): pl.pallas_call(functools.partial(finish_kernel, half), grid=(2 * half,),...]
    ppermute x1, waiting for transfers between devices: 0.01 us -> 2.95 us  [body(): lax.ppermute(left, 'ty', shift_pairs(ty, -1))]
    ppermute x1, waiting for transfers between devices: 11.3 us -> 9.08 us  [body(): early = lax.ppermute(early, 'comp', swap)]
    all_to_all x2, waiting for transfers between devices: 6.66 us -> 8.61 us  [exchanged(): lax.all_to_all(rows, ('tx', 'ty'), split_axis=0, concat_axis=0, tiled=True)]
    pallas_call x1, Pallas kernels: 3.92 us -> 2 us  [edges_of(): pl.pallas_call(edge_kernel, grid=(1,), in_specs=specs, out_specs=[pl.Bloc...]
  transfers between devices with their start and end apart: 18 -> 18, of which waited for: 6 -> 6; matrix products, arithmetic and copies ran while one was open for 0% -> 0% of each run, Pallas kernels for 17% -> 16%
where the time goes in v4:
time: 150 us; the launch traced here: 149 us
  starting transfers between devices  62.8 us (42%)
  Pallas kernels  46.7 us (31%)
  waiting for transfers between devices  32.5 us (22%)
  local copies, waits for them, and re-layouts  6.37 us (4%)
    all_to_all x2, starting transfers between devices, exchanged(): lax.all_to_all(rows, ('tx', 'ty'), split_axis=0, concat_axis=0, tiled=True)  19.9 us
    pallas_call x1, Pallas kernels, contributions(): pl.pallas_call(functools.partial(contribution_kernel, dims), in_specs=[pl...  15 us
    pallas_call x1, Pallas kernels, base_of(): pl.pallas_call(base_kernel, grid=(nfield,), in_specs=[pl.BlockSpec(memory...  12.6 us
    ppermute x1, waiting for transfers between devices, body(): early = lax.ppermute(early, 'comp', swap)  9.08 us
    all_to_all x2, waiting for transfers between devices, exchanged(): lax.all_to_all(rows, ('tx', 'ty'), split_axis=0, concat_axis=0, tiled=True)  8.61 us
    ppermute x1, starting transfers between devices, body(): lax.ppermute(bottom, 'tx', shift_pairs(tx, 1))  7.84 us
    pallas_call x1, Pallas kernels, finished(): pl.pallas_call(functools.partial(finish_kernel, half), grid=(2 * half,),...  7.44 us
    ppermute x1, waiting for transfers between devices, body(): above = lax.ppermute(x_high, 'tx', shift_pairs(tx, 1))  6.43 us
  transfers between devices with their start and end apart: 18, of which 6 were waited for; matrix products, arithmetic and copies ran while one was open for 0% of the time, Pallas kernels for 16%

profile of v4, /device:TPU:1, one launch (start us, length us, event | category | flops | bytes accessed | tf_op | source)
XLA Modules:
  0.0 149.4 jit_solution(13648522430810880534)
XLA Ops:
  0.6 15.0 %contributions.1 = (f32[513,4,128]{2,1,0:T(4,128)}, f32[1040,4,128]{2,1,0:T(4,128)}) custom-call(s32[1,512]{1,0:T(1,128)} %src_ref.1, s32[1,512]{1,0:T(1,128)} %bitcast.10, s32[1,512]{1,0:T(1,128)} %blk_ref.1, f32[1,16,128,512]{3,2,1,0:T(8,128)} %state_ref.3, bf16[1,512,128,128]{3,2,1,0:T(8,128)(2,1)} %weights_ref.1), custom_call_target="tpu_custom_call" | custom-call | flops 134217728 | bytes 25296896 | tf_op jit(solution)/shard_map/contributions/pallas_call | solution.py:146
  15.6 0.0 copy-start.13
  15.6 0.0 copy-start.2
  15.6 0.0 copy-start.3
  15.6 7.5 %all-to-all-start.1 = ((f32[16,65,4,128]{3,2,1,0:T(4,128)}), f32[16,65,4,128]{3,2,1,0:T(4,128)S(1)}, u32[]{:S(2)}, u32[]{:S(2)}) async-start(f32[16,65,4,128]{3,2,1,0:T(4,128)} %bitcast.9), calls=%async_computation.1 | async-start | bytes 4259840 | tf_op jit(solution)/shard_map/all_to_all | solution.py:580
  23.1 1.2 collective-permute-start
  24.4 0.0 copy-start
  24.4 2.2 %copy-done = f32[1,16,128,512]{3,2,1,0:T(8,128)S(1)} copy-done((f32[1,16,128,512]{3,2,1,0:T(8,128)S(1)}, f32[1,16,128,512]{3,2,1,0:T(8,128)}, u32[]{:S(2)}) %copy-start) | copy-done | bytes 4194328
  26.6 2.0 %edges.1 = (f32[40,512]{1,0:T(8,128)S(1)}, f32[40,512]{1,0:T(8,128)S(1)}, f32[40,128]{1,0:T(8,128)S(1)}, f32[40,128]{1,0:T(8,128)S(1)}) custom-call(f32[1,2]{1,0:T(1,128)S(1)} %broadcast_select_fusion.mix_ref, f32[1,16,128,512]{3,2,1,0:T(8,128)S(1)} %copy-done, f32[1,16,128,512]{3,2,1,0:T(8,128)S(1)} %copy-done, f32[1,16,128,512]{3,2,1,0:T(8,128)S(1)} %copy-done, ...), custom_call_target="tpu_custom_call" | custom-call | flops 1048576 | bytes 4194304 | tf_op jit(solution)/shard_map/edges/pallas_call | solution.py:378
  28.6 3.3 %collective-permute-start.1 = (f32[40,512]{1,0:T(8,128)S(1)}, f32[40,512]{1,0:T(8,128)S(1)}, u32[]{:S(2)}, u32[]{:S(2)}) collective-permute-start(f32[40,512]{1,0:T(8,128)S(1)} %get-tuple-element.31.x_high), channel_id=1, source_target_pairs={{0,4},{4,8},{8,12},{1,5},{5,9},{9,13},{2,6},{6,10},{10,14},{3,7},{... | collective-permute-start | bytes 245768 | tf_op jit(solution)/shard_map/ppermute | solution.py:597
  31.9 1.3 collective-permute-start.2
  33.2 3.9 %collective-permute-start.3 = (f32[40,128]{1,0:T(8,128)S(1)}, f32[40,128]{1,0:T(8,128)S(1)}, u32[]{:S(2)}, u32[]{:S(2)}) collective-permute-start(f32[40,128]{1,0:T(8,128)S(1)} %get-tuple-element.33.y_high), channel_id=1, source_target_pairs={{0,1},{1,2},{2,3},{4,5},{5,6},{6,7},{8,9},{9,10},{10,11},{12,13},{... | collective-permute-start | bytes 61448 | tf_op jit(solution)/shard_map/ppermute | solution.py:595
  37.1 1.9 %collective-permute-start.4 = (f32[40,128]{1,0:T(8,128)S(1)}, f32[40,128]{1,0:T(8,128)S(1)}, u32[]{:S(2)}, u32[]{:S(2)}) collective-permute-start(f32[40,128]{1,0:T(8,128)S(1)} %get-tuple-element.34.y_low), channel_id=1, source_target_pairs={{1,0},{2,1},{3,2},{5,4},{6,5},{7,6},{9,8},{10,9},{11,10},{13,12},{... | collective-permute-start | bytes 61448 | tf_op jit(solution)/shard_map/ppermute | solution.py:596
  39.0 9.1 %collective-permute-done.in_ref = f32[513,4,128]{2,1,0:T(4,128)} collective-permute-done((f32[513,4,128]{2,1,0:T(4,128)}, f32[513,4,128]{2,1,0:T(4,128)}, u32[]{:S(2)}, u32[]{:S(2)}) %collective-permute-start) | collective-permute-done | bytes 1050656 | tf_op jit(solution)/shard_map/ppermute | solution.py:586
  48.1 5.3 %place_in_slots.1 = f32[1040,4,128]{2,1,0:T(4,128)} custom-call(f32[513,4,128]{2,1,0:T(4,128)} %collective-permute-done.in_ref), custom_call_target="tpu_custom_call" | custom-call | flops 1050624 | bytes 3151872 | tf_op jit(solution)/shard_map/place_in_slots/pallas_call | solution.py:198
  53.4 0.0 collective-permute-done.3.left.before
  53.4 6.4 %collective-permute-done.1.above = f32[40,512]{1,0:T(8,128)S(1)} collective-permute-done((f32[40,512]{1,0:T(8,128)S(1)}, f32[40,512]{1,0:T(8,128)S(1)}, u32[]{:S(2)}, u32[]{:S(2)}) %collective-permute-start.1) | collective-permute-done | bytes 81952 | tf_op jit(solution)/shard_map/ppermute | solution.py:597
  59.8 5.3 %all-to-all-done.1 = f32[16,65,4,128]{3,2,1,0:T(4,128)S(1)} async-done(((f32[16,65,4,128]{3,2,1,0:T(4,128)}), f32[16,65,4,128]{3,2,1,0:T(4,128)S(1)}, u32[]{:S(2)}, u32[]{:S(2)}) %all-to-all-start.1) | async-done | bytes 2129952 | tf_op jit(solution)/shard_map/all_to_all | solution.py:580
  65.2 1.3 copy-done.4
  66.5 12.4 %all-to-all-start = ((f32[16,65,4,128]{3,2,1,0:T(4,128)}), f32[16,65,4,128]{3,2,1,0:T(4,128)S(1)}, u32[]{:S(2)}, u32[]{:S(2)}) async-start(f32[16,65,4,128]{3,2,1,0:T(4,128)} %bitcast.1), calls=%async_computation | async-start | bytes 4259840 | tf_op jit(solution)/shard_map/all_to_all | solution.py:580
  78.9 1.6 %copy-done.5 = f32[16,65,4,128]{3,2,1,0:T(4,128)S(1)} copy-done((f32[16,65,4,128]{3,2,1,0:T(4,128)S(1)}, f32[16,65,4,128]{3,2,1,0:T(4,128)}, u32[]{:S(2)}) %copy-start.5) | copy-done | bytes 2129944
  80.5 2.7 %sum_by_block.3 = (f32[4,128,512]{2,1,0:T(8,128)}, f32[4,512]{1,0:T(4,128)}, f32[4,512]{1,0:T(4,128)}, f32[4,128]{1,0:T(4,128)}, f32[4,128]{1,0:T(4,128)}) custom-call(f32[4160,128]{1,0:T(8,128)S(1)} %bitcast.8), custom_call_target="tpu_custom_call" | custom-call | flops 1073741824 | bytes 3145728 | tf_op jit(solution)/shard_map/sum_by_block/pallas_call | solution.py:266
  83.2 1.2 collective-permute-start.7
  84.5 3.8 %collective-permute-start.5 = (f32[80,128]{1,0:T(8,128)S(1)}, f32[80,128]{1,0:T(8,128)S(1)}, u32[]{:S(2)}, u32[]{:S(2)}) collective-permute-start(f32[80,128]{1,0:T(8,128)S(1)} %pad_maximum_fusion), channel_id=1, source_target_pairs={{0,1},{1,2},{2,3},{4,5},{5,6},{6,7},{8,9},{9,10},{10,11},{12,13},{... | collective-permute-start | bytes 122888 | tf_op jit(solution)/shard_map/ppermute | solution.py:607
  88.3 1.9 %collective-permute-start.6 = (f32[80,128]{1,0:T(8,128)S(1)}, f32[80,128]{1,0:T(8,128)S(1)}, u32[]{:S(2)}, u32[]{:S(2)}) collective-permute-start(f32[80,128]{1,0:T(8,128)S(1)} %pad_maximum_fusion.1), channel_id=1, source_target_pairs={{1,0},{2,1},{3,2},{5,4},{6,5},{7,6},{9,8},{10,9},{11,10},{13,12},{... | collective-permute-start | bytes 122888 | tf_op jit(solution)/shard_map/ppermute | solution.py:608
  90.3 0.0 collective-permute-done.5.corners_left
  90.3 5.4 %collective-permute-done.6.corners_right = f32[80,128]{1,0:T(8,128)S(1)} collective-permute-done((f32[80,128]{1,0:T(8,128)S(1)}, f32[80,128]{1,0:T(8,128)S(1)}, u32[]{:S(2)}, u32[]{:S(2)}) %collective-permute-start.6) | collective-permute-done | bytes 40992 | tf_op jit(solution)/shard_map/ppermute | solution.py:608
  95.6 0.1 broadcast_in_dim.8.rates_ref
  95.7 12.6 %base.1 = (f32[1,16,128,512]{3,2,1,0:T(8,128)}, f32[6,128,512]{2,1,0:T(8,128)S(1)}) custom-call(f32[1,16]{1,0:T(1,128)S(1)} %get-tuple-element.59.rate_ref, f32[1,2]{1,0:T(1,128)S(1)} %broadcast_select_fusion.mix_ref, f32[16,128]{1,0:T(8,128)S(1)} %broadcast_in_dim.8.rates_ref, f32[1,3,128,512]{3,2,1,0:T(8,128)S(1)} %copy-done.2, s32[128,512]{1,0:T(8,128)S(1)} %copy-done.3, ...), custom_call_target="tpu_custom_call" | custom-call | flops 41943040 | bytes 8388608 | tf_op jit(solution)/shard_map/base/pallas_call | solution.py:459
  108.3 1.1 copy-done.6
  109.4 1.9 %collective-permute-start.14 = (f32[4,128]{1,0:T(4,128)}, f32[4,128]{1,0:T(4,128)S(1)}, u32[]{:S(2)}, u32[]{:S(2)}) collective-permute-start(f32[4,128]{1,0:T(4,128)} %get-tuple-element.52), channel_id=1, source_target_pairs={{0,17},{1,18},{2,19},{16,1},{17,2},{18,3},{4,21},{5,22},{6,23},{20... | collective-permute-start | bytes 6152 | tf_op jit(solution)/shard_map/ppermute | solution.py:619
  111.3 3.6 %collective-permute-start.15 = (f32[4,128]{1,0:T(4,128)}, f32[4,128]{1,0:T(4,128)S(1)}, u32[]{:S(2)}, u32[]{:S(2)}) collective-permute-start(f32[4,128]{1,0:T(4,128)} %get-tuple-element.53), channel_id=1, source_target_pairs={{1,16},{2,17},{3,18},{17,0},{18,1},{19,2},{5,20},{6,21},{7,22},{21... | collective-permute-start | bytes 6152 | tf_op jit(solution)/shard_map/ppermute | solution.py:620
  115.0 1.5 collective-permute-start.12
  116.4 1.3 collective-permute-start.13
  117.7 3.3 %all-to-all-done = f32[16,65,4,128]{3,2,1,0:T(4,128)S(1)} async-done(((f32[16,65,4,128]{3,2,1,0:T(4,128)}), f32[16,65,4,128]{3,2,1,0:T(4,128)S(1)}, u32[]{:S(2)}, u32[]{:S(2)}) %all-to-all-start) | async-done | bytes 2129952 | tf_op jit(solution)/shard_map/all_to_all | solution.py:580
  121.0 1.8 %sum_by_block.2 = (f32[4,128,512]{2,1,0:T(8,128)S(1)}, f32[4,512]{1,0:T(4,128)S(1)}, f32[4,512]{1,0:T(4,128)S(1)}, f32[4,128]{1,0:T(4,128)S(1)}, f32[4,128]{1,0:T(4,128)S(1)}) custom-call(f32[4160,128]{1,0:T(8,128)S(1)} %bitcast.7), custom_call_target="tpu_custom_call" | custom-call | flops 1073741824 | bytes 3145728 | tf_op jit(solution)/shard_map/sum_by_block/pallas_call | solution.py:266
  122.8 0.0 collective-permute-done.14.rest_6_
  122.8 7.8 %collective-permute-start.8 = (f32[4,512]{1,0:T(4,128)S(1)}, f32[4,512]{1,0:T(4,128)S(1)}, u32[]{:S(2)}, u32[]{:S(2)}) collective-permute-start(f32[4,512]{1,0:T(4,128)S(1)} %get-tuple-element.46), channel_id=1, source_target_pairs={{0,4},{4,8},{8,12},{1,5},{5,9},{9,13},{2,6},{6,10},{10,14},{3,7},{... | collective-permute-start | bytes 24584 | tf_op jit(solution)/shard_map/ppermute | solution.py:625
  130.7 1.3 collective-permute-start.9
  132.0 0.0 collective-permute-done.12.rest_4_
  132.0 5.0 %collective-permute-start.10 = (f32[4,128]{1,0:T(4,128)S(1)}, f32[4,128]{1,0:T(4,128)S(1)}, u32[]{:S(2)}, u32[]{:S(2)}) collective-permute-start(f32[4,128]{1,0:T(4,128)S(1)} %get-tuple-element.48), channel_id=1, source_target_pairs={{0,1},{1,2},{2,3},{4,5},{5,6},{6,7},{8,9},{9,10},{10,11},{12,13},{... | collective-permute-start | bytes 6152 | tf_op jit(solution)/shard_map/ppermute | solution.py:627
  137.0 0.0 collective-permute-done.13.rest_5_
  137.0 1.9 %collective-permute-start.11 = (f32[4,128]{1,0:T(4,128)S(1)}, f32[4,128]{1,0:T(4,128)S(1)}, u32[]{:S(2)}, u32[]{:S(2)}) collective-permute-start(f32[4,128]{1,0:T(4,128)S(1)} %get-tuple-element.49), channel_id=1, source_target_pairs={{1,0},{2,1},{3,2},{5,4},{6,5},{7,6},{9,8},{10,9},{11,10},{13,12},{... | collective-permute-start | bytes 6152 | tf_op jit(solution)/shard_map/ppermute | solution.py:628
  138.9 0.0 collective-permute-done.7.late_ref
  138.9 3.0 %collective-permute-done.11.rest_3_ = f32[4,128]{1,0:T(4,128)S(1)} collective-permute-done((f32[4,128]{1,0:T(4,128)S(1)}, f32[4,128]{1,0:T(4,128)S(1)}, u32[]{:S(2)}, u32[]{:S(2)}) %collective-permute-start.11) | collective-permute-done | bytes 2080 | tf_op jit(solution)/shard_map/ppermute | solution.py:628
  141.9 0.0 collective-permute-done.8.rest_0_
  141.9 0.0 collective-permute-done.9.rest_1_
  141.9 7.4 %finish.1 = (f32[1,16,128,512]{3,2,1,0:T(8,128)}, f32[1,8,128,512]{3,2,1,0:T(8,128)}) custom-call(f32[1,8]{1,0:T(1,128)S(1)} %copy-done.12, f32[1,2]{1,0:T(1,128)S(1)} %broadcast_select_fusion.mix_ref, f32[6,128,512]{2,1,0:T(8,128)S(1)} %copy-done.7, f32[40,512]{1,0:T(8,128)S(1)} %collective-permute-done.1.above, ...), custom_call_target="tpu_custom_call", output_to_operand_aliasing={{0}: (7, {})} | custom-call | flops 10485760 | bytes 10485760 | tf_op jit(solution)/shard_map/finish/pallas_call | solution.py:534
  (29 shorter events, 0.1 us)
Async XLA Ops:
  15.6 8.8 %copy-start.13 = (f32[1,2]{1,0:T(1,128)S(1)}, f32[1,2]{1,0:T(1,128)}, u32[]{:S(2)}) copy-start(f32[1,2]{1,0:T(1,128)} %constant.14.clone) | copy-start | bytes 28
  15.6 8.8 %copy-start.2 = (f32[1,3,128,512]{3,2,1,0:T(8,128)S(1)}, f32[1,3,128,512]{3,2,1,0:T(8,128)}, u32[]{:S(2)}) copy-start(f32[1,3,128,512]{3,2,1,0:T(8,128)} %coefs_ref.1) | copy-start | bytes 2359300
  15.6 8.8 %copy-start.3 = (s32[128,512]{1,0:T(8,128)S(1)}, s32[128,512]{1,0:T(8,128)}, u32[]{:S(2)}) copy-start(s32[128,512]{1,0:T(8,128)} %land_ref) | copy-start | bytes 786436
  15.6 49.5 %all-to-all-start.1 = ((f32[16,65,4,128]{3,2,1,0:T(4,128)}), f32[16,65,4,128]{3,2,1,0:T(4,128)S(1)}, u32[]{:S(2)}, u32[]{:S(2)}) async-start(f32[16,65,4,128]{3,2,1,0:T(4,128)} %bitcast.9), calls=%async_computation.1 | async-start | bytes 4259840 | tf_op jit(solution)/shard_map/all_to_all | solution.py:580
  23.1 25.0 %collective-permute-start = (f32[513,4,128]{2,1,0:T(4,128)}, f32[513,4,128]{2,1,0:T(4,128)}, u32[]{:S(2)}, u32[]{:S(2)}) collective-permute-start(f32[513,4,128]{2,1,0:T(4,128)} %get-tuple-element.28), channel_id=1, source_target_pairs={{0,16},{16,0},{1,17},{17,1},{2,18},{18,2},{3,19},{19,3},{4,20},{20... | collective-permute-start | bytes 3151880 | tf_op jit(solution)/shard_map/ppermute | solution.py:586
  24.4 2.2 %copy-start = (f32[1,16,128,512]{3,2,1,0:T(8,128)S(1)}, f32[1,16,128,512]{3,2,1,0:T(8,128)}, u32[]{:S(2)}) copy-start(f32[1,16,128,512]{3,2,1,0:T(8,128)} %state_ref.3) | copy-start | bytes 12582916
  28.6 31.3 %copy-start.8 = (f32[40,128]{1,0:T(8,128)}, f32[40,128]{1,0:T(8,128)S(1)}, u32[]{:S(2)}) copy-start(f32[40,128]{1,0:T(8,128)S(1)} %get-tuple-element.34.y_low) | copy-start | bytes 61444
  28.6 31.3 %copy-start.10 = (f32[40,128]{1,0:T(8,128)}, f32[40,128]{1,0:T(8,128)S(1)}, u32[]{:S(2)}) copy-start(f32[40,128]{1,0:T(8,128)S(1)} %get-tuple-element.33.y_high) | copy-start | bytes 61444
  28.6 31.2 %collective-permute-start.1 = (f32[40,512]{1,0:T(8,128)S(1)}, f32[40,512]{1,0:T(8,128)S(1)}, u32[]{:S(2)}, u32[]{:S(2)}) collective-permute-start(f32[40,512]{1,0:T(8,128)S(1)} %get-tuple-element.31.x_high), channel_id=1, source_target_pairs={{0,4},{4,8},{8,12},{1,5},{5,9},{9,13},{2,6},{6,10},{10,14},{3,7},{... | collective-permute-start | bytes 245768 | tf_op jit(solution)/shard_map/ppermute | solution.py:597
  31.9 27.9 %collective-permute-start.2 = (f32[40,512]{1,0:T(8,128)S(1)}, f32[40,512]{1,0:T(8,128)S(1)}, u32[]{:S(2)}, u32[]{:S(2)}) collective-permute-start(f32[40,512]{1,0:T(8,128)S(1)} %get-tuple-element.32.x_low), channel_id=1, source_target_pairs={{4,0},{8,4},{12,8},{5,1},{9,5},{13,9},{6,2},{10,6},{14,10},{7,3},{... | collective-permute-start | bytes 245768 | tf_op jit(solution)/shard_map/ppermute | solution.py:598
  33.2 20.2 %collective-permute-start.3 = (f32[40,128]{1,0:T(8,128)S(1)}, f32[40,128]{1,0:T(8,128)S(1)}, u32[]{:S(2)}, u32[]{:S(2)}) collective-permute-start(f32[40,128]{1,0:T(8,128)S(1)} %get-tuple-element.33.y_high), channel_id=1, source_target_pairs={{0,1},{1,2},{2,3},{4,5},{5,6},{6,7},{8,9},{9,10},{10,11},{12,13},{... | collective-permute-start | bytes 61448 | tf_op jit(solution)/shard_map/ppermute | solution.py:595
  37.1 16.3 %collective-permute-start.4 = (f32[40,128]{1,0:T(8,128)S(1)}, f32[40,128]{1,0:T(8,128)S(1)}, u32[]{:S(2)}, u32[]{:S(2)}) collective-permute-start(f32[40,128]{1,0:T(8,128)S(1)} %get-tuple-element.34.y_low), channel_id=1, source_target_pairs={{1,0},{2,1},{3,2},{5,4},{6,5},{7,6},{9,8},{10,9},{11,10},{13,12},{... | collective-permute-start | bytes 61448 | tf_op jit(solution)/shard_map/ppermute | solution.py:596
  65.2 1.3 copy-start.4
  66.5 54.5 %all-to-all-start = ((f32[16,65,4,128]{3,2,1,0:T(4,128)}), f32[16,65,4,128]{3,2,1,0:T(4,128)S(1)}, u32[]{:S(2)}, u32[]{:S(2)}) async-start(f32[16,65,4,128]{3,2,1,0:T(4,128)} %bitcast.1), calls=%async_computation | async-start | bytes 4259840 | tf_op jit(solution)/shard_map/all_to_all | solution.py:580
  78.9 1.6 %copy-start.5 = (f32[16,65,4,128]{3,2,1,0:T(4,128)S(1)}, f32[16,65,4,128]{3,2,1,0:T(4,128)}, u32[]{:S(2)}) copy-start(f32[16,65,4,128]{3,2,1,0:T(4,128)} %copy-done.4) | copy-start | bytes 6389764
  80.5 9.8 %copy-start.12 = (f32[1,8]{1,0:T(1,128)S(1)}, f32[1,8]{1,0:T(1,128)}, u32[]{:S(2)}) copy-start(f32[1,8]{1,0:T(1,128)} %gamma_ref.1) | copy-start | bytes 100
  80.5 15.2 %copy-start.1 = (f32[1,16,128,512]{3,2,1,0:T(8,128)S(1)}, f32[1,16,128,512]{3,2,1,0:T(8,128)}, u32[]{:S(2)}) copy-start(f32[1,16,128,512]{3,2,1,0:T(8,128)} %state_ref.3) | copy-start | bytes 12582916
  80.5 15.2 %copy-start.9 = (f32[40,128]{1,0:T(8,128)S(1)}, f32[40,128]{1,0:T(8,128)}, u32[]{:S(2)}) copy-start(f32[40,128]{1,0:T(8,128)} %copy-done.8) | copy-start | bytes 61444
  80.5 15.2 %copy-start.11 = (f32[40,128]{1,0:T(8,128)S(1)}, f32[40,128]{1,0:T(8,128)}, u32[]{:S(2)}) copy-start(f32[40,128]{1,0:T(8,128)} %copy-done.10) | copy-start | bytes 61444
  83.2 55.7 %collective-permute-start.7 = (f32[4,128,512]{2,1,0:T(8,128)}, f32[4,128,512]{2,1,0:T(8,128)}, u32[]{:S(2)}, u32[]{:S(2)}) collective-permute-start(f32[4,128,512]{2,1,0:T(8,128)} %get-tuple-element.45), channel_id=1, source_target_pairs={{0,16},{16,0},{1,17},{17,1},{2,18},{18,2},{3,19},{19,3},{4,20},{20... | collective-permute-start | bytes 3145736 | tf_op jit(solution)/shard_map/ppermute | solution.py:615
  84.5 5.8 %collective-permute-start.5 = (f32[80,128]{1,0:T(8,128)S(1)}, f32[80,128]{1,0:T(8,128)S(1)}, u32[]{:S(2)}, u32[]{:S(2)}) collective-permute-start(f32[80,128]{1,0:T(8,128)S(1)} %pad_maximum_fusion), channel_id=1, source_target_pairs={{0,1},{1,2},{2,3},{4,5},{5,6},{6,7},{8,9},{9,10},{10,11},{12,13},{... | collective-permute-start | bytes 122888 | tf_op jit(solution)/shard_map/ppermute | solution.py:607
  88.3 7.3 %collective-permute-start.6 = (f32[80,128]{1,0:T(8,128)S(1)}, f32[80,128]{1,0:T(8,128)S(1)}, u32[]{:S(2)}, u32[]{:S(2)}) collective-permute-start(f32[80,128]{1,0:T(8,128)S(1)} %pad_maximum_fusion.1), channel_id=1, source_target_pairs={{1,0},{2,1},{3,2},{5,4},{6,5},{7,6},{9,8},{10,9},{11,10},{13,12},{... | collective-permute-start | bytes 122888 | tf_op jit(solution)/shard_map/ppermute | solution.py:608
  108.3 1.1 copy-start.6
  109.4 13.4 %collective-permute-start.14 = (f32[4,128]{1,0:T(4,128)}, f32[4,128]{1,0:T(4,128)S(1)}, u32[]{:S(2)}, u32[]{:S(2)}) collective-permute-start(f32[4,128]{1,0:T(4,128)} %get-tuple-element.52), channel_id=1, source_target_pairs={{0,17},{1,18},{2,19},{16,1},{17,2},{18,3},{4,21},{5,22},{6,23},{20... | collective-permute-start | bytes 6152 | tf_op jit(solution)/shard_map/ppermute | solution.py:619
  111.3 19.4 %collective-permute-start.15 = (f32[4,128]{1,0:T(4,128)}, f32[4,128]{1,0:T(4,128)S(1)}, u32[]{:S(2)}, u32[]{:S(2)}) collective-permute-start(f32[4,128]{1,0:T(4,128)} %get-tuple-element.53), channel_id=1, source_target_pairs={{1,16},{2,17},{3,18},{17,0},{18,1},{19,2},{5,20},{6,21},{7,22},{21... | collective-permute-start | bytes 6152 | tf_op jit(solution)/shard_map/ppermute | solution.py:620
  115.0 17.0 %collective-permute-start.12 = (f32[4,512]{1,0:T(4,128)}, f32[4,512]{1,0:T(4,128)S(1)}, u32[]{:S(2)}, u32[]{:S(2)}) collective-permute-start(f32[4,512]{1,0:T(4,128)} %get-tuple-element.50), channel_id=1, source_target_pairs={{0,20},{4,24},{8,28},{16,4},{20,8},{24,12},{1,21},{5,25},{9,29},{1... | collective-permute-start | bytes 24584 | tf_op jit(solution)/shard_map/ppermute | solution.py:617
  116.4 20.6 %collective-permute-start.13 = (f32[4,512]{1,0:T(4,128)}, f32[4,512]{1,0:T(4,128)S(1)}, u32[]{:S(2)}, u32[]{:S(2)}) collective-permute-start(f32[4,512]{1,0:T(4,128)} %get-tuple-element.51), channel_id=1, source_target_pairs={{4,16},{8,20},{12,24},{20,0},{24,4},{28,8},{5,17},{9,21},{13,25},{... | collective-permute-start | bytes 24584 | tf_op jit(solution)/shard_map/ppermute | solution.py:618
  121.0 20.9 %copy-start.7 = (f32[6,128,512]{2,1,0:T(8,128)S(1)}, f32[6,128,512]{2,1,0:T(8,128)}, u32[]{:S(2)}) copy-start(f32[6,128,512]{2,1,0:T(8,128)} %copy-done.6) | copy-start | bytes 4718596
  122.8 19.1 %collective-permute-start.8 = (f32[4,512]{1,0:T(4,128)S(1)}, f32[4,512]{1,0:T(4,128)S(1)}, u32[]{:S(2)}, u32[]{:S(2)}) collective-permute-start(f32[4,512]{1,0:T(4,128)S(1)} %get-tuple-element.46), channel_id=1, source_target_pairs={{0,4},{4,8},{8,12},{1,5},{5,9},{9,13},{2,6},{6,10},{10,14},{3,7},{... | collective-permute-start | bytes 24584 | tf_op jit(solution)/shard_map/ppermute | solution.py:625
  130.7 11.2 %collective-permute-start.9 = (f32[4,512]{1,0:T(4,128)S(1)}, f32[4,512]{1,0:T(4,128)S(1)}, u32[]{:S(2)}, u32[]{:S(2)}) collective-permute-start(f32[4,512]{1,0:T(4,128)S(1)} %get-tuple-element.47), channel_id=1, source_target_pairs={{4,0},{8,4},{12,8},{5,1},{9,5},{13,9},{6,2},{10,6},{14,10},{7,3},{... | collective-permute-start | bytes 24584 | tf_op jit(solution)/shard_map/ppermute | solution.py:626
  132.0 6.9 %collective-permute-start.10 = (f32[4,128]{1,0:T(4,128)S(1)}, f32[4,128]{1,0:T(4,128)S(1)}, u32[]{:S(2)}, u32[]{:S(2)}) collective-permute-start(f32[4,128]{1,0:T(4,128)S(1)} %get-tuple-element.48), channel_id=1, source_target_pairs={{0,1},{1,2},{2,3},{4,5},{5,6},{6,7},{8,9},{9,10},{10,11},{12,13},{... | collective-permute-start | bytes 6152 | tf_op jit(solution)/shard_map/ppermute | solution.py:627
  137.0 4.9 %collective-permute-start.11 = (f32[4,128]{1,0:T(4,128)S(1)}, f32[4,128]{1,0:T(4,128)S(1)}, u32[]{:S(2)}, u32[]{:S(2)}) collective-permute-start(f32[4,128]{1,0:T(4,128)S(1)} %get-tuple-element.49), channel_id=1, source_target_pairs={{1,0},{2,1},{3,2},{5,4},{6,5},{7,6},{9,8},{10,9},{11,10},{13,12},{... | collective-permute-start | bytes 6152 | tf_op jit(solution)/shard_map/ppermute | solution.py:628

commit v5 on v4

--- a/solution.py
+++ b/solution.py
@@ -79,7 +79,7 @@
     field_copies = [
         pltpu.make_async_copy(
             state_ref.at[0, f, :, pl.ds(q * width, width)],
-            cells.at[pl.ds((q * fields + f) * cells_x, cells_x), :],
+            cells.at[q, :, f, :],
             field_sems.at[f * parts + q],
         )
         for f in range(fields)
@@ -114,20 +114,29 @@
 
     def cells_of(p):
         x, part = split(pair_s[0, p], parts)
-        return cells[pl.ds(part * (fields * cells_x) + x, fields, stride=cells_x), :]
+        return cells[part, x]
+
+    zeros = jnp.zeros((fields, width), jnp.float32)
 
     def some_pairs(step, carry):
         weight_copy(step).wait()
-        for i in range(0, STEP_PAIRS, 2):
+        for i in range(0, STEP_PAIRS, 4):
             p = step * STEP_PAIRS + i
-            left = jnp.concatenate([cells_of(p), cells_of(p + 1)], axis=0).astype(jnp.bfloat16)
-            right = w_ref[pl.ds(p, 2)].reshape(2 * width, width)
-            both = lax.dot_general(left, right, NT, preferred_element_type=jnp.float32)
-            for j in range(2):
+            left = [
+                jnp.concatenate([cells_of(p + j), zeros][:: 1 - j % 2 * 2], axis=1) for j in range(4)
+            ]
+            left = jnp.concatenate(left, axis=0).astype(jnp.bfloat16)
+            w = [w_ref[p + j] for j in range(4)]
+            right = jnp.concatenate(
+                [jnp.concatenate(w[:2], axis=1), jnp.concatenate(w[2:], axis=1)], axis=0
+            )
+            four = lax.dot_general(left, right, NT, preferred_element_type=jnp.float32)
+            for j in range(4):
                 tile = pair_s[1, p + j]
                 slot = taken[tile]
                 taken[tile] = slot + 1
-                one = both[j * fields : (j + 1) * fields, j * width : (j + 1) * width]
+                at = j // 2 * width
+                one = four[j * fields : (j + 1) * fields, at : at + width]
                 early_ref[p + j] = one[:half]
                 late_ref[slot] = one[half:]
         return carry
@@ -149,7 +158,7 @@
         out_specs=[pl.BlockSpec(memory_space=pltpu.VMEM) for _ in shapes],
         out_shape=[jax.ShapeDtypeStruct(shape, jnp.float32) for shape in shapes],
         scratch_shapes=[
-            pltpu.VMEM((parts * fields * cells_x, width), jnp.float32),
+            pltpu.VMEM((parts, cells_x, fields, width), jnp.float32),
             pltpu.VMEM((pairs, width, width), jnp.bfloat16),
             pltpu.VMEM((2, 1, pairs), jnp.int32),
             pltpu.SMEM((2, pairs), jnp.int32),
@@ -203,7 +212,7 @@
             pltpu.SMEM((8, pairs), jnp.int32),
             pltpu.SemaphoreType.DMA,
         ],
-        compiler_params=pltpu.CompilerParams(vmem_limit_bytes=40 * 1024 * 1024),
+        compiler_params=pltpu.CompilerParams(vmem_limit_bytes=16 * 1024 * 1024),
         cost_estimate=pl.CostEstimate(
             flops=4 * rows.size, bytes_accessed=12 * rows.size, transcendentals=0
         ),
@@ -252,7 +261,7 @@
                 right_ref[pl.ds(f, 1), :] = tile.T[width - 1 :]
 
 
-def summed(rows, tiles, capacity, fields, cells_x, cells_y, width):
+def summed(rows, tiles, capacity, fields, cells_x, cells_y, width, grant):
     dims = (tiles, capacity, fields, cells_x, cells_y, width)
     slots = tiles * capacity
     blocks = cells_x * cells_y // width
@@ -271,7 +280,7 @@
             pltpu.VMEM((slots, fields * width), jnp.bfloat16),
             pltpu.VMEM((slots, fields * width), jnp.bfloat16),
         ],
-        compiler_params=pltpu.CompilerParams(vmem_limit_bytes=40 * 1024 * 1024),
+        compiler_params=pltpu.CompilerParams(vmem_limit_bytes=grant * 1024 * 1024),
         cost_estimate=pl.CostEstimate(
             flops=4 * blocks * slots * fields * width,
             bytes_accessed=4 * fields * width * (slots + blocks),
@@ -474,7 +483,7 @@
             pltpu.VMEM((4 * nfield, cells_y), jnp.float32),
             pltpu.VMEM((4 * nfield, cells_x), jnp.float32),
         ],
-        compiler_params=pltpu.CompilerParams(vmem_limit_bytes=40 * 1024 * 1024),
+        compiler_params=pltpu.CompilerParams(vmem_limit_bytes=24 * 1024 * 1024),
         cost_estimate=pl.CostEstimate(
             flops=40 * state.size, bytes_accessed=8 * state.size, transcendentals=0
         ),
@@ -483,83 +492,111 @@
 
 
 def finish_kernel(
-    half, gamma_ref, mix_ref, factors, above, below, before, after, base_ref, early_ref, late_ref, *rest
+    first, gamma_ref, mix_ref, above, below, before, after, top, bottom, left, right,
+    factors_ref, base_ref, recv_ref, *rest
 ):
-    early_rims, late_rims = rest[:4], rest[4:8]
-    new_ref, out_ref, wide, cols = rest[8:]
-    f = pl.program_id(0)
-    rate = gamma_ref[0, f]
+    new_ref, out_ref = rest[-11:-9]
+    factors, base, recv, wide, lines, sides, factor_sem, in_sems, out_sems = rest[-9:]
+    count, cells_x, cells_y = base.shape
     mix_b = mix_ref[0, 1]
-    cells_x, cells_y = base_ref.shape[2:]
     keep_row = above.shape[0] - 5
     keep = slice(keep_row, keep_row + 1)
 
-    def widen(recv_ref, rims, f):
-        top, bottom, left, right = (rim[pl.ds(f, 1), :] for rim in rims)
-        wide[STRIP - 1 : STRIP, :] = above[keep, :] * top * rate
-        wide[STRIP + cells_x : STRIP + cells_x + 1, :] = below[keep, :] * bottom * rate
-        sides = [before[keep, :] * left * rate, after[keep, :] * right * rate]
-        cols[...] = columns_of(jnp.concatenate(sides, axis=0))
+    def in_copies(f):
+        return (
+            pltpu.make_async_copy(recv_ref.at[f], recv.at[f], in_sems.at[0, f]),
+            pltpu.make_async_copy(base_ref.at[0, first + f], base.at[f], in_sems.at[1, f]),
+        )
+
+    def out_copies(f):
+        return (
+            pltpu.make_async_copy(recv.at[f], out_ref.at[0, first + f], out_sems.at[0, f]),
+            pltpu.make_async_copy(base.at[f], new_ref.at[0, first + f], out_sems.at[1, f]),
+        )
+
+    copy_factors = pltpu.make_async_copy(factors_ref, factors, factor_sem)
+    copy_factors.start()
+    for f in range(count):
+        for copy in in_copies(f):
+            copy.start()
+    lines[:count, :] = top[...] * above[keep, :]
+    lines[count:, :] = bottom[...] * below[keep, :]
+    sides[:count, :] = left[...] * before[keep, :]
+    sides[count:, :] = right[...] * after[keep, :]
+    copy_factors.wait()
+    lane = lax.broadcasted_iota(jnp.int32, (STRIP, cells_y), 1)
+
+    def one_field(f, carry):
+        rate = gamma_ref[0, first + f]
+        both = [sides[pl.ds(f, 1), :] * rate, sides[pl.ds(count + f, 1), :] * rate]
+        cols = columns_of(jnp.concatenate(both, axis=0))
+        wide[STRIP - 1 : STRIP, :] = lines[pl.ds(f, 1), :] * rate
+        wide[STRIP + cells_x : STRIP + cells_x + 1, :] = lines[pl.ds(count + f, 1), :] * rate
+        recv_in, base_in = in_copies(f)
+        recv_out, base_out = out_copies(f)
+        recv_in.wait()
+        recv_out.start()
         for i in range(0, cells_x, STRIP):
-            recv = recv_ref[0, i : i + STRIP, :]
-            out_ref[0, 0, i : i + STRIP, :] = recv
-            wide[STRIP + i : 2 * STRIP + i, :] = factors[0, i : i + STRIP, :] * recv * rate
-
-    @pl.when(f < half)
-    def _():
-        widen(early_ref, early_rims, f)
-
-    @pl.when(f >= half)
-    def _():
-        widen(late_ref, late_rims, f - half)
-
-    lane = lax.broadcasted_iota(jnp.int32, (STRIP, cells_y), 1)
-    for i in range(0, cells_x, STRIP):
-        rows = slice(i, i + STRIP)
-        mid = wide[STRIP + i : 2 * STRIP + i, :]
-        more = (factors[5, rows, :] - rate * factors[0, rows, :]) * mid
-        more += factors[1, rows, :] * wide[STRIP + i - 1 : 2 * STRIP + i - 1, :]
-        more += factors[2, rows, :] * wide[STRIP + i + 1 : 2 * STRIP + i + 1, :]
-        prior = jnp.where(lane == 0, cols[rows, 0:1], pltpu.roll(mid, 1, 1))
-        later = jnp.where(lane == cells_y - 1, cols[rows, 1:2], pltpu.roll(mid, cells_y - 1, 1))
-        more += factors[3, rows, :] * prior + factors[4, rows, :] * later
-        new_ref[0, 0, rows, :] = base_ref[0, 0, rows, :] + mix_b * (2.0 * mid + more)
-
-
-def finished(base, early, early_rims, late, late_rims, gamma, mix, factors, received):
-    half, cells_x, cells_y = early.shape
-    whole = lambda a: pl.BlockSpec(a.shape, lambda f: (0,) * a.ndim)
-    field = pl.BlockSpec((1, 1, cells_x, cells_y), lambda f: (0, f, 0, 0))
-    recv = lambda at: pl.BlockSpec((1, cells_x, cells_y), lambda f: (at(f), 0, 0))
+            rows = slice(i, i + STRIP)
+            wide[STRIP + i : 2 * STRIP + i, :] = factors[0, rows, :] * recv[f, rows, :] * rate
+        base_in.wait()
+        for i in range(0, cells_x, STRIP):
+            rows = slice(i, i + STRIP)
+            mid = wide[STRIP + i : 2 * STRIP + i, :]
+            more = (factors[5, rows, :] - rate * factors[0, rows, :]) * mid
+            more += factors[1, rows, :] * wide[STRIP + i - 1 : 2 * STRIP + i - 1, :]
+            more += factors[2, rows, :] * wide[STRIP + i + 1 : 2 * STRIP + i + 1, :]
+            prior = jnp.where(lane == 0, cols[rows, 0:1], pltpu.roll(mid, 1, 1))
+            later = jnp.where(lane == cells_y - 1, cols[rows, 1:2], pltpu.roll(mid, cells_y - 1, 1))
+            more += factors[3, rows, :] * prior + factors[4, rows, :] * later
+            base[f, rows, :] = base[f, rows, :] + mix_b * (2.0 * mid + more)
+        base_out.start()
+        return carry
+
+    lax.fori_loop(0, count, one_field, 0)
+    for f in range(count):
+        for copy in out_copies(f):
+            copy.wait()
+
+
+def finished(first, new_state, remapped, recv, rims, gamma, mix, factors, received):
+    count, cells_x, cells_y = recv.shape
+    chan = gamma.shape[1]
+    anywhere = pl.BlockSpec(memory_space=pl.ANY)
+    operands = [gamma, mix, *received, *rims, factors, new_state, recv]
+    specs = [pl.BlockSpec(memory_space=pltpu.SMEM)] * 2
+    specs += [pl.BlockSpec(memory_space=pltpu.VMEM)] * 8 + [anywhere] * 3
+    aliases = {11: 0}
+    if remapped is not None:
+        aliases[len(operands)] = 1
+        operands.append(remapped)
+        specs.append(anywhere)
     return pl.pallas_call(
-        functools.partial(finish_kernel, half),
-        grid=(2 * half,),
-        in_specs=[
-            pl.BlockSpec(memory_space=pltpu.SMEM),
-            pl.BlockSpec(memory_space=pltpu.SMEM),
-            whole(factors),
-            *[whole(lines) for lines in received],
-            field,
-            recv(lambda f: jnp.minimum(f, half - 1)),
-            recv(lambda f: jnp.maximum(f - half, 0)),
-            *[whole(rim) for rim in (*early_rims, *late_rims)],
-        ],
-        out_specs=[field, field],
+        functools.partial(finish_kernel, first),
+        in_specs=specs,
+        out_specs=[anywhere, anywhere],
         out_shape=[
-            jax.ShapeDtypeStruct(base.shape, jnp.float32),
-            jax.ShapeDtypeStruct((1, 2 * half, cells_x, cells_y), jnp.float32),
-        ],
-        input_output_aliases={7: 0},
+            jax.ShapeDtypeStruct(new_state.shape, jnp.float32),
+            jax.ShapeDtypeStruct((1, chan, cells_x, cells_y), jnp.float32),
+        ],
+        input_output_aliases=aliases,
         scratch_shapes=[
+            pltpu.VMEM(factors.shape, jnp.float32),
+            pltpu.VMEM((count, cells_x, cells_y), jnp.float32),
+            pltpu.VMEM((count, cells_x, cells_y), jnp.float32),
             pltpu.VMEM((cells_x + 2 * STRIP, cells_y), jnp.float32),
-            pltpu.VMEM((cells_x, 8), jnp.float32),
-        ],
-        compiler_params=pltpu.CompilerParams(vmem_limit_bytes=40 * 1024 * 1024),
+            pltpu.VMEM((2 * count, cells_y), jnp.float32),
+            pltpu.VMEM((2 * count, cells_x), jnp.float32),
+            pltpu.SemaphoreType.DMA,
+            pltpu.SemaphoreType.DMA((2, count)),
+            pltpu.SemaphoreType.DMA((2, count)),
+        ],
+        compiler_params=pltpu.CompilerParams(vmem_limit_bytes=24 * 1024 * 1024),
         cost_estimate=pl.CostEstimate(
-            flops=40 * early.size, bytes_accessed=40 * early.size, transcendentals=0
+            flops=20 * recv.size, bytes_accessed=20 * recv.size, transcendentals=0
         ),
         name="finish",
-    )(gamma, mix, factors, *received, base, early, late, *early_rims, *late_rims)
+    )(*operands)
 
 
 def body(state, coefs, land_sea, gamma, pair_src, pair_dev, pair_blk, weights):
@@ -579,8 +616,8 @@
         rows = rows.reshape(tiles, capacity + 1, rows.shape[1], width)
         return lax.all_to_all(rows, ("tx", "ty"), split_axis=0, concat_axis=0, tiled=True)
 
-    def add_up(rows):
-        return summed(rows, tiles, capacity, half, cells_x, cells_y, width)
+    def add_up(rows, grant):
+        return summed(rows, tiles, capacity, half, cells_x, cells_y, width, grant)
 
     late_in = exchanged(late)
     early = lax.ppermute(early, "comp", swap)
@@ -611,7 +648,7 @@
         (corners_left, corners_right),
     )
 
-    recv_late, top, bottom, left, right = add_up(late_in)
+    recv_late, top, bottom, left, right = add_up(late_in, 56)
     recv_late = lax.ppermute(recv_late, "comp", swap)
     rims_late = (
         lax.ppermute(bottom, ("comp", "tx"), crossed("tx", 1)),
@@ -620,16 +657,17 @@
         lax.ppermute(left, ("comp", "ty"), crossed("ty", -1)),
     )
     early_in, factors = lax.optimization_barrier((early_in, factors))
-    recv_early, top, bottom, left, right = add_up(early_in)
+    recv_early, top, bottom, left, right = add_up(early_in, 24)
     rims_early = (
         lax.ppermute(bottom, "tx", shift_pairs(tx, 1)),
         lax.ppermute(top, "tx", shift_pairs(tx, -1)),
         lax.ppermute(right, "ty", shift_pairs(ty, 1)),
         lax.ppermute(left, "ty", shift_pairs(ty, -1)),
     )
-    return finished(
-        base, recv_early, rims_early, recv_late, rims_late, gamma, mix, factors, received
-    )
+    rest = (gamma, mix, factors, received)
+    new_state, remapped = finished(half, base, None, recv_late, rims_late, *rest)
+    new_state, remapped = finished(0, new_state, remapped, recv_early, rims_early, *rest)
+    return new_state, remapped
 
 
 def solution(mesh):

time: 150 us -> 144 us (0.960)
  local copies, waits for them, and re-layouts: 6.37 us -> 2.31 us
    pallas_call x1, Pallas kernels: 15 us -> 10.8 us  [contributions(): pl.pallas_call(functools.partial(contribution_kernel, dims), in_specs=[pl...]
    unnamed x28 -> x20, local copies, waits for them, and re-layouts: 6.29 us -> 2.23 us
    pallas_call x2, Pallas kernels: 4.54 us -> 7.86 us  [summed(): pl.pallas_call(functools.partial(sum_kernel, dims), out_shape=[jax.ShapeD...]
    ppermute x1, waiting for transfers between devices: 2.95 us -> 0.01 us  [body(): lax.ppermute(left, 'ty', shift_pairs(ty, -1))]
    pallas_call x1 -> x2, Pallas kernels: 7.44 us -> 8.05 us  [finished(): pl.pallas_call(functools.partial(finish_kernel, first), in_specs=specs, o...]
  transfers between devices with their start and end apart: 18 -> 18, of which waited for: 6 -> 5; matrix products, arithmetic and copies ran while one was open for 0% -> 0% of each run, Pallas kernels for 16% -> 21%
where the time goes in v5:
time: 144 us; the launch traced here: 143 us
  starting transfers between devices  62.9 us (44%)
  Pallas kernels  45.3 us (31%)
  waiting for transfers between devices  31.7 us (22%)
  local copies, waits for them, and re-layouts  2.31 us (2%)
    all_to_all x2, starting transfers between devices, exchanged(): lax.all_to_all(rows, ('tx', 'ty'), split_axis=0, concat_axis=0, tiled=True)  19.8 us
    pallas_call x1, Pallas kernels, base_of(): pl.pallas_call(base_kernel, grid=(nfield,), in_specs=[pl.BlockSpec(memory...  12.6 us
    pallas_call x1, Pallas kernels, contributions(): pl.pallas_call(functools.partial(contribution_kernel, dims), in_specs=[pl...  10.8 us
    all_to_all x2, waiting for transfers between devices, exchanged(): lax.all_to_all(rows, ('tx', 'ty'), split_axis=0, concat_axis=0, tiled=True)  9.64 us
    ppermute x1, waiting for transfers between devices, body(): early = lax.ppermute(early, 'comp', swap)  9.06 us
    pallas_call x2, Pallas kernels, finished(): pl.pallas_call(functools.partial(finish_kernel, first), in_specs=specs, o...  8.05 us
    pallas_call x2, Pallas kernels, summed(): pl.pallas_call(functools.partial(sum_kernel, dims), out_shape=[jax.ShapeD...  7.86 us
    ppermute x1, starting transfers between devices, body(): lax.ppermute(bottom, 'tx', shift_pairs(tx, 1))  7.84 us
  transfers between devices with their start and end apart: 18, of which 5 were waited for; matrix products, arithmetic and copies ran while one was open for 0% of the time, Pallas kernels for 21%

profile of v5, /device:TPU:1, one launch (start us, length us, event | category | flops | bytes accessed | tf_op | source)
XLA Modules:
  0.0 143.3 jit_solution(10501579083642791098)
XLA Ops:
  0.6 10.8 %contributions.1 = (f32[513,4,128]{2,1,0:T(4,128)}, f32[1040,4,128]{2,1,0:T(4,128)}) custom-call(s32[1,512]{1,0:T(1,128)} %src_ref.1, s32[1,512]{1,0:T(1,128)} %bitcast.8, s32[1,512]{1,0:T(1,128)} %blk_ref.1, f32[1,16,128,512]{3,2,1,0:T(8,128)} %state_ref.3, bf16[1,512,128,128]{3,2,1,0:T(8,128)(2,1)} %weights_ref.1), custom_call_target="tpu_custom_call" | custom-call | flops 134217728 | bytes 25296896 | tf_op jit(solution)/shard_map/contributions/pallas_call | solution.py:155
  11.4 0.0 copy-start.9
  11.5 0.0 copy-start.2
  11.5 0.0 copy-start.3
  11.5 7.5 %all-to-all-start.1 = ((f32[16,65,4,128]{3,2,1,0:T(4,128)}), f32[16,65,4,128]{3,2,1,0:T(4,128)}, u32[]{:S(2)}, u32[]{:S(2)}) async-start(f32[16,65,4,128]{3,2,1,0:T(4,128)} %bitcast.7), calls=%async_computation.1 | async-start | bytes 4259840 | tf_op jit(solution)/shard_map/all_to_all | solution.py:617
  19.0 1.2 collective-permute-start
  20.2 0.0 copy-start
  20.2 2.2 %copy-done = f32[1,16,128,512]{3,2,1,0:T(8,128)S(1)} copy-done((f32[1,16,128,512]{3,2,1,0:T(8,128)S(1)}, f32[1,16,128,512]{3,2,1,0:T(8,128)}, u32[]{:S(2)}) %copy-start) | copy-done | bytes 4194328
  22.4 2.0 %edges.1 = (f32[40,512]{1,0:T(8,128)S(1)}, f32[40,512]{1,0:T(8,128)S(1)}, f32[40,128]{1,0:T(8,128)S(1)}, f32[40,128]{1,0:T(8,128)S(1)}) custom-call(f32[1,2]{1,0:T(1,128)S(1)} %broadcast_select_fusion.mix_ref, f32[1,16,128,512]{3,2,1,0:T(8,128)S(1)} %copy-done, f32[1,16,128,512]{3,2,1,0:T(8,128)S(1)} %copy-done, f32[1,16,128,512]{3,2,1,0:T(8,128)S(1)} %copy-done, ...), custom_call_target="tpu_custom_call" | custom-call | flops 1048576 | bytes 4194304 | tf_op jit(solution)/shard_map/edges/pallas_call | solution.py:387
  24.4 3.3 %collective-permute-start.1 = (f32[40,512]{1,0:T(8,128)S(1)}, f32[40,512]{1,0:T(8,128)S(1)}, u32[]{:S(2)}, u32[]{:S(2)}) collective-permute-start(f32[40,512]{1,0:T(8,128)S(1)} %get-tuple-element.33.x_high), channel_id=1, source_target_pairs={{0,4},{4,8},{8,12},{1,5},{5,9},{9,13},{2,6},{6,10},{10,14},{3,7},{... | collective-permute-start | bytes 245768 | tf_op jit(solution)/shard_map/ppermute | solution.py:634
  27.7 1.3 collective-permute-start.2
  29.0 3.9 %collective-permute-start.3 = (f32[40,128]{1,0:T(8,128)S(1)}, f32[40,128]{1,0:T(8,128)S(1)}, u32[]{:S(2)}, u32[]{:S(2)}) collective-permute-start(f32[40,128]{1,0:T(8,128)S(1)} %get-tuple-element.35.y_high), channel_id=1, source_target_pairs={{0,1},{1,2},{2,3},{4,5},{5,6},{6,7},{8,9},{9,10},{10,11},{12,13},{... | collective-permute-start | bytes 61448 | tf_op jit(solution)/shard_map/ppermute | solution.py:632
  32.9 1.9 %collective-permute-start.4 = (f32[40,128]{1,0:T(8,128)S(1)}, f32[40,128]{1,0:T(8,128)S(1)}, u32[]{:S(2)}, u32[]{:S(2)}) collective-permute-start(f32[40,128]{1,0:T(8,128)S(1)} %get-tuple-element.36.y_low), channel_id=1, source_target_pairs={{1,0},{2,1},{3,2},{5,4},{6,5},{7,6},{9,8},{10,9},{11,10},{13,12},{... | collective-permute-start | bytes 61448 | tf_op jit(solution)/shard_map/ppermute | solution.py:633
  34.8 9.1 %collective-permute-done.in_ref = f32[513,4,128]{2,1,0:T(4,128)S(1)} collective-permute-done((f32[513,4,128]{2,1,0:T(4,128)}, f32[513,4,128]{2,1,0:T(4,128)S(1)}, u32[]{:S(2)}, u32[]{:S(2)}) %collective-permute-start) | collective-permute-done | bytes 1050656 | tf_op jit(solution)/shard_map/ppermute | solution.py:623
  43.9 4.0 %place_in_slots.1 = f32[1040,4,128]{2,1,0:T(4,128)} custom-call(f32[513,4,128]{2,1,0:T(4,128)S(1)} %collective-permute-done.in_ref), custom_call_target="tpu_custom_call" | custom-call | flops 1050624 | bytes 3151872 | tf_op jit(solution)/shard_map/place_in_slots/pallas_call | solution.py:207
  47.9 0.0 collective-permute-done.3.left.before
  47.9 0.0 collective-permute-done.4.right.after
  47.9 7.7 %collective-permute-done.1.above = f32[40,512]{1,0:T(8,128)S(1)} collective-permute-done((f32[40,512]{1,0:T(8,128)S(1)}, f32[40,512]{1,0:T(8,128)S(1)}, u32[]{:S(2)}, u32[]{:S(2)}) %collective-permute-start.1) | collective-permute-done | bytes 81952 | tf_op jit(solution)/shard_map/ppermute | solution.py:634
  55.7 0.0 collective-permute-done.2.below
  55.7 5.4 %all-to-all-done.1 = f32[16,65,4,128]{3,2,1,0:T(4,128)} async-done(((f32[16,65,4,128]{3,2,1,0:T(4,128)}), f32[16,65,4,128]{3,2,1,0:T(4,128)}, u32[]{:S(2)}, u32[]{:S(2)}) %all-to-all-start.1) | async-done | bytes 2129952 | tf_op jit(solution)/shard_map/all_to_all | solution.py:617
  61.1 12.3 %all-to-all-start = ((f32[16,65,4,128]{3,2,1,0:T(4,128)}), f32[16,65,4,128]{3,2,1,0:T(4,128)}, u32[]{:S(2)}, u32[]{:S(2)}) async-start(f32[16,65,4,128]{3,2,1,0:T(4,128)} %bitcast.1), calls=%async_computation | async-start | bytes 4259840 | tf_op jit(solution)/shard_map/all_to_all | solution.py:617
  73.4 0.0 copy-start.1
  73.4 4.5 %sum_by_block.3 = (f32[4,128,512]{2,1,0:T(8,128)}, f32[4,512]{1,0:T(4,128)}, f32[4,512]{1,0:T(4,128)}, f32[4,128]{1,0:T(4,128)}, f32[4,128]{1,0:T(4,128)}) custom-call(f32[4160,128]{1,0:T(8,128)} %bitcast.5.in_ref), custom_call_target="tpu_custom_call" | custom-call | flops 1073741824 | bytes 3145728 | tf_op jit(solution)/shard_map/sum_by_block/pallas_call | solution.py:275
  77.9 1.2 collective-permute-start.15
  79.1 3.8 %collective-permute-start.5 = (f32[80,128]{1,0:T(8,128)S(1)}, f32[80,128]{1,0:T(8,128)S(1)}, u32[]{:S(2)}, u32[]{:S(2)}) collective-permute-start(f32[80,128]{1,0:T(8,128)S(1)} %pad_maximum_fusion), channel_id=1, source_target_pairs={{0,1},{1,2},{2,3},{4,5},{5,6},{6,7},{8,9},{9,10},{10,11},{12,13},{... | collective-permute-start | bytes 122888 | tf_op jit(solution)/shard_map/ppermute | solution.py:644
  82.9 1.9 %collective-permute-start.6 = (f32[80,128]{1,0:T(8,128)S(1)}, f32[80,128]{1,0:T(8,128)S(1)}, u32[]{:S(2)}, u32[]{:S(2)}) collective-permute-start(f32[80,128]{1,0:T(8,128)S(1)} %pad_maximum_fusion.1), channel_id=1, source_target_pairs={{1,0},{2,1},{3,2},{5,4},{6,5},{7,6},{9,8},{10,9},{11,10},{13,12},{... | collective-permute-start | bytes 122888 | tf_op jit(solution)/shard_map/ppermute | solution.py:645
  84.9 0.0 collective-permute-done.5.corners_left
  84.9 5.2 %collective-permute-done.6.corners_right = f32[80,128]{1,0:T(8,128)S(1)} collective-permute-done((f32[80,128]{1,0:T(8,128)S(1)}, f32[80,128]{1,0:T(8,128)S(1)}, u32[]{:S(2)}, u32[]{:S(2)}) %collective-permute-start.6) | collective-permute-done | bytes 40992 | tf_op jit(solution)/shard_map/ppermute | solution.py:645
  90.2 0.1 broadcast_in_dim.8.rates_ref
  90.2 12.6 %base.1 = (f32[1,16,128,512]{3,2,1,0:T(8,128)}, f32[6,128,512]{2,1,0:T(8,128)S(1)}) custom-call(f32[1,16]{1,0:T(1,128)S(1)} %get-tuple-element.63.rate_ref, f32[1,2]{1,0:T(1,128)S(1)} %broadcast_select_fusion.mix_ref, f32[16,128]{1,0:T(8,128)S(1)} %broadcast_in_dim.8.rates_ref, f32[1,3,128,512]{3,2,1,0:T(8,128)S(1)} %copy-done.2, s32[128,512]{1,0:T(8,128)S(1)} %copy-done.3, ...), custom_call_target="tpu_custom_call" | custom-call | flops 41943040 | bytes 8388608 | tf_op jit(solution)/shard_map/base/pallas_call | solution.py:468
  102.8 1.9 %collective-permute-start.13 = (f32[4,128]{1,0:T(4,128)S(1)}, f32[4,128]{1,0:T(4,128)S(1)}, u32[]{:S(2)}, u32[]{:S(2)}) collective-permute-start(f32[4,128]{1,0:T(4,128)S(1)} %copy-done.8), channel_id=1, source_target_pairs={{0,17},{1,18},{2,19},{16,1},{17,2},{18,3},{4,21},{5,22},{6,23},{20... | collective-permute-start | bytes 6152 | tf_op jit(solution)/shard_map/ppermute | solution.py:656
  104.8 3.6 %collective-permute-start.14 = (f32[4,128]{1,0:T(4,128)S(1)}, f32[4,128]{1,0:T(4,128)S(1)}, u32[]{:S(2)}, u32[]{:S(2)}) collective-permute-start(f32[4,128]{1,0:T(4,128)S(1)} %copy-done.7), channel_id=1, source_target_pairs={{1,16},{2,17},{3,18},{17,0},{18,1},{19,2},{5,20},{6,21},{7,22},{21... | collective-permute-start | bytes 6152 | tf_op jit(solution)/shard_map/ppermute | solution.py:657
  108.4 1.7 %collective-permute-start.11 = (f32[4,512]{1,0:T(4,128)S(1)}, f32[4,512]{1,0:T(4,128)S(1)}, u32[]{:S(2)}, u32[]{:S(2)}) collective-permute-start(f32[4,512]{1,0:T(4,128)S(1)} %copy-done.6), channel_id=1, source_target_pairs={{0,20},{4,24},{8,28},{16,4},{20,8},{24,12},{1,21},{5,25},{9,29},{1... | collective-permute-start | bytes 24584 | tf_op jit(solution)/shard_map/ppermute | solution.py:654
  110.1 1.3 collective-permute-start.12
  111.4 4.2 %all-to-all-done = f32[16,65,4,128]{3,2,1,0:T(4,128)} async-done(((f32[16,65,4,128]{3,2,1,0:T(4,128)}), f32[16,65,4,128]{3,2,1,0:T(4,128)}, u32[]{:S(2)}, u32[]{:S(2)}) %all-to-all-start) | async-done | bytes 2129952 | tf_op jit(solution)/shard_map/all_to_all | solution.py:617
  115.6 3.4 %sum_by_block.2 = (f32[4,128,512]{2,1,0:T(8,128)S(1)}, f32[4,512]{1,0:T(4,128)S(1)}, f32[4,512]{1,0:T(4,128)S(1)}, f32[4,128]{1,0:T(4,128)S(1)}, f32[4,128]{1,0:T(4,128)S(1)}) custom-call(f32[4160,128]{1,0:T(8,128)} %bitcast.3.in_ref), custom_call_target="tpu_custom_call" | custom-call | flops 1073741824 | bytes 3145728 | tf_op jit(solution)/shard_map/sum_by_block/pallas_call | solution.py:275
  119.1 0.0 collective-permute-done.13.left
  119.1 7.8 %collective-permute-start.7 = (f32[4,512]{1,0:T(4,128)S(1)}, f32[4,512]{1,0:T(4,128)S(1)}, u32[]{:S(2)}, u32[]{:S(2)}) collective-permute-start(f32[4,512]{1,0:T(4,128)S(1)} %get-tuple-element.44), channel_id=1, source_target_pairs={{0,4},{4,8},{8,12},{1,5},{5,9},{9,13},{2,6},{6,10},{10,14},{3,7},{... | collective-permute-start | bytes 24584 | tf_op jit(solution)/shard_map/ppermute | solution.py:662
  126.9 0.0 collective-permute-done.14.right
  126.9 1.3 collective-permute-start.8
  128.2 0.0 collective-permute-done.11.top
  128.2 5.0 %collective-permute-start.9 = (f32[4,128]{1,0:T(4,128)S(1)}, f32[4,128]{1,0:T(4,128)S(1)}, u32[]{:S(2)}, u32[]{:S(2)}) collective-permute-start(f32[4,128]{1,0:T(4,128)S(1)} %get-tuple-element.46), channel_id=1, source_target_pairs={{0,1},{1,2},{2,3},{4,5},{5,6},{6,7},{8,9},{9,10},{10,11},{12,13},{... | collective-permute-start | bytes 6152 | tf_op jit(solution)/shard_map/ppermute | solution.py:664
  133.2 1.9 %collective-permute-start.10 = (f32[4,128]{1,0:T(4,128)S(1)}, f32[4,128]{1,0:T(4,128)S(1)}, u32[]{:S(2)}, u32[]{:S(2)}) collective-permute-start(f32[4,128]{1,0:T(4,128)S(1)} %get-tuple-element.47), channel_id=1, source_target_pairs={{1,0},{2,1},{3,2},{5,4},{6,5},{7,6},{9,8},{10,9},{11,10},{13,12},{... | collective-permute-start | bytes 6152 | tf_op jit(solution)/shard_map/ppermute | solution.py:665
  135.2 0.0 collective-permute-done.15.recv_ref
  135.2 4.1 %finish.2 = (f32[1,16,128,512]{3,2,1,0:T(8,128)}, f32[1,8,128,512]{3,2,1,0:T(8,128)}) custom-call(f32[1,8]{1,0:T(1,128)S(1)} %copy-done.4, f32[1,2]{1,0:T(1,128)S(1)} %broadcast_select_fusion.mix_ref, f32[40,512]{1,0:T(8,128)S(1)} %collective-permute-done.1.above, f32[40,512]{1,0:T(8,128)S(1)} %collective-permute-done.2.below, ...), custom_call_target="tpu_custom_call", output_to_operand_aliasing={{0}: (11, {})} | custom-call | flops 5242880 | bytes 5242880 | tf_op jit(solution)/shard_map/finish/pallas_call | solution.py:574
  139.2 0.0 collective-permute-done.7.top
  139.3 0.0 collective-permute-done.8.bottom
  139.3 4.0 %finish.3 = (f32[1,16,128,512]{3,2,1,0:T(8,128)}, f32[1,8,128,512]{3,2,1,0:T(8,128)}) custom-call(f32[1,8]{1,0:T(1,128)S(1)} %copy-done.4, f32[1,2]{1,0:T(1,128)S(1)} %broadcast_select_fusion.mix_ref, f32[40,512]{1,0:T(8,128)S(1)} %collective-permute-done.1.above, ...), custom_call_target="tpu_custom_call", output_to_operand_aliasing={{0}: (11, {}), {1}: (13, {})} | custom-call | flops 5242880 | bytes 5242880 | tf_op jit(solution)/shard_map/finish/pallas_call | solution.py:574
  (22 shorter events, 0.1 us)
Async XLA Ops:
  11.4 8.7 %copy-start.9 = (f32[1,2]{1,0:T(1,128)S(1)}, f32[1,2]{1,0:T(1,128)}, u32[]{:S(2)}) copy-start(f32[1,2]{1,0:T(1,128)} %constant.14.clone) | copy-start | bytes 28
  11.5 8.7 %copy-start.2 = (f32[1,3,128,512]{3,2,1,0:T(8,128)S(1)}, f32[1,3,128,512]{3,2,1,0:T(8,128)}, u32[]{:S(2)}) copy-start(f32[1,3,128,512]{3,2,1,0:T(8,128)} %coefs_ref.1) | copy-start | bytes 2359300
  11.5 8.7 %copy-start.3 = (s32[128,512]{1,0:T(8,128)S(1)}, s32[128,512]{1,0:T(8,128)}, u32[]{:S(2)}) copy-start(s32[128,512]{1,0:T(8,128)} %land_ref) | copy-start | bytes 786436
  11.5 49.6 %all-to-all-start.1 = ((f32[16,65,4,128]{3,2,1,0:T(4,128)}), f32[16,65,4,128]{3,2,1,0:T(4,128)}, u32[]{:S(2)}, u32[]{:S(2)}) async-start(f32[16,65,4,128]{3,2,1,0:T(4,128)} %bitcast.7), calls=%async_computation.1 | async-start | bytes 4259840 | tf_op jit(solution)/shard_map/all_to_all | solution.py:617
  19.0 24.9 %collective-permute-start = (f32[513,4,128]{2,1,0:T(4,128)}, f32[513,4,128]{2,1,0:T(4,128)S(1)}, u32[]{:S(2)}, u32[]{:S(2)}) collective-permute-start(f32[513,4,128]{2,1,0:T(4,128)} %get-tuple-element.30), channel_id=1, source_target_pairs={{0,16},{16,0},{1,17},{17,1},{2,18},{18,2},{3,19},{19,3},{4,20},{20... | collective-permute-start | bytes 3151880 | tf_op jit(solution)/shard_map/ppermute | solution.py:623
  20.2 2.2 %copy-start = (f32[1,16,128,512]{3,2,1,0:T(8,128)S(1)}, f32[1,16,128,512]{3,2,1,0:T(8,128)}, u32[]{:S(2)}) copy-start(f32[1,16,128,512]{3,2,1,0:T(8,128)} %state_ref.3) | copy-start | bytes 12582916
  24.4 31.3 %collective-permute-start.1 = (f32[40,512]{1,0:T(8,128)S(1)}, f32[40,512]{1,0:T(8,128)S(1)}, u32[]{:S(2)}, u32[]{:S(2)}) collective-permute-start(f32[40,512]{1,0:T(8,128)S(1)} %get-tuple-element.33.x_high), channel_id=1, source_target_pairs={{0,4},{4,8},{8,12},{1,5},{5,9},{9,13},{2,6},{6,10},{10,14},{3,7},{... | collective-permute-start | bytes 245768 | tf_op jit(solution)/shard_map/ppermute | solution.py:634
  27.7 28.0 %collective-permute-start.2 = (f32[40,512]{1,0:T(8,128)S(1)}, f32[40,512]{1,0:T(8,128)S(1)}, u32[]{:S(2)}, u32[]{:S(2)}) collective-permute-start(f32[40,512]{1,0:T(8,128)S(1)} %get-tuple-element.34.x_low), channel_id=1, source_target_pairs={{4,0},{8,4},{12,8},{5,1},{9,5},{13,9},{6,2},{10,6},{14,10},{7,3},{... | collective-permute-start | bytes 245768 | tf_op jit(solution)/shard_map/ppermute | solution.py:635
  29.0 18.9 %collective-permute-start.3 = (f32[40,128]{1,0:T(8,128)S(1)}, f32[40,128]{1,0:T(8,128)S(1)}, u32[]{:S(2)}, u32[]{:S(2)}) collective-permute-start(f32[40,128]{1,0:T(8,128)S(1)} %get-tuple-element.35.y_high), channel_id=1, source_target_pairs={{0,1},{1,2},{2,3},{4,5},{5,6},{6,7},{8,9},{9,10},{10,11},{12,13},{... | collective-permute-start | bytes 61448 | tf_op jit(solution)/shard_map/ppermute | solution.py:632
  32.9 15.0 %collective-permute-start.4 = (f32[40,128]{1,0:T(8,128)S(1)}, f32[40,128]{1,0:T(8,128)S(1)}, u32[]{:S(2)}, u32[]{:S(2)}) collective-permute-start(f32[40,128]{1,0:T(8,128)S(1)} %get-tuple-element.36.y_low), channel_id=1, source_target_pairs={{1,0},{2,1},{3,2},{5,4},{6,5},{7,6},{9,8},{10,9},{11,10},{13,12},{... | collective-permute-start | bytes 61448 | tf_op jit(solution)/shard_map/ppermute | solution.py:633
  61.1 54.5 %all-to-all-start = ((f32[16,65,4,128]{3,2,1,0:T(4,128)}), f32[16,65,4,128]{3,2,1,0:T(4,128)}, u32[]{:S(2)}, u32[]{:S(2)}) async-start(f32[16,65,4,128]{3,2,1,0:T(4,128)} %bitcast.1), calls=%async_computation | async-start | bytes 4259840 | tf_op jit(solution)/shard_map/all_to_all | solution.py:617
  73.4 11.5 %copy-start.4 = (f32[1,8]{1,0:T(1,128)S(1)}, f32[1,8]{1,0:T(1,128)}, u32[]{:S(2)}) copy-start(f32[1,8]{1,0:T(1,128)} %gamma_ref.3) | copy-start | bytes 100
  73.4 16.8 %copy-start.1 = (f32[1,16,128,512]{3,2,1,0:T(8,128)S(1)}, f32[1,16,128,512]{3,2,1,0:T(8,128)}, u32[]{:S(2)}) copy-start(f32[1,16,128,512]{3,2,1,0:T(8,128)} %state_ref.3) | copy-start | bytes 12582916
  77.9 57.3 %collective-permute-start.15 = (f32[4,128,512]{2,1,0:T(8,128)}, f32[4,128,512]{2,1,0:T(8,128)}, u32[]{:S(2)}, u32[]{:S(2)}) collective-permute-start(f32[4,128,512]{2,1,0:T(8,128)} %get-tuple-element.54), channel_id=1, source_target_pairs={{0,16},{16,0},{1,17},{17,1},{2,18},{18,2},{3,19},{19,3},{4,20},{20... | collective-permute-start | bytes 3145736 | tf_op jit(solution)/shard_map/ppermute | solution.py:652
  79.1 5.8 %collective-permute-start.5 = (f32[80,128]{1,0:T(8,128)S(1)}, f32[80,128]{1,0:T(8,128)S(1)}, u32[]{:S(2)}, u32[]{:S(2)}) collective-permute-start(f32[80,128]{1,0:T(8,128)S(1)} %pad_maximum_fusion), channel_id=1, source_target_pairs={{0,1},{1,2},{2,3},{4,5},{5,6},{6,7},{8,9},{9,10},{10,11},{12,13},{... | collective-permute-start | bytes 122888 | tf_op jit(solution)/shard_map/ppermute | solution.py:644
  82.9 7.2 %collective-permute-start.6 = (f32[80,128]{1,0:T(8,128)S(1)}, f32[80,128]{1,0:T(8,128)S(1)}, u32[]{:S(2)}, u32[]{:S(2)}) collective-permute-start(f32[80,128]{1,0:T(8,128)S(1)} %pad_maximum_fusion.1), channel_id=1, source_target_pairs={{1,0},{2,1},{3,2},{5,4},{6,5},{7,6},{9,8},{10,9},{11,10},{13,12},{... | collective-permute-start | bytes 122888 | tf_op jit(solution)/shard_map/ppermute | solution.py:645
  90.2 12.6 %copy-start.8 = (f32[4,128]{1,0:T(4,128)S(1)}, f32[4,128]{1,0:T(4,128)}, u32[]{:S(2)}) copy-start(f32[4,128]{1,0:T(4,128)} %get-tuple-element.51) | copy-start | bytes 6148
  90.2 14.6 %copy-start.7 = (f32[4,128]{1,0:T(4,128)S(1)}, f32[4,128]{1,0:T(4,128)}, u32[]{:S(2)}) copy-start(f32[4,128]{1,0:T(4,128)} %get-tuple-element.52) | copy-start | bytes 6148
  90.2 18.2 %copy-start.6 = (f32[4,512]{1,0:T(4,128)S(1)}, f32[4,512]{1,0:T(4,128)}, u32[]{:S(2)}) copy-start(f32[4,512]{1,0:T(4,128)} %get-tuple-element.49) | copy-start | bytes 24580
  90.2 19.9 %copy-start.5 = (f32[4,512]{1,0:T(4,128)S(1)}, f32[4,512]{1,0:T(4,128)}, u32[]{:S(2)}) copy-start(f32[4,512]{1,0:T(4,128)} %get-tuple-element.50) | copy-start | bytes 24580
  102.8 16.2 %collective-permute-start.13 = (f32[4,128]{1,0:T(4,128)S(1)}, f32[4,128]{1,0:T(4,128)S(1)}, u32[]{:S(2)}, u32[]{:S(2)}) collective-permute-start(f32[4,128]{1,0:T(4,128)S(1)} %copy-done.8), channel_id=1, source_target_pairs={{0,17},{1,18},{2,19},{16,1},{17,2},{18,3},{4,21},{5,22},{6,23},{20... | collective-permute-start | bytes 6152 | tf_op jit(solution)/shard_map/ppermute | solution.py:656
  104.8 22.1 %collective-permute-start.14 = (f32[4,128]{1,0:T(4,128)S(1)}, f32[4,128]{1,0:T(4,128)S(1)}, u32[]{:S(2)}, u32[]{:S(2)}) collective-permute-start(f32[4,128]{1,0:T(4,128)S(1)} %copy-done.7), channel_id=1, source_target_pairs={{1,16},{2,17},{3,18},{17,0},{18,1},{19,2},{5,20},{6,21},{7,22},{21... | collective-permute-start | bytes 6152 | tf_op jit(solution)/shard_map/ppermute | solution.py:657
  108.4 19.8 %collective-permute-start.11 = (f32[4,512]{1,0:T(4,128)S(1)}, f32[4,512]{1,0:T(4,128)S(1)}, u32[]{:S(2)}, u32[]{:S(2)}) collective-permute-start(f32[4,512]{1,0:T(4,128)S(1)} %copy-done.6), channel_id=1, source_target_pairs={{0,20},{4,24},{8,28},{16,4},{20,8},{24,12},{1,21},{5,25},{9,29},{1... | collective-permute-start | bytes 24584 | tf_op jit(solution)/shard_map/ppermute | solution.py:654
  110.1 23.1 %collective-permute-start.12 = (f32[4,512]{1,0:T(4,128)S(1)}, f32[4,512]{1,0:T(4,128)S(1)}, u32[]{:S(2)}, u32[]{:S(2)}) collective-permute-start(f32[4,512]{1,0:T(4,128)S(1)} %copy-done.5), channel_id=1, source_target_pairs={{4,16},{8,20},{12,24},{20,0},{24,4},{28,8},{5,17},{9,21},{13,25},{... | collective-permute-start | bytes 24584 | tf_op jit(solution)/shard_map/ppermute | solution.py:655
  119.1 20.2 %collective-permute-start.7 = (f32[4,512]{1,0:T(4,128)S(1)}, f32[4,512]{1,0:T(4,128)S(1)}, u32[]{:S(2)}, u32[]{:S(2)}) collective-permute-start(f32[4,512]{1,0:T(4,128)S(1)} %get-tuple-element.44), channel_id=1, source_target_pairs={{0,4},{4,8},{8,12},{1,5},{5,9},{9,13},{2,6},{6,10},{10,14},{3,7},{... | collective-permute-start | bytes 24584 | tf_op jit(solution)/shard_map/ppermute | solution.py:662
  126.9 12.3 %collective-permute-start.8 = (f32[4,512]{1,0:T(4,128)S(1)}, f32[4,512]{1,0:T(4,128)S(1)}, u32[]{:S(2)}, u32[]{:S(2)}) collective-permute-start(f32[4,512]{1,0:T(4,128)S(1)} %get-tuple-element.45), channel_id=1, source_target_pairs={{4,0},{8,4},{12,8},{5,1},{9,5},{13,9},{6,2},{10,6},{14,10},{7,3},{... | collective-permute-start | bytes 24584 | tf_op jit(solution)/shard_map/ppermute | solution.py:663
  128.2 11.0 %collective-permute-start.9 = (f32[4,128]{1,0:T(4,128)S(1)}, f32[4,128]{1,0:T(4,128)S(1)}, u32[]{:S(2)}, u32[]{:S(2)}) collective-permute-start(f32[4,128]{1,0:T(4,128)S(1)} %get-tuple-element.46), channel_id=1, source_target_pairs={{0,1},{1,2},{2,3},{4,5},{5,6},{6,7},{8,9},{9,10},{10,11},{12,13},{... | collective-permute-start | bytes 6152 | tf_op jit(solution)/shard_map/ppermute | solution.py:664
  133.2 6.0 %collective-permute-start.10 = (f32[4,128]{1,0:T(4,128)S(1)}, f32[4,128]{1,0:T(4,128)S(1)}, u32[]{:S(2)}, u32[]{:S(2)}) collective-permute-start(f32[4,128]{1,0:T(4,128)S(1)} %get-tuple-element.47), channel_id=1, source_target_pairs={{1,0},{2,1},{3,2},{5,4},{6,5},{7,6},{9,8},{10,9},{11,10},{13,12},{... | collective-permute-start | bytes 6152 | tf_op jit(solution)/shard_map/ppermute | solution.py:665

commit v6 on v5

--- a/solution.py
+++ b/solution.py
@@ -30,7 +30,7 @@
     return lax.div(value, parts), lax.rem(value, parts)
 
 
-def slot_table(dev, blk, tiles, capacity):
+def ranks(dev, tiles):
     pairs = dev.shape[1]
     tile_of = lax.broadcasted_iota(jnp.int32, (tiles, pairs), 0)
     lane_of = lax.broadcasted_iota(jnp.int32, (tiles, pairs), 1)
@@ -40,7 +40,12 @@
     while shift < pairs:
         total = total + jnp.where(lane_of >= shift, pltpu.roll(total, shift, 1), 0.0)
         shift *= 2
-    rank = (jnp.sum(member * total, axis=0, keepdims=True) - 1.0).astype(jnp.int32)
+    return member, (jnp.sum(member * total, axis=0, keepdims=True) - 1.0).astype(jnp.int32)
+
+
+def slot_blocks(dev, blk, tiles, capacity):
+    member, rank = ranks(dev, tiles)
+    pairs = dev.shape[1]
     slot_of = lax.broadcasted_iota(jnp.int32, (LANES, pairs), 0) % capacity
     chosen = (slot_of == rank).astype(jnp.bfloat16)
 
@@ -51,12 +56,7 @@
 
     high, low = split(blk, 256)
     ids = spread(high.astype(jnp.float32)) * 256.0 + spread(low.astype(jnp.float32))
-    return rank, jnp.where(spread(jnp.ones(dev.shape, jnp.float32)) > 0.5, ids, -1.0)
-
-
-def put_ids(out, ids, tiles, capacity):
-    for t in range(tiles):
-        out[t * (capacity + 1) + capacity] = jnp.broadcast_to(ids[t : t + 1, :], out.shape[1:])
+    return jnp.where(spread(jnp.ones(dev.shape, jnp.float32)) > 0.5, ids, -1.0)
 
 
 def contribution_kernel(
@@ -103,8 +103,10 @@
     for copy in vector_copies:
         copy.wait()
     dev, blk = pair_v[0], pair_v[1]
-    _, ids = slot_table(dev, blk, tiles, capacity)
-    put_ids(late_ref, ids, tiles, capacity)
+    ids = slot_blocks(dev, blk, tiles, capacity)
+    for t in range(tiles):
+        row = jnp.broadcast_to(ids[t : t + 1, :], late_ref.shape[1:])
+        late_ref[t * (capacity + 1) + capacity] = row
     code = (dev * (cells_x * parts) + blk).astype(jnp.float32)
     for i in range(pairs // width):
         place = (pairs + i // half, slice(i % half, i % half + 1), slice(None))
@@ -183,13 +185,12 @@
     code = jnp.concatenate(
         [in_ref[pairs + i // half][i % half : i % half + 1] for i in range(pairs // width)], axis=1
     ).astype(jnp.int32)
-    dev, blk = split(code, blocks)
-    rank, ids = slot_table(dev, blk, tiles, capacity)
-    place_v[...] = jnp.broadcast_to(dev * (capacity + 1) + rank, place_v.shape)
+    dev, _ = split(code, blocks)
+    rank = ranks(dev, tiles)[1]
+    place_v[...] = jnp.broadcast_to(dev * capacity + rank, place_v.shape)
     copy = pltpu.make_async_copy(place_v, place_s, place_sem)
     copy.start()
     out_ref[...] = jnp.zeros_like(out_ref)
-    put_ids(out_ref, ids, tiles, capacity)
     copy.wait()
 
     def some_rows(step, carry):
@@ -203,7 +204,7 @@
 
 def placed_rows(rows, tiles, capacity, pairs, blocks):
     half, width = rows.shape[1:]
-    shape = (tiles * (capacity + 1), half, width)
+    shape = (tiles * capacity, half, width)
     return pl.pallas_call(
         functools.partial(place_kernel, (tiles, capacity, pairs, blocks)),
         out_shape=jax.ShapeDtypeStruct(shape, jnp.float32),
@@ -212,7 +213,7 @@
             pltpu.SMEM((8, pairs), jnp.int32),
             pltpu.SemaphoreType.DMA,
         ],
-        compiler_params=pltpu.CompilerParams(vmem_limit_bytes=16 * 1024 * 1024),
+        compiler_params=pltpu.CompilerParams(vmem_limit_bytes=10 * 1024 * 1024),
         cost_estimate=pl.CostEstimate(
             flops=4 * rows.size, bytes_accessed=12 * rows.size, transcendentals=0
         ),
@@ -220,11 +221,11 @@
     )(rows)
 
 
-def sum_kernel(dims, in_ref, out_ref, top_ref, bottom_ref, left_ref, right_ref, pick, high, low):
+def sum_kernel(dims, ids_ref, in_ref, out_ref, top_ref, bottom_ref, left_ref, right_ref, pick, high, low):
     tiles, capacity, fields, cells_x, cells_y, width = dims
     parts = cells_y // width
     group = LANES // capacity
-    stride = (capacity + 1) * fields
+    stride = in_ref.shape[0] // tiles
     block_of = lax.broadcasted_iota(jnp.int32, (cells_x * parts, LANES), 0)
     block_of = (block_of % cells_x) * parts + block_of // cells_x
     block_of = block_of.astype(jnp.float32)
@@ -234,7 +235,7 @@
         ids = None
         for i in range(group):
             source = k * group + i
-            row = in_ref[pl.ds(source * stride + capacity * fields, 1), :]
+            row = ids_ref[pl.ds(source, 1), :]
             ids = row if ids is None else jnp.where(lane // capacity == i, row, ids)
             for f in range(fields):
                 x = in_ref[pl.ds(source * stride + f, capacity, stride=fields), :]
@@ -261,7 +262,7 @@
                 right_ref[pl.ds(f, 1), :] = tile.T[width - 1 :]
 
 
-def summed(rows, tiles, capacity, fields, cells_x, cells_y, width, grant):
+def summed(ids, rows, tiles, capacity, fields, cells_x, cells_y, width, grant):
     dims = (tiles, capacity, fields, cells_x, cells_y, width)
     slots = tiles * capacity
     blocks = cells_x * cells_y // width
@@ -287,7 +288,7 @@
             transcendentals=0,
         ),
         name="sum_by_block",
-    )(rows.reshape(tiles * (capacity + 1) * fields, width))
+    )(ids, rows.reshape(-1, width))
 
 
 def stencil_factors(coefs, keep):
@@ -390,7 +391,7 @@
         in_specs=specs,
         out_specs=[pl.BlockSpec(shape, lambda i: (0, 0)) for shape in shapes],
         out_shape=[jax.ShapeDtypeStruct(shape, jnp.float32) for shape in shapes],
-        compiler_params=pltpu.CompilerParams(vmem_limit_bytes=40 * 1024 * 1024),
+        compiler_params=pltpu.CompilerParams(vmem_limit_bytes=24 * 1024 * 1024),
         cost_estimate=pl.CostEstimate(
             flops=state.size, bytes_accessed=4 * 1024 * 1024, transcendentals=0
         ),
@@ -483,7 +484,7 @@
             pltpu.VMEM((4 * nfield, cells_y), jnp.float32),
             pltpu.VMEM((4 * nfield, cells_x), jnp.float32),
         ],
-        compiler_params=pltpu.CompilerParams(vmem_limit_bytes=24 * 1024 * 1024),
+        compiler_params=pltpu.CompilerParams(vmem_limit_bytes=16 * 1024 * 1024),
         cost_estimate=pl.CostEstimate(
             flops=40 * state.size, bytes_accessed=8 * state.size, transcendentals=0
         ),
@@ -491,22 +492,21 @@
     )(rates, mix, *operands, state)
 
 
-def finish_kernel(
-    first, gamma_ref, mix_ref, above, below, before, after, top, bottom, left, right,
-    factors_ref, base_ref, recv_ref, *rest
-):
-    new_ref, out_ref = rest[-11:-9]
-    factors, base, recv, wide, lines, sides, factor_sem, in_sems, out_sems = rest[-9:]
+def finish_kernel(first, with_x, gamma_ref, mix_ref, above, below, before, after, factors, recv,
+                  left, right, *rest):
+    tops, rest = (rest[:2], rest[2:]) if with_x else (None, rest)
+    late, rest = (rest[:2], rest[2:]) if with_x else (None, rest)
+    base_ref, rest = rest[0], rest[1:]
+    new_ref, out_ref, done_ref = rest[-11:-8]
+    base, wide, lines, sides, outer, base_sems, out_sems, outer_sems = rest[-8:]
     count, cells_x, cells_y = base.shape
     mix_b = mix_ref[0, 1]
     keep_row = above.shape[0] - 5
     keep = slice(keep_row, keep_row + 1)
-
-    def in_copies(f):
-        return (
-            pltpu.make_async_copy(recv_ref.at[f], recv.at[f], in_sems.at[0, f]),
-            pltpu.make_async_copy(base_ref.at[0, first + f], base.at[f], in_sems.at[1, f]),
-        )
+    ends = (0, cells_x - STRIP)
+
+    def base_copy(f):
+        return pltpu.make_async_copy(base_ref.at[0, first + f], base.at[f], base_sems.at[f])
 
     def out_copies(f):
         return (
@@ -514,16 +514,25 @@
             pltpu.make_async_copy(base.at[f], new_ref.at[0, first + f], out_sems.at[1, f]),
         )
 
-    copy_factors = pltpu.make_async_copy(factors_ref, factors, factor_sem)
-    copy_factors.start()
+    def outer_copy(f, i, back):
+        there = (new_ref if back else base_ref).at[0, count + f, pl.ds(ends[i], STRIP), :]
+        here = outer.at[f, i]
+        pair = (here, there) if back else (there, here)
+        return pltpu.make_async_copy(*pair, outer_sems.at[f, i])
+
+    outer_rows = [(f, i) for f in range(count) for i in range(2)] if with_x else []
     for f in range(count):
-        for copy in in_copies(f):
-            copy.start()
-    lines[:count, :] = top[...] * above[keep, :]
-    lines[count:, :] = bottom[...] * below[keep, :]
+        base_copy(f).start()
+    for f, i in outer_rows:
+        outer_copy(f, i, False).start()
+    done_ref[...] = jnp.zeros_like(done_ref)
+    if with_x:
+        lines[:count, :] = tops[0][...] * above[keep, :]
+        lines[count:, :] = tops[1][...] * below[keep, :]
+    else:
+        lines[...] = jnp.zeros_like(lines)
     sides[:count, :] = left[...] * before[keep, :]
     sides[count:, :] = right[...] * after[keep, :]
-    copy_factors.wait()
     lane = lax.broadcasted_iota(jnp.int32, (STRIP, cells_y), 1)
 
     def one_field(f, carry):
@@ -532,14 +541,12 @@
         cols = columns_of(jnp.concatenate(both, axis=0))
         wide[STRIP - 1 : STRIP, :] = lines[pl.ds(f, 1), :] * rate
         wide[STRIP + cells_x : STRIP + cells_x + 1, :] = lines[pl.ds(count + f, 1), :] * rate
-        recv_in, base_in = in_copies(f)
-        recv_out, base_out = out_copies(f)
-        recv_in.wait()
-        recv_out.start()
+        to_out, to_new = out_copies(f)
+        to_out.start()
         for i in range(0, cells_x, STRIP):
             rows = slice(i, i + STRIP)
             wide[STRIP + i : 2 * STRIP + i, :] = factors[0, rows, :] * recv[f, rows, :] * rate
-        base_in.wait()
+        base_copy(f).wait()
         for i in range(0, cells_x, STRIP):
             rows = slice(i, i + STRIP)
             mid = wide[STRIP + i : 2 * STRIP + i, :]
@@ -550,48 +557,64 @@
             later = jnp.where(lane == cells_y - 1, cols[rows, 1:2], pltpu.roll(mid, cells_y - 1, 1))
             more += factors[3, rows, :] * prior + factors[4, rows, :] * later
             base[f, rows, :] = base[f, rows, :] + mix_b * (2.0 * mid + more)
-        base_out.start()
+        to_new.start()
         return carry
 
     lax.fori_loop(0, count, one_field, 0)
+    for f, i in outer_rows:
+        outer_copy(f, i, False).wait()
+        row = i * (STRIP - 1)
+        at = ends[i] + row
+        line = late[i][f : f + 1, :] * (above, below)[i][keep, :] * gamma_ref[0, count + f]
+        more = mix_b * factors[1 + i, at : at + 1, :] * line
+        outer[f, i, row : row + 1, :] = outer[f, i, row : row + 1, :] + more
+        outer_copy(f, i, True).start()
     for f in range(count):
         for copy in out_copies(f):
             copy.wait()
-
-
-def finished(first, new_state, remapped, recv, rims, gamma, mix, factors, received):
+    for f, i in outer_rows:
+        outer_copy(f, i, True).wait()
+
+
+def finished(
+    first, new_state, remapped, recv, x_rims, y_rims, late_rims, late_done, gamma, mix, factors, received
+):
     count, cells_x, cells_y = recv.shape
     chan = gamma.shape[1]
+    with_x = x_rims is not None
     anywhere = pl.BlockSpec(memory_space=pl.ANY)
-    operands = [gamma, mix, *received, *rims, factors, new_state, recv]
+    operands = [gamma, mix, *received, factors, recv, *y_rims]
+    if with_x:
+        operands += [*x_rims, *late_rims]
     specs = [pl.BlockSpec(memory_space=pltpu.SMEM)] * 2
-    specs += [pl.BlockSpec(memory_space=pltpu.VMEM)] * 8 + [anywhere] * 3
-    aliases = {11: 0}
+    specs += [pl.BlockSpec(memory_space=pltpu.VMEM)] * (len(operands) - 2) + [anywhere]
+    aliases = {len(operands): 0}
+    operands.append(new_state)
     if remapped is not None:
         aliases[len(operands)] = 1
-        operands.append(remapped)
-        specs.append(anywhere)
+        operands += [remapped, late_done]
+        specs += [anywhere, anywhere]
     return pl.pallas_call(
-        functools.partial(finish_kernel, first),
+        functools.partial(finish_kernel, first, with_x),
         in_specs=specs,
-        out_specs=[anywhere, anywhere],
+        out_specs=[anywhere, anywhere, pl.BlockSpec(memory_space=pltpu.VMEM)],
         out_shape=[
             jax.ShapeDtypeStruct(new_state.shape, jnp.float32),
             jax.ShapeDtypeStruct((1, chan, cells_x, cells_y), jnp.float32),
+            jax.ShapeDtypeStruct((8, LANES), jnp.float32),
         ],
         input_output_aliases=aliases,
         scratch_shapes=[
-            pltpu.VMEM(factors.shape, jnp.float32),
-            pltpu.VMEM((count, cells_x, cells_y), jnp.float32),
             pltpu.VMEM((count, cells_x, cells_y), jnp.float32),
             pltpu.VMEM((cells_x + 2 * STRIP, cells_y), jnp.float32),
             pltpu.VMEM((2 * count, cells_y), jnp.float32),
             pltpu.VMEM((2 * count, cells_x), jnp.float32),
-            pltpu.SemaphoreType.DMA,
+            pltpu.VMEM((count, 2, STRIP, cells_y), jnp.float32),
+            pltpu.SemaphoreType.DMA((count,)),
             pltpu.SemaphoreType.DMA((2, count)),
-            pltpu.SemaphoreType.DMA((2, count)),
+            pltpu.SemaphoreType.DMA((count, 2)),
         ],
-        compiler_params=pltpu.CompilerParams(vmem_limit_bytes=24 * 1024 * 1024),
+        compiler_params=pltpu.CompilerParams(vmem_limit_bytes=12 * 1024 * 1024),
         cost_estimate=pl.CostEstimate(
             flops=20 * recv.size, bytes_accessed=20 * recv.size, transcendentals=0
         ),
@@ -613,11 +636,11 @@
     swap = [(0, 1), (1, 0)]
 
     def exchanged(rows):
-        rows = rows.reshape(tiles, capacity + 1, rows.shape[1], width)
+        rows = rows.reshape(tiles, -1, half, width)
         return lax.all_to_all(rows, ("tx", "ty"), split_axis=0, concat_axis=0, tiled=True)
 
-    def add_up(rows, grant):
-        return summed(rows, tiles, capacity, half, cells_x, cells_y, width, grant)
+    def add_up(ids, rows, grant):
+        return summed(ids, rows, tiles, capacity, half, cells_x, cells_y, width, grant)
 
     late_in = exchanged(late)
     early = lax.ppermute(early, "comp", swap)
@@ -648,25 +671,35 @@
         (corners_left, corners_right),
     )
 
-    recv_late, top, bottom, left, right = add_up(late_in, 56)
+    ids_late = late_in[:, capacity, 0, :]
+    ids_early = lax.ppermute(ids_late, "comp", swap)
+    recv_late, top, bottom, left, right = add_up(ids_late, late_in, 56)
     recv_late = lax.ppermute(recv_late, "comp", swap)
-    rims_late = (
+    late_x = (
         lax.ppermute(bottom, ("comp", "tx"), crossed("tx", 1)),
         lax.ppermute(top, ("comp", "tx"), crossed("tx", -1)),
+    )
+    late_y = (
         lax.ppermute(right, ("comp", "ty"), crossed("ty", 1)),
         lax.ppermute(left, ("comp", "ty"), crossed("ty", -1)),
     )
-    early_in, factors = lax.optimization_barrier((early_in, factors))
-    recv_early, top, bottom, left, right = add_up(early_in, 24)
-    rims_early = (
+    rest = (gamma, mix, factors, received)
+    new_state, remapped, done = finished(
+        half, base, None, recv_late, None, late_y, None, None, *rest
+    )
+    early_in, done = lax.optimization_barrier((early_in, done))
+    recv_early, top, bottom, left, right = add_up(ids_early, early_in, 16)
+    early_x = (
         lax.ppermute(bottom, "tx", shift_pairs(tx, 1)),
         lax.ppermute(top, "tx", shift_pairs(tx, -1)),
+    )
+    early_y = (
         lax.ppermute(right, "ty", shift_pairs(ty, 1)),
         lax.ppermute(left, "ty", shift_pairs(ty, -1)),
     )
-    rest = (gamma, mix, factors, received)
-    new_state, remapped = finished(half, base, None, recv_late, rims_late, *rest)
-    new_state, remapped = finished(0, new_state, remapped, recv_early, rims_early, *rest)
+    new_state, remapped, _ = finished(
+        0, new_state, remapped, recv_early, early_x, early_y, late_x, done, *rest
+    )
     return new_state, remapped
 
 

time: 144 us -> 143 us (level)
  waiting for transfers between devices: 31.7 us -> 26 us
  starting transfers between devices: 62.9 us -> 65.8 us
    ppermute x1, waiting for transfers between devices: 5.25 us -> 0.01 us  [body(): corners_right = lax.ppermute(starts, 'ty', shift_pairs(ty, -1))]
    all_to_all x2, waiting for transfers between devices: 9.64 us -> 6.27 us  [exchanged(): lax.all_to_all(rows, ('tx', 'ty'), split_axis=0, concat_axis=0, tiled=True)]
    ppermute x1, waiting for transfers between devices: 0.01 us -> 2.95 us  [body(): lax.ppermute(left, 'ty', shift_pairs(ty, -1))]
    ppermute x1, starting transfers between devices: 1.93 us -> 4.83 us  [body(): lax.ppermute(right, ('comp', 'ty'), crossed('ty', 1))]
    ppermute x1, starting transfers between devices: 3.61 us -> 1.92 us  [body(): lax.ppermute(left, ('comp', 'ty'), crossed('ty', -1))]
    ppermute x1, starting transfers between devices: 1.7 us -> 3.18 us  [body(): lax.ppermute(bottom, ('comp', 'tx'), crossed('tx', 1))]
  transfers between devices with their start and end apart: 18 -> 19, of which waited for: 5 -> 5; matrix products, arithmetic and copies ran while one was open for 0% -> 1% of each run, Pallas kernels for 21% -> 21%
where the time goes in v6:
time: 143 us; the launch traced here: 142 us
  starting transfers between devices  65.8 us (46%)
  Pallas kernels  45.6 us (32%)
  waiting for transfers between devices  26 us (18%)
  local copies, waits for them, and re-layouts  3.66 us (3%)
    all_to_all x2, starting transfers between devices, exchanged(): lax.all_to_all(rows, ('tx', 'ty'), split_axis=0, concat_axis=0, tiled=True)  19.8 us
    pallas_call x1, Pallas kernels, base_of(): pl.pallas_call(base_kernel, grid=(nfield,), in_specs=[pl.BlockSpec(memory...  12.3 us
    pallas_call x1, Pallas kernels, contributions(): pl.pallas_call(functools.partial(contribution_kernel, dims), in_specs=[pl...  10.8 us
    ppermute x1, waiting for transfers between devices, body(): early = lax.ppermute(early, 'comp', swap)  9.06 us
    pallas_call x2, Pallas kernels, finished(): pl.pallas_call(functools.partial(finish_kernel, first, with_x), in_specs=...  8.59 us
    pallas_call x2, Pallas kernels, summed(): pl.pallas_call(functools.partial(sum_kernel, dims), out_shape=[jax.ShapeD...  7.87 us
    ppermute x1, starting transfers between devices, body(): lax.ppermute(bottom, 'tx', shift_pairs(tx, 1))  7.77 us
    ppermute x1, waiting for transfers between devices, body(): above = lax.ppermute(x_high, 'tx', shift_pairs(tx, 1))  7.71 us
  transfers between devices with their start and end apart: 19, of which 5 were waited for; matrix products, arithmetic and copies ran while one was open for 1% of the time, Pallas kernels for 21%

profile of v6, /device:TPU:1, one launch (start us, length us, event | category | flops | bytes accessed | tf_op | source)
XLA Modules:
  0.0 142.0 jit_solution(9211109685802314836)
XLA Ops:
  0.6 10.8 %contributions.1 = (f32[513,4,128]{2,1,0:T(4,128)}, f32[1040,4,128]{2,1,0:T(4,128)}) custom-call(s32[1,512]{1,0:T(1,128)} %src_ref.1, s32[1,512]{1,0:T(1,128)} %bitcast.13, s32[1,512]{1,0:T(1,128)} %blk_ref.1, f32[1,16,128,512]{3,2,1,0:T(8,128)} %state_ref.3, bf16[1,512,128,128]{3,2,1,0:T(8,128)(2,1)} %weights_ref.1), custom_call_target="tpu_custom_call" | custom-call | flops 134217728 | bytes 25296896 | tf_op jit(solution)/shard_map/contributions/pallas_call | solution.py:157
  11.4 0.0 copy-start.8
  11.5 0.0 copy-start.2
  11.5 0.0 copy-start.3
  11.5 7.5 %all-to-all-start = ((f32[16,65,4,128]{3,2,1,0:T(4,128)}), f32[16,65,4,128]{3,2,1,0:T(4,128)}, u32[]{:S(2)}, u32[]{:S(2)}) async-start(f32[16,65,4,128]{3,2,1,0:T(4,128)} %bitcast.10), calls=%async_computation | async-start | bytes 4259840 | tf_op jit(solution)/shard_map/all_to_all | solution.py:640
  19.0 1.2 collective-permute-start
  20.2 0.0 copy-start
  20.2 2.2 %copy-done = f32[1,16,128,512]{3,2,1,0:T(8,128)S(1)} copy-done((f32[1,16,128,512]{3,2,1,0:T(8,128)S(1)}, f32[1,16,128,512]{3,2,1,0:T(8,128)}, u32[]{:S(2)}) %copy-start) | copy-done | bytes 4194328
  22.4 2.0 %edges.1 = (f32[40,512]{1,0:T(8,128)S(1)}, f32[40,512]{1,0:T(8,128)S(1)}, f32[40,128]{1,0:T(8,128)S(1)}, f32[40,128]{1,0:T(8,128)S(1)}) custom-call(f32[1,2]{1,0:T(1,128)S(1)} %broadcast_select_fusion.mix_ref, f32[1,16,128,512]{3,2,1,0:T(8,128)S(1)} %copy-done, f32[1,16,128,512]{3,2,1,0:T(8,128)S(1)} %copy-done, f32[1,16,128,512]{3,2,1,0:T(8,128)S(1)} %copy-done, ...), custom_call_target="tpu_custom_call" | custom-call | flops 1048576 | bytes 4194304 | tf_op jit(solution)/shard_map/edges/pallas_call | solution.py:388
  24.4 3.3 %collective-permute-start.1 = (f32[40,512]{1,0:T(8,128)S(1)}, f32[40,512]{1,0:T(8,128)S(1)}, u32[]{:S(2)}, u32[]{:S(2)}) collective-permute-start(f32[40,512]{1,0:T(8,128)S(1)} %get-tuple-element.36.x_high), channel_id=1, source_target_pairs={{0,4},{4,8},{8,12},{1,5},{5,9},{9,13},{2,6},{6,10},{10,14},{3,7},{... | collective-permute-start | bytes 245768 | tf_op jit(solution)/shard_map/ppermute | solution.py:657
  27.7 1.3 collective-permute-start.2
  29.0 3.9 %collective-permute-start.3 = (f32[40,128]{1,0:T(8,128)S(1)}, f32[40,128]{1,0:T(8,128)S(1)}, u32[]{:S(2)}, u32[]{:S(2)}) collective-permute-start(f32[40,128]{1,0:T(8,128)S(1)} %get-tuple-element.38.y_high), channel_id=1, source_target_pairs={{0,1},{1,2},{2,3},{4,5},{5,6},{6,7},{8,9},{9,10},{10,11},{12,13},{... | collective-permute-start | bytes 61448 | tf_op jit(solution)/shard_map/ppermute | solution.py:655
  32.9 1.9 %collective-permute-start.4 = (f32[40,128]{1,0:T(8,128)S(1)}, f32[40,128]{1,0:T(8,128)S(1)}, u32[]{:S(2)}, u32[]{:S(2)}) collective-permute-start(f32[40,128]{1,0:T(8,128)S(1)} %get-tuple-element.39.y_low), channel_id=1, source_target_pairs={{1,0},{2,1},{3,2},{5,4},{6,5},{7,6},{9,8},{10,9},{11,10},{13,12},{... | collective-permute-start | bytes 61448 | tf_op jit(solution)/shard_map/ppermute | solution.py:656
  34.8 9.1 %collective-permute-done.in_ref = f32[513,4,128]{2,1,0:T(4,128)S(1)} collective-permute-done((f32[513,4,128]{2,1,0:T(4,128)}, f32[513,4,128]{2,1,0:T(4,128)S(1)}, u32[]{:S(2)}, u32[]{:S(2)}) %collective-permute-start) | collective-permute-done | bytes 1050656 | tf_op jit(solution)/shard_map/ppermute | solution.py:646
  43.9 4.0 %place_in_slots.1 = f32[1024,4,128]{2,1,0:T(4,128)} custom-call(f32[513,4,128]{2,1,0:T(4,128)S(1)} %collective-permute-done.in_ref), custom_call_target="tpu_custom_call" | custom-call | flops 1050624 | bytes 3151872 | tf_op jit(solution)/shard_map/place_in_slots/pallas_call | solution.py:208
  47.9 0.0 collective-permute-done.3.left.before
  47.9 0.0 collective-permute-done.4.right.after
  48.0 7.7 %collective-permute-done.1.above = f32[40,512]{1,0:T(8,128)S(1)} collective-permute-done((f32[40,512]{1,0:T(8,128)S(1)}, f32[40,512]{1,0:T(8,128)S(1)}, u32[]{:S(2)}, u32[]{:S(2)}) %collective-permute-start.1) | collective-permute-done | bytes 81952 | tf_op jit(solution)/shard_map/ppermute | solution.py:657
  55.7 0.0 collective-permute-done.2.below
  55.7 5.4 %all-to-all-done = f32[16,65,4,128]{3,2,1,0:T(4,128)} async-done(((f32[16,65,4,128]{3,2,1,0:T(4,128)}), f32[16,65,4,128]{3,2,1,0:T(4,128)}, u32[]{:S(2)}, u32[]{:S(2)}) %all-to-all-start) | async-done | bytes 2129952 | tf_op jit(solution)/shard_map/all_to_all | solution.py:640
  61.1 12.3 %all-to-all-start.1 = ((f32[16,64,4,128]{3,2,1,0:T(4,128)}), f32[16,64,4,128]{3,2,1,0:T(4,128)}, u32[]{:S(2)}, u32[]{:S(2)}) async-start(f32[16,64,4,128]{3,2,1,0:T(4,128)} %bitcast.4), calls=%async_computation.1 | async-start | bytes 4194304 | tf_op jit(solution)/shard_map/all_to_all | solution.py:640
  73.4 1.4 slice.20
  74.8 4.5 %sum_by_block.2 = (f32[4,128,512]{2,1,0:T(8,128)}, f32[4,512]{1,0:T(4,128)}, f32[4,512]{1,0:T(4,128)}, f32[4,128]{1,0:T(4,128)}, f32[4,128]{1,0:T(4,128)}) custom-call(f32[16,128]{1,0:T(8,128)} %bitcast.11, f32[4160,128]{1,0:T(8,128)} %bitcast.5.in_ref), custom_call_target="tpu_custom_call" | custom-call | flops 1073741824 | bytes 3145728 | tf_op jit(solution)/shard_map/sum_by_block/pallas_call | solution.py:276
  79.2 1.2 collective-permute-start.8
  80.5 3.8 %collective-permute-start.5 = (f32[80,128]{1,0:T(8,128)S(1)}, f32[80,128]{1,0:T(8,128)S(1)}, u32[]{:S(2)}, u32[]{:S(2)}) collective-permute-start(f32[80,128]{1,0:T(8,128)S(1)} %pad_maximum_fusion), channel_id=1, source_target_pairs={{0,1},{1,2},{2,3},{4,5},{5,6},{6,7},{8,9},{9,10},{10,11},{12,13},{... | collective-permute-start | bytes 122888 | tf_op jit(solution)/shard_map/ppermute | solution.py:667
  84.3 1.9 %collective-permute-start.6 = (f32[80,128]{1,0:T(8,128)S(1)}, f32[80,128]{1,0:T(8,128)S(1)}, u32[]{:S(2)}, u32[]{:S(2)}) collective-permute-start(f32[80,128]{1,0:T(8,128)S(1)} %pad_maximum_fusion.1), channel_id=1, source_target_pairs={{1,0},{2,1},{3,2},{5,4},{6,5},{7,6},{9,8},{10,9},{11,10},{13,12},{... | collective-permute-start | bytes 122888 | tf_op jit(solution)/shard_map/ppermute | solution.py:668
  86.2 0.3 collective-permute-start.7
  86.6 4.8 %collective-permute-start.9 = (f32[4,128]{1,0:T(4,128)}, f32[4,128]{1,0:T(4,128)S(1)}, u32[]{:S(2)}, u32[]{:S(2)}) collective-permute-start(f32[4,128]{1,0:T(4,128)} %get-tuple-element.47), channel_id=1, source_target_pairs={{0,17},{1,18},{2,19},{16,1},{17,2},{18,3},{4,21},{5,22},{6,23},{20... | collective-permute-start | bytes 6152 | tf_op jit(solution)/shard_map/ppermute | solution.py:683
  91.4 0.0 collective-permute-done.5.corners_left
  91.4 1.9 %collective-permute-start.10 = (f32[4,128]{1,0:T(4,128)}, f32[4,128]{1,0:T(4,128)S(1)}, u32[]{:S(2)}, u32[]{:S(2)}) collective-permute-start(f32[4,128]{1,0:T(4,128)} %get-tuple-element.48), channel_id=1, source_target_pairs={{1,16},{2,17},{3,18},{17,0},{18,1},{19,2},{5,20},{6,21},{7,22},{21... | collective-permute-start | bytes 6152 | tf_op jit(solution)/shard_map/ppermute | solution.py:684
  93.4 0.0 collective-permute-done.6.corners_right
  93.4 0.1 broadcast_in_dim.8.rates_ref
  93.4 12.3 %base.1 = (f32[1,16,128,512]{3,2,1,0:T(8,128)}, f32[6,128,512]{2,1,0:T(8,128)S(1)}) custom-call(f32[1,16]{1,0:T(1,128)S(1)} %get-tuple-element.69.rate_ref, f32[1,2]{1,0:T(1,128)S(1)} %broadcast_select_fusion.mix_ref, f32[16,128]{1,0:T(8,128)S(1)} %broadcast_in_dim.8.rates_ref, f32[1,3,128,512]{3,2,1,0:T(8,128)S(1)} %copy-done.2, s32[128,512]{1,0:T(8,128)S(1)} %copy-done.3, ...), custom_call_target="tpu_custom_call" | custom-call | flops 41943040 | bytes 8388608 | tf_op jit(solution)/shard_map/base/pallas_call | solution.py:469
  105.7 3.2 %collective-permute-start.15 = (f32[4,512]{1,0:T(4,128)S(1)}, f32[4,512]{1,0:T(4,128)S(1)}, u32[]{:S(2)}, u32[]{:S(2)}) collective-permute-start(f32[4,512]{1,0:T(4,128)S(1)} %copy-done.7), channel_id=1, source_target_pairs={{0,20},{4,24},{8,28},{16,4},{20,8},{24,12},{1,21},{5,25},{9,29},{1... | collective-permute-start | bytes 24584 | tf_op jit(solution)/shard_map/ppermute | solution.py:679
  108.9 1.3 collective-permute-start.16
  110.2 0.0 collective-permute-done.8.recv
  110.3 4.0 %finish.2 = (f32[1,16,128,512]{3,2,1,0:T(8,128)}, f32[1,8,128,512]{3,2,1,0:T(8,128)}, f32[8,128]{1,0:T(8,128)S(1)}) custom-call(f32[1,8]{1,0:T(1,128)S(1)} %copy-done.4, f32[1,2]{1,0:T(1,128)S(1)} %broadcast_select_fusion.mix_ref, f32[40,512]{1,0:T(8,128)S(1)} %collective-permute-done.1.above, ...), custom_call_target="tpu_custom_call", output_to_operand_aliasing={{0}: (10, {})} | custom-call | flops 5242880 | bytes 5242880 | tf_op jit(solution)/shard_map/finish/pallas_call | solution.py:597
  114.2 0.8 all-to-all-done.1
  115.0 0.0 collective-permute-done.7.ids_ref
  115.0 3.4 %sum_by_block.3 = (f32[4,128,512]{2,1,0:T(8,128)S(1)}, f32[4,512]{1,0:T(4,128)S(1)}, f32[4,512]{1,0:T(4,128)S(1)}, f32[4,128]{1,0:T(4,128)S(1)}, f32[4,128]{1,0:T(4,128)S(1)}) custom-call(f32[16,128]{1,0:T(8,128)S(1)} %collective-permute-done.7.ids_ref, f32[4096,128]{1,0:T(8,128)} %bitcast.6.in_ref), custom_call_target="tpu_custom_call" | custom-call | flops 1073741824 | bytes 3145728 | tf_op jit(solution)/shard_map/sum_by_block/pallas_call | solution.py:276
  118.5 7.8 %collective-permute-start.13 = (f32[4,512]{1,0:T(4,128)S(1)}, f32[4,512]{1,0:T(4,128)S(1)}, u32[]{:S(2)}, u32[]{:S(2)}) collective-permute-start(f32[4,512]{1,0:T(4,128)S(1)} %get-tuple-element.55), channel_id=1, source_target_pairs={{0,4},{4,8},{8,12},{1,5},{5,9},{9,13},{2,6},{6,10},{10,14},{3,7},{... | collective-permute-start | bytes 24584 | tf_op jit(solution)/shard_map/ppermute | solution.py:693
  126.2 1.3 collective-permute-start.14
  127.5 4.9 %collective-permute-start.11 = (f32[4,128]{1,0:T(4,128)S(1)}, f32[4,128]{1,0:T(4,128)S(1)}, u32[]{:S(2)}, u32[]{:S(2)}) collective-permute-start(f32[4,128]{1,0:T(4,128)S(1)} %get-tuple-element.53), channel_id=1, source_target_pairs={{0,1},{1,2},{2,3},{4,5},{5,6},{6,7},{8,9},{9,10},{10,11},{12,13},{... | collective-permute-start | bytes 6152 | tf_op jit(solution)/shard_map/ppermute | solution.py:697
  132.5 1.9 %collective-permute-start.12 = (f32[4,128]{1,0:T(4,128)S(1)}, f32[4,128]{1,0:T(4,128)S(1)}, u32[]{:S(2)}, u32[]{:S(2)}) collective-permute-start(f32[4,128]{1,0:T(4,128)S(1)} %get-tuple-element.54), channel_id=1, source_target_pairs={{1,0},{2,1},{3,2},{5,4},{6,5},{7,6},{9,8},{10,9},{11,10},{13,12},{... | collective-permute-start | bytes 6152 | tf_op jit(solution)/shard_map/ppermute | solution.py:698
  134.4 0.0 collective-permute-done.16.rest_3_
  134.4 0.0 collective-permute-done.11.left
  134.4 3.0 %collective-permute-done.12.right = f32[4,128]{1,0:T(4,128)S(1)} collective-permute-done((f32[4,128]{1,0:T(4,128)S(1)}, f32[4,128]{1,0:T(4,128)S(1)}, u32[]{:S(2)}, u32[]{:S(2)}) %collective-permute-start.12) | collective-permute-done | bytes 2080 | tf_op jit(solution)/shard_map/ppermute | solution.py:698
  137.4 4.6 %finish.3 = (f32[1,16,128,512]{3,2,1,0:T(8,128)}, f32[1,8,128,512]{3,2,1,0:T(8,128)}, f32[8,128]{1,0:T(8,128)}) custom-call(f32[1,8]{1,0:T(1,128)S(1)} %copy-done.4, f32[1,2]{1,0:T(1,128)S(1)} %broadcast_select_fusion.mix_ref, f32[40,512]{1,0:T(8,128)S(1)} %collective-permute-done.1.above, ...), custom_call_target="tpu_custom_call", output_to_operand_aliasing={{0}: (14, {}), {1}: (15, {})} | custom-call | flops 5242880 | bytes 5242880 | tf_op jit(solution)/shard_map/finish/pallas_call | solution.py:597
  (23 shorter events, 0.1 us)
Async XLA Ops:
  11.4 8.7 %copy-start.8 = (f32[1,2]{1,0:T(1,128)S(1)}, f32[1,2]{1,0:T(1,128)}, u32[]{:S(2)}) copy-start(f32[1,2]{1,0:T(1,128)} %constant.14.clone) | copy-start | bytes 28
  11.5 8.7 %copy-start.2 = (f32[1,3,128,512]{3,2,1,0:T(8,128)S(1)}, f32[1,3,128,512]{3,2,1,0:T(8,128)}, u32[]{:S(2)}) copy-start(f32[1,3,128,512]{3,2,1,0:T(8,128)} %coefs_ref.1) | copy-start | bytes 2359300
  11.5 8.7 %copy-start.3 = (s32[128,512]{1,0:T(8,128)S(1)}, s32[128,512]{1,0:T(8,128)}, u32[]{:S(2)}) copy-start(s32[128,512]{1,0:T(8,128)} %land_ref) | copy-start | bytes 786436
  11.5 49.6 %all-to-all-start = ((f32[16,65,4,128]{3,2,1,0:T(4,128)}), f32[16,65,4,128]{3,2,1,0:T(4,128)}, u32[]{:S(2)}, u32[]{:S(2)}) async-start(f32[16,65,4,128]{3,2,1,0:T(4,128)} %bitcast.10), calls=%async_computation | async-start | bytes 4259840 | tf_op jit(solution)/shard_map/all_to_all | solution.py:640
  19.0 24.9 %collective-permute-start = (f32[513,4,128]{2,1,0:T(4,128)}, f32[513,4,128]{2,1,0:T(4,128)S(1)}, u32[]{:S(2)}, u32[]{:S(2)}) collective-permute-start(f32[513,4,128]{2,1,0:T(4,128)} %get-tuple-element.33), channel_id=1, source_target_pairs={{0,16},{16,0},{1,17},{17,1},{2,18},{18,2},{3,19},{19,3},{4,20},{20... | collective-permute-start | bytes 3151880 | tf_op jit(solution)/shard_map/ppermute | solution.py:646
  20.2 2.2 %copy-start = (f32[1,16,128,512]{3,2,1,0:T(8,128)S(1)}, f32[1,16,128,512]{3,2,1,0:T(8,128)}, u32[]{:S(2)}) copy-start(f32[1,16,128,512]{3,2,1,0:T(8,128)} %state_ref.3) | copy-start | bytes 12582916
  24.4 31.3 %collective-permute-start.1 = (f32[40,512]{1,0:T(8,128)S(1)}, f32[40,512]{1,0:T(8,128)S(1)}, u32[]{:S(2)}, u32[]{:S(2)}) collective-permute-start(f32[40,512]{1,0:T(8,128)S(1)} %get-tuple-element.36.x_high), channel_id=1, source_target_pairs={{0,4},{4,8},{8,12},{1,5},{5,9},{9,13},{2,6},{6,10},{10,14},{3,7},{... | collective-permute-start | bytes 245768 | tf_op jit(solution)/shard_map/ppermute | solution.py:657
  27.7 28.0 %collective-permute-start.2 = (f32[40,512]{1,0:T(8,128)S(1)}, f32[40,512]{1,0:T(8,128)S(1)}, u32[]{:S(2)}, u32[]{:S(2)}) collective-permute-start(f32[40,512]{1,0:T(8,128)S(1)} %get-tuple-element.37.x_low), channel_id=1, source_target_pairs={{4,0},{8,4},{12,8},{5,1},{9,5},{13,9},{6,2},{10,6},{14,10},{7,3},{... | collective-permute-start | bytes 245768 | tf_op jit(solution)/shard_map/ppermute | solution.py:658
  29.0 18.9 %collective-permute-start.3 = (f32[40,128]{1,0:T(8,128)S(1)}, f32[40,128]{1,0:T(8,128)S(1)}, u32[]{:S(2)}, u32[]{:S(2)}) collective-permute-start(f32[40,128]{1,0:T(8,128)S(1)} %get-tuple-element.38.y_high), channel_id=1, source_target_pairs={{0,1},{1,2},{2,3},{4,5},{5,6},{6,7},{8,9},{9,10},{10,11},{12,13},{... | collective-permute-start | bytes 61448 | tf_op jit(solution)/shard_map/ppermute | solution.py:655
  32.9 15.0 %collective-permute-start.4 = (f32[40,128]{1,0:T(8,128)S(1)}, f32[40,128]{1,0:T(8,128)S(1)}, u32[]{:S(2)}, u32[]{:S(2)}) collective-permute-start(f32[40,128]{1,0:T(8,128)S(1)} %get-tuple-element.39.y_low), channel_id=1, source_target_pairs={{1,0},{2,1},{3,2},{5,4},{6,5},{7,6},{9,8},{10,9},{11,10},{13,12},{... | collective-permute-start | bytes 61448 | tf_op jit(solution)/shard_map/ppermute | solution.py:656
  61.1 53.9 %all-to-all-start.1 = ((f32[16,64,4,128]{3,2,1,0:T(4,128)}), f32[16,64,4,128]{3,2,1,0:T(4,128)}, u32[]{:S(2)}, u32[]{:S(2)}) async-start(f32[16,64,4,128]{3,2,1,0:T(4,128)} %bitcast.4), calls=%async_computation.1 | async-start | bytes 4194304 | tf_op jit(solution)/shard_map/all_to_all | solution.py:640
  74.8 11.5 %copy-start.5 = (f32[16,1,1,128]{3,2,1,0:T(1,128)S(1)}, f32[16,1,1,128]{3,2,1,0:T(1,128)}, u32[]{:S(2)}) copy-start(f32[16,1,1,128]{3,2,1,0:T(1,128)} %slice.20) | copy-start | bytes 24580
  74.8 11.8 %copy-start.4 = (f32[1,8]{1,0:T(1,128)S(1)}, f32[1,8]{1,0:T(1,128)}, u32[]{:S(2)}) copy-start(f32[1,8]{1,0:T(1,128)} %gamma_ref.3) | copy-start | bytes 100
  74.8 18.7 %copy-start.1 = (f32[1,16,128,512]{3,2,1,0:T(8,128)S(1)}, f32[1,16,128,512]{3,2,1,0:T(8,128)}, u32[]{:S(2)}) copy-start(f32[1,16,128,512]{3,2,1,0:T(8,128)} %state_ref.3) | copy-start | bytes 12582916
  79.2 31.0 %collective-permute-start.8 = (f32[4,128,512]{2,1,0:T(8,128)}, f32[4,128,512]{2,1,0:T(8,128)S(1)}, u32[]{:S(2)}, u32[]{:S(2)}) collective-permute-start(f32[4,128,512]{2,1,0:T(8,128)} %get-tuple-element.46), channel_id=1, source_target_pairs={{0,16},{16,0},{1,17},{17,1},{2,18},{18,2},{3,19},{19,3},{4,20},{20... | collective-permute-start | bytes 3145736 | tf_op jit(solution)/shard_map/ppermute | solution.py:677
  80.5 10.9 %collective-permute-start.5 = (f32[80,128]{1,0:T(8,128)S(1)}, f32[80,128]{1,0:T(8,128)S(1)}, u32[]{:S(2)}, u32[]{:S(2)}) collective-permute-start(f32[80,128]{1,0:T(8,128)S(1)} %pad_maximum_fusion), channel_id=1, source_target_pairs={{0,1},{1,2},{2,3},{4,5},{5,6},{6,7},{8,9},{9,10},{10,11},{12,13},{... | collective-permute-start | bytes 122888 | tf_op jit(solution)/shard_map/ppermute | solution.py:667
  84.3 9.1 %collective-permute-start.6 = (f32[80,128]{1,0:T(8,128)S(1)}, f32[80,128]{1,0:T(8,128)S(1)}, u32[]{:S(2)}, u32[]{:S(2)}) collective-permute-start(f32[80,128]{1,0:T(8,128)S(1)} %pad_maximum_fusion.1), channel_id=1, source_target_pairs={{1,0},{2,1},{3,2},{5,4},{6,5},{7,6},{9,8},{10,9},{11,10},{13,12},{... | collective-permute-start | bytes 122888 | tf_op jit(solution)/shard_map/ppermute | solution.py:668
  86.2 28.8 %collective-permute-start.7 = (f32[16,128]{1,0:T(8,128)S(1)}, f32[16,128]{1,0:T(8,128)S(1)}, u32[]{:S(2)}, u32[]{:S(2)}) collective-permute-start(f32[16,128]{1,0:T(8,128)S(1)} %bitcast.12), channel_id=1, source_target_pairs={{0,16},{16,0},{1,17},{17,1},{2,18},{18,2},{3,19},{19,3},{4,20},{20... | collective-permute-start | bytes 24584 | tf_op jit(solution)/shard_map/ppermute | solution.py:675
  86.6 22.3 %collective-permute-start.9 = (f32[4,128]{1,0:T(4,128)}, f32[4,128]{1,0:T(4,128)S(1)}, u32[]{:S(2)}, u32[]{:S(2)}) collective-permute-start(f32[4,128]{1,0:T(4,128)} %get-tuple-element.47), channel_id=1, source_target_pairs={{0,17},{1,18},{2,19},{16,1},{17,2},{18,3},{4,21},{5,22},{6,23},{20... | collective-permute-start | bytes 6152 | tf_op jit(solution)/shard_map/ppermute | solution.py:683
  91.4 18.8 %collective-permute-start.10 = (f32[4,128]{1,0:T(4,128)}, f32[4,128]{1,0:T(4,128)S(1)}, u32[]{:S(2)}, u32[]{:S(2)}) collective-permute-start(f32[4,128]{1,0:T(4,128)} %get-tuple-element.48), channel_id=1, source_target_pairs={{1,16},{2,17},{3,18},{17,0},{18,1},{19,2},{5,20},{6,21},{7,22},{21... | collective-permute-start | bytes 6152 | tf_op jit(solution)/shard_map/ppermute | solution.py:684
  93.4 12.3 %copy-start.7 = (f32[4,512]{1,0:T(4,128)S(1)}, f32[4,512]{1,0:T(4,128)}, u32[]{:S(2)}) copy-start(f32[4,512]{1,0:T(4,128)} %get-tuple-element.57) | copy-start | bytes 24580
  93.4 15.5 %copy-start.6 = (f32[4,512]{1,0:T(4,128)S(1)}, f32[4,512]{1,0:T(4,128)}, u32[]{:S(2)}) copy-start(f32[4,512]{1,0:T(4,128)} %get-tuple-element.58) | copy-start | bytes 24580
  105.7 26.7 %collective-permute-start.15 = (f32[4,512]{1,0:T(4,128)S(1)}, f32[4,512]{1,0:T(4,128)S(1)}, u32[]{:S(2)}, u32[]{:S(2)}) collective-permute-start(f32[4,512]{1,0:T(4,128)S(1)} %copy-done.7), channel_id=1, source_target_pairs={{0,20},{4,24},{8,28},{16,4},{20,8},{24,12},{1,21},{5,25},{9,29},{1... | collective-permute-start | bytes 24584 | tf_op jit(solution)/shard_map/ppermute | solution.py:679
  108.9 25.5 %collective-permute-start.16 = (f32[4,512]{1,0:T(4,128)S(1)}, f32[4,512]{1,0:T(4,128)S(1)}, u32[]{:S(2)}, u32[]{:S(2)}) collective-permute-start(f32[4,512]{1,0:T(4,128)S(1)} %copy-done.6), channel_id=1, source_target_pairs={{4,16},{8,20},{12,24},{20,0},{24,4},{28,8},{5,17},{9,21},{13,25},{... | collective-permute-start | bytes 24584 | tf_op jit(solution)/shard_map/ppermute | solution.py:680
  118.5 18.9 %collective-permute-start.13 = (f32[4,512]{1,0:T(4,128)S(1)}, f32[4,512]{1,0:T(4,128)S(1)}, u32[]{:S(2)}, u32[]{:S(2)}) collective-permute-start(f32[4,512]{1,0:T(4,128)S(1)} %get-tuple-element.55), channel_id=1, source_target_pairs={{0,4},{4,8},{8,12},{1,5},{5,9},{9,13},{2,6},{6,10},{10,14},{3,7},{... | collective-permute-start | bytes 24584 | tf_op jit(solution)/shard_map/ppermute | solution.py:693
  126.2 11.2 %collective-permute-start.14 = (f32[4,512]{1,0:T(4,128)S(1)}, f32[4,512]{1,0:T(4,128)S(1)}, u32[]{:S(2)}, u32[]{:S(2)}) collective-permute-start(f32[4,512]{1,0:T(4,128)S(1)} %get-tuple-element.56), channel_id=1, source_target_pairs={{4,0},{8,4},{12,8},{5,1},{9,5},{13,9},{6,2},{10,6},{14,10},{7,3},{... | collective-permute-start | bytes 24584 | tf_op jit(solution)/shard_map/ppermute | solution.py:694
  127.5 6.9 %collective-permute-start.11 = (f32[4,128]{1,0:T(4,128)S(1)}, f32[4,128]{1,0:T(4,128)S(1)}, u32[]{:S(2)}, u32[]{:S(2)}) collective-permute-start(f32[4,128]{1,0:T(4,128)S(1)} %get-tuple-element.53), channel_id=1, source_target_pairs={{0,1},{1,2},{2,3},{4,5},{5,6},{6,7},{8,9},{9,10},{10,11},{12,13},{... | collective-permute-start | bytes 6152 | tf_op jit(solution)/shard_map/ppermute | solution.py:697
  132.5 4.9 %collective-permute-start.12 = (f32[4,128]{1,0:T(4,128)S(1)}, f32[4,128]{1,0:T(4,128)S(1)}, u32[]{:S(2)}, u32[]{:S(2)}) collective-permute-start(f32[4,128]{1,0:T(4,128)S(1)} %get-tuple-element.54), channel_id=1, source_target_pairs={{1,0},{2,1},{3,2},{5,4},{6,5},{7,6},{9,8},{10,9},{11,10},{13,12},{... | collective-permute-start | bytes 6152 | tf_op jit(solution)/shard_map/ppermute | solution.py:698

commit v7 on v6

--- a/solution.py
+++ b/solution.py
@@ -221,17 +221,26 @@
     )(rows)
 
 
-def sum_kernel(dims, ids_ref, in_ref, out_ref, top_ref, bottom_ref, left_ref, right_ref, pick, high, low):
+def sum_kernel(dims, ids_ref, rows_ref, out_ref, top_ref, bottom_ref, left_ref, right_ref,
+               in_ref, pick, high, low, row_sems):
     tiles, capacity, fields, cells_x, cells_y, width = dims
     parts = cells_y // width
     group = LANES // capacity
     stride = in_ref.shape[0] // tiles
+
+    def rows_copy(k):
+        some = pl.ds(k * group * stride, group * stride)
+        return pltpu.make_async_copy(rows_ref.at[some, :], in_ref.at[some, :], row_sems.at[k])
+
+    for k in range(tiles // group):
+        rows_copy(k).start()
     block_of = lax.broadcasted_iota(jnp.int32, (cells_x * parts, LANES), 0)
     block_of = (block_of % cells_x) * parts + block_of // cells_x
     block_of = block_of.astype(jnp.float32)
     lane = lax.broadcasted_iota(jnp.int32, (1, LANES), 1)
     for k in range(tiles // group):
         columns = pl.ds(k * LANES, LANES)
+        rows_copy(k).wait()
         ids = None
         for i in range(group):
             source = k * group + i
@@ -264,6 +273,7 @@
 
 def summed(ids, rows, tiles, capacity, fields, cells_x, cells_y, width, grant):
     dims = (tiles, capacity, fields, cells_x, cells_y, width)
+    rows = rows.reshape(-1, width)
     slots = tiles * capacity
     blocks = cells_x * cells_y // width
     shapes = [
@@ -275,11 +285,14 @@
     ]
     return pl.pallas_call(
         functools.partial(sum_kernel, dims),
+        in_specs=[pl.BlockSpec(memory_space=pltpu.VMEM), pl.BlockSpec(memory_space=pl.ANY)],
         out_shape=[jax.ShapeDtypeStruct(shape, jnp.float32) for shape in shapes],
         scratch_shapes=[
+            pltpu.VMEM(rows.shape, jnp.float32),
             pltpu.VMEM((blocks, slots), jnp.bfloat16),
             pltpu.VMEM((slots, fields * width), jnp.bfloat16),
             pltpu.VMEM((slots, fields * width), jnp.bfloat16),
+            pltpu.SemaphoreType.DMA((tiles * capacity // LANES,)),
         ],
         compiler_params=pltpu.CompilerParams(vmem_limit_bytes=grant * 1024 * 1024),
         cost_estimate=pl.CostEstimate(
@@ -288,7 +301,7 @@
             transcendentals=0,
         ),
         name="sum_by_block",
-    )(ids, rows.reshape(-1, width))
+    )(ids, rows)
 
 
 def stencil_factors(coefs, keep):
@@ -409,9 +422,9 @@
     return out + (middle - rate * keep) * center
 
 
-def base_kernel(rate_ref, mix_ref, rates_ref, coefs_ref, land_ref, x_low, x_high, y_low, y_high,
+def base_kernel(half, rate_ref, mix_ref, rates_ref, coefs_ref, land_ref, x_low, x_high, y_low, y_high,
                 above, below, left, right, corners_left, corners_right, state_ref,
-                out_ref, factors, rows, cols):
+                out_ref, early_ref, factors, rows, cols):
     f = pl.program_id(0)
     nfield = rates_ref.shape[0]
     lines = line_count(nfield)
@@ -457,17 +470,22 @@
     )
     s1 = s + tendency(s, rate, factors, row[0], row[1], col[:, 0:1], col[:, 1:2])
     more = tendency(s1, rate, factors, row[2], row[3], col[:, 2:3], col[:, 3:4])
-    out_ref[0, 0] = mix_a * s + (1.0 - mix_a) * s1 + mix_b * more
-
-
-def base_of(state, coefs, land_sea, rates, mix, edges, received, corners):
+    total = mix_a * s + (1.0 - mix_a) * s1 + mix_b * more
+    out_ref[0, 0] = total
+
+    @pl.when(f < half)
+    def _():
+        early_ref[0] = total
+
+
+def base_of(state, coefs, land_sea, rates, mix, edges, received, corners, half):
     _, nfield, cells_x, cells_y = state.shape
     field = pl.BlockSpec((1, 1, cells_x, cells_y), lambda f: (0, f, 0, 0))
     whole = lambda a: pl.BlockSpec(a.shape, lambda f: (0,) * a.ndim)
     rates_wide = jnp.broadcast_to(rates.T, (nfield, LANES))
     operands = [rates_wide, coefs, land_sea, *edges, *received, *corners]
     return pl.pallas_call(
-        base_kernel,
+        functools.partial(base_kernel, half),
         grid=(nfield,),
         in_specs=[
             pl.BlockSpec(memory_space=pltpu.SMEM),
@@ -475,9 +493,14 @@
             *[whole(a) for a in operands],
             field,
         ],
-        out_specs=[field, pl.BlockSpec((6, cells_x, cells_y), lambda f: (0, 0, 0))],
+        out_specs=[
+            field,
+            pl.BlockSpec((1, cells_x, cells_y), lambda f: (jnp.minimum(f, half - 1), 0, 0)),
+            pl.BlockSpec((6, cells_x, cells_y), lambda f: (0, 0, 0)),
+        ],
         out_shape=[
             jax.ShapeDtypeStruct(state.shape, jnp.float32),
+            jax.ShapeDtypeStruct((half, cells_x, cells_y), jnp.float32),
             jax.ShapeDtypeStruct((6, cells_x, cells_y), jnp.float32),
         ],
         scratch_shapes=[
@@ -496,6 +519,7 @@
                   left, right, *rest):
     tops, rest = (rest[:2], rest[2:]) if with_x else (None, rest)
     late, rest = (rest[:2], rest[2:]) if with_x else (None, rest)
+    early_base, rest = (rest[0], rest[1:]) if with_x else (None, rest)
     base_ref, rest = rest[0], rest[1:]
     new_ref, out_ref, done_ref = rest[-11:-8]
     base, wide, lines, sides, outer, base_sems, out_sems, outer_sems = rest[-8:]
@@ -521,8 +545,9 @@
         return pltpu.make_async_copy(*pair, outer_sems.at[f, i])
 
     outer_rows = [(f, i) for f in range(count) for i in range(2)] if with_x else []
-    for f in range(count):
-        base_copy(f).start()
+    if not with_x:
+        for f in range(count):
+            base_copy(f).start()
     for f, i in outer_rows:
         outer_copy(f, i, False).start()
     done_ref[...] = jnp.zeros_like(done_ref)
@@ -546,7 +571,9 @@
         for i in range(0, cells_x, STRIP):
             rows = slice(i, i + STRIP)
             wide[STRIP + i : 2 * STRIP + i, :] = factors[0, rows, :] * recv[f, rows, :] * rate
-        base_copy(f).wait()
+        if not with_x:
+            base_copy(f).wait()
+        start = early_base if with_x else base
         for i in range(0, cells_x, STRIP):
             rows = slice(i, i + STRIP)
             mid = wide[STRIP + i : 2 * STRIP + i, :]
@@ -556,19 +583,23 @@
             prior = jnp.where(lane == 0, cols[rows, 0:1], pltpu.roll(mid, 1, 1))
             later = jnp.where(lane == cells_y - 1, cols[rows, 1:2], pltpu.roll(mid, cells_y - 1, 1))
             more += factors[3, rows, :] * prior + factors[4, rows, :] * later
-            base[f, rows, :] = base[f, rows, :] + mix_b * (2.0 * mid + more)
+            base[f, rows, :] = start[f, rows, :] + mix_b * (2.0 * mid + more)
         to_new.start()
         return carry
 
-    lax.fori_loop(0, count, one_field, 0)
-    for f, i in outer_rows:
-        outer_copy(f, i, False).wait()
-        row = i * (STRIP - 1)
-        at = ends[i] + row
-        line = late[i][f : f + 1, :] * (above, below)[i][keep, :] * gamma_ref[0, count + f]
-        more = mix_b * factors[1 + i, at : at + 1, :] * line
-        outer[f, i, row : row + 1, :] = outer[f, i, row : row + 1, :] + more
-        outer_copy(f, i, True).start()
+    def add_lines():
+        for f, i in outer_rows:
+            outer_copy(f, i, False).wait()
+            row = i * (STRIP - 1)
+            at = ends[i] + row
+            line = late[i][f : f + 1, :] * (above, below)[i][keep, :] * gamma_ref[0, count + f]
+            more = mix_b * factors[1 + i, at : at + 1, :] * line
+            outer[f, i, row : row + 1, :] = outer[f, i, row : row + 1, :] + more
+            outer_copy(f, i, True).start()
+
+    lax.fori_loop(0, count - 1, one_field, 0)
+    add_lines()
+    one_field(count - 1, 0)
     for f in range(count):
         for copy in out_copies(f):
             copy.wait()
@@ -577,7 +608,7 @@
 
 
 def finished(
-    first, new_state, remapped, recv, x_rims, y_rims, late_rims, late_done, gamma, mix, factors, received
+    first, new_state, remapped, recv, x_rims, y_rims, closing, gamma, mix, factors, received
 ):
     count, cells_x, cells_y = recv.shape
     chan = gamma.shape[1]
@@ -585,7 +616,8 @@
     anywhere = pl.BlockSpec(memory_space=pl.ANY)
     operands = [gamma, mix, *received, factors, recv, *y_rims]
     if with_x:
-        operands += [*x_rims, *late_rims]
+        late_rims, base_early, late_done = closing
+        operands += [*x_rims, *late_rims, base_early]
     specs = [pl.BlockSpec(memory_space=pltpu.SMEM)] * 2
     specs += [pl.BlockSpec(memory_space=pltpu.VMEM)] * (len(operands) - 2) + [anywhere]
     aliases = {len(operands): 0}
@@ -666,9 +698,9 @@
     starts = jnp.concatenate([above[:, :LANES], below[:, :LANES]], axis=0)
     corners_left = lax.ppermute(ends, "ty", shift_pairs(ty, 1))
     corners_right = lax.ppermute(starts, "ty", shift_pairs(ty, -1))
-    base, factors = base_of(
+    base, base_early, factors = base_of(
         state, coefs, land_after, rates, mix, (x_low, x_high, y_low, y_high), received,
-        (corners_left, corners_right),
+        (corners_left, corners_right), half,
     )
 
     ids_late = late_in[:, capacity, 0, :]
@@ -685,7 +717,7 @@
     )
     rest = (gamma, mix, factors, received)
     new_state, remapped, done = finished(
-        half, base, None, recv_late, None, late_y, None, None, *rest
+        half, base, None, recv_late, None, late_y, None, *rest
     )
     early_in, done = lax.optimization_barrier((early_in, done))
     recv_early, top, bottom, left, right = add_up(ids_early, early_in, 16)
@@ -698,7 +730,7 @@
         lax.ppermute(left, "ty", shift_pairs(ty, -1)),
     )
     new_state, remapped, _ = finished(
-        0, new_state, remapped, recv_early, early_x, early_y, late_x, done, *rest
+        0, new_state, remapped, recv_early, early_x, early_y, (late_x, base_early, done), *rest
     )
     return new_state, remapped
 

time: 143 us -> 142 us (level)
    unnamed x18 -> x22, local copies, waits for them, and re-layouts: 2.22 us -> 3.2 us
  transfers between devices with their start and end apart: 19 -> 19, of which waited for: 5 -> 4; matrix products, arithmetic and copies ran while one was open for 1% -> 1% of each run, Pallas kernels for 21% -> 22%
where the time goes in v7:
time: 142 us; the launch traced here: 141 us
  starting transfers between devices  64.7 us (46%)
  Pallas kernels  45.1 us (32%)
  waiting for transfers between devices  25.2 us (18%)
  local copies, waits for them, and re-layouts  4.64 us (3%)
    all_to_all x2, starting transfers between devices, exchanged(): lax.all_to_all(rows, ('tx', 'ty'), split_axis=0, concat_axis=0, tiled=True)  19.8 us
    pallas_call x1, Pallas kernels, base_of(): pl.pallas_call(functools.partial(base_kernel, half), grid=(nfield,), in_s...  12.3 us
    pallas_call x1, Pallas kernels, contributions(): pl.pallas_call(functools.partial(contribution_kernel, dims), in_specs=[pl...  10.8 us
    ppermute x1, waiting for transfers between devices, body(): early = lax.ppermute(early, 'comp', swap)  9.06 us
    pallas_call x2, Pallas kernels, summed(): pl.pallas_call(functools.partial(sum_kernel, dims), in_specs=[pl.BlockSpe...  8.34 us
    ppermute x1, waiting for transfers between devices, body(): above = lax.ppermute(x_high, 'tx', shift_pairs(tx, 1))  7.72 us
    pallas_call x2, Pallas kernels, finished(): pl.pallas_call(functools.partial(finish_kernel, first, with_x), in_specs=...  7.59 us
    ppermute x1, starting transfers between devices, body(): lax.ppermute(bottom, 'tx', shift_pairs(tx, 1))  6.6 us
  transfers between devices with their start and end apart: 19, of which 4 were waited for; matrix products, arithmetic and copies ran while one was open for 1% of the time, Pallas kernels for 22%

profile of v7, /device:TPU:1, one launch (start us, length us, event | category | flops | bytes accessed | tf_op | source)
XLA Modules:
  0.0 140.6 jit_solution(9806283473073534710)
XLA Ops:
  0.6 10.8 %contributions.1 = (f32[513,4,128]{2,1,0:T(4,128)}, f32[1040,4,128]{2,1,0:T(4,128)}) custom-call(s32[1,512]{1,0:T(1,128)} %src_ref.1, s32[1,512]{1,0:T(1,128)} %bitcast.13, s32[1,512]{1,0:T(1,128)} %blk_ref.1, f32[1,16,128,512]{3,2,1,0:T(8,128)} %state_ref.3, bf16[1,512,128,128]{3,2,1,0:T(8,128)(2,1)} %weights_ref.1), custom_call_target="tpu_custom_call" | custom-call | flops 134217728 | bytes 25296896 | tf_op jit(solution)/shard_map/contributions/pallas_call | solution.py:157
  11.4 0.0 copy-start.10
  11.5 0.0 copy-start.2
  11.5 0.0 copy-start.3
  11.5 7.5 %all-to-all-start = ((f32[16,65,4,128]{3,2,1,0:T(4,128)}), f32[16,65,4,128]{3,2,1,0:T(4,128)}, u32[]{:S(2)}, u32[]{:S(2)}) async-start(f32[16,65,4,128]{3,2,1,0:T(4,128)} %bitcast.10), calls=%async_computation | async-start | bytes 4259840 | tf_op jit(solution)/shard_map/all_to_all | solution.py:672
  19.0 1.2 collective-permute-start
  20.2 0.0 copy-start
  20.2 2.2 %copy-done = f32[1,16,128,512]{3,2,1,0:T(8,128)S(1)} copy-done((f32[1,16,128,512]{3,2,1,0:T(8,128)S(1)}, f32[1,16,128,512]{3,2,1,0:T(8,128)}, u32[]{:S(2)}) %copy-start) | copy-done | bytes 4194328
  22.4 2.0 %edges.1 = (f32[40,512]{1,0:T(8,128)S(1)}, f32[40,512]{1,0:T(8,128)S(1)}, f32[40,128]{1,0:T(8,128)S(1)}, f32[40,128]{1,0:T(8,128)S(1)}) custom-call(f32[1,2]{1,0:T(1,128)S(1)} %broadcast_select_fusion.mix_ref, f32[1,16,128,512]{3,2,1,0:T(8,128)S(1)} %copy-done, f32[1,16,128,512]{3,2,1,0:T(8,128)S(1)} %copy-done, f32[1,16,128,512]{3,2,1,0:T(8,128)S(1)} %copy-done, ...), custom_call_target="tpu_custom_call" | custom-call | flops 1048576 | bytes 4194304 | tf_op jit(solution)/shard_map/edges/pallas_call | solution.py:401
  24.4 3.3 %collective-permute-start.1 = (f32[40,512]{1,0:T(8,128)S(1)}, f32[40,512]{1,0:T(8,128)S(1)}, u32[]{:S(2)}, u32[]{:S(2)}) collective-permute-start(f32[40,512]{1,0:T(8,128)S(1)} %get-tuple-element.37.x_high), channel_id=1, source_target_pairs={{0,4},{4,8},{8,12},{1,5},{5,9},{9,13},{2,6},{6,10},{10,14},{3,7},{... | collective-permute-start | bytes 245768 | tf_op jit(solution)/shard_map/ppermute | solution.py:689
  27.7 1.3 collective-permute-start.2
  29.0 3.9 %collective-permute-start.3 = (f32[40,128]{1,0:T(8,128)S(1)}, f32[40,128]{1,0:T(8,128)S(1)}, u32[]{:S(2)}, u32[]{:S(2)}) collective-permute-start(f32[40,128]{1,0:T(8,128)S(1)} %get-tuple-element.39.y_high), channel_id=1, source_target_pairs={{0,1},{1,2},{2,3},{4,5},{5,6},{6,7},{8,9},{9,10},{10,11},{12,13},{... | collective-permute-start | bytes 61448 | tf_op jit(solution)/shard_map/ppermute | solution.py:687
  32.9 1.9 %collective-permute-start.4 = (f32[40,128]{1,0:T(8,128)S(1)}, f32[40,128]{1,0:T(8,128)S(1)}, u32[]{:S(2)}, u32[]{:S(2)}) collective-permute-start(f32[40,128]{1,0:T(8,128)S(1)} %get-tuple-element.40.y_low), channel_id=1, source_target_pairs={{1,0},{2,1},{3,2},{5,4},{6,5},{7,6},{9,8},{10,9},{11,10},{13,12},{... | collective-permute-start | bytes 61448 | tf_op jit(solution)/shard_map/ppermute | solution.py:688
  34.8 9.1 %collective-permute-done.in_ref = f32[513,4,128]{2,1,0:T(4,128)S(1)} collective-permute-done((f32[513,4,128]{2,1,0:T(4,128)}, f32[513,4,128]{2,1,0:T(4,128)S(1)}, u32[]{:S(2)}, u32[]{:S(2)}) %collective-permute-start) | collective-permute-done | bytes 1050656 | tf_op jit(solution)/shard_map/ppermute | solution.py:678
  43.9 4.0 %place_in_slots.1 = f32[1024,4,128]{2,1,0:T(4,128)} custom-call(f32[513,4,128]{2,1,0:T(4,128)S(1)} %collective-permute-done.in_ref), custom_call_target="tpu_custom_call" | custom-call | flops 1050624 | bytes 3151872 | tf_op jit(solution)/shard_map/place_in_slots/pallas_call | solution.py:208
  47.9 0.0 collective-permute-done.3.left.before
  47.9 7.7 %collective-permute-done.1.above = f32[40,512]{1,0:T(8,128)S(1)} collective-permute-done((f32[40,512]{1,0:T(8,128)S(1)}, f32[40,512]{1,0:T(8,128)S(1)}, u32[]{:S(2)}, u32[]{:S(2)}) %collective-permute-start.1) | collective-permute-done | bytes 81952 | tf_op jit(solution)/shard_map/ppermute | solution.py:689
  55.7 0.0 collective-permute-done.2.below
  55.7 5.4 %all-to-all-done = f32[16,65,4,128]{3,2,1,0:T(4,128)} async-done(((f32[16,65,4,128]{3,2,1,0:T(4,128)}), f32[16,65,4,128]{3,2,1,0:T(4,128)}, u32[]{:S(2)}, u32[]{:S(2)}) %all-to-all-start) | async-done | bytes 2129952 | tf_op jit(solution)/shard_map/all_to_all | solution.py:672
  61.1 12.3 %all-to-all-start.1 = ((f32[16,64,4,128]{3,2,1,0:T(4,128)}), f32[16,64,4,128]{3,2,1,0:T(4,128)}, u32[]{:S(2)}, u32[]{:S(2)}) async-start(f32[16,64,4,128]{3,2,1,0:T(4,128)} %bitcast.4), calls=%async_computation.1 | async-start | bytes 4194304 | tf_op jit(solution)/shard_map/all_to_all | solution.py:672
  73.4 1.4 slice.20
  74.8 5.2 %sum_by_block.2 = (f32[4,128,512]{2,1,0:T(8,128)}, f32[4,512]{1,0:T(4,128)}, f32[4,512]{1,0:T(4,128)}, f32[4,128]{1,0:T(4,128)}, f32[4,128]{1,0:T(4,128)}) custom-call(f32[16,128]{1,0:T(8,128)} %bitcast.11, f32[4160,128]{1,0:T(8,128)} %bitcast.5.rows_ref), custom_call_target="tpu_custom_call" | custom-call | flops 1073741824 | bytes 3145728 | tf_op jit(solution)/shard_map/sum_by_block/pallas_call | solution.py:286
  80.0 1.3 collective-permute-start.8
  81.3 3.8 %collective-permute-start.5 = (f32[80,128]{1,0:T(8,128)S(1)}, f32[80,128]{1,0:T(8,128)S(1)}, u32[]{:S(2)}, u32[]{:S(2)}) collective-permute-start(f32[80,128]{1,0:T(8,128)S(1)} %pad_maximum_fusion), channel_id=1, source_target_pairs={{0,1},{1,2},{2,3},{4,5},{5,6},{6,7},{8,9},{9,10},{10,11},{12,13},{... | collective-permute-start | bytes 122888 | tf_op jit(solution)/shard_map/ppermute | solution.py:699
  85.1 1.9 %collective-permute-start.6 = (f32[80,128]{1,0:T(8,128)S(1)}, f32[80,128]{1,0:T(8,128)S(1)}, u32[]{:S(2)}, u32[]{:S(2)}) collective-permute-start(f32[80,128]{1,0:T(8,128)S(1)} %pad_maximum_fusion.1), channel_id=1, source_target_pairs={{1,0},{2,1},{3,2},{5,4},{6,5},{7,6},{9,8},{10,9},{11,10},{13,12},{... | collective-permute-start | bytes 122888 | tf_op jit(solution)/shard_map/ppermute | solution.py:700
  87.1 0.3 collective-permute-start.7
  87.4 4.8 %collective-permute-start.9 = (f32[4,128]{1,0:T(4,128)}, f32[4,128]{1,0:T(4,128)S(1)}, u32[]{:S(2)}, u32[]{:S(2)}) collective-permute-start(f32[4,128]{1,0:T(4,128)} %get-tuple-element.48), channel_id=1, source_target_pairs={{0,17},{1,18},{2,19},{16,1},{17,2},{18,3},{4,21},{5,22},{6,23},{20... | collective-permute-start | bytes 6152 | tf_op jit(solution)/shard_map/ppermute | solution.py:715
  92.2 1.9 %collective-permute-start.10 = (f32[4,128]{1,0:T(4,128)}, f32[4,128]{1,0:T(4,128)S(1)}, u32[]{:S(2)}, u32[]{:S(2)}) collective-permute-start(f32[4,128]{1,0:T(4,128)} %get-tuple-element.49), channel_id=1, source_target_pairs={{1,16},{2,17},{3,18},{17,0},{18,1},{19,2},{5,20},{6,21},{7,22},{21... | collective-permute-start | bytes 6152 | tf_op jit(solution)/shard_map/ppermute | solution.py:716
  94.2 0.1 broadcast_in_dim.8.rates_ref
  94.3 12.3 %base.1 = (f32[1,16,128,512]{3,2,1,0:T(8,128)}, f32[4,128,512]{2,1,0:T(8,128)S(1)}, f32[6,128,512]{2,1,0:T(8,128)S(1)}) custom-call(f32[1,16]{1,0:T(1,128)S(1)} %get-tuple-element.71.rate_ref, f32[1,2]{1,0:T(1,128)S(1)} %broadcast_select_fusion.mix_ref, f32[16,128]{1,0:T(8,128)S(1)} %broadcast_in_dim.8.rates_ref, f32[1,3,128,512]{3,2,1,0:T(8,128)S(1)} %copy-done.2, ...), custom_call_target="tpu_custom_call" | custom-call | flops 41943040 | bytes 8388608 | tf_op jit(solution)/shard_map/base/pallas_call | solution.py:487
  106.6 1.0 copy-done.4
  107.6 3.2 %collective-permute-start.15 = (f32[4,512]{1,0:T(4,128)S(1)}, f32[4,512]{1,0:T(4,128)S(1)}, u32[]{:S(2)}, u32[]{:S(2)}) collective-permute-start(f32[4,512]{1,0:T(4,128)S(1)} %copy-done.9), channel_id=1, source_target_pairs={{0,20},{4,24},{8,28},{16,4},{20,8},{24,12},{1,21},{5,25},{9,29},{1... | collective-permute-start | bytes 24584 | tf_op jit(solution)/shard_map/ppermute | solution.py:711
  110.8 1.3 collective-permute-start.16
  112.1 0.0 collective-permute-done.10.right
  112.1 0.0 collective-permute-done.8.recv
  112.1 4.0 %finish.2 = (f32[1,16,128,512]{3,2,1,0:T(8,128)}, f32[1,8,128,512]{3,2,1,0:T(8,128)}, f32[8,128]{1,0:T(8,128)S(1)}) custom-call(f32[1,8]{1,0:T(1,128)S(1)} %copy-done.6, f32[1,2]{1,0:T(1,128)S(1)} %broadcast_select_fusion.mix_ref, f32[40,512]{1,0:T(8,128)S(1)} %collective-permute-done.1.above, ...), custom_call_target="tpu_custom_call", output_to_operand_aliasing={{0}: (10, {})} | custom-call | flops 5242880 | bytes 5242880 | tf_op jit(solution)/shard_map/finish/pallas_call | solution.py:629
  116.1 0.0 collective-permute-done.7.ids_ref
  116.1 3.1 %sum_by_block.3 = (f32[4,128,512]{2,1,0:T(8,128)S(1)}, f32[4,512]{1,0:T(4,128)S(1)}, f32[4,512]{1,0:T(4,128)S(1)}, f32[4,128]{1,0:T(4,128)S(1)}, f32[4,128]{1,0:T(4,128)S(1)}) custom-call(f32[16,128]{1,0:T(8,128)S(1)} %collective-permute-done.7.ids_ref, f32[4096,128]{1,0:T(8,128)} %bitcast.6.rows_ref), custom_call_target="tpu_custom_call" | custom-call | flops 1073741824 | bytes 3145728 | tf_op jit(solution)/shard_map/sum_by_block/pallas_call | solution.py:286
  119.2 6.6 %collective-permute-start.13 = (f32[4,512]{1,0:T(4,128)S(1)}, f32[4,512]{1,0:T(4,128)S(1)}, u32[]{:S(2)}, u32[]{:S(2)}) collective-permute-start(f32[4,512]{1,0:T(4,128)S(1)} %get-tuple-element.56), channel_id=1, source_target_pairs={{0,4},{4,8},{8,12},{1,5},{5,9},{9,13},{2,6},{6,10},{10,14},{3,7},{... | collective-permute-start | bytes 24584 | tf_op jit(solution)/shard_map/ppermute | solution.py:725
  125.8 1.3 collective-permute-start.14
  127.1 4.9 %collective-permute-start.11 = (f32[4,128]{1,0:T(4,128)S(1)}, f32[4,128]{1,0:T(4,128)S(1)}, u32[]{:S(2)}, u32[]{:S(2)}) collective-permute-start(f32[4,128]{1,0:T(4,128)S(1)} %get-tuple-element.54), channel_id=1, source_target_pairs={{0,1},{1,2},{2,3},{4,5},{5,6},{6,7},{8,9},{9,10},{10,11},{12,13},{... | collective-permute-start | bytes 6152 | tf_op jit(solution)/shard_map/ppermute | solution.py:729
  132.1 0.0 collective-permute-done.15.rest_2_
  132.1 1.9 %collective-permute-start.12 = (f32[4,128]{1,0:T(4,128)S(1)}, f32[4,128]{1,0:T(4,128)S(1)}, u32[]{:S(2)}, u32[]{:S(2)}) collective-permute-start(f32[4,128]{1,0:T(4,128)S(1)} %get-tuple-element.55), channel_id=1, source_target_pairs={{1,0},{2,1},{3,2},{5,4},{6,5},{7,6},{9,8},{10,9},{11,10},{13,12},{... | collective-permute-start | bytes 6152 | tf_op jit(solution)/shard_map/ppermute | solution.py:730
  134.0 0.0 collective-permute-done.11.left
  134.0 3.0 %collective-permute-done.12.right = f32[4,128]{1,0:T(4,128)S(1)} collective-permute-done((f32[4,128]{1,0:T(4,128)S(1)}, f32[4,128]{1,0:T(4,128)S(1)}, u32[]{:S(2)}, u32[]{:S(2)}) %collective-permute-start.12) | collective-permute-done | bytes 2080 | tf_op jit(solution)/shard_map/ppermute | solution.py:730
  137.0 0.0 collective-permute-done.13.rest_0_
  137.0 0.0 collective-permute-done.14.rest_1_
  137.0 3.6 %finish.3 = (f32[1,16,128,512]{3,2,1,0:T(8,128)}, f32[1,8,128,512]{3,2,1,0:T(8,128)}, f32[8,128]{1,0:T(8,128)}) custom-call(f32[1,8]{1,0:T(1,128)S(1)} %copy-done.6, f32[1,2]{1,0:T(1,128)S(1)} %broadcast_select_fusion.mix_ref, f32[40,512]{1,0:T(8,128)S(1)} %collective-permute-done.1.above, ...), custom_call_target="tpu_custom_call", output_to_operand_aliasing={{0}: (15, {}), {1}: (16, {})} | custom-call | flops 5242880 | bytes 5242880 | tf_op jit(solution)/shard_map/finish/pallas_call | solution.py:629
  (27 shorter events, 0.1 us)
Async XLA Ops:
  11.4 8.7 %copy-start.10 = (f32[1,2]{1,0:T(1,128)S(1)}, f32[1,2]{1,0:T(1,128)}, u32[]{:S(2)}) copy-start(f32[1,2]{1,0:T(1,128)} %constant.14.clone) | copy-start | bytes 28
  11.5 8.7 %copy-start.2 = (f32[1,3,128,512]{3,2,1,0:T(8,128)S(1)}, f32[1,3,128,512]{3,2,1,0:T(8,128)}, u32[]{:S(2)}) copy-start(f32[1,3,128,512]{3,2,1,0:T(8,128)} %coefs_ref.1) | copy-start | bytes 2359300
  11.5 8.7 %copy-start.3 = (s32[128,512]{1,0:T(8,128)S(1)}, s32[128,512]{1,0:T(8,128)}, u32[]{:S(2)}) copy-start(s32[128,512]{1,0:T(8,128)} %land_ref) | copy-start | bytes 786436
  11.5 49.6 %all-to-all-start = ((f32[16,65,4,128]{3,2,1,0:T(4,128)}), f32[16,65,4,128]{3,2,1,0:T(4,128)}, u32[]{:S(2)}, u32[]{:S(2)}) async-start(f32[16,65,4,128]{3,2,1,0:T(4,128)} %bitcast.10), calls=%async_computation | async-start | bytes 4259840 | tf_op jit(solution)/shard_map/all_to_all | solution.py:672
  19.0 24.9 %collective-permute-start = (f32[513,4,128]{2,1,0:T(4,128)}, f32[513,4,128]{2,1,0:T(4,128)S(1)}, u32[]{:S(2)}, u32[]{:S(2)}) collective-permute-start(f32[513,4,128]{2,1,0:T(4,128)} %get-tuple-element.34), channel_id=1, source_target_pairs={{0,16},{16,0},{1,17},{17,1},{2,18},{18,2},{3,19},{19,3},{4,20},{20... | collective-permute-start | bytes 3151880 | tf_op jit(solution)/shard_map/ppermute | solution.py:678
  20.2 2.2 %copy-start = (f32[1,16,128,512]{3,2,1,0:T(8,128)S(1)}, f32[1,16,128,512]{3,2,1,0:T(8,128)}, u32[]{:S(2)}) copy-start(f32[1,16,128,512]{3,2,1,0:T(8,128)} %state_ref.3) | copy-start | bytes 12582916
  24.4 31.3 %collective-permute-start.1 = (f32[40,512]{1,0:T(8,128)S(1)}, f32[40,512]{1,0:T(8,128)S(1)}, u32[]{:S(2)}, u32[]{:S(2)}) collective-permute-start(f32[40,512]{1,0:T(8,128)S(1)} %get-tuple-element.37.x_high), channel_id=1, source_target_pairs={{0,4},{4,8},{8,12},{1,5},{5,9},{9,13},{2,6},{6,10},{10,14},{3,7},{... | collective-permute-start | bytes 245768 | tf_op jit(solution)/shard_map/ppermute | solution.py:689
  27.7 28.0 %collective-permute-start.2 = (f32[40,512]{1,0:T(8,128)S(1)}, f32[40,512]{1,0:T(8,128)S(1)}, u32[]{:S(2)}, u32[]{:S(2)}) collective-permute-start(f32[40,512]{1,0:T(8,128)S(1)} %get-tuple-element.38.x_low), channel_id=1, source_target_pairs={{4,0},{8,4},{12,8},{5,1},{9,5},{13,9},{6,2},{10,6},{14,10},{7,3},{... | collective-permute-start | bytes 245768 | tf_op jit(solution)/shard_map/ppermute | solution.py:690
  29.0 18.9 %collective-permute-start.3 = (f32[40,128]{1,0:T(8,128)S(1)}, f32[40,128]{1,0:T(8,128)S(1)}, u32[]{:S(2)}, u32[]{:S(2)}) collective-permute-start(f32[40,128]{1,0:T(8,128)S(1)} %get-tuple-element.39.y_high), channel_id=1, source_target_pairs={{0,1},{1,2},{2,3},{4,5},{5,6},{6,7},{8,9},{9,10},{10,11},{12,13},{... | collective-permute-start | bytes 61448 | tf_op jit(solution)/shard_map/ppermute | solution.py:687
  32.9 15.0 %collective-permute-start.4 = (f32[40,128]{1,0:T(8,128)S(1)}, f32[40,128]{1,0:T(8,128)S(1)}, u32[]{:S(2)}, u32[]{:S(2)}) collective-permute-start(f32[40,128]{1,0:T(8,128)S(1)} %get-tuple-element.40.y_low), channel_id=1, source_target_pairs={{1,0},{2,1},{3,2},{5,4},{6,5},{7,6},{9,8},{10,9},{11,10},{13,12},{... | collective-permute-start | bytes 61448 | tf_op jit(solution)/shard_map/ppermute | solution.py:688
  61.1 55.0 %all-to-all-start.1 = ((f32[16,64,4,128]{3,2,1,0:T(4,128)}), f32[16,64,4,128]{3,2,1,0:T(4,128)}, u32[]{:S(2)}, u32[]{:S(2)}) async-start(f32[16,64,4,128]{3,2,1,0:T(4,128)} %bitcast.4), calls=%async_computation.1 | async-start | bytes 4194304 | tf_op jit(solution)/shard_map/all_to_all | solution.py:672
  74.8 12.3 %copy-start.7 = (f32[16,1,1,128]{3,2,1,0:T(1,128)S(1)}, f32[16,1,1,128]{3,2,1,0:T(1,128)}, u32[]{:S(2)}) copy-start(f32[16,1,1,128]{3,2,1,0:T(1,128)} %slice.20) | copy-start | bytes 24580
  74.8 12.6 %copy-start.6 = (f32[1,8]{1,0:T(1,128)S(1)}, f32[1,8]{1,0:T(1,128)}, u32[]{:S(2)}) copy-start(f32[1,8]{1,0:T(1,128)} %gamma_ref.3) | copy-start | bytes 100
  74.8 19.5 %copy-start.1 = (f32[1,16,128,512]{3,2,1,0:T(8,128)S(1)}, f32[1,16,128,512]{3,2,1,0:T(8,128)}, u32[]{:S(2)}) copy-start(f32[1,16,128,512]{3,2,1,0:T(8,128)} %state_ref.3) | copy-start | bytes 12582916
  80.0 32.1 %collective-permute-start.8 = (f32[4,128,512]{2,1,0:T(8,128)}, f32[4,128,512]{2,1,0:T(8,128)S(1)}, u32[]{:S(2)}, u32[]{:S(2)}) collective-permute-start(f32[4,128,512]{2,1,0:T(8,128)} %get-tuple-element.47), channel_id=1, source_target_pairs={{0,16},{16,0},{1,17},{17,1},{2,18},{18,2},{3,19},{19,3},{4,20},{20... | collective-permute-start | bytes 3145736 | tf_op jit(solution)/shard_map/ppermute | solution.py:709
  81.3 11.0 %collective-permute-start.5 = (f32[80,128]{1,0:T(8,128)S(1)}, f32[80,128]{1,0:T(8,128)S(1)}, u32[]{:S(2)}, u32[]{:S(2)}) collective-permute-start(f32[80,128]{1,0:T(8,128)S(1)} %pad_maximum_fusion), channel_id=1, source_target_pairs={{0,1},{1,2},{2,3},{4,5},{5,6},{6,7},{8,9},{9,10},{10,11},{12,13},{... | collective-permute-start | bytes 122888 | tf_op jit(solution)/shard_map/ppermute | solution.py:699
  85.1 9.1 %collective-permute-start.6 = (f32[80,128]{1,0:T(8,128)S(1)}, f32[80,128]{1,0:T(8,128)S(1)}, u32[]{:S(2)}, u32[]{:S(2)}) collective-permute-start(f32[80,128]{1,0:T(8,128)S(1)} %pad_maximum_fusion.1), channel_id=1, source_target_pairs={{1,0},{2,1},{3,2},{5,4},{6,5},{7,6},{9,8},{10,9},{11,10},{13,12},{... | collective-permute-start | bytes 122888 | tf_op jit(solution)/shard_map/ppermute | solution.py:700
  87.1 29.0 %collective-permute-start.7 = (f32[16,128]{1,0:T(8,128)S(1)}, f32[16,128]{1,0:T(8,128)S(1)}, u32[]{:S(2)}, u32[]{:S(2)}) collective-permute-start(f32[16,128]{1,0:T(8,128)S(1)} %bitcast.12), channel_id=1, source_target_pairs={{0,16},{16,0},{1,17},{17,1},{2,18},{18,2},{3,19},{19,3},{4,20},{20... | collective-permute-start | bytes 24584 | tf_op jit(solution)/shard_map/ppermute | solution.py:707
  87.4 23.4 %collective-permute-start.9 = (f32[4,128]{1,0:T(4,128)}, f32[4,128]{1,0:T(4,128)S(1)}, u32[]{:S(2)}, u32[]{:S(2)}) collective-permute-start(f32[4,128]{1,0:T(4,128)} %get-tuple-element.48), channel_id=1, source_target_pairs={{0,17},{1,18},{2,19},{16,1},{17,2},{18,3},{4,21},{5,22},{6,23},{20... | collective-permute-start | bytes 6152 | tf_op jit(solution)/shard_map/ppermute | solution.py:715
  92.2 19.8 %collective-permute-start.10 = (f32[4,128]{1,0:T(4,128)}, f32[4,128]{1,0:T(4,128)S(1)}, u32[]{:S(2)}, u32[]{:S(2)}) collective-permute-start(f32[4,128]{1,0:T(4,128)} %get-tuple-element.49), channel_id=1, source_target_pairs={{1,16},{2,17},{3,18},{17,0},{18,1},{19,2},{5,20},{6,21},{7,22},{21... | collective-permute-start | bytes 6152 | tf_op jit(solution)/shard_map/ppermute | solution.py:716
  94.3 13.3 %copy-start.9 = (f32[4,512]{1,0:T(4,128)S(1)}, f32[4,512]{1,0:T(4,128)}, u32[]{:S(2)}) copy-start(f32[4,512]{1,0:T(4,128)} %get-tuple-element.58) | copy-start | bytes 24580
  94.3 16.5 %copy-start.8 = (f32[4,512]{1,0:T(4,128)S(1)}, f32[4,512]{1,0:T(4,128)}, u32[]{:S(2)}) copy-start(f32[4,512]{1,0:T(4,128)} %get-tuple-element.59) | copy-start | bytes 24580
  106.6 1.0 copy-start.4
  107.6 24.5 %collective-permute-start.15 = (f32[4,512]{1,0:T(4,128)S(1)}, f32[4,512]{1,0:T(4,128)S(1)}, u32[]{:S(2)}, u32[]{:S(2)}) collective-permute-start(f32[4,512]{1,0:T(4,128)S(1)} %copy-done.9), channel_id=1, source_target_pairs={{0,20},{4,24},{8,28},{16,4},{20,8},{24,12},{1,21},{5,25},{9,29},{1... | collective-permute-start | bytes 24584 | tf_op jit(solution)/shard_map/ppermute | solution.py:711
  110.8 23.2 %collective-permute-start.16 = (f32[4,512]{1,0:T(4,128)S(1)}, f32[4,512]{1,0:T(4,128)S(1)}, u32[]{:S(2)}, u32[]{:S(2)}) collective-permute-start(f32[4,512]{1,0:T(4,128)S(1)} %copy-done.8), channel_id=1, source_target_pairs={{4,16},{8,20},{12,24},{20,0},{24,4},{28,8},{5,17},{9,21},{13,25},{... | collective-permute-start | bytes 24584 | tf_op jit(solution)/shard_map/ppermute | solution.py:712
  116.1 20.9 %copy-start.5 = (f32[4,128,512]{2,1,0:T(8,128)S(1)}, f32[4,128,512]{2,1,0:T(8,128)}, u32[]{:S(2)}) copy-start(f32[4,128,512]{2,1,0:T(8,128)} %copy-done.4) | copy-start | bytes 3145732
  119.2 17.8 %collective-permute-start.13 = (f32[4,512]{1,0:T(4,128)S(1)}, f32[4,512]{1,0:T(4,128)S(1)}, u32[]{:S(2)}, u32[]{:S(2)}) collective-permute-start(f32[4,512]{1,0:T(4,128)S(1)} %get-tuple-element.56), channel_id=1, source_target_pairs={{0,4},{4,8},{8,12},{1,5},{5,9},{9,13},{2,6},{6,10},{10,14},{3,7},{... | collective-permute-start | bytes 24584 | tf_op jit(solution)/shard_map/ppermute | solution.py:725
  125.8 11.2 %collective-permute-start.14 = (f32[4,512]{1,0:T(4,128)S(1)}, f32[4,512]{1,0:T(4,128)S(1)}, u32[]{:S(2)}, u32[]{:S(2)}) collective-permute-start(f32[4,512]{1,0:T(4,128)S(1)} %get-tuple-element.57), channel_id=1, source_target_pairs={{4,0},{8,4},{12,8},{5,1},{9,5},{13,9},{6,2},{10,6},{14,10},{7,3},{... | collective-permute-start | bytes 24584 | tf_op jit(solution)/shard_map/ppermute | solution.py:726
  127.1 6.9 %collective-permute-start.11 = (f32[4,128]{1,0:T(4,128)S(1)}, f32[4,128]{1,0:T(4,128)S(1)}, u32[]{:S(2)}, u32[]{:S(2)}) collective-permute-start(f32[4,128]{1,0:T(4,128)S(1)} %get-tuple-element.54), channel_id=1, source_target_pairs={{0,1},{1,2},{2,3},{4,5},{5,6},{6,7},{8,9},{9,10},{10,11},{12,13},{... | collective-permute-start | bytes 6152 | tf_op jit(solution)/shard_map/ppermute | solution.py:729
  132.1 4.9 %collective-permute-start.12 = (f32[4,128]{1,0:T(4,128)S(1)}, f32[4,128]{1,0:T(4,128)S(1)}, u32[]{:S(2)}, u32[]{:S(2)}) collective-permute-start(f32[4,128]{1,0:T(4,128)S(1)} %get-tuple-element.55), channel_id=1, source_target_pairs={{1,0},{2,1},{3,2},{5,4},{6,5},{7,6},{9,8},{10,9},{11,10},{13,12},{... | collective-permute-start | bytes 6152 | tf_op jit(solution)/shard_map/ppermute | solution.py:730

commit v8 on v7

--- a/solution.py
+++ b/solution.py
@@ -8,7 +8,7 @@
 from jax.sharding import PartitionSpec as P
 
 LANES = 128
-STEP_PAIRS = 64
+STEP_PAIRS = 128
 STRIP = 8
 NT = (((1,), (1,)), ((), ()))
 
@@ -721,13 +721,13 @@
     )
     early_in, done = lax.optimization_barrier((early_in, done))
     recv_early, top, bottom, left, right = add_up(ids_early, early_in, 16)
+    early_y = (
+        lax.ppermute(right, "ty", shift_pairs(ty, 1)),
+        lax.ppermute(left, "ty", shift_pairs(ty, -1)),
+    )
     early_x = (
         lax.ppermute(bottom, "tx", shift_pairs(tx, 1)),
         lax.ppermute(top, "tx", shift_pairs(tx, -1)),
-    )
-    early_y = (
-        lax.ppermute(right, "ty", shift_pairs(ty, 1)),
-        lax.ppermute(left, "ty", shift_pairs(ty, -1)),
     )
     new_state, remapped, _ = finished(
         0, new_state, remapped, recv_early, early_x, early_y, (late_x, base_early, done), *rest

time: 142 us -> 142 us (level)
  no operation moved by 1% of the time
where the time goes in v8:
time: 142 us; the launch traced here: 141 us
  starting transfers between devices  64.7 us (46%)
  Pallas kernels  45.2 us (32%)
  waiting for transfers between devices  25.2 us (18%)
  local copies, waits for them, and re-layouts  4.64 us (3%)
    all_to_all x2, starting transfers between devices, exchanged(): lax.all_to_all(rows, ('tx', 'ty'), split_axis=0, concat_axis=0, tiled=True)  19.8 us
    pallas_call x1, Pallas kernels, base_of(): pl.pallas_call(functools.partial(base_kernel, half), grid=(nfield,), in_s...  12.3 us
    pallas_call x1, Pallas kernels, contributions(): pl.pallas_call(functools.partial(contribution_kernel, dims), in_specs=[pl...  10.9 us
    ppermute x1, waiting for transfers between devices, body(): early = lax.ppermute(early, 'comp', swap)  9.05 us
    pallas_call x2, Pallas kernels, summed(): pl.pallas_call(functools.partial(sum_kernel, dims), in_specs=[pl.BlockSpe...  8.34 us
    ppermute x1, waiting for transfers between devices, body(): above = lax.ppermute(x_high, 'tx', shift_pairs(tx, 1))  7.74 us
    pallas_call x2, Pallas kernels, finished(): pl.pallas_call(functools.partial(finish_kernel, first, with_x), in_specs=...  7.59 us
    ppermute x1, starting transfers between devices, body(): lax.ppermute(bottom, 'tx', shift_pairs(tx, 1))  6.6 us
  transfers between devices with their start and end apart: 19, of which 4 were waited for; matrix products, arithmetic and copies ran while one was open for 1% of the time, Pallas kernels for 22%

profile of v8, /device:TPU:1, one launch (start us, length us, event | category | flops | bytes accessed | tf_op | source)
XLA Modules:
  0.0 140.8 jit_solution(11082926970452114800)
XLA Ops:
  0.6 10.9 %contributions.1 = (f32[513,4,128]{2,1,0:T(4,128)}, f32[1040,4,128]{2,1,0:T(4,128)}) custom-call(s32[1,512]{1,0:T(1,128)} %src_ref.1, s32[1,512]{1,0:T(1,128)} %bitcast.13, s32[1,512]{1,0:T(1,128)} %blk_ref.1, f32[1,16,128,512]{3,2,1,0:T(8,128)} %state_ref.3, bf16[1,512,128,128]{3,2,1,0:T(8,128)(2,1)} %weights_ref.1), custom_call_target="tpu_custom_call" | custom-call | flops 134217728 | bytes 25296896 | tf_op jit(solution)/shard_map/contributions/pallas_call | solution.py:157
  11.6 0.0 copy-start.10
  11.6 0.0 copy-start.2
  11.6 0.0 copy-start.3
  11.6 7.5 %all-to-all-start = ((f32[16,65,4,128]{3,2,1,0:T(4,128)}), f32[16,65,4,128]{3,2,1,0:T(4,128)}, u32[]{:S(2)}, u32[]{:S(2)}) async-start(f32[16,65,4,128]{3,2,1,0:T(4,128)} %bitcast.10), calls=%async_computation | async-start | bytes 4259840 | tf_op jit(solution)/shard_map/all_to_all | solution.py:672
  19.1 1.2 collective-permute-start
  20.3 0.0 copy-start
  20.4 2.2 %copy-done = f32[1,16,128,512]{3,2,1,0:T(8,128)S(1)} copy-done((f32[1,16,128,512]{3,2,1,0:T(8,128)S(1)}, f32[1,16,128,512]{3,2,1,0:T(8,128)}, u32[]{:S(2)}) %copy-start) | copy-done | bytes 4194328
  22.5 2.0 %edges.1 = (f32[40,512]{1,0:T(8,128)S(1)}, f32[40,512]{1,0:T(8,128)S(1)}, f32[40,128]{1,0:T(8,128)S(1)}, f32[40,128]{1,0:T(8,128)S(1)}) custom-call(f32[1,2]{1,0:T(1,128)S(1)} %broadcast_select_fusion.mix_ref, f32[1,16,128,512]{3,2,1,0:T(8,128)S(1)} %copy-done, f32[1,16,128,512]{3,2,1,0:T(8,128)S(1)} %copy-done, f32[1,16,128,512]{3,2,1,0:T(8,128)S(1)} %copy-done, ...), custom_call_target="tpu_custom_call" | custom-call | flops 1048576 | bytes 4194304 | tf_op jit(solution)/shard_map/edges/pallas_call | solution.py:401
  24.5 3.3 %collective-permute-start.1 = (f32[40,512]{1,0:T(8,128)S(1)}, f32[40,512]{1,0:T(8,128)S(1)}, u32[]{:S(2)}, u32[]{:S(2)}) collective-permute-start(f32[40,512]{1,0:T(8,128)S(1)} %get-tuple-element.37.x_high), channel_id=1, source_target_pairs={{0,4},{4,8},{8,12},{1,5},{5,9},{9,13},{2,6},{6,10},{10,14},{3,7},{... | collective-permute-start | bytes 245768 | tf_op jit(solution)/shard_map/ppermute | solution.py:689
  27.8 1.3 collective-permute-start.2
  29.1 3.9 %collective-permute-start.3 = (f32[40,128]{1,0:T(8,128)S(1)}, f32[40,128]{1,0:T(8,128)S(1)}, u32[]{:S(2)}, u32[]{:S(2)}) collective-permute-start(f32[40,128]{1,0:T(8,128)S(1)} %get-tuple-element.39.y_high), channel_id=1, source_target_pairs={{0,1},{1,2},{2,3},{4,5},{5,6},{6,7},{8,9},{9,10},{10,11},{12,13},{... | collective-permute-start | bytes 61448 | tf_op jit(solution)/shard_map/ppermute | solution.py:687
  33.0 1.9 %collective-permute-start.4 = (f32[40,128]{1,0:T(8,128)S(1)}, f32[40,128]{1,0:T(8,128)S(1)}, u32[]{:S(2)}, u32[]{:S(2)}) collective-permute-start(f32[40,128]{1,0:T(8,128)S(1)} %get-tuple-element.40.y_low), channel_id=1, source_target_pairs={{1,0},{2,1},{3,2},{5,4},{6,5},{7,6},{9,8},{10,9},{11,10},{13,12},{... | collective-permute-start | bytes 61448 | tf_op jit(solution)/shard_map/ppermute | solution.py:688
  35.0 9.1 %collective-permute-done.in_ref = f32[513,4,128]{2,1,0:T(4,128)S(1)} collective-permute-done((f32[513,4,128]{2,1,0:T(4,128)}, f32[513,4,128]{2,1,0:T(4,128)S(1)}, u32[]{:S(2)}, u32[]{:S(2)}) %collective-permute-start) | collective-permute-done | bytes 1050656 | tf_op jit(solution)/shard_map/ppermute | solution.py:678
  44.0 4.0 %place_in_slots.1 = f32[1024,4,128]{2,1,0:T(4,128)} custom-call(f32[513,4,128]{2,1,0:T(4,128)S(1)} %collective-permute-done.in_ref), custom_call_target="tpu_custom_call" | custom-call | flops 1050624 | bytes 3151872 | tf_op jit(solution)/shard_map/place_in_slots/pallas_call | solution.py:208
  48.0 0.0 collective-permute-done.3.left.before
  48.0 0.0 collective-permute-done.4.right.after
  48.1 7.7 %collective-permute-done.1.above = f32[40,512]{1,0:T(8,128)S(1)} collective-permute-done((f32[40,512]{1,0:T(8,128)S(1)}, f32[40,512]{1,0:T(8,128)S(1)}, u32[]{:S(2)}, u32[]{:S(2)}) %collective-permute-start.1) | collective-permute-done | bytes 81952 | tf_op jit(solution)/shard_map/ppermute | solution.py:689
  55.8 0.0 collective-permute-done.2.below
  55.8 5.4 %all-to-all-done = f32[16,65,4,128]{3,2,1,0:T(4,128)} async-done(((f32[16,65,4,128]{3,2,1,0:T(4,128)}), f32[16,65,4,128]{3,2,1,0:T(4,128)}, u32[]{:S(2)}, u32[]{:S(2)}) %all-to-all-start) | async-done | bytes 2129952 | tf_op jit(solution)/shard_map/all_to_all | solution.py:672
  61.3 12.3 %all-to-all-start.1 = ((f32[16,64,4,128]{3,2,1,0:T(4,128)}), f32[16,64,4,128]{3,2,1,0:T(4,128)}, u32[]{:S(2)}, u32[]{:S(2)}) async-start(f32[16,64,4,128]{3,2,1,0:T(4,128)} %bitcast.4), calls=%async_computation.1 | async-start | bytes 4194304 | tf_op jit(solution)/shard_map/all_to_all | solution.py:672
  73.5 1.4 slice.20
  74.9 5.2 %sum_by_block.2 = (f32[4,128,512]{2,1,0:T(8,128)}, f32[4,512]{1,0:T(4,128)}, f32[4,512]{1,0:T(4,128)}, f32[4,128]{1,0:T(4,128)}, f32[4,128]{1,0:T(4,128)}) custom-call(f32[16,128]{1,0:T(8,128)} %bitcast.11, f32[4160,128]{1,0:T(8,128)} %bitcast.5.rows_ref), custom_call_target="tpu_custom_call" | custom-call | flops 1073741824 | bytes 3145728 | tf_op jit(solution)/shard_map/sum_by_block/pallas_call | solution.py:286
  80.1 1.3 collective-permute-start.8
  81.4 3.8 %collective-permute-start.5 = (f32[80,128]{1,0:T(8,128)S(1)}, f32[80,128]{1,0:T(8,128)S(1)}, u32[]{:S(2)}, u32[]{:S(2)}) collective-permute-start(f32[80,128]{1,0:T(8,128)S(1)} %pad_maximum_fusion), channel_id=1, source_target_pairs={{0,1},{1,2},{2,3},{4,5},{5,6},{6,7},{8,9},{9,10},{10,11},{12,13},{... | collective-permute-start | bytes 122888 | tf_op jit(solution)/shard_map/ppermute | solution.py:699
  85.3 1.9 %collective-permute-start.6 = (f32[80,128]{1,0:T(8,128)S(1)}, f32[80,128]{1,0:T(8,128)S(1)}, u32[]{:S(2)}, u32[]{:S(2)}) collective-permute-start(f32[80,128]{1,0:T(8,128)S(1)} %pad_maximum_fusion.1), channel_id=1, source_target_pairs={{1,0},{2,1},{3,2},{5,4},{6,5},{7,6},{9,8},{10,9},{11,10},{13,12},{... | collective-permute-start | bytes 122888 | tf_op jit(solution)/shard_map/ppermute | solution.py:700
  87.2 0.3 collective-permute-start.7
  87.5 4.8 %collective-permute-start.9 = (f32[4,128]{1,0:T(4,128)}, f32[4,128]{1,0:T(4,128)S(1)}, u32[]{:S(2)}, u32[]{:S(2)}) collective-permute-start(f32[4,128]{1,0:T(4,128)} %get-tuple-element.48), channel_id=1, source_target_pairs={{0,17},{1,18},{2,19},{16,1},{17,2},{18,3},{4,21},{5,22},{6,23},{20... | collective-permute-start | bytes 6152 | tf_op jit(solution)/shard_map/ppermute | solution.py:715
  92.4 0.0 collective-permute-done.5.corners_left
  92.4 1.9 %collective-permute-start.10 = (f32[4,128]{1,0:T(4,128)}, f32[4,128]{1,0:T(4,128)S(1)}, u32[]{:S(2)}, u32[]{:S(2)}) collective-permute-start(f32[4,128]{1,0:T(4,128)} %get-tuple-element.49), channel_id=1, source_target_pairs={{1,16},{2,17},{3,18},{17,0},{18,1},{19,2},{5,20},{6,21},{7,22},{21... | collective-permute-start | bytes 6152 | tf_op jit(solution)/shard_map/ppermute | solution.py:716
  94.3 0.0 collective-permute-done.6.corners_right
  94.3 0.1 broadcast_in_dim.8.rates_ref
  94.4 12.3 %base.1 = (f32[1,16,128,512]{3,2,1,0:T(8,128)}, f32[4,128,512]{2,1,0:T(8,128)S(1)}, f32[6,128,512]{2,1,0:T(8,128)S(1)}) custom-call(f32[1,16]{1,0:T(1,128)S(1)} %get-tuple-element.71.rate_ref, f32[1,2]{1,0:T(1,128)S(1)} %broadcast_select_fusion.mix_ref, f32[16,128]{1,0:T(8,128)S(1)} %broadcast_in_dim.8.rates_ref, f32[1,3,128,512]{3,2,1,0:T(8,128)S(1)} %copy-done.2, ...), custom_call_target="tpu_custom_call" | custom-call | flops 41943040 | bytes 8388608 | tf_op jit(solution)/shard_map/base/pallas_call | solution.py:487
  106.7 1.0 copy-done.4
  107.7 3.2 %collective-permute-start.15 = (f32[4,512]{1,0:T(4,128)S(1)}, f32[4,512]{1,0:T(4,128)S(1)}, u32[]{:S(2)}, u32[]{:S(2)}) collective-permute-start(f32[4,512]{1,0:T(4,128)S(1)} %copy-done.9), channel_id=1, source_target_pairs={{0,20},{4,24},{8,28},{16,4},{20,8},{24,12},{1,21},{5,25},{9,29},{1... | collective-permute-start | bytes 24584 | tf_op jit(solution)/shard_map/ppermute | solution.py:711
  110.9 0.0 collective-permute-done.9.left
  110.9 1.3 collective-permute-start.16
  112.2 0.0 collective-permute-done.8.recv
  112.2 4.0 %finish.2 = (f32[1,16,128,512]{3,2,1,0:T(8,128)}, f32[1,8,128,512]{3,2,1,0:T(8,128)}, f32[8,128]{1,0:T(8,128)S(1)}) custom-call(f32[1,8]{1,0:T(1,128)S(1)} %copy-done.6, f32[1,2]{1,0:T(1,128)S(1)} %broadcast_select_fusion.mix_ref, f32[40,512]{1,0:T(8,128)S(1)} %collective-permute-done.1.above, ...), custom_call_target="tpu_custom_call", output_to_operand_aliasing={{0}: (10, {})} | custom-call | flops 5242880 | bytes 5242880 | tf_op jit(solution)/shard_map/finish/pallas_call | solution.py:629
  116.2 0.0 all-to-all-done.1
  116.2 3.1 %sum_by_block.3 = (f32[4,128,512]{2,1,0:T(8,128)S(1)}, f32[4,512]{1,0:T(4,128)S(1)}, f32[4,512]{1,0:T(4,128)S(1)}, f32[4,128]{1,0:T(4,128)S(1)}, f32[4,128]{1,0:T(4,128)S(1)}) custom-call(f32[16,128]{1,0:T(8,128)S(1)} %collective-permute-done.7.ids_ref, f32[4096,128]{1,0:T(8,128)} %bitcast.6.rows_ref), custom_call_target="tpu_custom_call" | custom-call | flops 1073741824 | bytes 3145728 | tf_op jit(solution)/shard_map/sum_by_block/pallas_call | solution.py:286
  119.4 6.6 %collective-permute-start.13 = (f32[4,512]{1,0:T(4,128)S(1)}, f32[4,512]{1,0:T(4,128)S(1)}, u32[]{:S(2)}, u32[]{:S(2)}) collective-permute-start(f32[4,512]{1,0:T(4,128)S(1)} %get-tuple-element.56), channel_id=1, source_target_pairs={{0,4},{4,8},{8,12},{1,5},{5,9},{9,13},{2,6},{6,10},{10,14},{3,7},{... | collective-permute-start | bytes 24584 | tf_op jit(solution)/shard_map/ppermute | solution.py:729
  126.0 1.3 collective-permute-start.14
  127.3 4.9 %collective-permute-start.11 = (f32[4,128]{1,0:T(4,128)S(1)}, f32[4,128]{1,0:T(4,128)S(1)}, u32[]{:S(2)}, u32[]{:S(2)}) collective-permute-start(f32[4,128]{1,0:T(4,128)S(1)} %get-tuple-element.54), channel_id=1, source_target_pairs={{0,1},{1,2},{2,3},{4,5},{5,6},{6,7},{8,9},{9,10},{10,11},{12,13},{... | collective-permute-start | bytes 6152 | tf_op jit(solution)/shard_map/ppermute | solution.py:725
  132.2 0.0 collective-permute-done.15.rest_2_
  132.2 1.9 %collective-permute-start.12 = (f32[4,128]{1,0:T(4,128)S(1)}, f32[4,128]{1,0:T(4,128)S(1)}, u32[]{:S(2)}, u32[]{:S(2)}) collective-permute-start(f32[4,128]{1,0:T(4,128)S(1)} %get-tuple-element.55), channel_id=1, source_target_pairs={{1,0},{2,1},{3,2},{5,4},{6,5},{7,6},{9,8},{10,9},{11,10},{13,12},{... | collective-permute-start | bytes 6152 | tf_op jit(solution)/shard_map/ppermute | solution.py:726
  134.2 3.0 %collective-permute-done.12.right = f32[4,128]{1,0:T(4,128)S(1)} collective-permute-done((f32[4,128]{1,0:T(4,128)S(1)}, f32[4,128]{1,0:T(4,128)S(1)}, u32[]{:S(2)}, u32[]{:S(2)}) %collective-permute-start.12) | collective-permute-done | bytes 2080 | tf_op jit(solution)/shard_map/ppermute | solution.py:726
  137.1 3.6 %finish.3 = (f32[1,16,128,512]{3,2,1,0:T(8,128)}, f32[1,8,128,512]{3,2,1,0:T(8,128)}, f32[8,128]{1,0:T(8,128)}) custom-call(f32[1,8]{1,0:T(1,128)S(1)} %copy-done.6, f32[1,2]{1,0:T(1,128)S(1)} %broadcast_select_fusion.mix_ref, f32[40,512]{1,0:T(8,128)S(1)} %collective-permute-done.1.above, ...), custom_call_target="tpu_custom_call", output_to_operand_aliasing={{0}: (15, {}), {1}: (16, {})} | custom-call | flops 5242880 | bytes 5242880 | tf_op jit(solution)/shard_map/finish/pallas_call | solution.py:629
  (27 shorter events, 0.1 us)
Async XLA Ops:
  11.6 8.7 %copy-start.10 = (f32[1,2]{1,0:T(1,128)S(1)}, f32[1,2]{1,0:T(1,128)}, u32[]{:S(2)}) copy-start(f32[1,2]{1,0:T(1,128)} %constant.14.clone) | copy-start | bytes 28
  11.6 8.7 %copy-start.2 = (f32[1,3,128,512]{3,2,1,0:T(8,128)S(1)}, f32[1,3,128,512]{3,2,1,0:T(8,128)}, u32[]{:S(2)}) copy-start(f32[1,3,128,512]{3,2,1,0:T(8,128)} %coefs_ref.1) | copy-start | bytes 2359300
  11.6 8.7 %copy-start.3 = (s32[128,512]{1,0:T(8,128)S(1)}, s32[128,512]{1,0:T(8,128)}, u32[]{:S(2)}) copy-start(s32[128,512]{1,0:T(8,128)} %land_ref) | copy-start | bytes 786436
  11.6 49.6 %all-to-all-start = ((f32[16,65,4,128]{3,2,1,0:T(4,128)}), f32[16,65,4,128]{3,2,1,0:T(4,128)}, u32[]{:S(2)}, u32[]{:S(2)}) async-start(f32[16,65,4,128]{3,2,1,0:T(4,128)} %bitcast.10), calls=%async_computation | async-start | bytes 4259840 | tf_op jit(solution)/shard_map/all_to_all | solution.py:672
  19.1 24.9 %collective-permute-start = (f32[513,4,128]{2,1,0:T(4,128)}, f32[513,4,128]{2,1,0:T(4,128)S(1)}, u32[]{:S(2)}, u32[]{:S(2)}) collective-permute-start(f32[513,4,128]{2,1,0:T(4,128)} %get-tuple-element.34), channel_id=1, source_target_pairs={{0,16},{16,0},{1,17},{17,1},{2,18},{18,2},{3,19},{19,3},{4,20},{20... | collective-permute-start | bytes 3151880 | tf_op jit(solution)/shard_map/ppermute | solution.py:678
  20.3 2.2 %copy-start = (f32[1,16,128,512]{3,2,1,0:T(8,128)S(1)}, f32[1,16,128,512]{3,2,1,0:T(8,128)}, u32[]{:S(2)}) copy-start(f32[1,16,128,512]{3,2,1,0:T(8,128)} %state_ref.3) | copy-start | bytes 12582916
  24.5 31.3 %collective-permute-start.1 = (f32[40,512]{1,0:T(8,128)S(1)}, f32[40,512]{1,0:T(8,128)S(1)}, u32[]{:S(2)}, u32[]{:S(2)}) collective-permute-start(f32[40,512]{1,0:T(8,128)S(1)} %get-tuple-element.37.x_high), channel_id=1, source_target_pairs={{0,4},{4,8},{8,12},{1,5},{5,9},{9,13},{2,6},{6,10},{10,14},{3,7},{... | collective-permute-start | bytes 245768 | tf_op jit(solution)/shard_map/ppermute | solution.py:689
  27.8 28.0 %collective-permute-start.2 = (f32[40,512]{1,0:T(8,128)S(1)}, f32[40,512]{1,0:T(8,128)S(1)}, u32[]{:S(2)}, u32[]{:S(2)}) collective-permute-start(f32[40,512]{1,0:T(8,128)S(1)} %get-tuple-element.38.x_low), channel_id=1, source_target_pairs={{4,0},{8,4},{12,8},{5,1},{9,5},{13,9},{6,2},{10,6},{14,10},{7,3},{... | collective-permute-start | bytes 245768 | tf_op jit(solution)/shard_map/ppermute | solution.py:690
  29.1 18.9 %collective-permute-start.3 = (f32[40,128]{1,0:T(8,128)S(1)}, f32[40,128]{1,0:T(8,128)S(1)}, u32[]{:S(2)}, u32[]{:S(2)}) collective-permute-start(f32[40,128]{1,0:T(8,128)S(1)} %get-tuple-element.39.y_high), channel_id=1, source_target_pairs={{0,1},{1,2},{2,3},{4,5},{5,6},{6,7},{8,9},{9,10},{10,11},{12,13},{... | collective-permute-start | bytes 61448 | tf_op jit(solution)/shard_map/ppermute | solution.py:687
  33.0 15.0 %collective-permute-start.4 = (f32[40,128]{1,0:T(8,128)S(1)}, f32[40,128]{1,0:T(8,128)S(1)}, u32[]{:S(2)}, u32[]{:S(2)}) collective-permute-start(f32[40,128]{1,0:T(8,128)S(1)} %get-tuple-element.40.y_low), channel_id=1, source_target_pairs={{1,0},{2,1},{3,2},{5,4},{6,5},{7,6},{9,8},{10,9},{11,10},{13,12},{... | collective-permute-start | bytes 61448 | tf_op jit(solution)/shard_map/ppermute | solution.py:688
  61.3 55.0 %all-to-all-start.1 = ((f32[16,64,4,128]{3,2,1,0:T(4,128)}), f32[16,64,4,128]{3,2,1,0:T(4,128)}, u32[]{:S(2)}, u32[]{:S(2)}) async-start(f32[16,64,4,128]{3,2,1,0:T(4,128)} %bitcast.4), calls=%async_computation.1 | async-start | bytes 4194304 | tf_op jit(solution)/shard_map/all_to_all | solution.py:672
  74.9 12.3 %copy-start.7 = (f32[16,1,1,128]{3,2,1,0:T(1,128)S(1)}, f32[16,1,1,128]{3,2,1,0:T(1,128)}, u32[]{:S(2)}) copy-start(f32[16,1,1,128]{3,2,1,0:T(1,128)} %slice.20) | copy-start | bytes 24580
  74.9 12.6 %copy-start.6 = (f32[1,8]{1,0:T(1,128)S(1)}, f32[1,8]{1,0:T(1,128)}, u32[]{:S(2)}) copy-start(f32[1,8]{1,0:T(1,128)} %gamma_ref.3) | copy-start | bytes 100
  74.9 19.5 %copy-start.1 = (f32[1,16,128,512]{3,2,1,0:T(8,128)S(1)}, f32[1,16,128,512]{3,2,1,0:T(8,128)}, u32[]{:S(2)}) copy-start(f32[1,16,128,512]{3,2,1,0:T(8,128)} %state_ref.3) | copy-start | bytes 12582916
  80.1 32.1 %collective-permute-start.8 = (f32[4,128,512]{2,1,0:T(8,128)}, f32[4,128,512]{2,1,0:T(8,128)S(1)}, u32[]{:S(2)}, u32[]{:S(2)}) collective-permute-start(f32[4,128,512]{2,1,0:T(8,128)} %get-tuple-element.47), channel_id=1, source_target_pairs={{0,16},{16,0},{1,17},{17,1},{2,18},{18,2},{3,19},{19,3},{4,20},{20... | collective-permute-start | bytes 3145736 | tf_op jit(solution)/shard_map/ppermute | solution.py:709
  81.4 11.0 %collective-permute-start.5 = (f32[80,128]{1,0:T(8,128)S(1)}, f32[80,128]{1,0:T(8,128)S(1)}, u32[]{:S(2)}, u32[]{:S(2)}) collective-permute-start(f32[80,128]{1,0:T(8,128)S(1)} %pad_maximum_fusion), channel_id=1, source_target_pairs={{0,1},{1,2},{2,3},{4,5},{5,6},{6,7},{8,9},{9,10},{10,11},{12,13},{... | collective-permute-start | bytes 122888 | tf_op jit(solution)/shard_map/ppermute | solution.py:699
  85.3 9.1 %collective-permute-start.6 = (f32[80,128]{1,0:T(8,128)S(1)}, f32[80,128]{1,0:T(8,128)S(1)}, u32[]{:S(2)}, u32[]{:S(2)}) collective-permute-start(f32[80,128]{1,0:T(8,128)S(1)} %pad_maximum_fusion.1), channel_id=1, source_target_pairs={{1,0},{2,1},{3,2},{5,4},{6,5},{7,6},{9,8},{10,9},{11,10},{13,12},{... | collective-permute-start | bytes 122888 | tf_op jit(solution)/shard_map/ppermute | solution.py:700
  87.2 29.0 %collective-permute-start.7 = (f32[16,128]{1,0:T(8,128)S(1)}, f32[16,128]{1,0:T(8,128)S(1)}, u32[]{:S(2)}, u32[]{:S(2)}) collective-permute-start(f32[16,128]{1,0:T(8,128)S(1)} %bitcast.12), channel_id=1, source_target_pairs={{0,16},{16,0},{1,17},{17,1},{2,18},{18,2},{3,19},{19,3},{4,20},{20... | collective-permute-start | bytes 24584 | tf_op jit(solution)/shard_map/ppermute | solution.py:707
  87.5 23.4 %collective-permute-start.9 = (f32[4,128]{1,0:T(4,128)}, f32[4,128]{1,0:T(4,128)S(1)}, u32[]{:S(2)}, u32[]{:S(2)}) collective-permute-start(f32[4,128]{1,0:T(4,128)} %get-tuple-element.48), channel_id=1, source_target_pairs={{0,17},{1,18},{2,19},{16,1},{17,2},{18,3},{4,21},{5,22},{6,23},{20... | collective-permute-start | bytes 6152 | tf_op jit(solution)/shard_map/ppermute | solution.py:715
  92.4 19.8 %collective-permute-start.10 = (f32[4,128]{1,0:T(4,128)}, f32[4,128]{1,0:T(4,128)S(1)}, u32[]{:S(2)}, u32[]{:S(2)}) collective-permute-start(f32[4,128]{1,0:T(4,128)} %get-tuple-element.49), channel_id=1, source_target_pairs={{1,16},{2,17},{3,18},{17,0},{18,1},{19,2},{5,20},{6,21},{7,22},{21... | collective-permute-start | bytes 6152 | tf_op jit(solution)/shard_map/ppermute | solution.py:716
  94.4 13.3 %copy-start.9 = (f32[4,512]{1,0:T(4,128)S(1)}, f32[4,512]{1,0:T(4,128)}, u32[]{:S(2)}) copy-start(f32[4,512]{1,0:T(4,128)} %get-tuple-element.58) | copy-start | bytes 24580
  94.4 16.5 %copy-start.8 = (f32[4,512]{1,0:T(4,128)S(1)}, f32[4,512]{1,0:T(4,128)}, u32[]{:S(2)}) copy-start(f32[4,512]{1,0:T(4,128)} %get-tuple-element.59) | copy-start | bytes 24580
  106.7 1.0 copy-start.4
  107.7 24.5 %collective-permute-start.15 = (f32[4,512]{1,0:T(4,128)S(1)}, f32[4,512]{1,0:T(4,128)S(1)}, u32[]{:S(2)}, u32[]{:S(2)}) collective-permute-start(f32[4,512]{1,0:T(4,128)S(1)} %copy-done.9), channel_id=1, source_target_pairs={{0,20},{4,24},{8,28},{16,4},{20,8},{24,12},{1,21},{5,25},{9,29},{1... | collective-permute-start | bytes 24584 | tf_op jit(solution)/shard_map/ppermute | solution.py:711
  110.9 23.2 %collective-permute-start.16 = (f32[4,512]{1,0:T(4,128)S(1)}, f32[4,512]{1,0:T(4,128)S(1)}, u32[]{:S(2)}, u32[]{:S(2)}) collective-permute-start(f32[4,512]{1,0:T(4,128)S(1)} %copy-done.8), channel_id=1, source_target_pairs={{4,16},{8,20},{12,24},{20,0},{24,4},{28,8},{5,17},{9,21},{13,25},{... | collective-permute-start | bytes 24584 | tf_op jit(solution)/shard_map/ppermute | solution.py:712
  116.2 20.9 %copy-start.5 = (f32[4,128,512]{2,1,0:T(8,128)S(1)}, f32[4,128,512]{2,1,0:T(8,128)}, u32[]{:S(2)}) copy-start(f32[4,128,512]{2,1,0:T(8,128)} %copy-done.4) | copy-start | bytes 3145732
  119.4 17.8 %collective-permute-start.13 = (f32[4,512]{1,0:T(4,128)S(1)}, f32[4,512]{1,0:T(4,128)S(1)}, u32[]{:S(2)}, u32[]{:S(2)}) collective-permute-start(f32[4,512]{1,0:T(4,128)S(1)} %get-tuple-element.56), channel_id=1, source_target_pairs={{0,4},{4,8},{8,12},{1,5},{5,9},{9,13},{2,6},{6,10},{10,14},{3,7},{... | collective-permute-start | bytes 24584 | tf_op jit(solution)/shard_map/ppermute | solution.py:729
  126.0 11.2 %collective-permute-start.14 = (f32[4,512]{1,0:T(4,128)S(1)}, f32[4,512]{1,0:T(4,128)S(1)}, u32[]{:S(2)}, u32[]{:S(2)}) collective-permute-start(f32[4,512]{1,0:T(4,128)S(1)} %get-tuple-element.57), channel_id=1, source_target_pairs={{4,0},{8,4},{12,8},{5,1},{9,5},{13,9},{6,2},{10,6},{14,10},{7,3},{... | collective-permute-start | bytes 24584 | tf_op jit(solution)/shard_map/ppermute | solution.py:730
  127.3 6.9 %collective-permute-start.11 = (f32[4,128]{1,0:T(4,128)S(1)}, f32[4,128]{1,0:T(4,128)S(1)}, u32[]{:S(2)}, u32[]{:S(2)}) collective-permute-start(f32[4,128]{1,0:T(4,128)S(1)} %get-tuple-element.54), channel_id=1, source_target_pairs={{0,1},{1,2},{2,3},{4,5},{5,6},{6,7},{8,9},{9,10},{10,11},{12,13},{... | collective-permute-start | bytes 6152 | tf_op jit(solution)/shard_map/ppermute | solution.py:725
  132.2 4.9 %collective-permute-start.12 = (f32[4,128]{1,0:T(4,128)S(1)}, f32[4,128]{1,0:T(4,128)S(1)}, u32[]{:S(2)}, u32[]{:S(2)}) collective-permute-start(f32[4,128]{1,0:T(4,128)S(1)} %get-tuple-element.55), channel_id=1, source_target_pairs={{1,0},{2,1},{3,2},{5,4},{6,5},{7,6},{9,8},{10,9},{11,10},{13,12},{... | collective-permute-start | bytes 6152 | tf_op jit(solution)/shard_map/ppermute | solution.py:726

commit v9 on v7

--- a/solution.py
+++ b/solution.py
@@ -15,6 +15,11 @@
 
 def shift_pairs(count, by):
     return [(i, i + by) for i in range(count) if 0 <= i + by < count]
+
+
+def neighbour_pairs(count, first):
+    lows = range(first, count - 1, 2)
+    return [(i, i + 1) for i in lows] + [(i + 1, i) for i in lows]
 
 
 def crossed(axis, by):
@@ -60,8 +65,8 @@
 
 
 def contribution_kernel(
-    dims, src_ref, dev_ref, blk_ref, state_ref, weights_ref, early_ref, late_ref,
-    cells, w_ref, pair_v, pair_s, taken, field_sems, weight_sems, pair_sems,
+    dims, src_ref, dev_ref, blk_ref, state_ref, weights_ref, early_out, late_ref,
+    cells, w_ref, early_ref, pair_v, pair_s, taken, field_sems, weight_sems, early_sems, pair_sems,
 ):
     tiles, capacity, pairs, fields, cells_x, cells_y, width = dims
     half = fields // 2
@@ -92,6 +97,13 @@
             weights_ref.at[0, some], w_ref.at[some], weight_sems.at[step]
         )
 
+    def early_copy(step):
+        first, count = step * STEP_PAIRS, STEP_PAIRS
+        if isinstance(step, int) and step == steps:
+            count = early_ref.shape[0] - pairs
+        some = pl.ds(first, count)
+        return pltpu.make_async_copy(early_ref.at[some], early_out.at[some], early_sems.at[step])
+
     for copy in scalar_copies + vector_copies + field_copies:
         copy.start()
     for step in range(steps):
@@ -111,6 +123,7 @@
     for i in range(pairs // width):
         place = (pairs + i // half, slice(i % half, i % half + 1), slice(None))
         early_ref[place] = code[:, i * width : (i + 1) * width]
+    early_copy(steps).start()
     for copy in scalar_copies + field_copies:
         copy.wait()
 
@@ -141,9 +154,12 @@
                 one = four[j * fields : (j + 1) * fields, at : at + width]
                 early_ref[p + j] = one[:half]
                 late_ref[slot] = one[half:]
+        early_copy(step).start()
         return carry
 
     lax.fori_loop(0, steps, some_pairs, 0)
+    for step in range(steps + 1):
+        early_copy(step).wait()
 
 
 def contributions(state, pair_src, pair_dev, pair_blk, weights, tiles, capacity, fields):
@@ -157,16 +173,21 @@
     return pl.pallas_call(
         functools.partial(contribution_kernel, dims),
         in_specs=[pl.BlockSpec(memory_space=pltpu.HBM)] * 5,
-        out_specs=[pl.BlockSpec(memory_space=pltpu.VMEM) for _ in shapes],
+        out_specs=[
+            pl.BlockSpec(memory_space=pl.ANY),
+            pl.BlockSpec(memory_space=pltpu.VMEM),
+        ],
         out_shape=[jax.ShapeDtypeStruct(shape, jnp.float32) for shape in shapes],
         scratch_shapes=[
             pltpu.VMEM((parts, cells_x, fields, width), jnp.float32),
             pltpu.VMEM((pairs, width, width), jnp.bfloat16),
+            pltpu.VMEM(shapes[0], jnp.float32),
             pltpu.VMEM((2, 1, pairs), jnp.int32),
             pltpu.SMEM((2, pairs), jnp.int32),
             pltpu.SMEM((tiles,), jnp.int32),
             pltpu.SemaphoreType.DMA((parts * fields,)),
             pltpu.SemaphoreType.DMA((pairs // STEP_PAIRS,)),
+            pltpu.SemaphoreType.DMA((pairs // STEP_PAIRS + 1,)),
             pltpu.SemaphoreType.DMA((4,)),
         ],
         compiler_params=pltpu.CompilerParams(vmem_limit_bytes=56 * 1024 * 1024),
@@ -221,7 +242,7 @@
     )(rows)
 
 
-def sum_kernel(dims, ids_ref, rows_ref, out_ref, top_ref, bottom_ref, left_ref, right_ref,
+def sum_kernel(dims, odd_ref, ids_ref, rows_ref, out_ref, x0_ref, x1_ref, y0_ref, y1_ref,
                in_ref, pick, high, low, row_sems):
     tiles, capacity, fields, cells_x, cells_y, width = dims
     parts = cells_y // width
@@ -239,13 +260,14 @@
     block_of = block_of.astype(jnp.float32)
     lane = lax.broadcasted_iota(jnp.int32, (1, LANES), 1)
     for k in range(tiles // group):
-        columns = pl.ds(k * LANES, LANES)
-        rows_copy(k).wait()
         ids = None
         for i in range(group):
-            source = k * group + i
-            row = ids_ref[pl.ds(source, 1), :]
+            row = ids_ref[pl.ds(k * group + i, 1), :]
             ids = row if ids is None else jnp.where(lane // capacity == i, row, ids)
+        pick[:, pl.ds(k * LANES, LANES)] = (block_of == ids).astype(jnp.bfloat16)
+    for k in range(tiles // group):
+        rows_copy(k).wait()
+        for source in range(k * group, (k + 1) * group):
             for f in range(fields):
                 x = in_ref[pl.ds(source * stride + f, capacity, stride=fields), :]
                 rounded = x.astype(jnp.bfloat16)
@@ -255,7 +277,8 @@
                 )
                 high[place] = rounded
                 low[place] = (x - rounded.astype(jnp.float32)).astype(jnp.bfloat16)
-        pick[:, columns] = (block_of == ids).astype(jnp.bfloat16)
+    odd_x, odd_y = odd_ref[0, 0] == 1, odd_ref[0, 1] == 1
+    columns = {}
     for q in range(parts):
         chosen = pick[pl.ds(q * cells_x, cells_x), :]
         total = jnp.dot(chosen, high[...], preferred_element_type=jnp.float32)
@@ -263,15 +286,18 @@
         for f in range(fields):
             tile = total[:, f * width : (f + 1) * width]
             out_ref[f, :, pl.ds(q * width, width)] = tile
-            top_ref[pl.ds(f, 1), pl.ds(q * width, width)] = tile[:1]
-            bottom_ref[pl.ds(f, 1), pl.ds(q * width, width)] = tile[cells_x - 1 :]
-            if q == 0:
-                left_ref[pl.ds(f, 1), :] = tile.T[:1]
-            if q == parts - 1:
-                right_ref[pl.ds(f, 1), :] = tile.T[width - 1 :]
-
-
-def summed(ids, rows, tiles, capacity, fields, cells_x, cells_y, width, grant):
+            top, bottom = tile[:1], tile[cells_x - 1 :]
+            x0_ref[pl.ds(f, 1), pl.ds(q * width, width)] = jnp.where(odd_x, bottom, top)
+            x1_ref[pl.ds(f, 1), pl.ds(q * width, width)] = jnp.where(odd_x, top, bottom)
+            if q in (0, parts - 1):
+                columns[q, f] = tile.T[:1] if q == 0 else tile.T[width - 1 :]
+    for f in range(fields):
+        left, right = columns[0, f], columns[parts - 1, f]
+        y0_ref[pl.ds(f, 1), :] = jnp.where(odd_y, right, left)
+        y1_ref[pl.ds(f, 1), :] = jnp.where(odd_y, left, right)
+
+
+def summed(odd, ids, rows, tiles, capacity, fields, cells_x, cells_y, width, grant):
     dims = (tiles, capacity, fields, cells_x, cells_y, width)
     rows = rows.reshape(-1, width)
     slots = tiles * capacity
@@ -285,7 +311,11 @@
     ]
     return pl.pallas_call(
         functools.partial(sum_kernel, dims),
-        in_specs=[pl.BlockSpec(memory_space=pltpu.VMEM), pl.BlockSpec(memory_space=pl.ANY)],
+        in_specs=[
+            pl.BlockSpec(memory_space=pltpu.SMEM),
+            pl.BlockSpec(memory_space=pltpu.VMEM),
+            pl.BlockSpec(memory_space=pl.ANY),
+        ],
         out_shape=[jax.ShapeDtypeStruct(shape, jnp.float32) for shape in shapes],
         scratch_shapes=[
             pltpu.VMEM(rows.shape, jnp.float32),
@@ -301,7 +331,7 @@
             transcendentals=0,
         ),
         name="sum_by_block",
-    )(ids, rows)
+    )(odd, ids, rows)
 
 
 def stencil_factors(coefs, keep):
@@ -519,7 +549,7 @@
                   left, right, *rest):
     tops, rest = (rest[:2], rest[2:]) if with_x else (None, rest)
     late, rest = (rest[:2], rest[2:]) if with_x else (None, rest)
-    early_base, rest = (rest[0], rest[1:]) if with_x else (None, rest)
+    early_base, odd_ref, rest = (*rest[:2], rest[2:]) if with_x else (None, None, rest)
     base_ref, rest = rest[0], rest[1:]
     new_ref, out_ref, done_ref = rest[-11:-8]
     base, wide, lines, sides, outer, base_sems, out_sems, outer_sems = rest[-8:]
@@ -552,12 +582,17 @@
         outer_copy(f, i, False).start()
     done_ref[...] = jnp.zeros_like(done_ref)
     if with_x:
-        lines[:count, :] = tops[0][...] * above[keep, :]
-        lines[count:, :] = tops[1][...] * below[keep, :]
+        for i, (pair, kept, low_keep, high_keep) in enumerate(
+            ((tops, lines, above, below), ((left, right), sides, before, after))
+        ):
+            odd = odd_ref[0, i] == 1
+            in_odd, in_even = pair[0][...], pair[1][...]
+            kept[:count, :] = jnp.where(odd, in_even, in_odd) * low_keep[keep, :]
+            kept[count:, :] = jnp.where(odd, in_odd, in_even) * high_keep[keep, :]
     else:
         lines[...] = jnp.zeros_like(lines)
-    sides[:count, :] = left[...] * before[keep, :]
-    sides[count:, :] = right[...] * after[keep, :]
+        sides[:count, :] = left[...] * before[keep, :]
+        sides[count:, :] = right[...] * after[keep, :]
     lane = lax.broadcasted_iota(jnp.int32, (STRIP, cells_y), 1)
 
     def one_field(f, carry):
@@ -616,10 +651,14 @@
     anywhere = pl.BlockSpec(memory_space=pl.ANY)
     operands = [gamma, mix, *received, factors, recv, *y_rims]
     if with_x:
-        late_rims, base_early, late_done = closing
+        late_rims, base_early, odd, late_done = closing
         operands += [*x_rims, *late_rims, base_early]
-    specs = [pl.BlockSpec(memory_space=pltpu.SMEM)] * 2
-    specs += [pl.BlockSpec(memory_space=pltpu.VMEM)] * (len(operands) - 2) + [anywhere]
+    scalars = pl.BlockSpec(memory_space=pltpu.SMEM)
+    specs = [scalars] * 2 + [pl.BlockSpec(memory_space=pltpu.VMEM)] * (len(operands) - 2)
+    if with_x:
+        operands.append(odd)
+        specs.append(scalars)
+    specs.append(anywhere)
     aliases = {len(operands): 0}
     operands.append(new_state)
     if remapped is not None:
@@ -671,8 +710,8 @@
         rows = rows.reshape(tiles, -1, half, width)
         return lax.all_to_all(rows, ("tx", "ty"), split_axis=0, concat_axis=0, tiled=True)
 
-    def add_up(ids, rows, grant):
-        return summed(ids, rows, tiles, capacity, half, cells_x, cells_y, width, grant)
+    def add_up(odd, ids, rows, grant):
+        return summed(odd, ids, rows, tiles, capacity, half, cells_x, cells_y, width, grant)
 
     late_in = exchanged(late)
     early = lax.ppermute(early, "comp", swap)
@@ -705,7 +744,7 @@
 
     ids_late = late_in[:, capacity, 0, :]
     ids_early = lax.ppermute(ids_late, "comp", swap)
-    recv_late, top, bottom, left, right = add_up(ids_late, late_in, 56)
+    recv_late, top, bottom, left, right = add_up(jnp.zeros((1, 2), jnp.int32), ids_late, late_in, 56)
     recv_late = lax.ppermute(recv_late, "comp", swap)
     late_x = (
         lax.ppermute(bottom, ("comp", "tx"), crossed("tx", 1)),
@@ -720,17 +759,18 @@
         half, base, None, recv_late, None, late_y, None, *rest
     )
     early_in, done = lax.optimization_barrier((early_in, done))
-    recv_early, top, bottom, left, right = add_up(ids_early, early_in, 16)
+    odd = jnp.stack([lax.axis_index("tx"), lax.axis_index("ty")]).astype(jnp.int32)[None] & 1
+    recv_early, x_odd, x_even, y_odd, y_even = add_up(odd, ids_early, early_in, 16)
     early_x = (
-        lax.ppermute(bottom, "tx", shift_pairs(tx, 1)),
-        lax.ppermute(top, "tx", shift_pairs(tx, -1)),
+        lax.ppermute(x_odd, "tx", neighbour_pairs(tx, 1)),
+        lax.ppermute(x_even, "tx", neighbour_pairs(tx, 0)),
     )
     early_y = (
-        lax.ppermute(right, "ty", shift_pairs(ty, 1)),
-        lax.ppermute(left, "ty", shift_pairs(ty, -1)),
+        lax.ppermute(y_odd, "ty", neighbour_pairs(ty, 1)),
+        lax.ppermute(y_even, "ty", neighbour_pairs(ty, 0)),
     )
     new_state, remapped, _ = finished(
-        0, new_state, remapped, recv_early, early_x, early_y, (late_x, base_early, done), *rest
+        0, new_state, remapped, recv_early, early_x, early_y, (late_x, base_early, odd, done), *rest
     )
     return new_state, remapped
 

time: 142 us -> 141 us (level)
  starting transfers between devices: 64.7 us -> 60.8 us
  local copies, waits for them, and re-layouts: 4.64 us -> 7.42 us
  Pallas kernels: 45.1 us -> 47.1 us
  waiting for transfers between devices: 25.2 us -> 23.4 us
    ppermute x4, starting transfers between devices: 14.7 us -> 10.8 us  [the longest x1 5.4 us: body(): lax.ppermute(x_even, 'tx', neighbour_pairs(tx, 0))]
    unnamed x22, local copies, waits for them, and re-layouts: 3.2 us -> 5.38 us
    ppermute x4, waiting for transfers between devices: 2.96 us -> 1.16 us  [the longest x1 1.15 us: body(): lax.ppermute(y_odd, 'ty', neighbour_pairs(ty, 1))]
  transfers between devices with their start and end apart: 19 -> 19, of which waited for: 4 -> 4; matrix products, arithmetic and copies ran while one was open for 1% -> 2% of each run, Pallas kernels for 22% -> 23%
where the time goes in v9:
time: 141 us; the launch traced here: 140 us
  starting transfers between devices  60.8 us (43%)
  Pallas kernels  47.1 us (33%)
  waiting for transfers between devices  23.4 us (17%)
  local copies, waits for them, and re-layouts  7.42 us (5%)
    all_to_all x2, starting transfers between devices, exchanged(): lax.all_to_all(rows, ('tx', 'ty'), split_axis=0, concat_axis=0, tiled=True)  19.8 us
    pallas_call x1, Pallas kernels, base_of(): pl.pallas_call(functools.partial(base_kernel, half), grid=(nfield,), in_s...  12.9 us
    pallas_call x1, Pallas kernels, contributions(): pl.pallas_call(functools.partial(contribution_kernel, dims), in_specs=[pl...  11.4 us
    ppermute x1, waiting for transfers between devices, body(): early = lax.ppermute(early, 'comp', swap)  9.06 us
    pallas_call x2, Pallas kernels, finished(): pl.pallas_call(functools.partial(finish_kernel, first, with_x), in_specs=...  8.59 us
    pallas_call x2, Pallas kernels, summed(): pl.pallas_call(functools.partial(sum_kernel, dims), in_specs=[pl.BlockSpe...  8.21 us
    ppermute x1, waiting for transfers between devices, body(): above = lax.ppermute(x_high, 'tx', shift_pairs(tx, 1))  7.72 us
    all_to_all x2, waiting for transfers between devices, exchanged(): lax.all_to_all(rows, ('tx', 'ty'), split_axis=0, concat_axis=0, tiled=True)  5.45 us
  transfers between devices with their start and end apart: 19, of which 4 were waited for; matrix products, arithmetic and copies ran while one was open for 2% of the time, Pallas kernels for 23%

profile of v9, /device:TPU:1, one launch (start us, length us, event | category | flops | bytes accessed | tf_op | source)
XLA Modules:
  0.0 139.8 jit_solution(5968693874999163799)
XLA Ops:
  0.6 11.4 %contributions.1 = (f32[513,4,128]{2,1,0:T(4,128)}, f32[1040,4,128]{2,1,0:T(4,128)}) custom-call(s32[1,512]{1,0:T(1,128)} %src_ref.1, s32[1,512]{1,0:T(1,128)} %bitcast.15, s32[1,512]{1,0:T(1,128)} %blk_ref.1, f32[1,16,128,512]{3,2,1,0:T(8,128)} %state_ref.3, bf16[1,512,128,128]{3,2,1,0:T(8,128)(2,1)} %weights_ref.1), custom_call_target="tpu_custom_call" | custom-call | flops 134217728 | bytes 25296896 | tf_op jit(solution)/shard_map/contributions/pallas_call | solution.py:173
  12.1 0.0 copy-start.10
  12.1 0.0 copy-start.2
  12.1 0.0 copy-start.3
  12.1 7.5 %all-to-all-start = ((f32[16,65,4,128]{3,2,1,0:T(4,128)}), f32[16,65,4,128]{3,2,1,0:T(4,128)}, u32[]{:S(2)}, u32[]{:S(2)}) async-start(f32[16,65,4,128]{3,2,1,0:T(4,128)} %bitcast.12), calls=%async_computation | async-start | bytes 4259840 | tf_op jit(solution)/shard_map/all_to_all | solution.py:711
  19.6 1.2 collective-permute-start
  20.8 0.0 copy-start
  20.8 2.2 %copy-done = f32[1,16,128,512]{3,2,1,0:T(8,128)S(1)} copy-done((f32[1,16,128,512]{3,2,1,0:T(8,128)S(1)}, f32[1,16,128,512]{3,2,1,0:T(8,128)}, u32[]{:S(2)}) %copy-start) | copy-done | bytes 4194328
  23.0 2.0 %edges.1 = (f32[40,512]{1,0:T(8,128)S(1)}, f32[40,512]{1,0:T(8,128)S(1)}, f32[40,128]{1,0:T(8,128)S(1)}, f32[40,128]{1,0:T(8,128)S(1)}) custom-call(f32[1,2]{1,0:T(1,128)S(1)} %broadcast_select_fusion.mix_ref, f32[1,16,128,512]{3,2,1,0:T(8,128)S(1)} %copy-done, f32[1,16,128,512]{3,2,1,0:T(8,128)S(1)} %copy-done, f32[1,16,128,512]{3,2,1,0:T(8,128)S(1)} %copy-done, ...), custom_call_target="tpu_custom_call" | custom-call | flops 1048576 | bytes 4194304 | tf_op jit(solution)/shard_map/edges/pallas_call | solution.py:431
  25.0 3.3 %collective-permute-start.1 = (f32[40,512]{1,0:T(8,128)S(1)}, f32[40,512]{1,0:T(8,128)S(1)}, u32[]{:S(2)}, u32[]{:S(2)}) collective-permute-start(f32[40,512]{1,0:T(8,128)S(1)} %get-tuple-element.37.x_high), channel_id=1, source_target_pairs={{0,4},{4,8},{8,12},{1,5},{5,9},{9,13},{2,6},{6,10},{10,14},{3,7},{... | collective-permute-start | bytes 245768 | tf_op jit(solution)/shard_map/ppermute | solution.py:728
  28.3 1.3 collective-permute-start.2
  29.6 3.9 %collective-permute-start.3 = (f32[40,128]{1,0:T(8,128)S(1)}, f32[40,128]{1,0:T(8,128)S(1)}, u32[]{:S(2)}, u32[]{:S(2)}) collective-permute-start(f32[40,128]{1,0:T(8,128)S(1)} %get-tuple-element.39.y_high), channel_id=1, source_target_pairs={{0,1},{1,2},{2,3},{4,5},{5,6},{6,7},{8,9},{9,10},{10,11},{12,13},{... | collective-permute-start | bytes 61448 | tf_op jit(solution)/shard_map/ppermute | solution.py:726
  33.5 1.9 %collective-permute-start.4 = (f32[40,128]{1,0:T(8,128)S(1)}, f32[40,128]{1,0:T(8,128)S(1)}, u32[]{:S(2)}, u32[]{:S(2)}) collective-permute-start(f32[40,128]{1,0:T(8,128)S(1)} %get-tuple-element.40.y_low), channel_id=1, source_target_pairs={{1,0},{2,1},{3,2},{5,4},{6,5},{7,6},{9,8},{10,9},{11,10},{13,12},{... | collective-permute-start | bytes 61448 | tf_op jit(solution)/shard_map/ppermute | solution.py:727
  35.4 9.1 %collective-permute-done.in_ref = f32[513,4,128]{2,1,0:T(4,128)S(1)} collective-permute-done((f32[513,4,128]{2,1,0:T(4,128)}, f32[513,4,128]{2,1,0:T(4,128)S(1)}, u32[]{:S(2)}, u32[]{:S(2)}) %collective-permute-start) | collective-permute-done | bytes 1050656 | tf_op jit(solution)/shard_map/ppermute | solution.py:717
  44.5 4.0 %place_in_slots.1 = f32[1024,4,128]{2,1,0:T(4,128)} custom-call(f32[513,4,128]{2,1,0:T(4,128)S(1)} %collective-permute-done.in_ref), custom_call_target="tpu_custom_call" | custom-call | flops 1050624 | bytes 3151872 | tf_op jit(solution)/shard_map/place_in_slots/pallas_call | solution.py:229
  48.5 0.0 collective-permute-done.3.left.before
  48.5 0.0 collective-permute-done.4.right.after
  48.6 7.7 %collective-permute-done.1.above = f32[40,512]{1,0:T(8,128)S(1)} collective-permute-done((f32[40,512]{1,0:T(8,128)S(1)}, f32[40,512]{1,0:T(8,128)S(1)}, u32[]{:S(2)}, u32[]{:S(2)}) %collective-permute-start.1) | collective-permute-done | bytes 81952 | tf_op jit(solution)/shard_map/ppermute | solution.py:728
  56.3 5.4 %all-to-all-done = f32[16,65,4,128]{3,2,1,0:T(4,128)} async-done(((f32[16,65,4,128]{3,2,1,0:T(4,128)}), f32[16,65,4,128]{3,2,1,0:T(4,128)}, u32[]{:S(2)}, u32[]{:S(2)}) %all-to-all-start) | async-done | bytes 2129952 | tf_op jit(solution)/shard_map/all_to_all | solution.py:711
  61.7 12.3 %all-to-all-start.1 = ((f32[16,64,4,128]{3,2,1,0:T(4,128)}), f32[16,64,4,128]{3,2,1,0:T(4,128)}, u32[]{:S(2)}, u32[]{:S(2)}) async-start(f32[16,64,4,128]{3,2,1,0:T(4,128)} %bitcast.6), calls=%async_computation.1 | async-start | bytes 4194304 | tf_op jit(solution)/shard_map/all_to_all | solution.py:711
  74.0 1.4 slice.20
  75.4 0.6 broadcast_5_odd_ref.2.odd_ref
  76.0 4.7 %sum_by_block.2 = (f32[4,128,512]{2,1,0:T(8,128)}, f32[4,512]{1,0:T(4,128)}, f32[4,512]{1,0:T(4,128)}, f32[4,128]{1,0:T(4,128)}, f32[4,128]{1,0:T(4,128)}) custom-call(s32[1,2]{1,0:T(1,128)} %broadcast_5_odd_ref.2.odd_ref, f32[16,128]{1,0:T(8,128)} %bitcast.13, f32[4160,128]{1,0:T(8,128)} %bitcast.7.rows_ref), custom_call_target="tpu_custom_call" | custom-call | flops 1073741824 | bytes 3145728 | tf_op jit(solution)/shard_map/sum_by_block/pallas_call | solution.py:312
  80.7 1.3 collective-permute-start.8
  82.0 3.8 %collective-permute-start.5 = (f32[80,128]{1,0:T(8,128)S(1)}, f32[80,128]{1,0:T(8,128)S(1)}, u32[]{:S(2)}, u32[]{:S(2)}) collective-permute-start(f32[80,128]{1,0:T(8,128)S(1)} %pad_maximum_fusion), channel_id=1, source_target_pairs={{0,1},{1,2},{2,3},{4,5},{5,6},{6,7},{8,9},{9,10},{10,11},{12,13},{... | collective-permute-start | bytes 122888 | tf_op jit(solution)/shard_map/ppermute | solution.py:738
  85.8 1.9 %collective-permute-start.6 = (f32[80,128]{1,0:T(8,128)S(1)}, f32[80,128]{1,0:T(8,128)S(1)}, u32[]{:S(2)}, u32[]{:S(2)}) collective-permute-start(f32[80,128]{1,0:T(8,128)S(1)} %pad_maximum_fusion.1), channel_id=1, source_target_pairs={{1,0},{2,1},{3,2},{5,4},{6,5},{7,6},{9,8},{10,9},{11,10},{13,12},{... | collective-permute-start | bytes 122888 | tf_op jit(solution)/shard_map/ppermute | solution.py:739
  87.7 0.3 collective-permute-start.7
  88.1 0.1 add_and_fusion.odd_ref.rest_5_
  88.1 4.8 %collective-permute-start.9 = (f32[4,128]{1,0:T(4,128)}, f32[4,128]{1,0:T(4,128)S(1)}, u32[]{:S(2)}, u32[]{:S(2)}) collective-permute-start(f32[4,128]{1,0:T(4,128)} %get-tuple-element.48), channel_id=1, source_target_pairs={{0,17},{1,18},{2,19},{16,1},{17,2},{18,3},{4,21},{5,22},{6,23},{20... | collective-permute-start | bytes 6152 | tf_op jit(solution)/shard_map/ppermute | solution.py:754
  93.0 0.0 collective-permute-done.5.corners_left
  93.0 1.9 %collective-permute-start.10 = (f32[4,128]{1,0:T(4,128)}, f32[4,128]{1,0:T(4,128)S(1)}, u32[]{:S(2)}, u32[]{:S(2)}) collective-permute-start(f32[4,128]{1,0:T(4,128)} %get-tuple-element.49), channel_id=1, source_target_pairs={{1,16},{2,17},{3,18},{17,0},{18,1},{19,2},{5,20},{6,21},{7,22},{21... | collective-permute-start | bytes 6152 | tf_op jit(solution)/shard_map/ppermute | solution.py:755
  94.9 0.0 collective-permute-done.6.corners_right
  95.0 0.1 broadcast_in_dim.9.rates_ref
  95.0 2.2 %copy-done.1 = f32[1,16,128,512]{3,2,1,0:T(8,128)S(1)} copy-done((f32[1,16,128,512]{3,2,1,0:T(8,128)S(1)}, f32[1,16,128,512]{3,2,1,0:T(8,128)}, u32[]{:S(2)}) %copy-start.1) | copy-done | bytes 4194328
  97.2 12.9 %base.1 = (f32[1,16,128,512]{3,2,1,0:T(8,128)}, f32[4,128,512]{2,1,0:T(8,128)S(1)}, f32[6,128,512]{2,1,0:T(8,128)S(1)}) custom-call(f32[1,16]{1,0:T(1,128)S(1)} %get-tuple-element.71.rate_ref, f32[1,2]{1,0:T(1,128)S(1)} %broadcast_select_fusion.mix_ref, f32[16,128]{1,0:T(8,128)S(1)} %broadcast_in_dim.9.rates_ref, f32[1,3,128,512]{3,2,1,0:T(8,128)S(1)} %copy-done.2, ...), custom_call_target="tpu_custom_call" | custom-call | flops 41943040 | bytes 8388608 | tf_op jit(solution)/shard_map/base/pallas_call | solution.py:517
  110.1 1.0 copy-done.4
  111.0 3.2 %collective-permute-start.15 = (f32[4,512]{1,0:T(4,128)S(1)}, f32[4,512]{1,0:T(4,128)S(1)}, u32[]{:S(2)}, u32[]{:S(2)}) collective-permute-start(f32[4,512]{1,0:T(4,128)S(1)} %copy-done.9), channel_id=1, source_target_pairs={{0,20},{4,24},{8,28},{16,4},{20,8},{24,12},{1,21},{5,25},{9,29},{1... | collective-permute-start | bytes 24584 | tf_op jit(solution)/shard_map/ppermute | solution.py:750
  114.2 0.0 collective-permute-done.9.left
  114.2 1.3 collective-permute-start.16
  115.6 0.0 collective-permute-done.8.recv
  115.6 4.8 %finish.2 = (f32[1,16,128,512]{3,2,1,0:T(8,128)}, f32[1,8,128,512]{3,2,1,0:T(8,128)}, f32[8,128]{1,0:T(8,128)S(1)}) custom-call(f32[1,8]{1,0:T(1,128)S(1)} %copy-done.6, f32[1,2]{1,0:T(1,128)S(1)} %broadcast_select_fusion.mix_ref, f32[40,512]{1,0:T(8,128)S(1)} %collective-permute-done.1.above, ...), custom_call_target="tpu_custom_call", output_to_operand_aliasing={{0}: (10, {})} | custom-call | flops 5242880 | bytes 5242880 | tf_op jit(solution)/shard_map/finish/pallas_call | solution.py:668
  120.4 3.5 %sum_by_block.3 = (f32[4,128,512]{2,1,0:T(8,128)S(1)}, f32[4,512]{1,0:T(4,128)S(1)}, f32[4,512]{1,0:T(4,128)S(1)}, f32[4,128]{1,0:T(4,128)S(1)}, f32[4,128]{1,0:T(4,128)S(1)}) custom-call(s32[1,2]{1,0:T(1,128)S(1)} %add_and_fusion.odd_ref.rest_5_, f32[16,128]{1,0:T(8,128)S(1)} %collective-permute-done.7.ids_ref, f32[4096,128]{1,0:T(8,128)} %bitcast.8.rows_ref), custom_call_target="tpu_custom_call" | custom-call | flops 1073741824 | bytes 3145728 | tf_op jit(solution)/shard_map/sum_by_block/pallas_call | solution.py:312
  123.9 0.7 collective-permute-start.13
  124.6 5.4 %collective-permute-start.14 = (f32[4,512]{1,0:T(4,128)S(1)}, f32[4,512]{1,0:T(4,128)S(1)}, u32[]{:S(2)}, u32[]{:S(2)}) collective-permute-start(f32[4,512]{1,0:T(4,128)S(1)} %get-tuple-element.57), channel_id=1, source_target_pairs={{0,4},{8,12},{4,0},{12,8},{1,5},{9,13},{5,1},{13,9},{2,6},{10,14},... | collective-permute-start | bytes 24584 | tf_op jit(solution)/shard_map/ppermute | solution.py:766
  130.0 4.7 %collective-permute-start.11 = (f32[4,128]{1,0:T(4,128)S(1)}, f32[4,128]{1,0:T(4,128)S(1)}, u32[]{:S(2)}, u32[]{:S(2)}) collective-permute-start(f32[4,128]{1,0:T(4,128)S(1)} %get-tuple-element.54), channel_id=1, source_target_pairs={{1,2},{2,1},{5,6},{6,5},{9,10},{10,9},{13,14},{14,13},{17,18},{18,... | collective-permute-start | bytes 6152 | tf_op jit(solution)/shard_map/ppermute | solution.py:769
  134.7 0.1 collective-permute-start.12
  134.8 1.2 collective-permute-done.11.left
  136.0 3.8 %finish.3 = (f32[1,16,128,512]{3,2,1,0:T(8,128)}, f32[1,8,128,512]{3,2,1,0:T(8,128)}, f32[8,128]{1,0:T(8,128)}) custom-call(f32[1,8]{1,0:T(1,128)S(1)} %copy-done.6, f32[1,2]{1,0:T(1,128)S(1)} %broadcast_select_fusion.mix_ref, f32[40,512]{1,0:T(8,128)S(1)} %collective-permute-done.1.above, ...), custom_call_target="tpu_custom_call", output_to_operand_aliasing={{0}: (16, {}), {1}: (17, {})} | custom-call | flops 5242880 | bytes 5242880 | tf_op jit(solution)/shard_map/finish/pallas_call | solution.py:668
  (29 shorter events, 0.1 us)
Async XLA Ops:
  12.1 8.7 %copy-start.10 = (f32[1,2]{1,0:T(1,128)S(1)}, f32[1,2]{1,0:T(1,128)}, u32[]{:S(2)}) copy-start(f32[1,2]{1,0:T(1,128)} %constant.24.clone) | copy-start | bytes 28
  12.1 8.7 %copy-start.2 = (f32[1,3,128,512]{3,2,1,0:T(8,128)S(1)}, f32[1,3,128,512]{3,2,1,0:T(8,128)}, u32[]{:S(2)}) copy-start(f32[1,3,128,512]{3,2,1,0:T(8,128)} %coefs_ref.1) | copy-start | bytes 2359300
  12.1 8.7 %copy-start.3 = (s32[128,512]{1,0:T(8,128)S(1)}, s32[128,512]{1,0:T(8,128)}, u32[]{:S(2)}) copy-start(s32[128,512]{1,0:T(8,128)} %land_ref) | copy-start | bytes 786436
  12.1 49.6 %all-to-all-start = ((f32[16,65,4,128]{3,2,1,0:T(4,128)}), f32[16,65,4,128]{3,2,1,0:T(4,128)}, u32[]{:S(2)}, u32[]{:S(2)}) async-start(f32[16,65,4,128]{3,2,1,0:T(4,128)} %bitcast.12), calls=%async_computation | async-start | bytes 4259840 | tf_op jit(solution)/shard_map/all_to_all | solution.py:711
  19.6 24.9 %collective-permute-start = (f32[513,4,128]{2,1,0:T(4,128)}, f32[513,4,128]{2,1,0:T(4,128)S(1)}, u32[]{:S(2)}, u32[]{:S(2)}) collective-permute-start(f32[513,4,128]{2,1,0:T(4,128)} %get-tuple-element.34), channel_id=1, source_target_pairs={{0,16},{16,0},{1,17},{17,1},{2,18},{18,2},{3,19},{19,3},{4,20},{20... | collective-permute-start | bytes 3151880 | tf_op jit(solution)/shard_map/ppermute | solution.py:717
  20.8 2.2 %copy-start = (f32[1,16,128,512]{3,2,1,0:T(8,128)S(1)}, f32[1,16,128,512]{3,2,1,0:T(8,128)}, u32[]{:S(2)}) copy-start(f32[1,16,128,512]{3,2,1,0:T(8,128)} %state_ref.3) | copy-start | bytes 12582916
  25.0 31.3 %collective-permute-start.1 = (f32[40,512]{1,0:T(8,128)S(1)}, f32[40,512]{1,0:T(8,128)S(1)}, u32[]{:S(2)}, u32[]{:S(2)}) collective-permute-start(f32[40,512]{1,0:T(8,128)S(1)} %get-tuple-element.37.x_high), channel_id=1, source_target_pairs={{0,4},{4,8},{8,12},{1,5},{5,9},{9,13},{2,6},{6,10},{10,14},{3,7},{... | collective-permute-start | bytes 245768 | tf_op jit(solution)/shard_map/ppermute | solution.py:728
  28.3 28.0 %collective-permute-start.2 = (f32[40,512]{1,0:T(8,128)S(1)}, f32[40,512]{1,0:T(8,128)S(1)}, u32[]{:S(2)}, u32[]{:S(2)}) collective-permute-start(f32[40,512]{1,0:T(8,128)S(1)} %get-tuple-element.38.x_low), channel_id=1, source_target_pairs={{4,0},{8,4},{12,8},{5,1},{9,5},{13,9},{6,2},{10,6},{14,10},{7,3},{... | collective-permute-start | bytes 245768 | tf_op jit(solution)/shard_map/ppermute | solution.py:729
  29.6 18.9 %collective-permute-start.3 = (f32[40,128]{1,0:T(8,128)S(1)}, f32[40,128]{1,0:T(8,128)S(1)}, u32[]{:S(2)}, u32[]{:S(2)}) collective-permute-start(f32[40,128]{1,0:T(8,128)S(1)} %get-tuple-element.39.y_high), channel_id=1, source_target_pairs={{0,1},{1,2},{2,3},{4,5},{5,6},{6,7},{8,9},{9,10},{10,11},{12,13},{... | collective-permute-start | bytes 61448 | tf_op jit(solution)/shard_map/ppermute | solution.py:726
  33.5 15.0 %collective-permute-start.4 = (f32[40,128]{1,0:T(8,128)S(1)}, f32[40,128]{1,0:T(8,128)S(1)}, u32[]{:S(2)}, u32[]{:S(2)}) collective-permute-start(f32[40,128]{1,0:T(8,128)S(1)} %get-tuple-element.40.y_low), channel_id=1, source_target_pairs={{1,0},{2,1},{3,2},{5,4},{6,5},{7,6},{9,8},{10,9},{11,10},{13,12},{... | collective-permute-start | bytes 61448 | tf_op jit(solution)/shard_map/ppermute | solution.py:727
  61.7 58.6 %all-to-all-start.1 = ((f32[16,64,4,128]{3,2,1,0:T(4,128)}), f32[16,64,4,128]{3,2,1,0:T(4,128)}, u32[]{:S(2)}, u32[]{:S(2)}) async-start(f32[16,64,4,128]{3,2,1,0:T(4,128)} %bitcast.6), calls=%async_computation.1 | async-start | bytes 4194304 | tf_op jit(solution)/shard_map/all_to_all | solution.py:711
  74.0 7.9 %copy-start.6 = (f32[1,8]{1,0:T(1,128)S(1)}, f32[1,8]{1,0:T(1,128)}, u32[]{:S(2)}) copy-start(f32[1,8]{1,0:T(1,128)} %gamma_ref.3) | copy-start | bytes 100
  76.0 11.8 %copy-start.7 = (f32[16,1,1,128]{3,2,1,0:T(1,128)S(1)}, f32[16,1,1,128]{3,2,1,0:T(1,128)}, u32[]{:S(2)}) copy-start(f32[16,1,1,128]{3,2,1,0:T(1,128)} %slice.20) | copy-start | bytes 24580
  80.7 34.9 %collective-permute-start.8 = (f32[4,128,512]{2,1,0:T(8,128)}, f32[4,128,512]{2,1,0:T(8,128)}, u32[]{:S(2)}, u32[]{:S(2)}) collective-permute-start(f32[4,128,512]{2,1,0:T(8,128)} %get-tuple-element.47), channel_id=1, source_target_pairs={{0,16},{16,0},{1,17},{17,1},{2,18},{18,2},{3,19},{19,3},{4,20},{20... | collective-permute-start | bytes 3145736 | tf_op jit(solution)/shard_map/ppermute | solution.py:748
  82.0 11.0 %collective-permute-start.5 = (f32[80,128]{1,0:T(8,128)S(1)}, f32[80,128]{1,0:T(8,128)S(1)}, u32[]{:S(2)}, u32[]{:S(2)}) collective-permute-start(f32[80,128]{1,0:T(8,128)S(1)} %pad_maximum_fusion), channel_id=1, source_target_pairs={{0,1},{1,2},{2,3},{4,5},{5,6},{6,7},{8,9},{9,10},{10,11},{12,13},{... | collective-permute-start | bytes 122888 | tf_op jit(solution)/shard_map/ppermute | solution.py:738
  85.8 9.1 %collective-permute-start.6 = (f32[80,128]{1,0:T(8,128)S(1)}, f32[80,128]{1,0:T(8,128)S(1)}, u32[]{:S(2)}, u32[]{:S(2)}) collective-permute-start(f32[80,128]{1,0:T(8,128)S(1)} %pad_maximum_fusion.1), channel_id=1, source_target_pairs={{1,0},{2,1},{3,2},{5,4},{6,5},{7,6},{9,8},{10,9},{11,10},{13,12},{... | collective-permute-start | bytes 122888 | tf_op jit(solution)/shard_map/ppermute | solution.py:739
  87.7 32.6 %collective-permute-start.7 = (f32[16,128]{1,0:T(8,128)S(1)}, f32[16,128]{1,0:T(8,128)S(1)}, u32[]{:S(2)}, u32[]{:S(2)}) collective-permute-start(f32[16,128]{1,0:T(8,128)S(1)} %bitcast.14), channel_id=1, source_target_pairs={{0,16},{16,0},{1,17},{17,1},{2,18},{18,2},{3,19},{19,3},{4,20},{20... | collective-permute-start | bytes 24584 | tf_op jit(solution)/shard_map/ppermute | solution.py:746
  88.1 26.1 %collective-permute-start.9 = (f32[4,128]{1,0:T(4,128)}, f32[4,128]{1,0:T(4,128)S(1)}, u32[]{:S(2)}, u32[]{:S(2)}) collective-permute-start(f32[4,128]{1,0:T(4,128)} %get-tuple-element.48), channel_id=1, source_target_pairs={{0,17},{1,18},{2,19},{16,1},{17,2},{18,3},{4,21},{5,22},{6,23},{20... | collective-permute-start | bytes 6152 | tf_op jit(solution)/shard_map/ppermute | solution.py:754
  93.0 22.5 %collective-permute-start.10 = (f32[4,128]{1,0:T(4,128)}, f32[4,128]{1,0:T(4,128)S(1)}, u32[]{:S(2)}, u32[]{:S(2)}) collective-permute-start(f32[4,128]{1,0:T(4,128)} %get-tuple-element.49), channel_id=1, source_target_pairs={{1,16},{2,17},{3,18},{17,0},{18,1},{19,2},{5,20},{6,21},{7,22},{21... | collective-permute-start | bytes 6152 | tf_op jit(solution)/shard_map/ppermute | solution.py:755
  95.0 2.2 %copy-start.1 = (f32[1,16,128,512]{3,2,1,0:T(8,128)S(1)}, f32[1,16,128,512]{3,2,1,0:T(8,128)}, u32[]{:S(2)}) copy-start(f32[1,16,128,512]{3,2,1,0:T(8,128)} %state_ref.3) | copy-start | bytes 12582916
  97.2 13.8 %copy-start.9 = (f32[4,512]{1,0:T(4,128)S(1)}, f32[4,512]{1,0:T(4,128)}, u32[]{:S(2)}) copy-start(f32[4,512]{1,0:T(4,128)} %get-tuple-element.58) | copy-start | bytes 24580
  97.2 17.0 %copy-start.8 = (f32[4,512]{1,0:T(4,128)S(1)}, f32[4,512]{1,0:T(4,128)}, u32[]{:S(2)}) copy-start(f32[4,512]{1,0:T(4,128)} %get-tuple-element.59) | copy-start | bytes 24580
  110.1 1.0 copy-start.4
  111.0 23.7 %collective-permute-start.15 = (f32[4,512]{1,0:T(4,128)S(1)}, f32[4,512]{1,0:T(4,128)S(1)}, u32[]{:S(2)}, u32[]{:S(2)}) collective-permute-start(f32[4,512]{1,0:T(4,128)S(1)} %copy-done.9), channel_id=1, source_target_pairs={{0,20},{4,24},{8,28},{16,4},{20,8},{24,12},{1,21},{5,25},{9,29},{1... | collective-permute-start | bytes 24584 | tf_op jit(solution)/shard_map/ppermute | solution.py:750
  114.2 20.6 %collective-permute-start.16 = (f32[4,512]{1,0:T(4,128)S(1)}, f32[4,512]{1,0:T(4,128)S(1)}, u32[]{:S(2)}, u32[]{:S(2)}) collective-permute-start(f32[4,512]{1,0:T(4,128)S(1)} %copy-done.8), channel_id=1, source_target_pairs={{4,16},{8,20},{12,24},{20,0},{24,4},{28,8},{5,17},{9,21},{13,25},{... | collective-permute-start | bytes 24584 | tf_op jit(solution)/shard_map/ppermute | solution.py:751
  120.4 15.6 %copy-start.5 = (f32[4,128,512]{2,1,0:T(8,128)S(1)}, f32[4,128,512]{2,1,0:T(8,128)}, u32[]{:S(2)}) copy-start(f32[4,128,512]{2,1,0:T(8,128)} %copy-done.4) | copy-start | bytes 3145732
  123.9 12.0 %collective-permute-start.13 = (f32[4,512]{1,0:T(4,128)S(1)}, f32[4,512]{1,0:T(4,128)S(1)}, u32[]{:S(2)}, u32[]{:S(2)}) collective-permute-start(f32[4,512]{1,0:T(4,128)S(1)} %get-tuple-element.56), channel_id=1, source_target_pairs={{4,8},{8,4},{5,9},{9,5},{6,10},{10,6},{7,11},{11,7},{20,24},{24,20... | collective-permute-start | bytes 24584 | tf_op jit(solution)/shard_map/ppermute | solution.py:765
  124.6 11.4 %collective-permute-start.14 = (f32[4,512]{1,0:T(4,128)S(1)}, f32[4,512]{1,0:T(4,128)S(1)}, u32[]{:S(2)}, u32[]{:S(2)}) collective-permute-start(f32[4,512]{1,0:T(4,128)S(1)} %get-tuple-element.57), channel_id=1, source_target_pairs={{0,4},{8,12},{4,0},{12,8},{1,5},{9,13},{5,1},{13,9},{2,6},{10,14},... | collective-permute-start | bytes 24584 | tf_op jit(solution)/shard_map/ppermute | solution.py:766
  130.0 6.0 %collective-permute-start.11 = (f32[4,128]{1,0:T(4,128)S(1)}, f32[4,128]{1,0:T(4,128)S(1)}, u32[]{:S(2)}, u32[]{:S(2)}) collective-permute-start(f32[4,128]{1,0:T(4,128)S(1)} %get-tuple-element.54), channel_id=1, source_target_pairs={{1,2},{2,1},{5,6},{6,5},{9,10},{10,9},{13,14},{14,13},{17,18},{18,... | collective-permute-start | bytes 6152 | tf_op jit(solution)/shard_map/ppermute | solution.py:769
  134.7 1.2 collective-permute-start.12

commit v10 on v9

--- a/solution.py
+++ b/solution.py
@@ -65,8 +65,8 @@
 
 
 def contribution_kernel(
-    dims, src_ref, dev_ref, blk_ref, state_ref, weights_ref, early_out, late_ref,
-    cells, w_ref, early_ref, pair_v, pair_s, taken, field_sems, weight_sems, early_sems, pair_sems,
+    dims, src_ref, dev_ref, blk_ref, state_ref, weights_ref, early_ref, late_ref,
+    cells, w_ref, pair_v, pair_s, taken, field_sems, weight_sems, pair_sems,
 ):
     tiles, capacity, pairs, fields, cells_x, cells_y, width = dims
     half = fields // 2
@@ -97,13 +97,6 @@
             weights_ref.at[0, some], w_ref.at[some], weight_sems.at[step]
         )
 
-    def early_copy(step):
-        first, count = step * STEP_PAIRS, STEP_PAIRS
-        if isinstance(step, int) and step == steps:
-            count = early_ref.shape[0] - pairs
-        some = pl.ds(first, count)
-        return pltpu.make_async_copy(early_ref.at[some], early_out.at[some], early_sems.at[step])
-
     for copy in scalar_copies + vector_copies + field_copies:
         copy.start()
     for step in range(steps):
@@ -123,7 +116,6 @@
     for i in range(pairs // width):
         place = (pairs + i // half, slice(i % half, i % half + 1), slice(None))
         early_ref[place] = code[:, i * width : (i + 1) * width]
-    early_copy(steps).start()
     for copy in scalar_copies + field_copies:
         copy.wait()
 
@@ -154,12 +146,9 @@
                 one = four[j * fields : (j + 1) * fields, at : at + width]
                 early_ref[p + j] = one[:half]
                 late_ref[slot] = one[half:]
-        early_copy(step).start()
         return carry
 
     lax.fori_loop(0, steps, some_pairs, 0)
-    for step in range(steps + 1):
-        early_copy(step).wait()
 
 
 def contributions(state, pair_src, pair_dev, pair_blk, weights, tiles, capacity, fields):
@@ -173,21 +162,16 @@
     return pl.pallas_call(
         functools.partial(contribution_kernel, dims),
         in_specs=[pl.BlockSpec(memory_space=pltpu.HBM)] * 5,
-        out_specs=[
-            pl.BlockSpec(memory_space=pl.ANY),
-            pl.BlockSpec(memory_space=pltpu.VMEM),
-        ],
+        out_specs=[pl.BlockSpec(memory_space=pltpu.VMEM) for _ in shapes],
         out_shape=[jax.ShapeDtypeStruct(shape, jnp.float32) for shape in shapes],
         scratch_shapes=[
             pltpu.VMEM((parts, cells_x, fields, width), jnp.float32),
             pltpu.VMEM((pairs, width, width), jnp.bfloat16),
-            pltpu.VMEM(shapes[0], jnp.float32),
             pltpu.VMEM((2, 1, pairs), jnp.int32),
             pltpu.SMEM((2, pairs), jnp.int32),
             pltpu.SMEM((tiles,), jnp.int32),
             pltpu.SemaphoreType.DMA((parts * fields,)),
             pltpu.SemaphoreType.DMA((pairs // STEP_PAIRS,)),
-            pltpu.SemaphoreType.DMA((pairs // STEP_PAIRS + 1,)),
             pltpu.SemaphoreType.DMA((4,)),
         ],
         compiler_params=pltpu.CompilerParams(vmem_limit_bytes=56 * 1024 * 1024),
@@ -242,8 +226,10 @@
     )(rows)
 
 
-def sum_kernel(dims, odd_ref, ids_ref, rows_ref, out_ref, x0_ref, x1_ref, y0_ref, y1_ref,
-               in_ref, pick, high, low, row_sems):
+def sum_kernel(dims, paired, *refs):
+    odd_ref, refs = (refs[0], refs[1:]) if paired else (None, refs)
+    ids_ref, rows_ref, out_ref, x0_ref, x1_ref, y0_ref, y1_ref = refs[:7]
+    in_ref, pick, high, low, row_sems = refs[7:]
     tiles, capacity, fields, cells_x, cells_y, width = dims
     parts = cells_y // width
     group = LANES // capacity
@@ -260,14 +246,12 @@
     block_of = block_of.astype(jnp.float32)
     lane = lax.broadcasted_iota(jnp.int32, (1, LANES), 1)
     for k in range(tiles // group):
+        rows_copy(k).wait()
         ids = None
         for i in range(group):
-            row = ids_ref[pl.ds(k * group + i, 1), :]
+            source = k * group + i
+            row = ids_ref[pl.ds(source, 1), :]
             ids = row if ids is None else jnp.where(lane // capacity == i, row, ids)
-        pick[:, pl.ds(k * LANES, LANES)] = (block_of == ids).astype(jnp.bfloat16)
-    for k in range(tiles // group):
-        rows_copy(k).wait()
-        for source in range(k * group, (k + 1) * group):
             for f in range(fields):
                 x = in_ref[pl.ds(source * stride + f, capacity, stride=fields), :]
                 rounded = x.astype(jnp.bfloat16)
@@ -277,7 +261,14 @@
                 )
                 high[place] = rounded
                 low[place] = (x - rounded.astype(jnp.float32)).astype(jnp.bfloat16)
-    odd_x, odd_y = odd_ref[0, 0] == 1, odd_ref[0, 1] == 1
+        pick[:, pl.ds(k * LANES, LANES)] = (block_of == ids).astype(jnp.bfloat16)
+
+    def in_order(i, low_rim, high_rim):
+        if not paired:
+            return low_rim, high_rim
+        odd = odd_ref[0, i] == 1
+        return jnp.where(odd, high_rim, low_rim), jnp.where(odd, low_rim, high_rim)
+
     columns = {}
     for q in range(parts):
         chosen = pick[pl.ds(q * cells_x, cells_x), :]
@@ -286,20 +277,20 @@
         for f in range(fields):
             tile = total[:, f * width : (f + 1) * width]
             out_ref[f, :, pl.ds(q * width, width)] = tile
-            top, bottom = tile[:1], tile[cells_x - 1 :]
-            x0_ref[pl.ds(f, 1), pl.ds(q * width, width)] = jnp.where(odd_x, bottom, top)
-            x1_ref[pl.ds(f, 1), pl.ds(q * width, width)] = jnp.where(odd_x, top, bottom)
+            rims = in_order(0, tile[:1], tile[cells_x - 1 :])
+            for rim_ref, rim in zip((x0_ref, x1_ref), rims):
+                rim_ref[pl.ds(f, 1), pl.ds(q * width, width)] = rim
             if q in (0, parts - 1):
                 columns[q, f] = tile.T[:1] if q == 0 else tile.T[width - 1 :]
     for f in range(fields):
-        left, right = columns[0, f], columns[parts - 1, f]
-        y0_ref[pl.ds(f, 1), :] = jnp.where(odd_y, right, left)
-        y1_ref[pl.ds(f, 1), :] = jnp.where(odd_y, left, right)
+        rims = in_order(1, columns[0, f], columns[parts - 1, f])
+        y0_ref[pl.ds(f, 1), :], y1_ref[pl.ds(f, 1), :] = rims
 
 
 def summed(odd, ids, rows, tiles, capacity, fields, cells_x, cells_y, width, grant):
     dims = (tiles, capacity, fields, cells_x, cells_y, width)
     rows = rows.reshape(-1, width)
+    flags = [] if odd is None else [pl.BlockSpec(memory_space=pltpu.SMEM)]
     slots = tiles * capacity
     blocks = cells_x * cells_y // width
     shapes = [
@@ -310,12 +301,9 @@
         (fields, cells_x),
     ]
     return pl.pallas_call(
-        functools.partial(sum_kernel, dims),
-        in_specs=[
-            pl.BlockSpec(memory_space=pltpu.SMEM),
-            pl.BlockSpec(memory_space=pltpu.VMEM),
-            pl.BlockSpec(memory_space=pl.ANY),
-        ],
+        functools.partial(sum_kernel, dims, odd is not None),
+        in_specs=flags
+        + [pl.BlockSpec(memory_space=pltpu.VMEM), pl.BlockSpec(memory_space=pl.ANY)],
         out_shape=[jax.ShapeDtypeStruct(shape, jnp.float32) for shape in shapes],
         scratch_shapes=[
             pltpu.VMEM(rows.shape, jnp.float32),
@@ -331,7 +319,7 @@
             transcendentals=0,
         ),
         name="sum_by_block",
-    )(odd, ids, rows)
+    )(*([] if odd is None else [odd]), ids, rows)
 
 
 def stencil_factors(coefs, keep):
@@ -537,7 +525,7 @@
             pltpu.VMEM((4 * nfield, cells_y), jnp.float32),
             pltpu.VMEM((4 * nfield, cells_x), jnp.float32),
         ],
-        compiler_params=pltpu.CompilerParams(vmem_limit_bytes=16 * 1024 * 1024),
+        compiler_params=pltpu.CompilerParams(vmem_limit_bytes=56 * 1024 * 1024),
         cost_estimate=pl.CostEstimate(
             flops=40 * state.size, bytes_accessed=8 * state.size, transcendentals=0
         ),
@@ -744,7 +732,7 @@
 
     ids_late = late_in[:, capacity, 0, :]
     ids_early = lax.ppermute(ids_late, "comp", swap)
-    recv_late, top, bottom, left, right = add_up(jnp.zeros((1, 2), jnp.int32), ids_late, late_in, 56)
+    recv_late, top, bottom, left, right = add_up(None, ids_late, late_in, 50)
     recv_late = lax.ppermute(recv_late, "comp", swap)
     late_x = (
         lax.ppermute(bottom, ("comp", "tx"), crossed("tx", 1)),

time: 141 us -> 140 us (level)
  local copies, waits for them, and re-layouts: 7.42 us -> 4.93 us
  Pallas kernels: 47.1 us -> 49.5 us
    pallas_call x1, Pallas kernels: 12.9 us -> 16.5 us  [base_of(): pl.pallas_call(functools.partial(base_kernel, half), grid=(nfield,), in_s...]
    unnamed x22 -> x48, local copies, waits for them, and re-layouts: 5.38 us -> 3.68 us
  transfers between devices with their start and end apart: 19 -> 19, of which waited for: 4 -> 4; matrix products, arithmetic and copies ran while one was open for 2% -> 1% of each run, Pallas kernels for 23% -> 25%
where the time goes in v10:
time: 140 us; the launch traced here: 139 us
  starting transfers between devices  60.9 us (44%)
  Pallas kernels  49.5 us (35%)
  waiting for transfers between devices  22 us (16%)
  local copies, waits for them, and re-layouts  4.93 us (4%)
    all_to_all x2, starting transfers between devices, exchanged(): lax.all_to_all(rows, ('tx', 'ty'), split_axis=0, concat_axis=0, tiled=True)  19.9 us
    pallas_call x1, Pallas kernels, base_of(): pl.pallas_call(functools.partial(base_kernel, half), grid=(nfield,), in_s...  16.5 us
    pallas_call x1, Pallas kernels, contributions(): pl.pallas_call(functools.partial(contribution_kernel, dims), in_specs=[pl...  10.8 us
    ppermute x1, waiting for transfers between devices, body(): early = lax.ppermute(early, 'comp', swap)  9.06 us
    pallas_call x2, Pallas kernels, finished(): pl.pallas_call(functools.partial(finish_kernel, first, with_x), in_specs=...  7.95 us
    pallas_call x2, Pallas kernels, summed(): pl.pallas_call(functools.partial(sum_kernel, dims, odd is not None), in_s...  7.02 us
    ppermute x1, waiting for transfers between devices, body(): above = lax.ppermute(x_high, 'tx', shift_pairs(tx, 1))  6.47 us
    ppermute x1, starting transfers between devices, body(): lax.ppermute(x_even, 'tx', neighbour_pairs(tx, 0))  5.42 us
  transfers between devices with their start and end apart: 19, of which 4 were waited for; matrix products, arithmetic and copies ran while one was open for 1% of the time, Pallas kernels for 25%

profile of v10, /device:TPU:1, one launch (start us, length us, event | category | flops | bytes accessed | tf_op | source)
XLA Modules:
  0.0 138.6 jit_solution(3192346522119471458)
XLA Ops:
  0.6 10.8 %contributions.1 = (f32[513,4,128]{2,1,0:T(4,128)}, f32[1040,4,128]{2,1,0:T(4,128)}) custom-call(s32[1,512]{1,0:T(1,128)} %src_ref.1, s32[1,512]{1,0:T(1,128)} %bitcast.16, s32[1,512]{1,0:T(1,128)} %blk_ref.1, f32[1,16,128,512]{3,2,1,0:T(8,128)} %state_ref.3, bf16[1,512,128,128]{3,2,1,0:T(8,128)(2,1)} %weights_ref.1), custom_call_target="tpu_custom_call" | custom-call | flops 134217728 | bytes 25296896 | tf_op jit(solution)/shard_map/contributions/pallas_call | solution.py:162
  11.4 0.0 copy-start.23
  11.5 0.0 copy-start.1
  11.5 0.0 copy-start.2
  11.5 7.5 %all-to-all-start = ((f32[16,65,4,128]{3,2,1,0:T(4,128)}), f32[16,65,4,128]{3,2,1,0:T(4,128)S(1)}, u32[]{:S(2)}, u32[]{:S(2)}) async-start(f32[16,65,4,128]{3,2,1,0:T(4,128)} %bitcast.15), calls=%async_computation | async-start | bytes 4259840 | tf_op jit(solution)/shard_map/all_to_all | solution.py:699
  19.0 1.2 collective-permute-start
  20.2 0.0 copy-start
  20.2 2.2 %copy-done = f32[1,16,128,512]{3,2,1,0:T(8,128)S(1)} copy-done((f32[1,16,128,512]{3,2,1,0:T(8,128)S(1)}, f32[1,16,128,512]{3,2,1,0:T(8,128)}, u32[]{:S(2)}) %copy-start) | copy-done | bytes 4194328
  22.4 2.0 %edges.1 = (f32[40,512]{1,0:T(8,128)S(1)}, f32[40,512]{1,0:T(8,128)S(1)}, f32[40,128]{1,0:T(8,128)S(1)}, f32[40,128]{1,0:T(8,128)S(1)}) custom-call(f32[1,2]{1,0:T(1,128)S(1)} %broadcast_select_fusion.mix_ref, f32[1,16,128,512]{3,2,1,0:T(8,128)S(1)} %copy-done, f32[1,16,128,512]{3,2,1,0:T(8,128)S(1)} %copy-done, f32[1,16,128,512]{3,2,1,0:T(8,128)S(1)} %copy-done, ...), custom_call_target="tpu_custom_call" | custom-call | flops 1048576 | bytes 4194304 | tf_op jit(solution)/shard_map/edges/pallas_call | solution.py:419
  24.4 3.3 %collective-permute-start.1 = (f32[40,512]{1,0:T(8,128)S(1)}, f32[40,512]{1,0:T(8,128)S(1)}, u32[]{:S(2)}, u32[]{:S(2)}) collective-permute-start(f32[40,512]{1,0:T(8,128)S(1)} %get-tuple-element.37.x_high), channel_id=1, source_target_pairs={{0,4},{4,8},{8,12},{1,5},{5,9},{9,13},{2,6},{6,10},{10,14},{3,7},{... | collective-permute-start | bytes 245768 | tf_op jit(solution)/shard_map/ppermute | solution.py:716
  27.7 1.3 collective-permute-start.2
  29.0 3.9 %collective-permute-start.3 = (f32[40,128]{1,0:T(8,128)S(1)}, f32[40,128]{1,0:T(8,128)S(1)}, u32[]{:S(2)}, u32[]{:S(2)}) collective-permute-start(f32[40,128]{1,0:T(8,128)S(1)} %get-tuple-element.39.y_high), channel_id=1, source_target_pairs={{0,1},{1,2},{2,3},{4,5},{5,6},{6,7},{8,9},{9,10},{10,11},{12,13},{... | collective-permute-start | bytes 61448 | tf_op jit(solution)/shard_map/ppermute | solution.py:714
  33.0 1.9 %collective-permute-start.4 = (f32[40,128]{1,0:T(8,128)S(1)}, f32[40,128]{1,0:T(8,128)S(1)}, u32[]{:S(2)}, u32[]{:S(2)}) collective-permute-start(f32[40,128]{1,0:T(8,128)S(1)} %get-tuple-element.40.y_low), channel_id=1, source_target_pairs={{1,0},{2,1},{3,2},{5,4},{6,5},{7,6},{9,8},{10,9},{11,10},{13,12},{... | collective-permute-start | bytes 61448 | tf_op jit(solution)/shard_map/ppermute | solution.py:715
  34.9 9.1 %collective-permute-done.in_ref = f32[513,4,128]{2,1,0:T(4,128)} collective-permute-done((f32[513,4,128]{2,1,0:T(4,128)}, f32[513,4,128]{2,1,0:T(4,128)}, u32[]{:S(2)}, u32[]{:S(2)}) %collective-permute-start) | collective-permute-done | bytes 1050656 | tf_op jit(solution)/shard_map/ppermute | solution.py:705
  43.9 5.2 %place_in_slots.1 = f32[1024,4,128]{2,1,0:T(4,128)} custom-call(f32[513,4,128]{2,1,0:T(4,128)} %collective-permute-done.in_ref), custom_call_target="tpu_custom_call" | custom-call | flops 1050624 | bytes 3151872 | tf_op jit(solution)/shard_map/place_in_slots/pallas_call | solution.py:213
  49.2 0.0 collective-permute-done.3.left.before
  49.2 0.0 collective-permute-done.4.right.after
  49.2 6.5 %collective-permute-done.1.above = f32[40,512]{1,0:T(8,128)S(1)} collective-permute-done((f32[40,512]{1,0:T(8,128)S(1)}, f32[40,512]{1,0:T(8,128)S(1)}, u32[]{:S(2)}, u32[]{:S(2)}) %collective-permute-start.1) | collective-permute-done | bytes 81952 | tf_op jit(solution)/shard_map/ppermute | solution.py:716
  55.7 0.0 collective-permute-done.2.below
  55.7 5.3 %all-to-all-done = f32[16,65,4,128]{3,2,1,0:T(4,128)S(1)} async-done(((f32[16,65,4,128]{3,2,1,0:T(4,128)}), f32[16,65,4,128]{3,2,1,0:T(4,128)S(1)}, u32[]{:S(2)}, u32[]{:S(2)}) %all-to-all-start) | async-done | bytes 2129952 | tf_op jit(solution)/shard_map/all_to_all | solution.py:699
  61.0 12.4 %all-to-all-start.1 = ((f32[16,64,4,128]{3,2,1,0:T(4,128)}), f32[16,64,4,128]{3,2,1,0:T(4,128)}, u32[]{:S(2)}, u32[]{:S(2)}) async-start(f32[16,64,4,128]{3,2,1,0:T(4,128)} %bitcast.6), calls=%async_computation.1 | async-start | bytes 4194304 | tf_op jit(solution)/shard_map/all_to_all | solution.py:699
  73.5 3.2 %sum_by_block.2 = (f32[4,128,512]{2,1,0:T(8,128)}, f32[4,512]{1,0:T(4,128)S(1)}, f32[4,512]{1,0:T(4,128)S(1)}, f32[4,128]{1,0:T(4,128)S(1)}, f32[4,128]{1,0:T(4,128)S(1)}) custom-call(f32[16,128]{1,0:T(8,128)S(1)} %bitcast.13, f32[4160,128]{1,0:T(8,128)S(1)} %bitcast.12), custom_call_target="tpu_custom_call" | custom-call | flops 1073741824 | bytes 3145728 | tf_op jit(solution)/shard_map/sum_by_block/pallas_call | solution.py:303
  76.7 1.3 collective-permute-start.8
  78.0 0.6 pad_bitcast_fusion
  78.6 3.8 %collective-permute-start.5 = (f32[80,128]{1,0:T(8,128)S(1)}, f32[80,128]{1,0:T(8,128)S(1)}, u32[]{:S(2)}, u32[]{:S(2)}) collective-permute-start(f32[80,128]{1,0:T(8,128)S(1)} %pad_maximum_fusion), channel_id=1, source_target_pairs={{0,1},{1,2},{2,3},{4,5},{5,6},{6,7},{8,9},{9,10},{10,11},{12,13},{... | collective-permute-start | bytes 122888 | tf_op jit(solution)/shard_map/ppermute | solution.py:726
  82.4 1.9 %collective-permute-start.6 = (f32[80,128]{1,0:T(8,128)S(1)}, f32[80,128]{1,0:T(8,128)S(1)}, u32[]{:S(2)}, u32[]{:S(2)}) collective-permute-start(f32[80,128]{1,0:T(8,128)S(1)} %pad_maximum_fusion.1), channel_id=1, source_target_pairs={{1,0},{2,1},{3,2},{5,4},{6,5},{7,6},{9,8},{10,9},{11,10},{13,12},{... | collective-permute-start | bytes 122888 | tf_op jit(solution)/shard_map/ppermute | solution.py:727
  84.4 0.3 collective-permute-start.7
  84.7 0.1 add_and_fusion.refs_0_.rest_5_
  84.8 4.9 %collective-permute-start.9 = (f32[4,128]{1,0:T(4,128)S(1)}, f32[4,128]{1,0:T(4,128)S(1)}, u32[]{:S(2)}, u32[]{:S(2)}) collective-permute-start(f32[4,128]{1,0:T(4,128)S(1)} %get-tuple-element.48), channel_id=1, source_target_pairs={{0,17},{1,18},{2,19},{16,1},{17,2},{18,3},{4,21},{5,22},{6,23},{20... | collective-permute-start | bytes 6152 | tf_op jit(solution)/shard_map/ppermute | solution.py:742
  89.6 0.0 collective-permute-done.5.corners_left
  89.6 1.9 %collective-permute-start.10 = (f32[4,128]{1,0:T(4,128)S(1)}, f32[4,128]{1,0:T(4,128)S(1)}, u32[]{:S(2)}, u32[]{:S(2)}) collective-permute-start(f32[4,128]{1,0:T(4,128)S(1)} %get-tuple-element.49), channel_id=1, source_target_pairs={{1,16},{2,17},{3,18},{17,0},{18,1},{19,2},{5,20},{6,21},{7,22},{21... | collective-permute-start | bytes 6152 | tf_op jit(solution)/shard_map/ppermute | solution.py:743
  91.6 0.7 broadcast_in_dim.9.rates_ref
  92.3 16.5 %base.1 = (f32[1,16,128,512]{3,2,1,0:T(8,128)}, f32[4,128,512]{2,1,0:T(8,128)}, f32[6,128,512]{2,1,0:T(8,128)}) custom-call(f32[1,16]{1,0:T(1,128)} %get-tuple-element.71.rate_ref, f32[1,2]{1,0:T(1,128)} %copy-done.18, f32[16,128]{1,0:T(8,128)} %broadcast_in_dim.9.rates_ref, f32[1,3,128,512]{3,2,1,0:T(8,128)} %coefs_ref.1, s32[128,512]{1,0:T(8,128)} %land_ref, ...), custom_call_target="tpu_custom_call" | custom-call | flops 41943040 | bytes 8388608 | tf_op jit(solution)/shard_map/base/pallas_call | solution.py:505
  108.8 3.2 %collective-permute-start.15 = (f32[4,512]{1,0:T(4,128)S(1)}, f32[4,512]{1,0:T(4,128)S(1)}, u32[]{:S(2)}, u32[]{:S(2)}) collective-permute-start(f32[4,512]{1,0:T(4,128)S(1)} %get-tuple-element.58), channel_id=1, source_target_pairs={{0,20},{4,24},{8,28},{16,4},{20,8},{24,12},{1,21},{5,25},{9,29},{1... | collective-permute-start | bytes 24584 | tf_op jit(solution)/shard_map/ppermute | solution.py:738
  112.0 1.3 collective-permute-start.16
  113.3 0.0 collective-permute-done.10.right
  113.3 0.0 collective-permute-done.8.recv
  113.4 1.4 %copy-done.3 = f32[6,128,512]{2,1,0:T(8,128)S(1)} copy-done((f32[6,128,512]{2,1,0:T(8,128)S(1)}, f32[6,128,512]{2,1,0:T(8,128)}, u32[]{:S(2)}) %copy-start.3) | copy-done | bytes 1572888
  114.8 4.2 %finish.2 = (f32[1,16,128,512]{3,2,1,0:T(8,128)}, f32[1,8,128,512]{3,2,1,0:T(8,128)}, f32[8,128]{1,0:T(8,128)S(1)}) custom-call(f32[1,8]{1,0:T(1,128)S(1)} %copy-done.20, f32[1,2]{1,0:T(1,128)S(1)} %copy-done.19, f32[40,512]{1,0:T(8,128)S(1)} %copy-done.7, f32[40,512]{1,0:T(8,128)S(1)} %copy-done.9, ...), custom_call_target="tpu_custom_call", output_to_operand_aliasing={{0}: (10, {})} | custom-call | flops 5242880 | bytes 5242880 | tf_op jit(solution)/shard_map/finish/pallas_call | solution.py:656
  119.0 0.0 all-to-all-done.1
  119.0 0.0 collective-permute-done.7.refs_1_
  119.0 3.8 %sum_by_block.3 = (f32[4,128,512]{2,1,0:T(8,128)S(1)}, f32[4,512]{1,0:T(4,128)S(1)}, f32[4,512]{1,0:T(4,128)S(1)}, f32[4,128]{1,0:T(4,128)S(1)}, f32[4,128]{1,0:T(4,128)S(1)}) custom-call(s32[1,2]{1,0:T(1,128)S(1)} %add_and_fusion.refs_0_.rest_5_, f32[16,128]{1,0:T(8,128)S(1)} %collective-permute-done.7.refs_1_, f32[4096,128]{1,0:T(8,128)} %bitcast.8.refs_2_), custom_call_target="tpu_custom_call" | custom-call | flops 1073741824 | bytes 3145728 | tf_op jit(solution)/shard_map/sum_by_block/pallas_call | solution.py:303
  122.8 0.7 collective-permute-start.13
  123.4 5.4 %collective-permute-start.14 = (f32[4,512]{1,0:T(4,128)S(1)}, f32[4,512]{1,0:T(4,128)S(1)}, u32[]{:S(2)}, u32[]{:S(2)}) collective-permute-start(f32[4,512]{1,0:T(4,128)S(1)} %get-tuple-element.57), channel_id=1, source_target_pairs={{0,4},{8,12},{4,0},{12,8},{1,5},{9,13},{5,1},{13,9},{2,6},{10,14},... | collective-permute-start | bytes 24584 | tf_op jit(solution)/shard_map/ppermute | solution.py:754
  128.9 4.7 %collective-permute-start.11 = (f32[4,128]{1,0:T(4,128)S(1)}, f32[4,128]{1,0:T(4,128)S(1)}, u32[]{:S(2)}, u32[]{:S(2)}) collective-permute-start(f32[4,128]{1,0:T(4,128)S(1)} %get-tuple-element.54), channel_id=1, source_target_pairs={{1,2},{2,1},{5,6},{6,5},{9,10},{10,9},{13,14},{14,13},{17,18},{18,... | collective-permute-start | bytes 6152 | tf_op jit(solution)/shard_map/ppermute | solution.py:757
  133.6 0.1 collective-permute-start.12
  133.7 1.2 collective-permute-done.11.left
  134.8 3.8 %finish.3 = (f32[1,16,128,512]{3,2,1,0:T(8,128)}, f32[1,8,128,512]{3,2,1,0:T(8,128)}, f32[8,128]{1,0:T(8,128)}) custom-call(f32[1,8]{1,0:T(1,128)S(1)} %copy-done.20, f32[1,2]{1,0:T(1,128)S(1)} %copy-done.19, f32[40,512]{1,0:T(8,128)S(1)} %copy-done.7, f32[40,512]{1,0:T(8,128)S(1)} %copy-done.9, ...), custom_call_target="tpu_custom_call", output_to_operand_aliasing={{0}: (16, {}), {1}: (17, {})} | custom-call | flops 5242880 | bytes 5242880 | tf_op jit(solution)/shard_map/finish/pallas_call | solution.py:656
  (54 shorter events, 0.1 us)
Async XLA Ops:
  11.4 8.7 %copy-start.23 = (f32[1,2]{1,0:T(1,128)S(1)}, f32[1,2]{1,0:T(1,128)}, u32[]{:S(2)}) copy-start(f32[1,2]{1,0:T(1,128)} %constant.23.clone) | copy-start | bytes 28
  11.5 8.7 %copy-start.1 = (f32[1,3,128,512]{3,2,1,0:T(8,128)S(1)}, f32[1,3,128,512]{3,2,1,0:T(8,128)}, u32[]{:S(2)}) copy-start(f32[1,3,128,512]{3,2,1,0:T(8,128)} %coefs_ref.1) | copy-start | bytes 2359300
  11.5 8.7 %copy-start.2 = (s32[128,512]{1,0:T(8,128)S(1)}, s32[128,512]{1,0:T(8,128)}, u32[]{:S(2)}) copy-start(s32[128,512]{1,0:T(8,128)} %land_ref) | copy-start | bytes 786436
  11.5 49.5 %all-to-all-start = ((f32[16,65,4,128]{3,2,1,0:T(4,128)}), f32[16,65,4,128]{3,2,1,0:T(4,128)S(1)}, u32[]{:S(2)}, u32[]{:S(2)}) async-start(f32[16,65,4,128]{3,2,1,0:T(4,128)} %bitcast.15), calls=%async_computation | async-start | bytes 4259840 | tf_op jit(solution)/shard_map/all_to_all | solution.py:699
  19.0 25.0 %collective-permute-start = (f32[513,4,128]{2,1,0:T(4,128)}, f32[513,4,128]{2,1,0:T(4,128)}, u32[]{:S(2)}, u32[]{:S(2)}) collective-permute-start(f32[513,4,128]{2,1,0:T(4,128)} %get-tuple-element.34), channel_id=1, source_target_pairs={{0,16},{16,0},{1,17},{17,1},{2,18},{18,2},{3,19},{19,3},{4,20},{20... | collective-permute-start | bytes 3151880 | tf_op jit(solution)/shard_map/ppermute | solution.py:705
  20.2 2.2 %copy-start = (f32[1,16,128,512]{3,2,1,0:T(8,128)S(1)}, f32[1,16,128,512]{3,2,1,0:T(8,128)}, u32[]{:S(2)}) copy-start(f32[1,16,128,512]{3,2,1,0:T(8,128)} %state_ref.3) | copy-start | bytes 12582916
  22.4 2.0 %copy-start.18 = (f32[1,2]{1,0:T(1,128)}, f32[1,2]{1,0:T(1,128)S(1)}, u32[]{:S(2)}) copy-start(f32[1,2]{1,0:T(1,128)S(1)} %broadcast_select_fusion.mix_ref) | copy-start | bytes 28
  24.4 31.3 %copy-start.16 = (f32[40,128]{1,0:T(8,128)}, f32[40,128]{1,0:T(8,128)S(1)}, u32[]{:S(2)}) copy-start(f32[40,128]{1,0:T(8,128)S(1)} %get-tuple-element.40.y_low) | copy-start | bytes 61444
  24.4 31.3 %copy-start.17 = (f32[40,128]{1,0:T(8,128)}, f32[40,128]{1,0:T(8,128)S(1)}, u32[]{:S(2)}) copy-start(f32[40,128]{1,0:T(8,128)S(1)} %get-tuple-element.39.y_high) | copy-start | bytes 61444
  24.4 36.6 %copy-start.14 = (f32[40,512]{1,0:T(8,128)}, f32[40,512]{1,0:T(8,128)S(1)}, u32[]{:S(2)}) copy-start(f32[40,512]{1,0:T(8,128)S(1)} %get-tuple-element.38.x_low) | copy-start | bytes 245764
  24.4 36.6 %copy-start.15 = (f32[40,512]{1,0:T(8,128)}, f32[40,512]{1,0:T(8,128)S(1)}, u32[]{:S(2)}) copy-start(f32[40,512]{1,0:T(8,128)S(1)} %get-tuple-element.37.x_high) | copy-start | bytes 245764
  24.4 31.2 %collective-permute-start.1 = (f32[40,512]{1,0:T(8,128)S(1)}, f32[40,512]{1,0:T(8,128)S(1)}, u32[]{:S(2)}, u32[]{:S(2)}) collective-permute-start(f32[40,512]{1,0:T(8,128)S(1)} %get-tuple-element.37.x_high), channel_id=1, source_target_pairs={{0,4},{4,8},{8,12},{1,5},{5,9},{9,13},{2,6},{6,10},{10,14},{3,7},{... | collective-permute-start | bytes 245768 | tf_op jit(solution)/shard_map/ppermute | solution.py:716
  27.7 27.9 %collective-permute-start.2 = (f32[40,512]{1,0:T(8,128)S(1)}, f32[40,512]{1,0:T(8,128)S(1)}, u32[]{:S(2)}, u32[]{:S(2)}) collective-permute-start(f32[40,512]{1,0:T(8,128)S(1)} %get-tuple-element.38.x_low), channel_id=1, source_target_pairs={{4,0},{8,4},{12,8},{5,1},{9,5},{13,9},{6,2},{10,6},{14,10},{7,3},{... | collective-permute-start | bytes 245768 | tf_op jit(solution)/shard_map/ppermute | solution.py:717
  29.0 20.1 %collective-permute-start.3 = (f32[40,128]{1,0:T(8,128)S(1)}, f32[40,128]{1,0:T(8,128)S(1)}, u32[]{:S(2)}, u32[]{:S(2)}) collective-permute-start(f32[40,128]{1,0:T(8,128)S(1)} %get-tuple-element.39.y_high), channel_id=1, source_target_pairs={{0,1},{1,2},{2,3},{4,5},{5,6},{6,7},{8,9},{9,10},{10,11},{12,13},{... | collective-permute-start | bytes 61448 | tf_op jit(solution)/shard_map/ppermute | solution.py:714
  33.0 16.2 %collective-permute-start.4 = (f32[40,128]{1,0:T(8,128)S(1)}, f32[40,128]{1,0:T(8,128)S(1)}, u32[]{:S(2)}, u32[]{:S(2)}) collective-permute-start(f32[40,128]{1,0:T(8,128)S(1)} %get-tuple-element.40.y_low), channel_id=1, source_target_pairs={{1,0},{2,1},{3,2},{5,4},{6,5},{7,6},{9,8},{10,9},{11,10},{13,12},{... | collective-permute-start | bytes 61448 | tf_op jit(solution)/shard_map/ppermute | solution.py:715
  49.2 27.5 %copy-start.10 = (f32[40,128]{1,0:T(8,128)}, f32[40,128]{1,0:T(8,128)S(1)}, u32[]{:S(2)}) copy-start(f32[40,128]{1,0:T(8,128)S(1)} %collective-permute-done.3.left.before) | copy-start | bytes 61444
  49.2 27.5 %copy-start.12 = (f32[40,128]{1,0:T(8,128)}, f32[40,128]{1,0:T(8,128)S(1)}, u32[]{:S(2)}) copy-start(f32[40,128]{1,0:T(8,128)S(1)} %collective-permute-done.4.right.after) | copy-start | bytes 61444
  55.7 22.9 %copy-start.6 = (f32[40,512]{1,0:T(8,128)}, f32[40,512]{1,0:T(8,128)S(1)}, u32[]{:S(2)}) copy-start(f32[40,512]{1,0:T(8,128)S(1)} %collective-permute-done.1.above) | copy-start | bytes 245764
  55.7 22.9 %copy-start.8 = (f32[40,512]{1,0:T(8,128)}, f32[40,512]{1,0:T(8,128)S(1)}, u32[]{:S(2)}) copy-start(f32[40,512]{1,0:T(8,128)S(1)} %collective-permute-done.2.below) | copy-start | bytes 245764
  61.0 57.9 %all-to-all-start.1 = ((f32[16,64,4,128]{3,2,1,0:T(4,128)}), f32[16,64,4,128]{3,2,1,0:T(4,128)}, u32[]{:S(2)}, u32[]{:S(2)}) async-start(f32[16,64,4,128]{3,2,1,0:T(4,128)} %bitcast.6), calls=%async_computation.1 | async-start | bytes 4194304 | tf_op jit(solution)/shard_map/all_to_all | solution.py:699
  73.4 4.6 %copy-start.20 = (f32[1,8]{1,0:T(1,128)S(1)}, f32[1,8]{1,0:T(1,128)}, u32[]{:S(2)}) copy-start(f32[1,8]{1,0:T(1,128)} %gamma_ref.3) | copy-start | bytes 100
  76.7 36.6 %collective-permute-start.8 = (f32[4,128,512]{2,1,0:T(8,128)}, f32[4,128,512]{2,1,0:T(8,128)S(1)}, u32[]{:S(2)}, u32[]{:S(2)}) collective-permute-start(f32[4,128,512]{2,1,0:T(8,128)} %get-tuple-element.47), channel_id=1, source_target_pairs={{0,16},{16,0},{1,17},{17,1},{2,18},{18,2},{3,19},{19,3},{4,20},{20... | collective-permute-start | bytes 3145736 | tf_op jit(solution)/shard_map/ppermute | solution.py:736
  78.6 11.0 %collective-permute-start.5 = (f32[80,128]{1,0:T(8,128)S(1)}, f32[80,128]{1,0:T(8,128)S(1)}, u32[]{:S(2)}, u32[]{:S(2)}) collective-permute-start(f32[80,128]{1,0:T(8,128)S(1)} %pad_maximum_fusion), channel_id=1, source_target_pairs={{0,1},{1,2},{2,3},{4,5},{5,6},{6,7},{8,9},{9,10},{10,11},{12,13},{... | collective-permute-start | bytes 122888 | tf_op jit(solution)/shard_map/ppermute | solution.py:726
  82.4 9.1 %collective-permute-start.6 = (f32[80,128]{1,0:T(8,128)S(1)}, f32[80,128]{1,0:T(8,128)S(1)}, u32[]{:S(2)}, u32[]{:S(2)}) collective-permute-start(f32[80,128]{1,0:T(8,128)S(1)} %pad_maximum_fusion.1), channel_id=1, source_target_pairs={{1,0},{2,1},{3,2},{5,4},{6,5},{7,6},{9,8},{10,9},{11,10},{13,12},{... | collective-permute-start | bytes 122888 | tf_op jit(solution)/shard_map/ppermute | solution.py:727
  84.4 34.6 %collective-permute-start.7 = (f32[16,128]{1,0:T(8,128)S(1)}, f32[16,128]{1,0:T(8,128)S(1)}, u32[]{:S(2)}, u32[]{:S(2)}) collective-permute-start(f32[16,128]{1,0:T(8,128)S(1)} %bitcast.14), channel_id=1, source_target_pairs={{0,16},{16,0},{1,17},{17,1},{2,18},{18,2},{3,19},{19,3},{4,20},{20... | collective-permute-start | bytes 24584 | tf_op jit(solution)/shard_map/ppermute | solution.py:734
  84.8 27.2 %collective-permute-start.9 = (f32[4,128]{1,0:T(4,128)S(1)}, f32[4,128]{1,0:T(4,128)S(1)}, u32[]{:S(2)}, u32[]{:S(2)}) collective-permute-start(f32[4,128]{1,0:T(4,128)S(1)} %get-tuple-element.48), channel_id=1, source_target_pairs={{0,17},{1,18},{2,19},{16,1},{17,2},{18,3},{4,21},{5,22},{6,23},{20... | collective-permute-start | bytes 6152 | tf_op jit(solution)/shard_map/ppermute | solution.py:742
  89.6 2.6 %copy-start.21 = (f32[80,128]{1,0:T(8,128)}, f32[80,128]{1,0:T(8,128)S(1)}, u32[]{:S(2)}) copy-start(f32[80,128]{1,0:T(8,128)S(1)} %collective-permute-done.5.corners_left) | copy-start | bytes 122884
  89.6 23.6 %collective-permute-start.10 = (f32[4,128]{1,0:T(4,128)S(1)}, f32[4,128]{1,0:T(4,128)S(1)}, u32[]{:S(2)}, u32[]{:S(2)}) collective-permute-start(f32[4,128]{1,0:T(4,128)S(1)} %get-tuple-element.49), channel_id=1, source_target_pairs={{1,16},{2,17},{3,18},{17,0},{18,1},{19,2},{5,20},{6,21},{7,22},{21... | collective-permute-start | bytes 6152 | tf_op jit(solution)/shard_map/ppermute | solution.py:743
  91.6 0.7 copy-start.22
  92.3 21.0 %copy-start.7 = (f32[40,512]{1,0:T(8,128)S(1)}, f32[40,512]{1,0:T(8,128)}, u32[]{:S(2)}) copy-start(f32[40,512]{1,0:T(8,128)} %copy-done.6) | copy-start | bytes 245764
  92.3 21.1 %copy-start.9 = (f32[40,512]{1,0:T(8,128)S(1)}, f32[40,512]{1,0:T(8,128)}, u32[]{:S(2)}) copy-start(f32[40,512]{1,0:T(8,128)} %copy-done.8) | copy-start | bytes 245764
  92.3 21.1 %copy-start.11 = (f32[40,128]{1,0:T(8,128)S(1)}, f32[40,128]{1,0:T(8,128)}, u32[]{:S(2)}) copy-start(f32[40,128]{1,0:T(8,128)} %copy-done.10) | copy-start | bytes 61444
  92.3 21.1 %copy-start.13 = (f32[40,128]{1,0:T(8,128)S(1)}, f32[40,128]{1,0:T(8,128)}, u32[]{:S(2)}) copy-start(f32[40,128]{1,0:T(8,128)} %copy-done.12) | copy-start | bytes 61444
  92.3 21.1 %copy-start.19 = (f32[1,2]{1,0:T(1,128)S(1)}, f32[1,2]{1,0:T(1,128)}, u32[]{:S(2)}) copy-start(f32[1,2]{1,0:T(1,128)} %copy-done.18) | copy-start | bytes 28
  108.8 24.8 %collective-permute-start.15 = (f32[4,512]{1,0:T(4,128)S(1)}, f32[4,512]{1,0:T(4,128)S(1)}, u32[]{:S(2)}, u32[]{:S(2)}) collective-permute-start(f32[4,512]{1,0:T(4,128)S(1)} %get-tuple-element.58), channel_id=1, source_target_pairs={{0,20},{4,24},{8,28},{16,4},{20,8},{24,12},{1,21},{5,25},{9,29},{1... | collective-permute-start | bytes 24584 | tf_op jit(solution)/shard_map/ppermute | solution.py:738
  112.0 21.7 %collective-permute-start.16 = (f32[4,512]{1,0:T(4,128)S(1)}, f32[4,512]{1,0:T(4,128)S(1)}, u32[]{:S(2)}, u32[]{:S(2)}) collective-permute-start(f32[4,512]{1,0:T(4,128)S(1)} %get-tuple-element.59), channel_id=1, source_target_pairs={{4,16},{8,20},{12,24},{20,0},{24,4},{28,8},{5,17},{9,21},{13,25},{... | collective-permute-start | bytes 24584 | tf_op jit(solution)/shard_map/ppermute | solution.py:739
  113.3 1.4 %copy-start.3 = (f32[6,128,512]{2,1,0:T(8,128)S(1)}, f32[6,128,512]{2,1,0:T(8,128)}, u32[]{:S(2)}) copy-start(f32[6,128,512]{2,1,0:T(8,128)} %get-tuple-element.45.factors) | copy-start | bytes 4718596
  118.9 15.9 %copy-start.4 = (f32[6,128,512]{2,1,0:T(8,128)S(1)}, f32[6,128,512]{2,1,0:T(8,128)}, u32[]{:S(2)}) copy-start(f32[6,128,512]{2,1,0:T(8,128)} %get-tuple-element.45.factors) | copy-start | bytes 4718596
  118.9 15.9 %copy-start.5 = (f32[4,128,512]{2,1,0:T(8,128)S(1)}, f32[4,128,512]{2,1,0:T(8,128)}, u32[]{:S(2)}) copy-start(f32[4,128,512]{2,1,0:T(8,128)} %get-tuple-element.60.rest_4_) | copy-start | bytes 3145732
  122.8 12.0 %collective-permute-start.13 = (f32[4,512]{1,0:T(4,128)S(1)}, f32[4,512]{1,0:T(4,128)S(1)}, u32[]{:S(2)}, u32[]{:S(2)}) collective-permute-start(f32[4,512]{1,0:T(4,128)S(1)} %get-tuple-element.56), channel_id=1, source_target_pairs={{4,8},{8,4},{5,9},{9,5},{6,10},{10,6},{7,11},{11,7},{20,24},{24,20... | collective-permute-start | bytes 24584 | tf_op jit(solution)/shard_map/ppermute | solution.py:753
  123.4 11.4 %collective-permute-start.14 = (f32[4,512]{1,0:T(4,128)S(1)}, f32[4,512]{1,0:T(4,128)S(1)}, u32[]{:S(2)}, u32[]{:S(2)}) collective-permute-start(f32[4,512]{1,0:T(4,128)S(1)} %get-tuple-element.57), channel_id=1, source_target_pairs={{0,4},{8,12},{4,0},{12,8},{1,5},{9,13},{5,1},{13,9},{2,6},{10,14},... | collective-permute-start | bytes 24584 | tf_op jit(solution)/shard_map/ppermute | solution.py:754
  128.9 5.9 %collective-permute-start.11 = (f32[4,128]{1,0:T(4,128)S(1)}, f32[4,128]{1,0:T(4,128)S(1)}, u32[]{:S(2)}, u32[]{:S(2)}) collective-permute-start(f32[4,128]{1,0:T(4,128)S(1)} %get-tuple-element.54), channel_id=1, source_target_pairs={{1,2},{2,1},{5,6},{6,5},{9,10},{10,9},{13,14},{14,13},{17,18},{18,... | collective-permute-start | bytes 6152 | tf_op jit(solution)/shard_map/ppermute | solution.py:757
  133.6 1.2 collective-permute-start.12

commit v11 on v10

--- a/solution.py
+++ b/solution.py
@@ -10,7 +10,12 @@
 LANES = 128
 STEP_PAIRS = 64
 STRIP = 8
+PER_STEP = 2
 NT = (((1,), (1,)), ((), ()))
+
+
+def pinned(space, *arrays):
+    return [pltpu.with_memory_space_constraint(a, space) for a in arrays]
 
 
 def shift_pairs(count, by):
@@ -22,11 +27,10 @@
     return [(i, i + 1) for i in lows] + [(i + 1, i) for i in lows]
 
 
-def crossed(axis, by):
+def crossed(axis, first):
     count = lax.axis_size(axis)
-    return [
-        (c * count + i, (1 - c) * count + j) for c in range(2) for i, j in shift_pairs(count, by)
-    ]
+    pairs = neighbour_pairs(count, first)
+    return [(c * count + i, (1 - c) * count + j) for c in range(2) for i, j in pairs]
 
 
 def split(value, parts):
@@ -174,14 +178,14 @@
             pltpu.SemaphoreType.DMA((pairs // STEP_PAIRS,)),
             pltpu.SemaphoreType.DMA((4,)),
         ],
-        compiler_params=pltpu.CompilerParams(vmem_limit_bytes=56 * 1024 * 1024),
+        compiler_params=pltpu.CompilerParams(vmem_limit_bytes=40 * 1024 * 1024),
         cost_estimate=pl.CostEstimate(
             flops=2 * pairs * fields * width * width,
             bytes_accessed=2 * pairs * width * width + 8 * rows * fields * width,
             transcendentals=0,
         ),
         name="contributions",
-    )(pair_src, pair_dev.reshape(1, pairs), pair_blk, state, weights)
+    )(*pinned(pltpu.HBM, pair_src, pair_dev.reshape(1, pairs), pair_blk, state, weights))
 
 
 def place_kernel(dims, in_ref, out_ref, place_v, place_s, place_sem):
@@ -229,7 +233,8 @@
 def sum_kernel(dims, paired, *refs):
     odd_ref, refs = (refs[0], refs[1:]) if paired else (None, refs)
     ids_ref, rows_ref, out_ref, x0_ref, x1_ref, y0_ref, y1_ref = refs[:7]
-    in_ref, pick, high, low, row_sems = refs[7:]
+    pick, high, low, *copied = refs[7:]
+    in_ref, row_sems = copied if copied else (rows_ref, None)
     tiles, capacity, fields, cells_x, cells_y, width = dims
     parts = cells_y // width
     group = LANES // capacity
@@ -239,14 +244,15 @@
         some = pl.ds(k * group * stride, group * stride)
         return pltpu.make_async_copy(rows_ref.at[some, :], in_ref.at[some, :], row_sems.at[k])
 
-    for k in range(tiles // group):
+    for k in range(tiles // group if copied else 0):
         rows_copy(k).start()
     block_of = lax.broadcasted_iota(jnp.int32, (cells_x * parts, LANES), 0)
     block_of = (block_of % cells_x) * parts + block_of // cells_x
     block_of = block_of.astype(jnp.float32)
     lane = lax.broadcasted_iota(jnp.int32, (1, LANES), 1)
     for k in range(tiles // group):
-        rows_copy(k).wait()
+        if copied:
+            rows_copy(k).wait()
         ids = None
         for i in range(group):
             source = k * group + i
@@ -287,10 +293,16 @@
         y0_ref[pl.ds(f, 1), :], y1_ref[pl.ds(f, 1), :] = rims
 
 
-def summed(odd, ids, rows, tiles, capacity, fields, cells_x, cells_y, width, grant):
+def summed(odd, ids, rows, tiles, capacity, fields, cells_x, cells_y, width, space):
     dims = (tiles, capacity, fields, cells_x, cells_y, width)
     rows = rows.reshape(-1, width)
     flags = [] if odd is None else [pl.BlockSpec(memory_space=pltpu.SMEM)]
+    copied = []
+    if space is pltpu.HBM:
+        copied = [
+            pltpu.VMEM(rows.shape, jnp.float32),
+            pltpu.SemaphoreType.DMA((tiles * capacity // LANES,)),
+        ]
     slots = tiles * capacity
     blocks = cells_x * cells_y // width
     shapes = [
@@ -303,23 +315,22 @@
     return pl.pallas_call(
         functools.partial(sum_kernel, dims, odd is not None),
         in_specs=flags
-        + [pl.BlockSpec(memory_space=pltpu.VMEM), pl.BlockSpec(memory_space=pl.ANY)],
+        + [pl.BlockSpec(memory_space=pltpu.VMEM), pl.BlockSpec(memory_space=space)],
         out_shape=[jax.ShapeDtypeStruct(shape, jnp.float32) for shape in shapes],
         scratch_shapes=[
-            pltpu.VMEM(rows.shape, jnp.float32),
             pltpu.VMEM((blocks, slots), jnp.bfloat16),
             pltpu.VMEM((slots, fields * width), jnp.bfloat16),
             pltpu.VMEM((slots, fields * width), jnp.bfloat16),
-            pltpu.SemaphoreType.DMA((tiles * capacity // LANES,)),
-        ],
-        compiler_params=pltpu.CompilerParams(vmem_limit_bytes=grant * 1024 * 1024),
+        ]
+        + copied,
+        compiler_params=pltpu.CompilerParams(vmem_limit_bytes=24 * 1024 * 1024),
         cost_estimate=pl.CostEstimate(
             flops=4 * blocks * slots * fields * width,
             bytes_accessed=4 * fields * width * (slots + blocks),
             transcendentals=0,
         ),
         name="sum_by_block",
-    )(*([] if odd is None else [odd]), ids, rows)
+    )(*([] if odd is None else [odd]), ids, *pinned(space, rows))
 
 
 def stencil_factors(coefs, keep):
@@ -427,7 +438,7 @@
             flops=state.size, bytes_accessed=4 * 1024 * 1024, transcendentals=0
         ),
         name="edges",
-    )(mix, *[state] * 4, *[coefs] * 4, *[land_sea] * 4)
+    )(mix, *pinned(pltpu.HBM, *[state] * 4), *[coefs] * 4, *[land_sea] * 4)
 
 
 def outer_section(center, across, along, factors, rate):
@@ -479,32 +490,37 @@
             kept[pl.ds(i % 2 * nfield, nfield), :] = center
             kept[pl.ds((2 + i % 2) * nfield, nfield), :] = section
 
-    rate = rate_ref[0, f]
     mix_a, mix_b = mix_ref[0, 0], mix_ref[0, 1]
-    s = state_ref[0, 0]
-    row = [rows[pl.ds(i * nfield + f, 1), :] for i in range(4)]
-    col = columns_of(
-        jnp.concatenate([cols[pl.ds(i * nfield + f, 1), :] for i in range(4)], axis=0)
-    )
-    s1 = s + tendency(s, rate, factors, row[0], row[1], col[:, 0:1], col[:, 1:2])
-    more = tendency(s1, rate, factors, row[2], row[3], col[:, 2:3], col[:, 3:4])
-    total = mix_a * s + (1.0 - mix_a) * s1 + mix_b * more
-    out_ref[0, 0] = total
-
-    @pl.when(f < half)
-    def _():
-        early_ref[0] = total
+    for j in range(PER_STEP):
+        field = f * PER_STEP + j
+        rate = rate_ref[0, field]
+        s = state_ref[0, j]
+        row = [rows[pl.ds(i * nfield + field, 1), :] for i in range(4)]
+        col = columns_of(
+            jnp.concatenate([cols[pl.ds(i * nfield + field, 1), :] for i in range(4)], axis=0)
+        )
+        s1 = s + tendency(s, rate, factors, row[0], row[1], col[:, 0:1], col[:, 1:2])
+        more = tendency(s1, rate, factors, row[2], row[3], col[:, 2:3], col[:, 3:4])
+        total = mix_a * s + (1.0 - mix_a) * s1 + mix_b * more
+        out_ref[0, j] = total
+
+        @pl.when(field < half)
+        def _():
+            early_ref[j] = total
 
 
 def base_of(state, coefs, land_sea, rates, mix, edges, received, corners, half):
     _, nfield, cells_x, cells_y = state.shape
-    field = pl.BlockSpec((1, 1, cells_x, cells_y), lambda f: (0, f, 0, 0))
+    field = pl.BlockSpec((1, PER_STEP, cells_x, cells_y), lambda f: (0, f, 0, 0))
+    early = pl.BlockSpec(
+        (PER_STEP, cells_x, cells_y), lambda f: (jnp.minimum(f, half // PER_STEP - 1), 0, 0)
+    )
     whole = lambda a: pl.BlockSpec(a.shape, lambda f: (0,) * a.ndim)
     rates_wide = jnp.broadcast_to(rates.T, (nfield, LANES))
     operands = [rates_wide, coefs, land_sea, *edges, *received, *corners]
     return pl.pallas_call(
         functools.partial(base_kernel, half),
-        grid=(nfield,),
+        grid=(nfield // PER_STEP,),
         in_specs=[
             pl.BlockSpec(memory_space=pltpu.SMEM),
             pl.BlockSpec(memory_space=pltpu.SMEM),
@@ -513,7 +529,7 @@
         ],
         out_specs=[
             field,
-            pl.BlockSpec((1, cells_x, cells_y), lambda f: (jnp.minimum(f, half - 1), 0, 0)),
+            early,
             pl.BlockSpec((6, cells_x, cells_y), lambda f: (0, 0, 0)),
         ],
         out_shape=[
@@ -525,20 +541,20 @@
             pltpu.VMEM((4 * nfield, cells_y), jnp.float32),
             pltpu.VMEM((4 * nfield, cells_x), jnp.float32),
         ],
-        compiler_params=pltpu.CompilerParams(vmem_limit_bytes=56 * 1024 * 1024),
+        compiler_params=pltpu.CompilerParams(vmem_limit_bytes=24 * 1024 * 1024),
         cost_estimate=pl.CostEstimate(
             flops=40 * state.size, bytes_accessed=8 * state.size, transcendentals=0
         ),
         name="base",
-    )(rates, mix, *operands, state)
+    )(rates, mix, *operands, *pinned(pltpu.HBM, state))
 
 
 def finish_kernel(first, with_x, gamma_ref, mix_ref, above, below, before, after, factors, recv,
                   left, right, *rest):
     tops, rest = (rest[:2], rest[2:]) if with_x else (None, rest)
     late, rest = (rest[:2], rest[2:]) if with_x else (None, rest)
-    early_base, odd_ref, rest = (*rest[:2], rest[2:]) if with_x else (None, None, rest)
-    base_ref, rest = rest[0], rest[1:]
+    early_base, rest = (rest[0], rest[1:]) if with_x else (None, rest)
+    odd_ref, base_ref, rest = rest[0], rest[1], rest[2:]
     new_ref, out_ref, done_ref = rest[-11:-8]
     base, wide, lines, sides, outer, base_sems, out_sems, outer_sems = rest[-8:]
     count, cells_x, cells_y = base.shape
@@ -569,18 +585,21 @@
     for f, i in outer_rows:
         outer_copy(f, i, False).start()
     done_ref[...] = jnp.zeros_like(done_ref)
+    def in_order(i, pair):
+        odd = odd_ref[0, i] == 1
+        in_odd, in_even = pair[0][...], pair[1][...]
+        return jnp.where(odd, in_even, in_odd), jnp.where(odd, in_odd, in_even)
+
     if with_x:
-        for i, (pair, kept, low_keep, high_keep) in enumerate(
-            ((tops, lines, above, below), ((left, right), sides, before, after))
-        ):
-            odd = odd_ref[0, i] == 1
-            in_odd, in_even = pair[0][...], pair[1][...]
-            kept[:count, :] = jnp.where(odd, in_even, in_odd) * low_keep[keep, :]
-            kept[count:, :] = jnp.where(odd, in_odd, in_even) * high_keep[keep, :]
+        top, bottom = in_order(0, tops)
+        lines[:count, :] = top * above[keep, :]
+        lines[count:, :] = bottom * below[keep, :]
+        late = in_order(0, late)
     else:
         lines[...] = jnp.zeros_like(lines)
-        sides[:count, :] = left[...] * before[keep, :]
-        sides[count:, :] = right[...] * after[keep, :]
+    left, right = in_order(1, (left, right))
+    sides[:count, :] = left * before[keep, :]
+    sides[count:, :] = right * after[keep, :]
     lane = lax.broadcasted_iota(jnp.int32, (STRIP, cells_y), 1)
 
     def one_field(f, carry):
@@ -631,7 +650,7 @@
 
 
 def finished(
-    first, new_state, remapped, recv, x_rims, y_rims, closing, gamma, mix, factors, received
+    first, new_state, remapped, recv, odd, x_rims, y_rims, closing, gamma, mix, factors, received
 ):
     count, cells_x, cells_y = recv.shape
     chan = gamma.shape[1]
@@ -639,14 +658,12 @@
     anywhere = pl.BlockSpec(memory_space=pl.ANY)
     operands = [gamma, mix, *received, factors, recv, *y_rims]
     if with_x:
-        late_rims, base_early, odd, late_done = closing
+        late_rims, base_early, late_done = closing
         operands += [*x_rims, *late_rims, base_early]
     scalars = pl.BlockSpec(memory_space=pltpu.SMEM)
     specs = [scalars] * 2 + [pl.BlockSpec(memory_space=pltpu.VMEM)] * (len(operands) - 2)
-    if with_x:
-        operands.append(odd)
-        specs.append(scalars)
-    specs.append(anywhere)
+    operands.append(odd)
+    specs += [scalars, anywhere]
     aliases = {len(operands): 0}
     operands.append(new_state)
     if remapped is not None:
@@ -698,8 +715,8 @@
         rows = rows.reshape(tiles, -1, half, width)
         return lax.all_to_all(rows, ("tx", "ty"), split_axis=0, concat_axis=0, tiled=True)
 
-    def add_up(odd, ids, rows, grant):
-        return summed(odd, ids, rows, tiles, capacity, half, cells_x, cells_y, width, grant)
+    def add_up(odd, ids, rows, space):
+        return summed(odd, ids, rows, tiles, capacity, half, cells_x, cells_y, width, space)
 
     late_in = exchanged(late)
     early = lax.ppermute(early, "comp", swap)
@@ -732,23 +749,23 @@
 
     ids_late = late_in[:, capacity, 0, :]
     ids_early = lax.ppermute(ids_late, "comp", swap)
-    recv_late, top, bottom, left, right = add_up(None, ids_late, late_in, 50)
+    odd = jnp.stack([lax.axis_index("tx"), lax.axis_index("ty")]).astype(jnp.int32)[None] & 1
+    recv_late, x_odd, x_even, y_odd, y_even = add_up(odd, ids_late, late_in, pltpu.HBM)
     recv_late = lax.ppermute(recv_late, "comp", swap)
     late_x = (
-        lax.ppermute(bottom, ("comp", "tx"), crossed("tx", 1)),
-        lax.ppermute(top, ("comp", "tx"), crossed("tx", -1)),
+        lax.ppermute(x_odd, ("comp", "tx"), crossed("tx", 1)),
+        lax.ppermute(x_even, ("comp", "tx"), crossed("tx", 0)),
     )
     late_y = (
-        lax.ppermute(right, ("comp", "ty"), crossed("ty", 1)),
-        lax.ppermute(left, ("comp", "ty"), crossed("ty", -1)),
+        lax.ppermute(y_odd, ("comp", "ty"), crossed("ty", 1)),
+        lax.ppermute(y_even, ("comp", "ty"), crossed("ty", 0)),
     )
     rest = (gamma, mix, factors, received)
     new_state, remapped, done = finished(
-        half, base, None, recv_late, None, late_y, None, *rest
+        half, base, None, recv_late, odd, None, late_y, None, *rest
     )
     early_in, done = lax.optimization_barrier((early_in, done))
-    odd = jnp.stack([lax.axis_index("tx"), lax.axis_index("ty")]).astype(jnp.int32)[None] & 1
-    recv_early, x_odd, x_even, y_odd, y_even = add_up(odd, ids_early, early_in, 16)
+    recv_early, x_odd, x_even, y_odd, y_even = add_up(odd, ids_early, early_in, pltpu.VMEM)
     early_x = (
         lax.ppermute(x_odd, "tx", neighbour_pairs(tx, 1)),
         lax.ppermute(x_even, "tx", neighbour_pairs(tx, 0)),
@@ -758,7 +775,7 @@
         lax.ppermute(y_even, "ty", neighbour_pairs(ty, 0)),
     )
     new_state, remapped, _ = finished(
-        0, new_state, remapped, recv_early, early_x, early_y, (late_x, base_early, odd, done), *rest
+        0, new_state, remapped, recv_early, odd, early_x, early_y, (late_x, base_early, done), *rest
     )
     return new_state, remapped
 

time: 140 us -> 138 us (0.986)
  waiting for transfers between devices: 22 us -> 28.1 us
  Pallas kernels: 49.5 us -> 44.7 us
  local copies, waits for them, and re-layouts: 4.93 us -> 1.85 us
    pallas_call x1, Pallas kernels: 16.5 us -> 12.1 us  [base_of(): pl.pallas_call(functools.partial(base_kernel, half), grid=(nfield // PER_...]
    ppermute x1, starting transfers between devices: 5.42 us -> 9.5 us  [body(): lax.ppermute(x_even, 'tx', neighbour_pairs(tx, 0))]
    all_to_all x2, waiting for transfers between devices: 5.33 us -> 8.02 us  [exchanged(): lax.all_to_all(rows, ('tx', 'ty'), split_axis=0, concat_axis=0, tiled=True)]
    unnamed x48 -> x12, local copies, waits for them, and re-layouts: 3.68 us -> 1.01 us
    ppermute x1, starting transfers between devices: 4.68 us -> 2.66 us  [body(): lax.ppermute(y_odd, 'ty', neighbour_pairs(ty, 1))]
  transfers between devices with their start and end apart: 19 -> 19, of which waited for: 4 -> 6; matrix products, arithmetic and copies ran while one was open for 1% -> 1% of each run, Pallas kernels for 25% -> 22%
where the time goes in v11:
time: 138 us; the launch traced here: 137 us
  starting transfers between devices  61.6 us (45%)
  Pallas kernels  44.7 us (32%)
  waiting for transfers between devices  28.1 us (20%)
  local copies, waits for them, and re-layouts  1.85 us (1%)
    all_to_all x2, starting transfers between devices, exchanged(): lax.all_to_all(rows, ('tx', 'ty'), split_axis=0, concat_axis=0, tiled=True)  19.8 us
    pallas_call x1, Pallas kernels, base_of(): pl.pallas_call(functools.partial(base_kernel, half), grid=(nfield // PER_...  12.1 us
    pallas_call x1, Pallas kernels, contributions(): pl.pallas_call(functools.partial(contribution_kernel, dims), in_specs=[pl...  10.8 us
    ppermute x1, waiting for transfers between devices, body(): early = lax.ppermute(early, 'comp', swap)  10 us
    ppermute x1, starting transfers between devices, body(): lax.ppermute(x_even, 'tx', neighbour_pairs(tx, 0))  9.5 us
    all_to_all x2, waiting for transfers between devices, exchanged(): lax.all_to_all(rows, ('tx', 'ty'), split_axis=0, concat_axis=0, tiled=True)  8.02 us
    ppermute x1, waiting for transfers between devices, body(): above = lax.ppermute(x_high, 'tx', shift_pairs(tx, 1))  7.72 us
    pallas_call x2, Pallas kernels, finished(): pl.pallas_call(functools.partial(finish_kernel, first, with_x), in_specs=...  7.55 us
  transfers between devices with their start and end apart: 19, of which 6 were waited for; matrix products, arithmetic and copies ran while one was open for 1% of the time, Pallas kernels for 22%

profile of v11, /device:TPU:1, one launch (start us, length us, event | category | flops | bytes accessed | tf_op | source)
XLA Modules:
  0.0 137.2 jit_solution(6730011897337442860)
XLA Ops:
  0.6 10.8 %contributions.1 = (f32[513,4,128]{2,1,0:T(4,128)}, f32[1040,4,128]{2,1,0:T(4,128)}) custom-call(s32[1,512]{1,0:T(1,128)} %src_ref.1, s32[1,512]{1,0:T(1,128)} %bitcast.14, s32[1,512]{1,0:T(1,128)} %blk_ref.1, f32[1,16,128,512]{3,2,1,0:T(8,128)} %state_ref.3, bf16[1,512,128,128]{3,2,1,0:T(8,128)(2,1)} %weights_ref.1), custom_call_target="tpu_custom_call" | custom-call | flops 134217728 | bytes 25296896 | tf_op jit(solution)/shard_map/contributions/pallas_call | solution.py:166
  11.4 0.0 copy-start.5
  11.5 0.0 copy-start
  11.5 0.0 copy-start.1
  11.5 7.5 %all-to-all-start = ((f32[16,65,4,128]{3,2,1,0:T(4,128)}), f32[16,65,4,128]{3,2,1,0:T(4,128)}, u32[]{:S(2)}, u32[]{:S(2)}) async-start(f32[16,65,4,128]{3,2,1,0:T(4,128)} %bitcast.4), calls=%async_computation | async-start | bytes 4259840 | tf_op jit(solution)/shard_map/all_to_all | solution.py:716
  19.0 1.2 collective-permute-start
  20.2 3.2 %edges.1 = (f32[40,512]{1,0:T(8,128)S(1)}, f32[40,512]{1,0:T(8,128)S(1)}, f32[40,128]{1,0:T(8,128)S(1)}, f32[40,128]{1,0:T(8,128)S(1)}) custom-call(f32[1,2]{1,0:T(1,128)S(1)} %broadcast_select_fusion.mix_ref, f32[1,16,128,512]{3,2,1,0:T(8,128)} %state_ref.3, f32[1,16,128,512]{3,2,1,0:T(8,128)} %state_ref.3, f32[1,16,128,512]{3,2,1,0:T(8,128)} %state_ref.3, ...), custom_call_target="tpu_custom_call" | custom-call | flops 1048576 | bytes 4194304 | tf_op jit(solution)/shard_map/edges/pallas_call | solution.py:430
  23.4 3.3 %collective-permute-start.1 = (f32[40,512]{1,0:T(8,128)S(1)}, f32[40,512]{1,0:T(8,128)S(1)}, u32[]{:S(2)}, u32[]{:S(2)}) collective-permute-start(f32[40,512]{1,0:T(8,128)S(1)} %get-tuple-element.37.x_high), channel_id=1, source_target_pairs={{0,4},{4,8},{8,12},{1,5},{5,9},{9,13},{2,6},{6,10},{10,14},{3,7},{... | collective-permute-start | bytes 245768 | tf_op jit(solution)/shard_map/ppermute | solution.py:733
  26.7 1.3 collective-permute-start.2
  28.0 3.9 %collective-permute-start.3 = (f32[40,128]{1,0:T(8,128)S(1)}, f32[40,128]{1,0:T(8,128)S(1)}, u32[]{:S(2)}, u32[]{:S(2)}) collective-permute-start(f32[40,128]{1,0:T(8,128)S(1)} %get-tuple-element.39.y_high), channel_id=1, source_target_pairs={{0,1},{1,2},{2,3},{4,5},{5,6},{6,7},{8,9},{9,10},{10,11},{12,13},{... | collective-permute-start | bytes 61448 | tf_op jit(solution)/shard_map/ppermute | solution.py:731
  31.9 1.9 %collective-permute-start.4 = (f32[40,128]{1,0:T(8,128)S(1)}, f32[40,128]{1,0:T(8,128)S(1)}, u32[]{:S(2)}, u32[]{:S(2)}) collective-permute-start(f32[40,128]{1,0:T(8,128)S(1)} %get-tuple-element.40.y_low), channel_id=1, source_target_pairs={{1,0},{2,1},{3,2},{5,4},{6,5},{7,6},{9,8},{10,9},{11,10},{13,12},{... | collective-permute-start | bytes 61448 | tf_op jit(solution)/shard_map/ppermute | solution.py:732
  33.9 10.0 %collective-permute-done.in_ref = f32[513,4,128]{2,1,0:T(4,128)S(1)} collective-permute-done((f32[513,4,128]{2,1,0:T(4,128)}, f32[513,4,128]{2,1,0:T(4,128)S(1)}, u32[]{:S(2)}, u32[]{:S(2)}) %collective-permute-start) | collective-permute-done | bytes 1050656 | tf_op jit(solution)/shard_map/ppermute | solution.py:722
  43.9 4.0 %place_in_slots.1 = f32[1024,4,128]{2,1,0:T(4,128)} custom-call(f32[513,4,128]{2,1,0:T(4,128)S(1)} %collective-permute-done.in_ref), custom_call_target="tpu_custom_call" | custom-call | flops 1050624 | bytes 3151872 | tf_op jit(solution)/shard_map/place_in_slots/pallas_call | solution.py:217
  47.9 0.0 collective-permute-done.3.left.before
  47.9 0.0 collective-permute-done.4.right.after
  48.0 7.7 %collective-permute-done.1.above = f32[40,512]{1,0:T(8,128)S(1)} collective-permute-done((f32[40,512]{1,0:T(8,128)S(1)}, f32[40,512]{1,0:T(8,128)S(1)}, u32[]{:S(2)}, u32[]{:S(2)}) %collective-permute-start.1) | collective-permute-done | bytes 81952 | tf_op jit(solution)/shard_map/ppermute | solution.py:733
  55.7 0.0 collective-permute-done.2.below
  55.7 5.4 %all-to-all-done = f32[16,65,4,128]{3,2,1,0:T(4,128)} async-done(((f32[16,65,4,128]{3,2,1,0:T(4,128)}), f32[16,65,4,128]{3,2,1,0:T(4,128)}, u32[]{:S(2)}, u32[]{:S(2)}) %all-to-all-start) | async-done | bytes 2129952 | tf_op jit(solution)/shard_map/all_to_all | solution.py:716
  61.1 12.3 %all-to-all-start.1 = ((f32[16,64,4,128]{3,2,1,0:T(4,128)}), f32[16,64,4,128]{3,2,1,0:T(4,128)}, u32[]{:S(2)}, u32[]{:S(2)}) async-start(f32[16,64,4,128]{3,2,1,0:T(4,128)} %bitcast.6), calls=%async_computation.1 | async-start | bytes 4194304 | tf_op jit(solution)/shard_map/all_to_all | solution.py:716
  73.4 0.1 add_and_fusion.refs_0_.rest_0_.rest_5_
  73.5 0.8 slice.20
  74.2 3.6 %sum_by_block.2 = (f32[4,128,512]{2,1,0:T(8,128)S(1)}, f32[4,512]{1,0:T(4,128)S(1)}, f32[4,512]{1,0:T(4,128)S(1)}, f32[4,128]{1,0:T(4,128)S(1)}, f32[4,128]{1,0:T(4,128)S(1)}) custom-call(s32[1,2]{1,0:T(1,128)S(1)} %add_and_fusion.refs_0_.rest_0_.rest_5_, f32[16,128]{1,0:T(8,128)S(1)} %bitcast.12, f32[4160,128]{1,0:T(8,128)} %bitcast.7.refs_2_), custom_call_target="tpu_custom_call" | custom-call | flops 1073741824 | bytes 3145728 | tf_op jit(solution)/shard_map/sum_by_block/pallas_call | solution.py:315
  77.8 1.3 collective-permute-start.8
  79.1 3.8 %collective-permute-start.5 = (f32[80,128]{1,0:T(8,128)S(1)}, f32[80,128]{1,0:T(8,128)S(1)}, u32[]{:S(2)}, u32[]{:S(2)}) collective-permute-start(f32[80,128]{1,0:T(8,128)S(1)} %pad_maximum_fusion), channel_id=1, source_target_pairs={{0,1},{1,2},{2,3},{4,5},{5,6},{6,7},{8,9},{9,10},{10,11},{12,13},{... | collective-permute-start | bytes 122888 | tf_op jit(solution)/shard_map/ppermute | solution.py:743
  83.0 1.9 %collective-permute-start.6 = (f32[80,128]{1,0:T(8,128)S(1)}, f32[80,128]{1,0:T(8,128)S(1)}, u32[]{:S(2)}, u32[]{:S(2)}) collective-permute-start(f32[80,128]{1,0:T(8,128)S(1)} %pad_maximum_fusion.1), channel_id=1, source_target_pairs={{1,0},{2,1},{3,2},{5,4},{6,5},{7,6},{9,8},{10,9},{11,10},{13,12},{... | collective-permute-start | bytes 122888 | tf_op jit(solution)/shard_map/ppermute | solution.py:744
  84.9 0.3 collective-permute-start.7
  85.2 4.8 %collective-permute-start.9 = (f32[4,128]{1,0:T(4,128)S(1)}, f32[4,128]{1,0:T(4,128)S(1)}, u32[]{:S(2)}, u32[]{:S(2)}) collective-permute-start(f32[4,128]{1,0:T(4,128)S(1)} %get-tuple-element.48), channel_id=1, source_target_pairs={{1,18},{2,17},{17,2},{18,1},{5,22},{6,21},{21,6},{22,5},{9,26},{10... | collective-permute-start | bytes 6152 | tf_op jit(solution)/shard_map/ppermute | solution.py:760
  90.1 0.0 collective-permute-done.5.corners_left
  90.1 0.1 collective-permute-start.10
  90.2 0.0 collective-permute-done.6.corners_right
  90.2 0.1 broadcast_in_dim.9.rates_ref
  90.2 12.1 %base.1 = (f32[1,16,128,512]{3,2,1,0:T(8,128)}, f32[4,128,512]{2,1,0:T(8,128)S(1)}, f32[6,128,512]{2,1,0:T(8,128)S(1)}) custom-call(f32[1,16]{1,0:T(1,128)S(1)} %get-tuple-element.71.rate_ref, f32[1,2]{1,0:T(1,128)S(1)} %broadcast_select_fusion.mix_ref, f32[16,128]{1,0:T(8,128)S(1)} %broadcast_in_dim.9.rates_ref, f32[1,3,128,512]{3,2,1,0:T(8,128)S(1)} %copy-done, ...), custom_call_target="tpu_custom_call" | custom-call | flops 41943040 | bytes 8388608 | tf_op jit(solution)/shard_map/base/pallas_call | solution.py:521
  102.3 1.0 copy-done.2
  103.3 0.6 collective-permute-start.15
  103.9 0.2 collective-permute-done.9.left
  104.1 4.4 %collective-permute-start.16 = (f32[4,512]{1,0:T(4,128)S(1)}, f32[4,512]{1,0:T(4,128)S(1)}, u32[]{:S(2)}, u32[]{:S(2)}) collective-permute-start(f32[4,512]{1,0:T(4,128)S(1)} %get-tuple-element.59), channel_id=1, source_target_pairs={{0,20},{8,28},{4,16},{12,24},{16,4},{24,12},{20,0},{28,8},{1,21},{... | collective-permute-start | bytes 24584 | tf_op jit(solution)/shard_map/ppermute | solution.py:757
  108.5 3.9 %finish.2 = (f32[1,16,128,512]{3,2,1,0:T(8,128)}, f32[1,8,128,512]{3,2,1,0:T(8,128)}, f32[8,128]{1,0:T(8,128)S(1)}) custom-call(f32[1,8]{1,0:T(1,128)S(1)} %copy-done.4, f32[1,2]{1,0:T(1,128)S(1)} %broadcast_select_fusion.mix_ref, f32[40,512]{1,0:T(8,128)S(1)} %collective-permute-done.1.above, ...), custom_call_target="tpu_custom_call", output_to_operand_aliasing={{0}: (11, {})} | custom-call | flops 5242880 | bytes 5242880 | tf_op jit(solution)/shard_map/finish/pallas_call | solution.py:673
  112.5 2.6 %all-to-all-done.1 = f32[16,64,4,128]{3,2,1,0:T(4,128)} async-done(((f32[16,64,4,128]{3,2,1,0:T(4,128)}), f32[16,64,4,128]{3,2,1,0:T(4,128)}, u32[]{:S(2)}, u32[]{:S(2)}) %all-to-all-start.1) | async-done | bytes 2097184 | tf_op jit(solution)/shard_map/all_to_all | solution.py:716
  115.0 0.0 collective-permute-done.7.refs_1_
  115.0 3.4 %sum_by_block.3 = (f32[4,128,512]{2,1,0:T(8,128)S(1)}, f32[4,512]{1,0:T(4,128)S(1)}, f32[4,512]{1,0:T(4,128)S(1)}, f32[4,128]{1,0:T(4,128)S(1)}, f32[4,128]{1,0:T(4,128)S(1)}) custom-call(s32[1,2]{1,0:T(1,128)S(1)} %add_and_fusion.refs_0_.rest_0_.rest_5_, f32[16,128]{1,0:T(8,128)S(1)} %collective-permute-done.7.refs_1_, f32[4096,128]{1,0:T(8,128)} %bitcast.8.refs_2_), custom_call_target="tpu_custom_call" | custom-call | flops 1073741824 | bytes 3145728 | tf_op jit(solution)/shard_map/sum_by_block/pallas_call | solution.py:315
  118.5 0.7 collective-permute-start.13
  119.1 9.5 %collective-permute-start.14 = (f32[4,512]{1,0:T(4,128)S(1)}, f32[4,512]{1,0:T(4,128)S(1)}, u32[]{:S(2)}, u32[]{:S(2)}) collective-permute-start(f32[4,512]{1,0:T(4,128)S(1)} %get-tuple-element.57), channel_id=1, source_target_pairs={{0,4},{8,12},{4,0},{12,8},{1,5},{9,13},{5,1},{13,9},{2,6},{10,14},... | collective-permute-start | bytes 24584 | tf_op jit(solution)/shard_map/ppermute | solution.py:771
  128.6 2.7 %collective-permute-start.11 = (f32[4,128]{1,0:T(4,128)S(1)}, f32[4,128]{1,0:T(4,128)S(1)}, u32[]{:S(2)}, u32[]{:S(2)}) collective-permute-start(f32[4,128]{1,0:T(4,128)S(1)} %get-tuple-element.54), channel_id=1, source_target_pairs={{1,2},{2,1},{5,6},{6,5},{9,10},{10,9},{13,14},{14,13},{17,18},{18,... | collective-permute-start | bytes 6152 | tf_op jit(solution)/shard_map/ppermute | solution.py:774
  131.3 0.0 collective-permute-done.15.rest_2_
  131.3 0.1 collective-permute-start.12
  131.4 2.1 %collective-permute-done.11.left = f32[4,128]{1,0:T(4,128)S(1)} collective-permute-done((f32[4,128]{1,0:T(4,128)S(1)}, f32[4,128]{1,0:T(4,128)S(1)}, u32[]{:S(2)}, u32[]{:S(2)}) %collective-permute-start.11) | collective-permute-done | bytes 2080 | tf_op jit(solution)/shard_map/ppermute | solution.py:774
  133.5 0.0 collective-permute-done.12.right
  133.5 3.6 %finish.3 = (f32[1,16,128,512]{3,2,1,0:T(8,128)}, f32[1,8,128,512]{3,2,1,0:T(8,128)}, f32[8,128]{1,0:T(8,128)}) custom-call(f32[1,8]{1,0:T(1,128)S(1)} %copy-done.4, f32[1,2]{1,0:T(1,128)S(1)} %broadcast_select_fusion.mix_ref, f32[40,512]{1,0:T(8,128)S(1)} %collective-permute-done.1.above, ...), custom_call_target="tpu_custom_call", output_to_operand_aliasing={{0}: (16, {}), {1}: (17, {})} | custom-call | flops 5242880 | bytes 5242880 | tf_op jit(solution)/shard_map/finish/pallas_call | solution.py:673
  (18 shorter events, 0.1 us)
Async XLA Ops:
  11.4 8.7 %copy-start.5 = (f32[1,2]{1,0:T(1,128)S(1)}, f32[1,2]{1,0:T(1,128)}, u32[]{:S(2)}) copy-start(f32[1,2]{1,0:T(1,128)} %constant.23.clone) | copy-start | bytes 28
  11.5 8.7 %copy-start = (f32[1,3,128,512]{3,2,1,0:T(8,128)S(1)}, f32[1,3,128,512]{3,2,1,0:T(8,128)}, u32[]{:S(2)}) copy-start(f32[1,3,128,512]{3,2,1,0:T(8,128)} %coefs_ref.1) | copy-start | bytes 2359300
  11.5 8.7 %copy-start.1 = (s32[128,512]{1,0:T(8,128)S(1)}, s32[128,512]{1,0:T(8,128)}, u32[]{:S(2)}) copy-start(s32[128,512]{1,0:T(8,128)} %land_ref) | copy-start | bytes 786436
  11.5 49.6 %all-to-all-start = ((f32[16,65,4,128]{3,2,1,0:T(4,128)}), f32[16,65,4,128]{3,2,1,0:T(4,128)}, u32[]{:S(2)}, u32[]{:S(2)}) async-start(f32[16,65,4,128]{3,2,1,0:T(4,128)} %bitcast.4), calls=%async_computation | async-start | bytes 4259840 | tf_op jit(solution)/shard_map/all_to_all | solution.py:716
  19.0 24.9 %collective-permute-start = (f32[513,4,128]{2,1,0:T(4,128)}, f32[513,4,128]{2,1,0:T(4,128)S(1)}, u32[]{:S(2)}, u32[]{:S(2)}) collective-permute-start(f32[513,4,128]{2,1,0:T(4,128)} %get-tuple-element.34), channel_id=1, source_target_pairs={{0,16},{16,0},{1,17},{17,1},{2,18},{18,2},{3,19},{19,3},{4,20},{20... | collective-permute-start | bytes 3151880 | tf_op jit(solution)/shard_map/ppermute | solution.py:722
  23.4 32.2 %collective-permute-start.1 = (f32[40,512]{1,0:T(8,128)S(1)}, f32[40,512]{1,0:T(8,128)S(1)}, u32[]{:S(2)}, u32[]{:S(2)}) collective-permute-start(f32[40,512]{1,0:T(8,128)S(1)} %get-tuple-element.37.x_high), channel_id=1, source_target_pairs={{0,4},{4,8},{8,12},{1,5},{5,9},{9,13},{2,6},{6,10},{10,14},{3,7},{... | collective-permute-start | bytes 245768 | tf_op jit(solution)/shard_map/ppermute | solution.py:733
  26.7 28.9 %collective-permute-start.2 = (f32[40,512]{1,0:T(8,128)S(1)}, f32[40,512]{1,0:T(8,128)S(1)}, u32[]{:S(2)}, u32[]{:S(2)}) collective-permute-start(f32[40,512]{1,0:T(8,128)S(1)} %get-tuple-element.38.x_low), channel_id=1, source_target_pairs={{4,0},{8,4},{12,8},{5,1},{9,5},{13,9},{6,2},{10,6},{14,10},{7,3},{... | collective-permute-start | bytes 245768 | tf_op jit(solution)/shard_map/ppermute | solution.py:734
  28.0 19.9 %collective-permute-start.3 = (f32[40,128]{1,0:T(8,128)S(1)}, f32[40,128]{1,0:T(8,128)S(1)}, u32[]{:S(2)}, u32[]{:S(2)}) collective-permute-start(f32[40,128]{1,0:T(8,128)S(1)} %get-tuple-element.39.y_high), channel_id=1, source_target_pairs={{0,1},{1,2},{2,3},{4,5},{5,6},{6,7},{8,9},{9,10},{10,11},{12,13},{... | collective-permute-start | bytes 61448 | tf_op jit(solution)/shard_map/ppermute | solution.py:731
  31.9 16.0 %collective-permute-start.4 = (f32[40,128]{1,0:T(8,128)S(1)}, f32[40,128]{1,0:T(8,128)S(1)}, u32[]{:S(2)}, u32[]{:S(2)}) collective-permute-start(f32[40,128]{1,0:T(8,128)S(1)} %get-tuple-element.40.y_low), channel_id=1, source_target_pairs={{1,0},{2,1},{3,2},{5,4},{6,5},{7,6},{9,8},{10,9},{11,10},{13,12},{... | collective-permute-start | bytes 61448 | tf_op jit(solution)/shard_map/ppermute | solution.py:732
  61.1 53.9 %all-to-all-start.1 = ((f32[16,64,4,128]{3,2,1,0:T(4,128)}), f32[16,64,4,128]{3,2,1,0:T(4,128)}, u32[]{:S(2)}, u32[]{:S(2)}) async-start(f32[16,64,4,128]{3,2,1,0:T(4,128)} %bitcast.6), calls=%async_computation.1 | async-start | bytes 4194304 | tf_op jit(solution)/shard_map/all_to_all | solution.py:716
  74.2 11.0 %copy-start.4 = (f32[1,8]{1,0:T(1,128)S(1)}, f32[1,8]{1,0:T(1,128)}, u32[]{:S(2)}) copy-start(f32[1,8]{1,0:T(1,128)} %gamma_ref.3) | copy-start | bytes 100
  77.8 30.7 %collective-permute-start.8 = (f32[4,128,512]{2,1,0:T(8,128)S(1)}, f32[4,128,512]{2,1,0:T(8,128)S(1)}, u32[]{:S(2)}, u32[]{:S(2)}) collective-permute-start(f32[4,128,512]{2,1,0:T(8,128)S(1)} %get-tuple-element.47), channel_id=1, source_target_pairs={{0,16},{16,0},{1,17},{17,1},{2,18},{18,2},{3,19},{19,3},{4,20},{20... | collective-permute-start | bytes 3145736 | tf_op jit(solution)/shard_map/ppermute | solution.py:754
  79.1 10.9 %collective-permute-start.5 = (f32[80,128]{1,0:T(8,128)S(1)}, f32[80,128]{1,0:T(8,128)S(1)}, u32[]{:S(2)}, u32[]{:S(2)}) collective-permute-start(f32[80,128]{1,0:T(8,128)S(1)} %pad_maximum_fusion), channel_id=1, source_target_pairs={{0,1},{1,2},{2,3},{4,5},{5,6},{6,7},{8,9},{9,10},{10,11},{12,13},{... | collective-permute-start | bytes 122888 | tf_op jit(solution)/shard_map/ppermute | solution.py:743
  83.0 7.2 %collective-permute-start.6 = (f32[80,128]{1,0:T(8,128)S(1)}, f32[80,128]{1,0:T(8,128)S(1)}, u32[]{:S(2)}, u32[]{:S(2)}) collective-permute-start(f32[80,128]{1,0:T(8,128)S(1)} %pad_maximum_fusion.1), channel_id=1, source_target_pairs={{1,0},{2,1},{3,2},{5,4},{6,5},{7,6},{9,8},{10,9},{11,10},{13,12},{... | collective-permute-start | bytes 122888 | tf_op jit(solution)/shard_map/ppermute | solution.py:744
  84.9 30.1 %collective-permute-start.7 = (f32[16,128]{1,0:T(8,128)S(1)}, f32[16,128]{1,0:T(8,128)S(1)}, u32[]{:S(2)}, u32[]{:S(2)}) collective-permute-start(f32[16,128]{1,0:T(8,128)S(1)} %bitcast.13), channel_id=1, source_target_pairs={{0,16},{16,0},{1,17},{17,1},{2,18},{18,2},{3,19},{19,3},{4,20},{20... | collective-permute-start | bytes 24584 | tf_op jit(solution)/shard_map/ppermute | solution.py:751
  85.2 18.9 %collective-permute-start.9 = (f32[4,128]{1,0:T(4,128)S(1)}, f32[4,128]{1,0:T(4,128)S(1)}, u32[]{:S(2)}, u32[]{:S(2)}) collective-permute-start(f32[4,128]{1,0:T(4,128)S(1)} %get-tuple-element.48), channel_id=1, source_target_pairs={{1,18},{2,17},{17,2},{18,1},{5,22},{6,21},{21,6},{22,5},{9,26},{10... | collective-permute-start | bytes 6152 | tf_op jit(solution)/shard_map/ppermute | solution.py:760
  90.1 18.5 %collective-permute-start.10 = (f32[4,128]{1,0:T(4,128)S(1)}, f32[4,128]{1,0:T(4,128)S(1)}, u32[]{:S(2)}, u32[]{:S(2)}) collective-permute-start(f32[4,128]{1,0:T(4,128)S(1)} %get-tuple-element.49), channel_id=1, source_target_pairs={{0,17},{2,19},{1,16},{3,18},{16,1},{18,3},{17,0},{19,2},{4,21},{6,... | collective-permute-start | bytes 6152 | tf_op jit(solution)/shard_map/ppermute | solution.py:761
  102.3 1.0 copy-start.2
  103.3 28.0 %collective-permute-start.15 = (f32[4,512]{1,0:T(4,128)S(1)}, f32[4,512]{1,0:T(4,128)S(1)}, u32[]{:S(2)}, u32[]{:S(2)}) collective-permute-start(f32[4,512]{1,0:T(4,128)S(1)} %get-tuple-element.58), channel_id=1, source_target_pairs={{4,24},{8,20},{20,8},{24,4},{5,25},{9,21},{21,9},{25,5},{6,26},{10... | collective-permute-start | bytes 24584 | tf_op jit(solution)/shard_map/ppermute | solution.py:756
  104.1 27.3 %collective-permute-start.16 = (f32[4,512]{1,0:T(4,128)S(1)}, f32[4,512]{1,0:T(4,128)S(1)}, u32[]{:S(2)}, u32[]{:S(2)}) collective-permute-start(f32[4,512]{1,0:T(4,128)S(1)} %get-tuple-element.59), channel_id=1, source_target_pairs={{0,20},{8,28},{4,16},{12,24},{16,4},{24,12},{20,0},{28,8},{1,21},{... | collective-permute-start | bytes 24584 | tf_op jit(solution)/shard_map/ppermute | solution.py:757
  112.4 21.1 %copy-start.3 = (f32[4,128,512]{2,1,0:T(8,128)S(1)}, f32[4,128,512]{2,1,0:T(8,128)}, u32[]{:S(2)}) copy-start(f32[4,128,512]{2,1,0:T(8,128)} %copy-done.2) | copy-start | bytes 3145732
  118.5 15.1 %collective-permute-start.13 = (f32[4,512]{1,0:T(4,128)S(1)}, f32[4,512]{1,0:T(4,128)S(1)}, u32[]{:S(2)}, u32[]{:S(2)}) collective-permute-start(f32[4,512]{1,0:T(4,128)S(1)} %get-tuple-element.56), channel_id=1, source_target_pairs={{4,8},{8,4},{5,9},{9,5},{6,10},{10,6},{7,11},{11,7},{20,24},{24,20... | collective-permute-start | bytes 24584 | tf_op jit(solution)/shard_map/ppermute | solution.py:770
  119.1 14.4 %collective-permute-start.14 = (f32[4,512]{1,0:T(4,128)S(1)}, f32[4,512]{1,0:T(4,128)S(1)}, u32[]{:S(2)}, u32[]{:S(2)}) collective-permute-start(f32[4,512]{1,0:T(4,128)S(1)} %get-tuple-element.57), channel_id=1, source_target_pairs={{0,4},{8,12},{4,0},{12,8},{1,5},{9,13},{5,1},{13,9},{2,6},{10,14},... | collective-permute-start | bytes 24584 | tf_op jit(solution)/shard_map/ppermute | solution.py:771
  128.6 4.9 %collective-permute-start.11 = (f32[4,128]{1,0:T(4,128)S(1)}, f32[4,128]{1,0:T(4,128)S(1)}, u32[]{:S(2)}, u32[]{:S(2)}) collective-permute-start(f32[4,128]{1,0:T(4,128)S(1)} %get-tuple-element.54), channel_id=1, source_target_pairs={{1,2},{2,1},{5,6},{6,5},{9,10},{10,9},{13,14},{14,13},{17,18},{18,... | collective-permute-start | bytes 6152 | tf_op jit(solution)/shard_map/ppermute | solution.py:774
  131.3 2.2 %collective-permute-start.12 = (f32[4,128]{1,0:T(4,128)S(1)}, f32[4,128]{1,0:T(4,128)S(1)}, u32[]{:S(2)}, u32[]{:S(2)}) collective-permute-start(f32[4,128]{1,0:T(4,128)S(1)} %get-tuple-element.55), channel_id=1, source_target_pairs={{0,1},{2,3},{1,0},{3,2},{4,5},{6,7},{5,4},{7,6},{8,9},{10,11},{9,8... | collective-permute-start | bytes 6152 | tf_op jit(solution)/shard_map/ppermute | solution.py:775

commit v12 on v11

--- a/solution.py
+++ b/solution.py
@@ -230,11 +230,8 @@
     )(rows)
 
 
-def sum_kernel(dims, paired, *refs):
-    odd_ref, refs = (refs[0], refs[1:]) if paired else (None, refs)
-    ids_ref, rows_ref, out_ref, x0_ref, x1_ref, y0_ref, y1_ref = refs[:7]
-    pick, high, low, *copied = refs[7:]
-    in_ref, row_sems = copied if copied else (rows_ref, None)
+def sum_kernel(dims, odd_ref, ids_ref, rows_ref, out_ref, x0_ref, x1_ref, y0_ref, y1_ref,
+               pick, high, low, in_ref, row_sems):
     tiles, capacity, fields, cells_x, cells_y, width = dims
     parts = cells_y // width
     group = LANES // capacity
@@ -244,20 +241,21 @@
         some = pl.ds(k * group * stride, group * stride)
         return pltpu.make_async_copy(rows_ref.at[some, :], in_ref.at[some, :], row_sems.at[k])
 
-    for k in range(tiles // group if copied else 0):
+    for k in range(tiles // group):
         rows_copy(k).start()
     block_of = lax.broadcasted_iota(jnp.int32, (cells_x * parts, LANES), 0)
     block_of = (block_of % cells_x) * parts + block_of // cells_x
     block_of = block_of.astype(jnp.float32)
     lane = lax.broadcasted_iota(jnp.int32, (1, LANES), 1)
     for k in range(tiles // group):
-        if copied:
-            rows_copy(k).wait()
         ids = None
         for i in range(group):
-            source = k * group + i
-            row = ids_ref[pl.ds(source, 1), :]
+            row = ids_ref[pl.ds(k * group + i, 1), :]
             ids = row if ids is None else jnp.where(lane // capacity == i, row, ids)
+        pick[:, pl.ds(k * LANES, LANES)] = (block_of == ids).astype(jnp.bfloat16)
+    for k in range(tiles // group):
+        rows_copy(k).wait()
+        for source in range(k * group, (k + 1) * group):
             for f in range(fields):
                 x = in_ref[pl.ds(source * stride + f, capacity, stride=fields), :]
                 rounded = x.astype(jnp.bfloat16)
@@ -267,12 +265,9 @@
                 )
                 high[place] = rounded
                 low[place] = (x - rounded.astype(jnp.float32)).astype(jnp.bfloat16)
-        pick[:, pl.ds(k * LANES, LANES)] = (block_of == ids).astype(jnp.bfloat16)
 
     def in_order(i, low_rim, high_rim):
-        if not paired:
-            return low_rim, high_rim
-        odd = odd_ref[0, i] == 1
+        odd = odd_ref[i : i + 1, :] == 1.0
         return jnp.where(odd, high_rim, low_rim), jnp.where(odd, low_rim, high_rim)
 
     columns = {}
@@ -293,16 +288,9 @@
         y0_ref[pl.ds(f, 1), :], y1_ref[pl.ds(f, 1), :] = rims
 
 
-def summed(odd, ids, rows, tiles, capacity, fields, cells_x, cells_y, width, space):
+def summed(odd, ids, rows, tiles, capacity, fields, cells_x, cells_y, width):
     dims = (tiles, capacity, fields, cells_x, cells_y, width)
     rows = rows.reshape(-1, width)
-    flags = [] if odd is None else [pl.BlockSpec(memory_space=pltpu.SMEM)]
-    copied = []
-    if space is pltpu.HBM:
-        copied = [
-            pltpu.VMEM(rows.shape, jnp.float32),
-            pltpu.SemaphoreType.DMA((tiles * capacity // LANES,)),
-        ]
     slots = tiles * capacity
     blocks = cells_x * cells_y // width
     shapes = [
@@ -313,16 +301,17 @@
         (fields, cells_x),
     ]
     return pl.pallas_call(
-        functools.partial(sum_kernel, dims, odd is not None),
-        in_specs=flags
-        + [pl.BlockSpec(memory_space=pltpu.VMEM), pl.BlockSpec(memory_space=space)],
+        functools.partial(sum_kernel, dims),
+        in_specs=[pl.BlockSpec(memory_space=pltpu.VMEM)] * 2
+        + [pl.BlockSpec(memory_space=pltpu.HBM)],
         out_shape=[jax.ShapeDtypeStruct(shape, jnp.float32) for shape in shapes],
         scratch_shapes=[
             pltpu.VMEM((blocks, slots), jnp.bfloat16),
             pltpu.VMEM((slots, fields * width), jnp.bfloat16),
             pltpu.VMEM((slots, fields * width), jnp.bfloat16),
-        ]
-        + copied,
+            pltpu.VMEM(rows.shape, jnp.float32),
+            pltpu.SemaphoreType.DMA((tiles * capacity // LANES,)),
+        ],
         compiler_params=pltpu.CompilerParams(vmem_limit_bytes=24 * 1024 * 1024),
         cost_estimate=pl.CostEstimate(
             flops=4 * blocks * slots * fields * width,
@@ -330,7 +319,7 @@
             transcendentals=0,
         ),
         name="sum_by_block",
-    )(*([] if odd is None else [odd]), ids, *pinned(space, rows))
+    )(odd, ids, *pinned(pltpu.HBM, rows))
 
 
 def stencil_factors(coefs, keep):
@@ -715,8 +704,8 @@
         rows = rows.reshape(tiles, -1, half, width)
         return lax.all_to_all(rows, ("tx", "ty"), split_axis=0, concat_axis=0, tiled=True)
 
-    def add_up(odd, ids, rows, space):
-        return summed(odd, ids, rows, tiles, capacity, half, cells_x, cells_y, width, space)
+    def add_up(odd, ids, rows):
+        return summed(odd, ids, rows, tiles, capacity, half, cells_x, cells_y, width)
 
     late_in = exchanged(late)
     early = lax.ppermute(early, "comp", swap)
@@ -750,7 +739,8 @@
     ids_late = late_in[:, capacity, 0, :]
     ids_early = lax.ppermute(ids_late, "comp", swap)
     odd = jnp.stack([lax.axis_index("tx"), lax.axis_index("ty")]).astype(jnp.int32)[None] & 1
-    recv_late, x_odd, x_even, y_odd, y_even = add_up(odd, ids_late, late_in, pltpu.HBM)
+    odd_lanes = jnp.broadcast_to(odd.T.astype(jnp.float32), (2, LANES))
+    recv_late, x_odd, x_even, y_odd, y_even = add_up(odd_lanes, ids_late, late_in)
     recv_late = lax.ppermute(recv_late, "comp", swap)
     late_x = (
         lax.ppermute(x_odd, ("comp", "tx"), crossed("tx", 1)),
@@ -765,7 +755,7 @@
         half, base, None, recv_late, odd, None, late_y, None, *rest
     )
     early_in, done = lax.optimization_barrier((early_in, done))
-    recv_early, x_odd, x_even, y_odd, y_even = add_up(odd, ids_early, early_in, pltpu.VMEM)
+    recv_early, x_odd, x_even, y_odd, y_even = add_up(odd_lanes, ids_early, early_in)
     early_x = (
         lax.ppermute(x_odd, "tx", neighbour_pairs(tx, 1)),
         lax.ppermute(x_even, "tx", neighbour_pairs(tx, 0)),

time: 138 us -> 138 us (level)
  transfers between devices with their start and end apart: 19 -> 19, of which waited for: 6 -> 6; matrix products, arithmetic and copies ran while one was open for 1% -> 1% of each run, Pallas kernels for 22% -> 21%
where the time goes in v12:
time: 138 us; the launch traced here: 137 us
  starting transfers between devices  61.6 us (45%)
  Pallas kernels  43.7 us (32%)
  waiting for transfers between devices  28.5 us (21%)
  local copies, waits for them, and re-layouts  1.92 us (1%)
    all_to_all x2, starting transfers between devices, exchanged(): lax.all_to_all(rows, ('tx', 'ty'), split_axis=0, concat_axis=0, tiled=True)  19.8 us
    pallas_call x1, Pallas kernels, base_of(): pl.pallas_call(functools.partial(base_kernel, half), grid=(nfield // PER_...  12.1 us
    pallas_call x1, Pallas kernels, contributions(): pl.pallas_call(functools.partial(contribution_kernel, dims), in_specs=[pl...  10.8 us
    ppermute x1, waiting for transfers between devices, body(): early = lax.ppermute(early, 'comp', swap)  10 us
    ppermute x1, starting transfers between devices, body(): lax.ppermute(x_even, 'tx', neighbour_pairs(tx, 0))  9.55 us
    all_to_all x2, waiting for transfers between devices, exchanged(): lax.all_to_all(rows, ('tx', 'ty'), split_axis=0, concat_axis=0, tiled=True)  8.37 us
    ppermute x1, waiting for transfers between devices, body(): above = lax.ppermute(x_high, 'tx', shift_pairs(tx, 1))  7.72 us
    pallas_call x2, Pallas kernels, finished(): pl.pallas_call(functools.partial(finish_kernel, first, with_x), in_specs=...  7.55 us
  transfers between devices with their start and end apart: 19, of which 6 were waited for; matrix products, arithmetic and copies ran while one was open for 1% of the time, Pallas kernels for 21%

profile of v12, /device:TPU:1, one launch (start us, length us, event | category | flops | bytes accessed | tf_op | source)
XLA Modules:
  0.0 136.8 jit_solution(16848360075522378722)
XLA Ops:
  0.6 10.8 %contributions.1 = (f32[513,4,128]{2,1,0:T(4,128)}, f32[1040,4,128]{2,1,0:T(4,128)}) custom-call(s32[1,512]{1,0:T(1,128)} %src_ref.1, s32[1,512]{1,0:T(1,128)} %bitcast.16, s32[1,512]{1,0:T(1,128)} %blk_ref.1, f32[1,16,128,512]{3,2,1,0:T(8,128)} %state_ref.3, bf16[1,512,128,128]{3,2,1,0:T(8,128)(2,1)} %weights_ref.1), custom_call_target="tpu_custom_call" | custom-call | flops 134217728 | bytes 25296896 | tf_op jit(solution)/shard_map/contributions/pallas_call | solution.py:166
  11.4 0.0 copy-start.5
  11.5 0.0 copy-start
  11.5 0.0 copy-start.1
  11.5 7.5 %all-to-all-start = ((f32[16,65,4,128]{3,2,1,0:T(4,128)}), f32[16,65,4,128]{3,2,1,0:T(4,128)}, u32[]{:S(2)}, u32[]{:S(2)}) async-start(f32[16,65,4,128]{3,2,1,0:T(4,128)} %bitcast.4), calls=%async_computation | async-start | bytes 4259840 | tf_op jit(solution)/shard_map/all_to_all | solution.py:705
  19.0 1.2 collective-permute-start
  20.2 3.2 %edges.1 = (f32[40,512]{1,0:T(8,128)S(1)}, f32[40,512]{1,0:T(8,128)S(1)}, f32[40,128]{1,0:T(8,128)S(1)}, f32[40,128]{1,0:T(8,128)S(1)}) custom-call(f32[1,2]{1,0:T(1,128)S(1)} %broadcast_select_fusion.mix_ref, f32[1,16,128,512]{3,2,1,0:T(8,128)} %state_ref.3, f32[1,16,128,512]{3,2,1,0:T(8,128)} %state_ref.3, f32[1,16,128,512]{3,2,1,0:T(8,128)} %state_ref.3, ...), custom_call_target="tpu_custom_call" | custom-call | flops 1048576 | bytes 4194304 | tf_op jit(solution)/shard_map/edges/pallas_call | solution.py:419
  23.4 3.3 %collective-permute-start.1 = (f32[40,512]{1,0:T(8,128)S(1)}, f32[40,512]{1,0:T(8,128)S(1)}, u32[]{:S(2)}, u32[]{:S(2)}) collective-permute-start(f32[40,512]{1,0:T(8,128)S(1)} %get-tuple-element.37.x_high), channel_id=1, source_target_pairs={{0,4},{4,8},{8,12},{1,5},{5,9},{9,13},{2,6},{6,10},{10,14},{3,7},{... | collective-permute-start | bytes 245768 | tf_op jit(solution)/shard_map/ppermute | solution.py:722
  26.7 1.3 collective-permute-start.2
  28.0 3.9 %collective-permute-start.3 = (f32[40,128]{1,0:T(8,128)S(1)}, f32[40,128]{1,0:T(8,128)S(1)}, u32[]{:S(2)}, u32[]{:S(2)}) collective-permute-start(f32[40,128]{1,0:T(8,128)S(1)} %get-tuple-element.39.y_high), channel_id=1, source_target_pairs={{0,1},{1,2},{2,3},{4,5},{5,6},{6,7},{8,9},{9,10},{10,11},{12,13},{... | collective-permute-start | bytes 61448 | tf_op jit(solution)/shard_map/ppermute | solution.py:720
  31.9 1.9 %collective-permute-start.4 = (f32[40,128]{1,0:T(8,128)S(1)}, f32[40,128]{1,0:T(8,128)S(1)}, u32[]{:S(2)}, u32[]{:S(2)}) collective-permute-start(f32[40,128]{1,0:T(8,128)S(1)} %get-tuple-element.40.y_low), channel_id=1, source_target_pairs={{1,0},{2,1},{3,2},{5,4},{6,5},{7,6},{9,8},{10,9},{11,10},{13,12},{... | collective-permute-start | bytes 61448 | tf_op jit(solution)/shard_map/ppermute | solution.py:721
  33.9 10.0 %collective-permute-done.in_ref = f32[513,4,128]{2,1,0:T(4,128)S(1)} collective-permute-done((f32[513,4,128]{2,1,0:T(4,128)}, f32[513,4,128]{2,1,0:T(4,128)S(1)}, u32[]{:S(2)}, u32[]{:S(2)}) %collective-permute-start) | collective-permute-done | bytes 1050656 | tf_op jit(solution)/shard_map/ppermute | solution.py:711
  43.9 4.0 %place_in_slots.1 = f32[1024,4,128]{2,1,0:T(4,128)} custom-call(f32[513,4,128]{2,1,0:T(4,128)S(1)} %collective-permute-done.in_ref), custom_call_target="tpu_custom_call" | custom-call | flops 1050624 | bytes 3151872 | tf_op jit(solution)/shard_map/place_in_slots/pallas_call | solution.py:217
  47.9 0.0 collective-permute-done.4.right.after
  47.9 7.7 %collective-permute-done.1.above = f32[40,512]{1,0:T(8,128)S(1)} collective-permute-done((f32[40,512]{1,0:T(8,128)S(1)}, f32[40,512]{1,0:T(8,128)S(1)}, u32[]{:S(2)}, u32[]{:S(2)}) %collective-permute-start.1) | collective-permute-done | bytes 81952 | tf_op jit(solution)/shard_map/ppermute | solution.py:722
  55.7 0.0 collective-permute-done.2.below
  55.7 5.4 %all-to-all-done = f32[16,65,4,128]{3,2,1,0:T(4,128)} async-done(((f32[16,65,4,128]{3,2,1,0:T(4,128)}), f32[16,65,4,128]{3,2,1,0:T(4,128)}, u32[]{:S(2)}, u32[]{:S(2)}) %all-to-all-start) | async-done | bytes 2129952 | tf_op jit(solution)/shard_map/all_to_all | solution.py:705
  61.1 12.3 %all-to-all-start.1 = ((f32[16,64,4,128]{3,2,1,0:T(4,128)}), f32[16,64,4,128]{3,2,1,0:T(4,128)}, u32[]{:S(2)}, u32[]{:S(2)}) async-start(f32[16,64,4,128]{3,2,1,0:T(4,128)} %bitcast.6), calls=%async_computation.1 | async-start | bytes 4194304 | tf_op jit(solution)/shard_map/all_to_all | solution.py:705
  73.4 0.1 fusion
  73.5 0.8 slice.20
  74.3 0.1 broadcast_in_dim.15.odd_ref
  74.3 3.0 %sum_by_block.2 = (f32[4,128,512]{2,1,0:T(8,128)S(1)}, f32[4,512]{1,0:T(4,128)S(1)}, f32[4,512]{1,0:T(4,128)S(1)}, f32[4,128]{1,0:T(4,128)S(1)}, f32[4,128]{1,0:T(4,128)S(1)}) custom-call(f32[2,128]{1,0:T(2,128)S(1)} %broadcast_in_dim.15.odd_ref, f32[16,128]{1,0:T(8,128)S(1)} %bitcast.14, f32[4160,128]{1,0:T(8,128)} %bitcast.7.rows_ref), custom_call_target="tpu_custom_call" | custom-call | flops 1073741824 | bytes 3145728 | tf_op jit(solution)/shard_map/sum_by_block/pallas_call | solution.py:303
  77.3 1.3 collective-permute-start.8
  78.6 3.8 %collective-permute-start.5 = (f32[80,128]{1,0:T(8,128)S(1)}, f32[80,128]{1,0:T(8,128)S(1)}, u32[]{:S(2)}, u32[]{:S(2)}) collective-permute-start(f32[80,128]{1,0:T(8,128)S(1)} %pad_maximum_fusion), channel_id=1, source_target_pairs={{0,1},{1,2},{2,3},{4,5},{5,6},{6,7},{8,9},{9,10},{10,11},{12,13},{... | collective-permute-start | bytes 122888 | tf_op jit(solution)/shard_map/ppermute | solution.py:732
  82.5 1.9 %collective-permute-start.6 = (f32[80,128]{1,0:T(8,128)S(1)}, f32[80,128]{1,0:T(8,128)S(1)}, u32[]{:S(2)}, u32[]{:S(2)}) collective-permute-start(f32[80,128]{1,0:T(8,128)S(1)} %pad_maximum_fusion.1), channel_id=1, source_target_pairs={{1,0},{2,1},{3,2},{5,4},{6,5},{7,6},{9,8},{10,9},{11,10},{13,12},{... | collective-permute-start | bytes 122888 | tf_op jit(solution)/shard_map/ppermute | solution.py:733
  84.4 0.3 collective-permute-start.7
  84.7 0.1 add_and_fusion.1.rest_0_.rest_5_
  84.8 4.8 %collective-permute-start.9 = (f32[4,128]{1,0:T(4,128)S(1)}, f32[4,128]{1,0:T(4,128)S(1)}, u32[]{:S(2)}, u32[]{:S(2)}) collective-permute-start(f32[4,128]{1,0:T(4,128)S(1)} %get-tuple-element.48), channel_id=1, source_target_pairs={{1,18},{2,17},{17,2},{18,1},{5,22},{6,21},{21,6},{22,5},{9,26},{10... | collective-permute-start | bytes 6152 | tf_op jit(solution)/shard_map/ppermute | solution.py:750
  89.7 0.1 collective-permute-start.10
  89.7 0.2 collective-permute-done.6.corners_right
  90.0 0.1 broadcast_in_dim.14.rates_ref
  90.0 12.1 %base.1 = (f32[1,16,128,512]{3,2,1,0:T(8,128)}, f32[4,128,512]{2,1,0:T(8,128)S(1)}, f32[6,128,512]{2,1,0:T(8,128)S(1)}) custom-call(f32[1,16]{1,0:T(1,128)S(1)} %get-tuple-element.71.rate_ref, f32[1,2]{1,0:T(1,128)S(1)} %broadcast_select_fusion.mix_ref, f32[16,128]{1,0:T(8,128)S(1)} %broadcast_in_dim.14.rates_ref, f32[1,3,128,512]{3,2,1,0:T(8,128)S(1)} %copy-done, ...), custom_call_target="tpu_custom_call" | custom-call | flops 41943040 | bytes 8388608 | tf_op jit(solution)/shard_map/base/pallas_call | solution.py:510
  102.1 1.0 copy-done.2
  103.1 0.6 collective-permute-start.15
  103.7 0.0 collective-permute-done.9.left
  103.8 4.4 %collective-permute-start.16 = (f32[4,512]{1,0:T(4,128)S(1)}, f32[4,512]{1,0:T(4,128)S(1)}, u32[]{:S(2)}, u32[]{:S(2)}) collective-permute-start(f32[4,512]{1,0:T(4,128)S(1)} %get-tuple-element.59), channel_id=1, source_target_pairs={{0,20},{8,28},{4,16},{12,24},{16,4},{24,12},{20,0},{28,8},{1,21},{... | collective-permute-start | bytes 24584 | tf_op jit(solution)/shard_map/ppermute | solution.py:747
  108.1 3.9 %finish.2 = (f32[1,16,128,512]{3,2,1,0:T(8,128)}, f32[1,8,128,512]{3,2,1,0:T(8,128)}, f32[8,128]{1,0:T(8,128)S(1)}) custom-call(f32[1,8]{1,0:T(1,128)S(1)} %copy-done.4, f32[1,2]{1,0:T(1,128)S(1)} %broadcast_select_fusion.mix_ref, f32[40,512]{1,0:T(8,128)S(1)} %collective-permute-done.1.above, ...), custom_call_target="tpu_custom_call", output_to_operand_aliasing={{0}: (11, {})} | custom-call | flops 5242880 | bytes 5242880 | tf_op jit(solution)/shard_map/finish/pallas_call | solution.py:662
  112.0 2.9 %all-to-all-done.1 = f32[16,64,4,128]{3,2,1,0:T(4,128)} async-done(((f32[16,64,4,128]{3,2,1,0:T(4,128)}), f32[16,64,4,128]{3,2,1,0:T(4,128)}, u32[]{:S(2)}, u32[]{:S(2)}) %all-to-all-start.1) | async-done | bytes 2097184 | tf_op jit(solution)/shard_map/all_to_all | solution.py:705
  115.0 3.0 %sum_by_block.3 = (f32[4,128,512]{2,1,0:T(8,128)S(1)}, f32[4,512]{1,0:T(4,128)S(1)}, f32[4,512]{1,0:T(4,128)S(1)}, f32[4,128]{1,0:T(4,128)S(1)}, f32[4,128]{1,0:T(4,128)S(1)}) custom-call(f32[2,128]{1,0:T(2,128)S(1)} %broadcast_in_dim.15.odd_ref, f32[16,128]{1,0:T(8,128)S(1)} %collective-permute-done.7.ids_ref, f32[4096,128]{1,0:T(8,128)} %bitcast.10.rows_ref), custom_call_target="tpu_custom_call" | custom-call | flops 1073741824 | bytes 3145728 | tf_op jit(solution)/shard_map/sum_by_block/pallas_call | solution.py:303
  118.0 0.7 collective-permute-start.13
  118.6 9.6 %collective-permute-start.14 = (f32[4,512]{1,0:T(4,128)S(1)}, f32[4,512]{1,0:T(4,128)S(1)}, u32[]{:S(2)}, u32[]{:S(2)}) collective-permute-start(f32[4,512]{1,0:T(4,128)S(1)} %get-tuple-element.57), channel_id=1, source_target_pairs={{0,4},{8,12},{4,0},{12,8},{1,5},{9,13},{5,1},{13,9},{2,6},{10,14},... | collective-permute-start | bytes 24584 | tf_op jit(solution)/shard_map/ppermute | solution.py:761
  128.2 2.7 %collective-permute-start.11 = (f32[4,128]{1,0:T(4,128)S(1)}, f32[4,128]{1,0:T(4,128)S(1)}, u32[]{:S(2)}, u32[]{:S(2)}) collective-permute-start(f32[4,128]{1,0:T(4,128)S(1)} %get-tuple-element.54), channel_id=1, source_target_pairs={{1,2},{2,1},{5,6},{6,5},{9,10},{10,9},{13,14},{14,13},{17,18},{18,... | collective-permute-start | bytes 6152 | tf_op jit(solution)/shard_map/ppermute | solution.py:764
  130.9 0.0 collective-permute-done.15.rest_2_
  130.9 0.1 collective-permute-start.12
  131.0 0.0 collective-permute-done.16.rest_3_
  131.0 2.1 %collective-permute-done.11.left = f32[4,128]{1,0:T(4,128)S(1)} collective-permute-done((f32[4,128]{1,0:T(4,128)S(1)}, f32[4,128]{1,0:T(4,128)S(1)}, u32[]{:S(2)}, u32[]{:S(2)}) %collective-permute-start.11) | collective-permute-done | bytes 2080 | tf_op jit(solution)/shard_map/ppermute | solution.py:764
  133.1 0.0 collective-permute-done.14.rest_1_
  133.1 3.6 %finish.3 = (f32[1,16,128,512]{3,2,1,0:T(8,128)}, f32[1,8,128,512]{3,2,1,0:T(8,128)}, f32[8,128]{1,0:T(8,128)}) custom-call(f32[1,8]{1,0:T(1,128)S(1)} %copy-done.4, f32[1,2]{1,0:T(1,128)S(1)} %broadcast_select_fusion.mix_ref, f32[40,512]{1,0:T(8,128)S(1)} %collective-permute-done.1.above, ...), custom_call_target="tpu_custom_call", output_to_operand_aliasing={{0}: (16, {}), {1}: (17, {})} | custom-call | flops 5242880 | bytes 5242880 | tf_op jit(solution)/shard_map/finish/pallas_call | solution.py:662
  (20 shorter events, 0.1 us)
Async XLA Ops:
  11.4 8.7 %copy-start.5 = (f32[1,2]{1,0:T(1,128)S(1)}, f32[1,2]{1,0:T(1,128)}, u32[]{:S(2)}) copy-start(f32[1,2]{1,0:T(1,128)} %constant.23.clone) | copy-start | bytes 28
  11.5 8.7 %copy-start = (f32[1,3,128,512]{3,2,1,0:T(8,128)S(1)}, f32[1,3,128,512]{3,2,1,0:T(8,128)}, u32[]{:S(2)}) copy-start(f32[1,3,128,512]{3,2,1,0:T(8,128)} %coefs_ref.1) | copy-start | bytes 2359300
  11.5 8.7 %copy-start.1 = (s32[128,512]{1,0:T(8,128)S(1)}, s32[128,512]{1,0:T(8,128)}, u32[]{:S(2)}) copy-start(s32[128,512]{1,0:T(8,128)} %land_ref) | copy-start | bytes 786436
  11.5 49.6 %all-to-all-start = ((f32[16,65,4,128]{3,2,1,0:T(4,128)}), f32[16,65,4,128]{3,2,1,0:T(4,128)}, u32[]{:S(2)}, u32[]{:S(2)}) async-start(f32[16,65,4,128]{3,2,1,0:T(4,128)} %bitcast.4), calls=%async_computation | async-start | bytes 4259840 | tf_op jit(solution)/shard_map/all_to_all | solution.py:705
  19.0 24.9 %collective-permute-start = (f32[513,4,128]{2,1,0:T(4,128)}, f32[513,4,128]{2,1,0:T(4,128)S(1)}, u32[]{:S(2)}, u32[]{:S(2)}) collective-permute-start(f32[513,4,128]{2,1,0:T(4,128)} %get-tuple-element.34), channel_id=1, source_target_pairs={{0,16},{16,0},{1,17},{17,1},{2,18},{18,2},{3,19},{19,3},{4,20},{20... | collective-permute-start | bytes 3151880 | tf_op jit(solution)/shard_map/ppermute | solution.py:711
  23.4 32.2 %collective-permute-start.1 = (f32[40,512]{1,0:T(8,128)S(1)}, f32[40,512]{1,0:T(8,128)S(1)}, u32[]{:S(2)}, u32[]{:S(2)}) collective-permute-start(f32[40,512]{1,0:T(8,128)S(1)} %get-tuple-element.37.x_high), channel_id=1, source_target_pairs={{0,4},{4,8},{8,12},{1,5},{5,9},{9,13},{2,6},{6,10},{10,14},{3,7},{... | collective-permute-start | bytes 245768 | tf_op jit(solution)/shard_map/ppermute | solution.py:722
  26.7 28.9 %collective-permute-start.2 = (f32[40,512]{1,0:T(8,128)S(1)}, f32[40,512]{1,0:T(8,128)S(1)}, u32[]{:S(2)}, u32[]{:S(2)}) collective-permute-start(f32[40,512]{1,0:T(8,128)S(1)} %get-tuple-element.38.x_low), channel_id=1, source_target_pairs={{4,0},{8,4},{12,8},{5,1},{9,5},{13,9},{6,2},{10,6},{14,10},{7,3},{... | collective-permute-start | bytes 245768 | tf_op jit(solution)/shard_map/ppermute | solution.py:723
  28.0 19.9 %collective-permute-start.3 = (f32[40,128]{1,0:T(8,128)S(1)}, f32[40,128]{1,0:T(8,128)S(1)}, u32[]{:S(2)}, u32[]{:S(2)}) collective-permute-start(f32[40,128]{1,0:T(8,128)S(1)} %get-tuple-element.39.y_high), channel_id=1, source_target_pairs={{0,1},{1,2},{2,3},{4,5},{5,6},{6,7},{8,9},{9,10},{10,11},{12,13},{... | collective-permute-start | bytes 61448 | tf_op jit(solution)/shard_map/ppermute | solution.py:720
  31.9 16.0 %collective-permute-start.4 = (f32[40,128]{1,0:T(8,128)S(1)}, f32[40,128]{1,0:T(8,128)S(1)}, u32[]{:S(2)}, u32[]{:S(2)}) collective-permute-start(f32[40,128]{1,0:T(8,128)S(1)} %get-tuple-element.40.y_low), channel_id=1, source_target_pairs={{1,0},{2,1},{3,2},{5,4},{6,5},{7,6},{9,8},{10,9},{11,10},{13,12},{... | collective-permute-start | bytes 61448 | tf_op jit(solution)/shard_map/ppermute | solution.py:721
  61.1 53.9 %all-to-all-start.1 = ((f32[16,64,4,128]{3,2,1,0:T(4,128)}), f32[16,64,4,128]{3,2,1,0:T(4,128)}, u32[]{:S(2)}, u32[]{:S(2)}) async-start(f32[16,64,4,128]{3,2,1,0:T(4,128)} %bitcast.6), calls=%async_computation.1 | async-start | bytes 4194304 | tf_op jit(solution)/shard_map/all_to_all | solution.py:705
  73.4 5.2 %copy-start.4 = (f32[1,8]{1,0:T(1,128)S(1)}, f32[1,8]{1,0:T(1,128)}, u32[]{:S(2)}) copy-start(f32[1,8]{1,0:T(1,128)} %gamma_ref.3) | copy-start | bytes 100
  77.3 30.8 %collective-permute-start.8 = (f32[4,128,512]{2,1,0:T(8,128)S(1)}, f32[4,128,512]{2,1,0:T(8,128)S(1)}, u32[]{:S(2)}, u32[]{:S(2)}) collective-permute-start(f32[4,128,512]{2,1,0:T(8,128)S(1)} %get-tuple-element.47), channel_id=1, source_target_pairs={{0,16},{16,0},{1,17},{17,1},{2,18},{18,2},{3,19},{19,3},{4,20},{20... | collective-permute-start | bytes 3145736 | tf_op jit(solution)/shard_map/ppermute | solution.py:744
  78.6 11.0 %collective-permute-start.5 = (f32[80,128]{1,0:T(8,128)S(1)}, f32[80,128]{1,0:T(8,128)S(1)}, u32[]{:S(2)}, u32[]{:S(2)}) collective-permute-start(f32[80,128]{1,0:T(8,128)S(1)} %pad_maximum_fusion), channel_id=1, source_target_pairs={{0,1},{1,2},{2,3},{4,5},{5,6},{6,7},{8,9},{9,10},{10,11},{12,13},{... | collective-permute-start | bytes 122888 | tf_op jit(solution)/shard_map/ppermute | solution.py:732
  82.5 7.5 %collective-permute-start.6 = (f32[80,128]{1,0:T(8,128)S(1)}, f32[80,128]{1,0:T(8,128)S(1)}, u32[]{:S(2)}, u32[]{:S(2)}) collective-permute-start(f32[80,128]{1,0:T(8,128)S(1)} %pad_maximum_fusion.1), channel_id=1, source_target_pairs={{1,0},{2,1},{3,2},{5,4},{6,5},{7,6},{9,8},{10,9},{11,10},{13,12},{... | collective-permute-start | bytes 122888 | tf_op jit(solution)/shard_map/ppermute | solution.py:733
  84.4 30.6 %collective-permute-start.7 = (f32[16,128]{1,0:T(8,128)S(1)}, f32[16,128]{1,0:T(8,128)S(1)}, u32[]{:S(2)}, u32[]{:S(2)}) collective-permute-start(f32[16,128]{1,0:T(8,128)S(1)} %bitcast.15), channel_id=1, source_target_pairs={{0,16},{16,0},{1,17},{17,1},{2,18},{18,2},{3,19},{19,3},{4,20},{20... | collective-permute-start | bytes 24584 | tf_op jit(solution)/shard_map/ppermute | solution.py:740
  84.8 18.9 %collective-permute-start.9 = (f32[4,128]{1,0:T(4,128)S(1)}, f32[4,128]{1,0:T(4,128)S(1)}, u32[]{:S(2)}, u32[]{:S(2)}) collective-permute-start(f32[4,128]{1,0:T(4,128)S(1)} %get-tuple-element.48), channel_id=1, source_target_pairs={{1,18},{2,17},{17,2},{18,1},{5,22},{6,21},{21,6},{22,5},{9,26},{10... | collective-permute-start | bytes 6152 | tf_op jit(solution)/shard_map/ppermute | solution.py:750
  89.7 18.5 %collective-permute-start.10 = (f32[4,128]{1,0:T(4,128)S(1)}, f32[4,128]{1,0:T(4,128)S(1)}, u32[]{:S(2)}, u32[]{:S(2)}) collective-permute-start(f32[4,128]{1,0:T(4,128)S(1)} %get-tuple-element.49), channel_id=1, source_target_pairs={{0,17},{2,19},{1,16},{3,18},{16,1},{18,3},{17,0},{19,2},{4,21},{6,... | collective-permute-start | bytes 6152 | tf_op jit(solution)/shard_map/ppermute | solution.py:751
  102.1 1.0 copy-start.2
  103.1 27.8 %collective-permute-start.15 = (f32[4,512]{1,0:T(4,128)S(1)}, f32[4,512]{1,0:T(4,128)S(1)}, u32[]{:S(2)}, u32[]{:S(2)}) collective-permute-start(f32[4,512]{1,0:T(4,128)S(1)} %get-tuple-element.58), channel_id=1, source_target_pairs={{4,24},{8,20},{20,8},{24,4},{5,25},{9,21},{21,9},{25,5},{6,26},{10... | collective-permute-start | bytes 24584 | tf_op jit(solution)/shard_map/ppermute | solution.py:746
  103.8 27.2 %collective-permute-start.16 = (f32[4,512]{1,0:T(4,128)S(1)}, f32[4,512]{1,0:T(4,128)S(1)}, u32[]{:S(2)}, u32[]{:S(2)}) collective-permute-start(f32[4,512]{1,0:T(4,128)S(1)} %get-tuple-element.59), channel_id=1, source_target_pairs={{0,20},{8,28},{4,16},{12,24},{16,4},{24,12},{20,0},{28,8},{1,21},{... | collective-permute-start | bytes 24584 | tf_op jit(solution)/shard_map/ppermute | solution.py:747
  112.0 21.1 %copy-start.3 = (f32[4,128,512]{2,1,0:T(8,128)S(1)}, f32[4,128,512]{2,1,0:T(8,128)}, u32[]{:S(2)}) copy-start(f32[4,128,512]{2,1,0:T(8,128)} %copy-done.2) | copy-start | bytes 3145732
  118.0 15.1 %collective-permute-start.13 = (f32[4,512]{1,0:T(4,128)S(1)}, f32[4,512]{1,0:T(4,128)S(1)}, u32[]{:S(2)}, u32[]{:S(2)}) collective-permute-start(f32[4,512]{1,0:T(4,128)S(1)} %get-tuple-element.56), channel_id=1, source_target_pairs={{4,8},{8,4},{5,9},{9,5},{6,10},{10,6},{7,11},{11,7},{20,24},{24,20... | collective-permute-start | bytes 24584 | tf_op jit(solution)/shard_map/ppermute | solution.py:760
  118.6 14.5 %collective-permute-start.14 = (f32[4,512]{1,0:T(4,128)S(1)}, f32[4,512]{1,0:T(4,128)S(1)}, u32[]{:S(2)}, u32[]{:S(2)}) collective-permute-start(f32[4,512]{1,0:T(4,128)S(1)} %get-tuple-element.57), channel_id=1, source_target_pairs={{0,4},{8,12},{4,0},{12,8},{1,5},{9,13},{5,1},{13,9},{2,6},{10,14},... | collective-permute-start | bytes 24584 | tf_op jit(solution)/shard_map/ppermute | solution.py:761
  128.2 4.9 %collective-permute-start.11 = (f32[4,128]{1,0:T(4,128)S(1)}, f32[4,128]{1,0:T(4,128)S(1)}, u32[]{:S(2)}, u32[]{:S(2)}) collective-permute-start(f32[4,128]{1,0:T(4,128)S(1)} %get-tuple-element.54), channel_id=1, source_target_pairs={{1,2},{2,1},{5,6},{6,5},{9,10},{10,9},{13,14},{14,13},{17,18},{18,... | collective-permute-start | bytes 6152 | tf_op jit(solution)/shard_map/ppermute | solution.py:764
  130.9 2.2 %collective-permute-start.12 = (f32[4,128]{1,0:T(4,128)S(1)}, f32[4,128]{1,0:T(4,128)S(1)}, u32[]{:S(2)}, u32[]{:S(2)}) collective-permute-start(f32[4,128]{1,0:T(4,128)S(1)} %get-tuple-element.55), channel_id=1, source_target_pairs={{0,1},{2,3},{1,0},{3,2},{4,5},{6,7},{5,4},{7,6},{8,9},{10,11},{9,8... | collective-permute-start | bytes 6152 | tf_op jit(solution)/shard_map/ppermute | solution.py:765

commit v13 on v12

--- a/solution.py
+++ b/solution.py
@@ -109,18 +109,7 @@
     for t in range(tiles):
         taken[t] = t * (capacity + 1)
 
-    for copy in vector_copies:
-        copy.wait()
-    dev, blk = pair_v[0], pair_v[1]
-    ids = slot_blocks(dev, blk, tiles, capacity)
-    for t in range(tiles):
-        row = jnp.broadcast_to(ids[t : t + 1, :], late_ref.shape[1:])
-        late_ref[t * (capacity + 1) + capacity] = row
-    code = (dev * (cells_x * parts) + blk).astype(jnp.float32)
-    for i in range(pairs // width):
-        place = (pairs + i // half, slice(i % half, i % half + 1), slice(None))
-        early_ref[place] = code[:, i * width : (i + 1) * width]
-    for copy in scalar_copies + field_copies:
+    for copy in vector_copies + scalar_copies + field_copies:
         copy.wait()
 
     def cells_of(p):
@@ -129,8 +118,7 @@
 
     zeros = jnp.zeros((fields, width), jnp.float32)
 
-    def some_pairs(step, carry):
-        weight_copy(step).wait()
+    def work(step):
         for i in range(0, STEP_PAIRS, 4):
             p = step * STEP_PAIRS + i
             left = [
@@ -150,9 +138,25 @@
                 one = four[j * fields : (j + 1) * fields, at : at + width]
                 early_ref[p + j] = one[:half]
                 late_ref[slot] = one[half:]
+
+    def some_pairs(step, carry):
+        weight_copy(step).wait()
+        work(step)
         return carry
 
-    lax.fori_loop(0, steps, some_pairs, 0)
+    weight_copy(0).wait()
+    dev, blk = pair_v[0], pair_v[1]
+    ids = slot_blocks(dev, blk, tiles, capacity)
+    code = (dev * (cells_x * parts) + blk).astype(jnp.float32)
+    work(0)
+    for t in range(tiles):
+        row = jnp.broadcast_to(ids[t : t + 1, :], late_ref.shape[1:])
+        late_ref[t * (capacity + 1) + capacity] = row
+    for i in range(pairs // width):
+        place = (pairs + i // half, slice(i % half, i % half + 1), slice(None))
+        early_ref[place] = code[:, i * width : (i + 1) * width]
+
+    lax.fori_loop(1, steps, some_pairs, 0)
 
 
 def contributions(state, pair_src, pair_dev, pair_blk, weights, tiles, capacity, fields):

time: 138 us -> 138 us (level)
  no operation moved by 1% of the time
where the time goes in v13:
time: 138 us; the launch traced here: 137 us
  starting transfers between devices  61.6 us (45%)
  Pallas kernels  44.3 us (32%)
  waiting for transfers between devices  28.5 us (21%)
  local copies, waits for them, and re-layouts  1.92 us (1%)
    all_to_all x2, starting transfers between devices, exchanged(): lax.all_to_all(rows, ('tx', 'ty'), split_axis=0, concat_axis=0, tiled=True)  19.8 us
    pallas_call x1, Pallas kernels, base_of(): pl.pallas_call(functools.partial(base_kernel, half), grid=(nfield // PER_...  12.1 us
    pallas_call x1, Pallas kernels, contributions(): pl.pallas_call(functools.partial(contribution_kernel, dims), in_specs=[pl...  11.4 us
    ppermute x1, waiting for transfers between devices, body(): early = lax.ppermute(early, 'comp', swap)  10 us
    ppermute x1, starting transfers between devices, body(): lax.ppermute(x_even, 'tx', neighbour_pairs(tx, 0))  9.55 us
    all_to_all x2, waiting for transfers between devices, exchanged(): lax.all_to_all(rows, ('tx', 'ty'), split_axis=0, concat_axis=0, tiled=True)  8.38 us
    ppermute x1, waiting for transfers between devices, body(): above = lax.ppermute(x_high, 'tx', shift_pairs(tx, 1))  7.72 us
    pallas_call x2, Pallas kernels, finished(): pl.pallas_call(functools.partial(finish_kernel, first, with_x), in_specs=...  7.55 us
  transfers between devices with their start and end apart: 19, of which 6 were waited for; matrix products, arithmetic and copies ran while one was open for 1% of the time, Pallas kernels for 21%

profile of v13, /device:TPU:1, one launch (start us, length us, event | category | flops | bytes accessed | tf_op | source)
XLA Modules:
  0.0 137.4 jit_solution(17775462303847419447)
XLA Ops:
  0.6 11.4 %contributions.1 = (f32[513,4,128]{2,1,0:T(4,128)}, f32[1040,4,128]{2,1,0:T(4,128)}) custom-call(s32[1,512]{1,0:T(1,128)} %src_ref.1, s32[1,512]{1,0:T(1,128)} %bitcast.16, s32[1,512]{1,0:T(1,128)} %blk_ref.1, f32[1,16,128,512]{3,2,1,0:T(8,128)} %state_ref.3, bf16[1,512,128,128]{3,2,1,0:T(8,128)(2,1)} %weights_ref.1), custom_call_target="tpu_custom_call" | custom-call | flops 134217728 | bytes 25296896 | tf_op jit(solution)/shard_map/contributions/pallas_call | solution.py:170
  12.1 0.0 copy-start.5
  12.1 0.0 copy-start
  12.1 0.0 copy-start.1
  12.1 7.5 %all-to-all-start = ((f32[16,65,4,128]{3,2,1,0:T(4,128)}), f32[16,65,4,128]{3,2,1,0:T(4,128)}, u32[]{:S(2)}, u32[]{:S(2)}) async-start(f32[16,65,4,128]{3,2,1,0:T(4,128)} %bitcast.4), calls=%async_computation | async-start | bytes 4259840 | tf_op jit(solution)/shard_map/all_to_all | solution.py:709
  19.6 1.2 collective-permute-start
  20.9 3.2 %edges.1 = (f32[40,512]{1,0:T(8,128)S(1)}, f32[40,512]{1,0:T(8,128)S(1)}, f32[40,128]{1,0:T(8,128)S(1)}, f32[40,128]{1,0:T(8,128)S(1)}) custom-call(f32[1,2]{1,0:T(1,128)S(1)} %broadcast_select_fusion.mix_ref, f32[1,16,128,512]{3,2,1,0:T(8,128)} %state_ref.3, f32[1,16,128,512]{3,2,1,0:T(8,128)} %state_ref.3, f32[1,16,128,512]{3,2,1,0:T(8,128)} %state_ref.3, ...), custom_call_target="tpu_custom_call" | custom-call | flops 1048576 | bytes 4194304 | tf_op jit(solution)/shard_map/edges/pallas_call | solution.py:423
  24.1 3.3 %collective-permute-start.1 = (f32[40,512]{1,0:T(8,128)S(1)}, f32[40,512]{1,0:T(8,128)S(1)}, u32[]{:S(2)}, u32[]{:S(2)}) collective-permute-start(f32[40,512]{1,0:T(8,128)S(1)} %get-tuple-element.37.x_high), channel_id=1, source_target_pairs={{0,4},{4,8},{8,12},{1,5},{5,9},{9,13},{2,6},{6,10},{10,14},{3,7},{... | collective-permute-start | bytes 245768 | tf_op jit(solution)/shard_map/ppermute | solution.py:726
  27.4 1.3 collective-permute-start.2
  28.7 3.9 %collective-permute-start.3 = (f32[40,128]{1,0:T(8,128)S(1)}, f32[40,128]{1,0:T(8,128)S(1)}, u32[]{:S(2)}, u32[]{:S(2)}) collective-permute-start(f32[40,128]{1,0:T(8,128)S(1)} %get-tuple-element.39.y_high), channel_id=1, source_target_pairs={{0,1},{1,2},{2,3},{4,5},{5,6},{6,7},{8,9},{9,10},{10,11},{12,13},{... | collective-permute-start | bytes 61448 | tf_op jit(solution)/shard_map/ppermute | solution.py:724
  32.6 1.9 %collective-permute-start.4 = (f32[40,128]{1,0:T(8,128)S(1)}, f32[40,128]{1,0:T(8,128)S(1)}, u32[]{:S(2)}, u32[]{:S(2)}) collective-permute-start(f32[40,128]{1,0:T(8,128)S(1)} %get-tuple-element.40.y_low), channel_id=1, source_target_pairs={{1,0},{2,1},{3,2},{5,4},{6,5},{7,6},{9,8},{10,9},{11,10},{13,12},{... | collective-permute-start | bytes 61448 | tf_op jit(solution)/shard_map/ppermute | solution.py:725
  34.5 10.0 %collective-permute-done.in_ref = f32[513,4,128]{2,1,0:T(4,128)S(1)} collective-permute-done((f32[513,4,128]{2,1,0:T(4,128)}, f32[513,4,128]{2,1,0:T(4,128)S(1)}, u32[]{:S(2)}, u32[]{:S(2)}) %collective-permute-start) | collective-permute-done | bytes 1050656 | tf_op jit(solution)/shard_map/ppermute | solution.py:715
  44.5 4.0 %place_in_slots.1 = f32[1024,4,128]{2,1,0:T(4,128)} custom-call(f32[513,4,128]{2,1,0:T(4,128)S(1)} %collective-permute-done.in_ref), custom_call_target="tpu_custom_call" | custom-call | flops 1050624 | bytes 3151872 | tf_op jit(solution)/shard_map/place_in_slots/pallas_call | solution.py:221
  48.6 0.0 collective-permute-done.3.left.before
  48.6 0.0 collective-permute-done.4.right.after
  48.6 7.7 %collective-permute-done.1.above = f32[40,512]{1,0:T(8,128)S(1)} collective-permute-done((f32[40,512]{1,0:T(8,128)S(1)}, f32[40,512]{1,0:T(8,128)S(1)}, u32[]{:S(2)}, u32[]{:S(2)}) %collective-permute-start.1) | collective-permute-done | bytes 81952 | tf_op jit(solution)/shard_map/ppermute | solution.py:726
  56.3 5.4 %all-to-all-done = f32[16,65,4,128]{3,2,1,0:T(4,128)} async-done(((f32[16,65,4,128]{3,2,1,0:T(4,128)}), f32[16,65,4,128]{3,2,1,0:T(4,128)}, u32[]{:S(2)}, u32[]{:S(2)}) %all-to-all-start) | async-done | bytes 2129952 | tf_op jit(solution)/shard_map/all_to_all | solution.py:709
  61.8 12.3 %all-to-all-start.1 = ((f32[16,64,4,128]{3,2,1,0:T(4,128)}), f32[16,64,4,128]{3,2,1,0:T(4,128)}, u32[]{:S(2)}, u32[]{:S(2)}) async-start(f32[16,64,4,128]{3,2,1,0:T(4,128)} %bitcast.6), calls=%async_computation.1 | async-start | bytes 4194304 | tf_op jit(solution)/shard_map/all_to_all | solution.py:709
  74.1 0.1 fusion
  74.1 0.8 slice.20
  74.9 0.1 broadcast_in_dim.15.odd_ref
  75.0 3.0 %sum_by_block.2 = (f32[4,128,512]{2,1,0:T(8,128)S(1)}, f32[4,512]{1,0:T(4,128)S(1)}, f32[4,512]{1,0:T(4,128)S(1)}, f32[4,128]{1,0:T(4,128)S(1)}, f32[4,128]{1,0:T(4,128)S(1)}) custom-call(f32[2,128]{1,0:T(2,128)S(1)} %broadcast_in_dim.15.odd_ref, f32[16,128]{1,0:T(8,128)S(1)} %bitcast.14, f32[4160,128]{1,0:T(8,128)} %bitcast.7.rows_ref), custom_call_target="tpu_custom_call" | custom-call | flops 1073741824 | bytes 3145728 | tf_op jit(solution)/shard_map/sum_by_block/pallas_call | solution.py:307
  78.0 1.3 collective-permute-start.8
  79.3 3.8 %collective-permute-start.5 = (f32[80,128]{1,0:T(8,128)S(1)}, f32[80,128]{1,0:T(8,128)S(1)}, u32[]{:S(2)}, u32[]{:S(2)}) collective-permute-start(f32[80,128]{1,0:T(8,128)S(1)} %pad_maximum_fusion), channel_id=1, source_target_pairs={{0,1},{1,2},{2,3},{4,5},{5,6},{6,7},{8,9},{9,10},{10,11},{12,13},{... | collective-permute-start | bytes 122888 | tf_op jit(solution)/shard_map/ppermute | solution.py:736
  83.1 1.9 %collective-permute-start.6 = (f32[80,128]{1,0:T(8,128)S(1)}, f32[80,128]{1,0:T(8,128)S(1)}, u32[]{:S(2)}, u32[]{:S(2)}) collective-permute-start(f32[80,128]{1,0:T(8,128)S(1)} %pad_maximum_fusion.1), channel_id=1, source_target_pairs={{1,0},{2,1},{3,2},{5,4},{6,5},{7,6},{9,8},{10,9},{11,10},{13,12},{... | collective-permute-start | bytes 122888 | tf_op jit(solution)/shard_map/ppermute | solution.py:737
  85.1 0.3 collective-permute-start.7
  85.4 0.1 add_and_fusion.1.rest_0_.rest_5_
  85.5 4.8 %collective-permute-start.9 = (f32[4,128]{1,0:T(4,128)S(1)}, f32[4,128]{1,0:T(4,128)S(1)}, u32[]{:S(2)}, u32[]{:S(2)}) collective-permute-start(f32[4,128]{1,0:T(4,128)S(1)} %get-tuple-element.48), channel_id=1, source_target_pairs={{1,18},{2,17},{17,2},{18,1},{5,22},{6,21},{21,6},{22,5},{9,26},{10... | collective-permute-start | bytes 6152 | tf_op jit(solution)/shard_map/ppermute | solution.py:754
  90.3 0.1 collective-permute-start.10
  90.4 0.2 collective-permute-done.6.corners_right
  90.6 0.1 broadcast_in_dim.14.rates_ref
  90.7 12.1 %base.1 = (f32[1,16,128,512]{3,2,1,0:T(8,128)}, f32[4,128,512]{2,1,0:T(8,128)S(1)}, f32[6,128,512]{2,1,0:T(8,128)S(1)}) custom-call(f32[1,16]{1,0:T(1,128)S(1)} %get-tuple-element.71.rate_ref, f32[1,2]{1,0:T(1,128)S(1)} %broadcast_select_fusion.mix_ref, f32[16,128]{1,0:T(8,128)S(1)} %broadcast_in_dim.14.rates_ref, f32[1,3,128,512]{3,2,1,0:T(8,128)S(1)} %copy-done, ...), custom_call_target="tpu_custom_call" | custom-call | flops 41943040 | bytes 8388608 | tf_op jit(solution)/shard_map/base/pallas_call | solution.py:514
  102.8 1.0 copy-done.2
  103.7 0.6 collective-permute-start.15
  104.4 4.4 %collective-permute-start.16 = (f32[4,512]{1,0:T(4,128)S(1)}, f32[4,512]{1,0:T(4,128)S(1)}, u32[]{:S(2)}, u32[]{:S(2)}) collective-permute-start(f32[4,512]{1,0:T(4,128)S(1)} %get-tuple-element.59), channel_id=1, source_target_pairs={{0,20},{8,28},{4,16},{12,24},{16,4},{24,12},{20,0},{28,8},{1,21},{... | collective-permute-start | bytes 24584 | tf_op jit(solution)/shard_map/ppermute | solution.py:751
  108.8 0.0 collective-permute-done.10.right
  108.8 3.9 %finish.2 = (f32[1,16,128,512]{3,2,1,0:T(8,128)}, f32[1,8,128,512]{3,2,1,0:T(8,128)}, f32[8,128]{1,0:T(8,128)S(1)}) custom-call(f32[1,8]{1,0:T(1,128)S(1)} %copy-done.4, f32[1,2]{1,0:T(1,128)S(1)} %broadcast_select_fusion.mix_ref, f32[40,512]{1,0:T(8,128)S(1)} %collective-permute-done.1.above, ...), custom_call_target="tpu_custom_call", output_to_operand_aliasing={{0}: (11, {})} | custom-call | flops 5242880 | bytes 5242880 | tf_op jit(solution)/shard_map/finish/pallas_call | solution.py:666
  112.7 2.9 %all-to-all-done.1 = f32[16,64,4,128]{3,2,1,0:T(4,128)} async-done(((f32[16,64,4,128]{3,2,1,0:T(4,128)}), f32[16,64,4,128]{3,2,1,0:T(4,128)}, u32[]{:S(2)}, u32[]{:S(2)}) %all-to-all-start.1) | async-done | bytes 2097184 | tf_op jit(solution)/shard_map/all_to_all | solution.py:709
  115.6 0.0 collective-permute-done.7.ids_ref
  115.6 3.0 %sum_by_block.3 = (f32[4,128,512]{2,1,0:T(8,128)S(1)}, f32[4,512]{1,0:T(4,128)S(1)}, f32[4,512]{1,0:T(4,128)S(1)}, f32[4,128]{1,0:T(4,128)S(1)}, f32[4,128]{1,0:T(4,128)S(1)}) custom-call(f32[2,128]{1,0:T(2,128)S(1)} %broadcast_in_dim.15.odd_ref, f32[16,128]{1,0:T(8,128)S(1)} %collective-permute-done.7.ids_ref, f32[4096,128]{1,0:T(8,128)} %bitcast.10.rows_ref), custom_call_target="tpu_custom_call" | custom-call | flops 1073741824 | bytes 3145728 | tf_op jit(solution)/shard_map/sum_by_block/pallas_call | solution.py:307
  118.6 0.7 collective-permute-start.13
  119.3 9.6 %collective-permute-start.14 = (f32[4,512]{1,0:T(4,128)S(1)}, f32[4,512]{1,0:T(4,128)S(1)}, u32[]{:S(2)}, u32[]{:S(2)}) collective-permute-start(f32[4,512]{1,0:T(4,128)S(1)} %get-tuple-element.57), channel_id=1, source_target_pairs={{0,4},{8,12},{4,0},{12,8},{1,5},{9,13},{5,1},{13,9},{2,6},{10,14},... | collective-permute-start | bytes 24584 | tf_op jit(solution)/shard_map/ppermute | solution.py:765
  128.9 2.7 %collective-permute-start.11 = (f32[4,128]{1,0:T(4,128)S(1)}, f32[4,128]{1,0:T(4,128)S(1)}, u32[]{:S(2)}, u32[]{:S(2)}) collective-permute-start(f32[4,128]{1,0:T(4,128)S(1)} %get-tuple-element.54), channel_id=1, source_target_pairs={{1,2},{2,1},{5,6},{6,5},{9,10},{10,9},{13,14},{14,13},{17,18},{18,... | collective-permute-start | bytes 6152 | tf_op jit(solution)/shard_map/ppermute | solution.py:768
  131.5 0.0 collective-permute-done.15.rest_2_
  131.5 0.1 collective-permute-start.12
  131.6 0.0 collective-permute-done.16.rest_3_
  131.6 2.1 %collective-permute-done.11.left = f32[4,128]{1,0:T(4,128)S(1)} collective-permute-done((f32[4,128]{1,0:T(4,128)S(1)}, f32[4,128]{1,0:T(4,128)S(1)}, u32[]{:S(2)}, u32[]{:S(2)}) %collective-permute-start.11) | collective-permute-done | bytes 2080 | tf_op jit(solution)/shard_map/ppermute | solution.py:768
  133.8 3.6 %finish.3 = (f32[1,16,128,512]{3,2,1,0:T(8,128)}, f32[1,8,128,512]{3,2,1,0:T(8,128)}, f32[8,128]{1,0:T(8,128)}) custom-call(f32[1,8]{1,0:T(1,128)S(1)} %copy-done.4, f32[1,2]{1,0:T(1,128)S(1)} %broadcast_select_fusion.mix_ref, f32[40,512]{1,0:T(8,128)S(1)} %collective-permute-done.1.above, ...), custom_call_target="tpu_custom_call", output_to_operand_aliasing={{0}: (16, {}), {1}: (17, {})} | custom-call | flops 5242880 | bytes 5242880 | tf_op jit(solution)/shard_map/finish/pallas_call | solution.py:666
  (20 shorter events, 0.1 us)
Async XLA Ops:
  12.1 8.8 %copy-start.5 = (f32[1,2]{1,0:T(1,128)S(1)}, f32[1,2]{1,0:T(1,128)}, u32[]{:S(2)}) copy-start(f32[1,2]{1,0:T(1,128)} %constant.23.clone) | copy-start | bytes 28
  12.1 8.7 %copy-start = (f32[1,3,128,512]{3,2,1,0:T(8,128)S(1)}, f32[1,3,128,512]{3,2,1,0:T(8,128)}, u32[]{:S(2)}) copy-start(f32[1,3,128,512]{3,2,1,0:T(8,128)} %coefs_ref.1) | copy-start | bytes 2359300
  12.1 8.7 %copy-start.1 = (s32[128,512]{1,0:T(8,128)S(1)}, s32[128,512]{1,0:T(8,128)}, u32[]{:S(2)}) copy-start(s32[128,512]{1,0:T(8,128)} %land_ref) | copy-start | bytes 786436
  12.1 49.6 %all-to-all-start = ((f32[16,65,4,128]{3,2,1,0:T(4,128)}), f32[16,65,4,128]{3,2,1,0:T(4,128)}, u32[]{:S(2)}, u32[]{:S(2)}) async-start(f32[16,65,4,128]{3,2,1,0:T(4,128)} %bitcast.4), calls=%async_computation | async-start | bytes 4259840 | tf_op jit(solution)/shard_map/all_to_all | solution.py:709
  19.6 24.9 %collective-permute-start = (f32[513,4,128]{2,1,0:T(4,128)}, f32[513,4,128]{2,1,0:T(4,128)S(1)}, u32[]{:S(2)}, u32[]{:S(2)}) collective-permute-start(f32[513,4,128]{2,1,0:T(4,128)} %get-tuple-element.34), channel_id=1, source_target_pairs={{0,16},{16,0},{1,17},{17,1},{2,18},{18,2},{3,19},{19,3},{4,20},{20... | collective-permute-start | bytes 3151880 | tf_op jit(solution)/shard_map/ppermute | solution.py:715
  24.1 32.2 %collective-permute-start.1 = (f32[40,512]{1,0:T(8,128)S(1)}, f32[40,512]{1,0:T(8,128)S(1)}, u32[]{:S(2)}, u32[]{:S(2)}) collective-permute-start(f32[40,512]{1,0:T(8,128)S(1)} %get-tuple-element.37.x_high), channel_id=1, source_target_pairs={{0,4},{4,8},{8,12},{1,5},{5,9},{9,13},{2,6},{6,10},{10,14},{3,7},{... | collective-permute-start | bytes 245768 | tf_op jit(solution)/shard_map/ppermute | solution.py:726
  27.4 28.9 %collective-permute-start.2 = (f32[40,512]{1,0:T(8,128)S(1)}, f32[40,512]{1,0:T(8,128)S(1)}, u32[]{:S(2)}, u32[]{:S(2)}) collective-permute-start(f32[40,512]{1,0:T(8,128)S(1)} %get-tuple-element.38.x_low), channel_id=1, source_target_pairs={{4,0},{8,4},{12,8},{5,1},{9,5},{13,9},{6,2},{10,6},{14,10},{7,3},{... | collective-permute-start | bytes 245768 | tf_op jit(solution)/shard_map/ppermute | solution.py:727
  28.7 19.9 %collective-permute-start.3 = (f32[40,128]{1,0:T(8,128)S(1)}, f32[40,128]{1,0:T(8,128)S(1)}, u32[]{:S(2)}, u32[]{:S(2)}) collective-permute-start(f32[40,128]{1,0:T(8,128)S(1)} %get-tuple-element.39.y_high), channel_id=1, source_target_pairs={{0,1},{1,2},{2,3},{4,5},{5,6},{6,7},{8,9},{9,10},{10,11},{12,13},{... | collective-permute-start | bytes 61448 | tf_op jit(solution)/shard_map/ppermute | solution.py:724
  32.6 16.0 %collective-permute-start.4 = (f32[40,128]{1,0:T(8,128)S(1)}, f32[40,128]{1,0:T(8,128)S(1)}, u32[]{:S(2)}, u32[]{:S(2)}) collective-permute-start(f32[40,128]{1,0:T(8,128)S(1)} %get-tuple-element.40.y_low), channel_id=1, source_target_pairs={{1,0},{2,1},{3,2},{5,4},{6,5},{7,6},{9,8},{10,9},{11,10},{13,12},{... | collective-permute-start | bytes 61448 | tf_op jit(solution)/shard_map/ppermute | solution.py:725
  61.8 53.9 %all-to-all-start.1 = ((f32[16,64,4,128]{3,2,1,0:T(4,128)}), f32[16,64,4,128]{3,2,1,0:T(4,128)}, u32[]{:S(2)}, u32[]{:S(2)}) async-start(f32[16,64,4,128]{3,2,1,0:T(4,128)} %bitcast.6), calls=%async_computation.1 | async-start | bytes 4194304 | tf_op jit(solution)/shard_map/all_to_all | solution.py:709
  74.0 5.2 %copy-start.4 = (f32[1,8]{1,0:T(1,128)S(1)}, f32[1,8]{1,0:T(1,128)}, u32[]{:S(2)}) copy-start(f32[1,8]{1,0:T(1,128)} %gamma_ref.3) | copy-start | bytes 100
  78.0 30.8 %collective-permute-start.8 = (f32[4,128,512]{2,1,0:T(8,128)S(1)}, f32[4,128,512]{2,1,0:T(8,128)S(1)}, u32[]{:S(2)}, u32[]{:S(2)}) collective-permute-start(f32[4,128,512]{2,1,0:T(8,128)S(1)} %get-tuple-element.47), channel_id=1, source_target_pairs={{0,16},{16,0},{1,17},{17,1},{2,18},{18,2},{3,19},{19,3},{4,20},{20... | collective-permute-start | bytes 3145736 | tf_op jit(solution)/shard_map/ppermute | solution.py:748
  79.3 11.0 %collective-permute-start.5 = (f32[80,128]{1,0:T(8,128)S(1)}, f32[80,128]{1,0:T(8,128)S(1)}, u32[]{:S(2)}, u32[]{:S(2)}) collective-permute-start(f32[80,128]{1,0:T(8,128)S(1)} %pad_maximum_fusion), channel_id=1, source_target_pairs={{0,1},{1,2},{2,3},{4,5},{5,6},{6,7},{8,9},{9,10},{10,11},{12,13},{... | collective-permute-start | bytes 122888 | tf_op jit(solution)/shard_map/ppermute | solution.py:736
  83.1 7.5 %collective-permute-start.6 = (f32[80,128]{1,0:T(8,128)S(1)}, f32[80,128]{1,0:T(8,128)S(1)}, u32[]{:S(2)}, u32[]{:S(2)}) collective-permute-start(f32[80,128]{1,0:T(8,128)S(1)} %pad_maximum_fusion.1), channel_id=1, source_target_pairs={{1,0},{2,1},{3,2},{5,4},{6,5},{7,6},{9,8},{10,9},{11,10},{13,12},{... | collective-permute-start | bytes 122888 | tf_op jit(solution)/shard_map/ppermute | solution.py:737
  85.1 30.6 %collective-permute-start.7 = (f32[16,128]{1,0:T(8,128)S(1)}, f32[16,128]{1,0:T(8,128)S(1)}, u32[]{:S(2)}, u32[]{:S(2)}) collective-permute-start(f32[16,128]{1,0:T(8,128)S(1)} %bitcast.15), channel_id=1, source_target_pairs={{0,16},{16,0},{1,17},{17,1},{2,18},{18,2},{3,19},{19,3},{4,20},{20... | collective-permute-start | bytes 24584 | tf_op jit(solution)/shard_map/ppermute | solution.py:744
  85.5 18.9 %collective-permute-start.9 = (f32[4,128]{1,0:T(4,128)S(1)}, f32[4,128]{1,0:T(4,128)S(1)}, u32[]{:S(2)}, u32[]{:S(2)}) collective-permute-start(f32[4,128]{1,0:T(4,128)S(1)} %get-tuple-element.48), channel_id=1, source_target_pairs={{1,18},{2,17},{17,2},{18,1},{5,22},{6,21},{21,6},{22,5},{9,26},{10... | collective-permute-start | bytes 6152 | tf_op jit(solution)/shard_map/ppermute | solution.py:754
  90.3 18.5 %collective-permute-start.10 = (f32[4,128]{1,0:T(4,128)S(1)}, f32[4,128]{1,0:T(4,128)S(1)}, u32[]{:S(2)}, u32[]{:S(2)}) collective-permute-start(f32[4,128]{1,0:T(4,128)S(1)} %get-tuple-element.49), channel_id=1, source_target_pairs={{0,17},{2,19},{1,16},{3,18},{16,1},{18,3},{17,0},{19,2},{4,21},{6,... | collective-permute-start | bytes 6152 | tf_op jit(solution)/shard_map/ppermute | solution.py:755
  102.8 1.0 copy-start.2
  103.7 27.8 %collective-permute-start.15 = (f32[4,512]{1,0:T(4,128)S(1)}, f32[4,512]{1,0:T(4,128)S(1)}, u32[]{:S(2)}, u32[]{:S(2)}) collective-permute-start(f32[4,512]{1,0:T(4,128)S(1)} %get-tuple-element.58), channel_id=1, source_target_pairs={{4,24},{8,20},{20,8},{24,4},{5,25},{9,21},{21,9},{25,5},{6,26},{10... | collective-permute-start | bytes 24584 | tf_op jit(solution)/shard_map/ppermute | solution.py:750
  104.4 27.2 %collective-permute-start.16 = (f32[4,512]{1,0:T(4,128)S(1)}, f32[4,512]{1,0:T(4,128)S(1)}, u32[]{:S(2)}, u32[]{:S(2)}) collective-permute-start(f32[4,512]{1,0:T(4,128)S(1)} %get-tuple-element.59), channel_id=1, source_target_pairs={{0,20},{8,28},{4,16},{12,24},{16,4},{24,12},{20,0},{28,8},{1,21},{... | collective-permute-start | bytes 24584 | tf_op jit(solution)/shard_map/ppermute | solution.py:751
  112.7 21.1 %copy-start.3 = (f32[4,128,512]{2,1,0:T(8,128)S(1)}, f32[4,128,512]{2,1,0:T(8,128)}, u32[]{:S(2)}) copy-start(f32[4,128,512]{2,1,0:T(8,128)} %copy-done.2) | copy-start | bytes 3145732
  118.6 15.1 %collective-permute-start.13 = (f32[4,512]{1,0:T(4,128)S(1)}, f32[4,512]{1,0:T(4,128)S(1)}, u32[]{:S(2)}, u32[]{:S(2)}) collective-permute-start(f32[4,512]{1,0:T(4,128)S(1)} %get-tuple-element.56), channel_id=1, source_target_pairs={{4,8},{8,4},{5,9},{9,5},{6,10},{10,6},{7,11},{11,7},{20,24},{24,20... | collective-permute-start | bytes 24584 | tf_op jit(solution)/shard_map/ppermute | solution.py:764
  119.3 14.5 %collective-permute-start.14 = (f32[4,512]{1,0:T(4,128)S(1)}, f32[4,512]{1,0:T(4,128)S(1)}, u32[]{:S(2)}, u32[]{:S(2)}) collective-permute-start(f32[4,512]{1,0:T(4,128)S(1)} %get-tuple-element.57), channel_id=1, source_target_pairs={{0,4},{8,12},{4,0},{12,8},{1,5},{9,13},{5,1},{13,9},{2,6},{10,14},... | collective-permute-start | bytes 24584 | tf_op jit(solution)/shard_map/ppermute | solution.py:765
  128.9 4.9 %collective-permute-start.11 = (f32[4,128]{1,0:T(4,128)S(1)}, f32[4,128]{1,0:T(4,128)S(1)}, u32[]{:S(2)}, u32[]{:S(2)}) collective-permute-start(f32[4,128]{1,0:T(4,128)S(1)} %get-tuple-element.54), channel_id=1, source_target_pairs={{1,2},{2,1},{5,6},{6,5},{9,10},{10,9},{13,14},{14,13},{17,18},{18,... | collective-permute-start | bytes 6152 | tf_op jit(solution)/shard_map/ppermute | solution.py:768
  131.5 2.2 %collective-permute-start.12 = (f32[4,128]{1,0:T(4,128)S(1)}, f32[4,128]{1,0:T(4,128)S(1)}, u32[]{:S(2)}, u32[]{:S(2)}) collective-permute-start(f32[4,128]{1,0:T(4,128)S(1)} %get-tuple-element.55), channel_id=1, source_target_pairs={{0,1},{2,3},{1,0},{3,2},{4,5},{6,7},{5,4},{7,6},{8,9},{10,11},{9,8... | collective-permute-start | bytes 6152 | tf_op jit(solution)/shard_map/ppermute | solution.py:769

commit v14 on v12

--- a/solution.py
+++ b/solution.py
@@ -271,6 +271,7 @@
         return jnp.where(odd, high_rim, low_rim), jnp.where(odd, low_rim, high_rim)
 
     columns = {}
+    column_of = lax.broadcasted_iota(jnp.int32, (cells_x, width), 1)
     for q in range(parts):
         chosen = pick[pl.ds(q * cells_x, cells_x), :]
         total = jnp.dot(chosen, high[...], preferred_element_type=jnp.float32)
@@ -281,11 +282,13 @@
             rims = in_order(0, tile[:1], tile[cells_x - 1 :])
             for rim_ref, rim in zip((x0_ref, x1_ref), rims):
                 rim_ref[pl.ds(f, 1), pl.ds(q * width, width)] = rim
-            if q in (0, parts - 1):
-                columns[q, f] = tile.T[:1] if q == 0 else tile.T[width - 1 :]
-    for f in range(fields):
-        rims = in_order(1, columns[0, f], columns[parts - 1, f])
-        y0_ref[pl.ds(f, 1), :], y1_ref[pl.ds(f, 1), :] = rims
+            for edge, at in ((0, 0), (parts - 1, width - 1)):
+                if q == edge:
+                    moved = (f - at) % width
+                    tile = pltpu.roll(tile, moved, 1) if moved else tile
+                    columns[at] = jnp.where(column_of == f, tile, columns.get(at, 0.0))
+    low_rims, high_rims = (columns[at].T[:fields] for at in (0, width - 1))
+    y0_ref[...], y1_ref[...] = in_order(1, low_rims, high_rims)
 
 
 def summed(odd, ids, rows, tiles, capacity, fields, cells_x, cells_y, width):
@@ -538,7 +541,7 @@
     )(rates, mix, *operands, *pinned(pltpu.HBM, state))
 
 
-def finish_kernel(first, with_x, gamma_ref, mix_ref, above, below, before, after, factors, recv,
+def finish_kernel(first, with_x, rates_ref, mix_ref, above, below, before, after, factors, recv,
                   left, right, *rest):
     tops, rest = (rest[:2], rest[2:]) if with_x else (None, rest)
     late, rest = (rest[:2], rest[2:]) if with_x else (None, rest)
@@ -547,7 +550,7 @@
     new_ref, out_ref, done_ref = rest[-11:-8]
     base, wide, lines, sides, outer, base_sems, out_sems, outer_sems = rest[-8:]
     count, cells_x, cells_y = base.shape
-    mix_b = mix_ref[0, 1]
+    mix_b = jnp.broadcast_to(mix_ref[1:2, 0:1], (STRIP, cells_y))
     keep_row = above.shape[0] - 5
     keep = slice(keep_row, keep_row + 1)
     ends = (0, cells_x - STRIP)
@@ -575,8 +578,8 @@
         outer_copy(f, i, False).start()
     done_ref[...] = jnp.zeros_like(done_ref)
     def in_order(i, pair):
-        odd = odd_ref[0, i] == 1
         in_odd, in_even = pair[0][...], pair[1][...]
+        odd = jnp.broadcast_to(odd_ref[i : i + 1, 0:1], in_odd.shape) == 1.0
         return jnp.where(odd, in_even, in_odd), jnp.where(odd, in_odd, in_even)
 
     if with_x:
@@ -592,11 +595,12 @@
     lane = lax.broadcasted_iota(jnp.int32, (STRIP, cells_y), 1)
 
     def one_field(f, carry):
-        rate = gamma_ref[0, first + f]
-        both = [sides[pl.ds(f, 1), :] * rate, sides[pl.ds(count + f, 1), :] * rate]
+        rate = jnp.broadcast_to(rates_ref[pl.ds(first + f, 1), 0:1], (STRIP, cells_y))
+        line_rate, side_rate = rate[:1], rate[:1, :cells_x]
+        both = [sides[pl.ds(f, 1), :] * side_rate, sides[pl.ds(count + f, 1), :] * side_rate]
         cols = columns_of(jnp.concatenate(both, axis=0))
-        wide[STRIP - 1 : STRIP, :] = lines[pl.ds(f, 1), :] * rate
-        wide[STRIP + cells_x : STRIP + cells_x + 1, :] = lines[pl.ds(count + f, 1), :] * rate
+        wide[STRIP - 1 : STRIP, :] = lines[pl.ds(f, 1), :] * line_rate
+        wide[STRIP + cells_x : STRIP + cells_x + 1, :] = lines[pl.ds(count + f, 1), :] * line_rate
         to_out, to_new = out_copies(f)
         to_out.start()
         for i in range(0, cells_x, STRIP):
@@ -623,8 +627,9 @@
             outer_copy(f, i, False).wait()
             row = i * (STRIP - 1)
             at = ends[i] + row
-            line = late[i][f : f + 1, :] * (above, below)[i][keep, :] * gamma_ref[0, count + f]
-            more = mix_b * factors[1 + i, at : at + 1, :] * line
+            rate = jnp.broadcast_to(rates_ref[count + f : count + f + 1, 0:1], (1, cells_y))
+            line = late[i][f : f + 1, :] * (above, below)[i][keep, :] * rate
+            more = mix_b[:1] * factors[1 + i, at : at + 1, :] * line
             outer[f, i, row : row + 1, :] = outer[f, i, row : row + 1, :] + more
             outer_copy(f, i, True).start()
 
@@ -639,20 +644,18 @@
 
 
 def finished(
-    first, new_state, remapped, recv, odd, x_rims, y_rims, closing, gamma, mix, factors, received
+    first, new_state, remapped, recv, odd, x_rims, y_rims, closing, rates, mix, factors, received
 ):
     count, cells_x, cells_y = recv.shape
-    chan = gamma.shape[1]
+    chan = 2 * count
     with_x = x_rims is not None
     anywhere = pl.BlockSpec(memory_space=pl.ANY)
-    operands = [gamma, mix, *received, factors, recv, *y_rims]
+    operands = [rates, mix, *received, factors, recv, *y_rims]
     if with_x:
         late_rims, base_early, late_done = closing
         operands += [*x_rims, *late_rims, base_early]
-    scalars = pl.BlockSpec(memory_space=pltpu.SMEM)
-    specs = [scalars] * 2 + [pl.BlockSpec(memory_space=pltpu.VMEM)] * (len(operands) - 2)
     operands.append(odd)
-    specs += [scalars, anywhere]
+    specs = [pl.BlockSpec(memory_space=pltpu.VMEM)] * len(operands) + [anywhere]
     aliases = {len(operands): 0}
     operands.append(new_state)
     if remapped is not None:
@@ -750,9 +753,10 @@
         lax.ppermute(y_odd, ("comp", "ty"), crossed("ty", 1)),
         lax.ppermute(y_even, ("comp", "ty"), crossed("ty", 0)),
     )
-    rest = (gamma, mix, factors, received)
+    lanes = lambda a: jnp.broadcast_to(a.T, (a.shape[1], LANES))
+    rest = (lanes(rates), lanes(mix), factors, received)
     new_state, remapped, done = finished(
-        half, base, None, recv_late, odd, None, late_y, None, *rest
+        half, base, None, recv_late, odd_lanes, None, late_y, None, *rest
     )
     early_in, done = lax.optimization_barrier((early_in, done))
     recv_early, x_odd, x_even, y_odd, y_even = add_up(odd_lanes, ids_early, early_in)
@@ -765,7 +769,7 @@
         lax.ppermute(y_even, "ty", neighbour_pairs(ty, 0)),
     )
     new_state, remapped, _ = finished(
-        0, new_state, remapped, recv_early, odd, early_x, early_y, (late_x, base_early, done), *rest
+        0, new_state, remapped, recv_early, odd_lanes, early_x, early_y, (late_x, base_early, done), *rest
     )
     return new_state, remapped
 

time: 138 us -> 138 us (level)
  no operation moved by 1% of the time
where the time goes in v14:
time: 138 us; the launch traced here: 137 us
  starting transfers between devices  61.5 us (45%)
  Pallas kernels  43.3 us (31%)
  waiting for transfers between devices  29 us (21%)
  local copies, waits for them, and re-layouts  1.99 us (1%)
    all_to_all x2, starting transfers between devices, exchanged(): lax.all_to_all(rows, ('tx', 'ty'), split_axis=0, concat_axis=0, tiled=True)  19.8 us
    pallas_call x1, Pallas kernels, base_of(): pl.pallas_call(functools.partial(base_kernel, half), grid=(nfield // PER_...  12.1 us
    pallas_call x1, Pallas kernels, contributions(): pl.pallas_call(functools.partial(contribution_kernel, dims), in_specs=[pl...  10.8 us
    ppermute x1, waiting for transfers between devices, body(): early = lax.ppermute(early, 'comp', swap)  10 us
    ppermute x1, starting transfers between devices, body(): lax.ppermute(x_even, 'tx', neighbour_pairs(tx, 0))  9.55 us
    all_to_all x2, waiting for transfers between devices, exchanged(): lax.all_to_all(rows, ('tx', 'ty'), split_axis=0, concat_axis=0, tiled=True)  8.77 us
    ppermute x1, waiting for transfers between devices, body(): above = lax.ppermute(x_high, 'tx', shift_pairs(tx, 1))  7.72 us
    pallas_call x2, Pallas kernels, finished(): pl.pallas_call(functools.partial(finish_kernel, first, with_x), in_specs=...  7.12 us
  transfers between devices with their start and end apart: 19, of which 6 were waited for; matrix products, arithmetic and copies ran while one was open for 1% of the time, Pallas kernels for 21%

profile of v14, /device:TPU:1, one launch (start us, length us, event | category | flops | bytes accessed | tf_op | source)
XLA Modules:
  0.0 136.8 jit_solution(9556178791883812893)
XLA Ops:
  0.6 10.8 %contributions.1 = (f32[513,4,128]{2,1,0:T(4,128)}, f32[1040,4,128]{2,1,0:T(4,128)}) custom-call(s32[1,512]{1,0:T(1,128)} %src_ref.1, s32[1,512]{1,0:T(1,128)} %bitcast.16, s32[1,512]{1,0:T(1,128)} %blk_ref.1, f32[1,16,128,512]{3,2,1,0:T(8,128)} %state_ref.3, bf16[1,512,128,128]{3,2,1,0:T(8,128)(2,1)} %weights_ref.1), custom_call_target="tpu_custom_call" | custom-call | flops 134217728 | bytes 25296896 | tf_op jit(solution)/shard_map/contributions/pallas_call | solution.py:166
  11.4 0.0 copy-start.4
  11.5 0.0 copy-start
  11.5 0.0 copy-start.1
  11.5 7.5 %all-to-all-start = ((f32[16,65,4,128]{3,2,1,0:T(4,128)}), f32[16,65,4,128]{3,2,1,0:T(4,128)}, u32[]{:S(2)}, u32[]{:S(2)}) async-start(f32[16,65,4,128]{3,2,1,0:T(4,128)} %bitcast.5), calls=%async_computation | async-start | bytes 4259840 | tf_op jit(solution)/shard_map/all_to_all | solution.py:708
  19.0 1.2 collective-permute-start
  20.2 3.2 %edges.1 = (f32[40,512]{1,0:T(8,128)S(1)}, f32[40,512]{1,0:T(8,128)S(1)}, f32[40,128]{1,0:T(8,128)S(1)}, f32[40,128]{1,0:T(8,128)S(1)}) custom-call(f32[1,2]{1,0:T(1,128)S(1)} %get-tuple-element.72.mix_ref, f32[1,16,128,512]{3,2,1,0:T(8,128)} %state_ref.3, f32[1,16,128,512]{3,2,1,0:T(8,128)} %state_ref.3, f32[1,16,128,512]{3,2,1,0:T(8,128)} %state_ref.3, ...), custom_call_target="tpu_custom_call" | custom-call | flops 1048576 | bytes 4194304 | tf_op jit(solution)/shard_map/edges/pallas_call | solution.py:422
  23.4 3.3 %collective-permute-start.1 = (f32[40,512]{1,0:T(8,128)S(1)}, f32[40,512]{1,0:T(8,128)S(1)}, u32[]{:S(2)}, u32[]{:S(2)}) collective-permute-start(f32[40,512]{1,0:T(8,128)S(1)} %get-tuple-element.37.x_high), channel_id=1, source_target_pairs={{0,4},{4,8},{8,12},{1,5},{5,9},{9,13},{2,6},{6,10},{10,14},{3,7},{... | collective-permute-start | bytes 245768 | tf_op jit(solution)/shard_map/ppermute | solution.py:725
  26.7 1.3 collective-permute-start.2
  28.0 3.9 %collective-permute-start.3 = (f32[40,128]{1,0:T(8,128)S(1)}, f32[40,128]{1,0:T(8,128)S(1)}, u32[]{:S(2)}, u32[]{:S(2)}) collective-permute-start(f32[40,128]{1,0:T(8,128)S(1)} %get-tuple-element.39.y_high), channel_id=1, source_target_pairs={{0,1},{1,2},{2,3},{4,5},{5,6},{6,7},{8,9},{9,10},{10,11},{12,13},{... | collective-permute-start | bytes 61448 | tf_op jit(solution)/shard_map/ppermute | solution.py:723
  31.9 1.9 %collective-permute-start.4 = (f32[40,128]{1,0:T(8,128)S(1)}, f32[40,128]{1,0:T(8,128)S(1)}, u32[]{:S(2)}, u32[]{:S(2)}) collective-permute-start(f32[40,128]{1,0:T(8,128)S(1)} %get-tuple-element.40.y_low), channel_id=1, source_target_pairs={{1,0},{2,1},{3,2},{5,4},{6,5},{7,6},{9,8},{10,9},{11,10},{13,12},{... | collective-permute-start | bytes 61448 | tf_op jit(solution)/shard_map/ppermute | solution.py:724
  33.9 10.0 %collective-permute-done.in_ref = f32[513,4,128]{2,1,0:T(4,128)S(1)} collective-permute-done((f32[513,4,128]{2,1,0:T(4,128)}, f32[513,4,128]{2,1,0:T(4,128)S(1)}, u32[]{:S(2)}, u32[]{:S(2)}) %collective-permute-start) | collective-permute-done | bytes 1050656 | tf_op jit(solution)/shard_map/ppermute | solution.py:714
  43.9 4.0 %place_in_slots.1 = f32[1024,4,128]{2,1,0:T(4,128)} custom-call(f32[513,4,128]{2,1,0:T(4,128)S(1)} %collective-permute-done.in_ref), custom_call_target="tpu_custom_call" | custom-call | flops 1050624 | bytes 3151872 | tf_op jit(solution)/shard_map/place_in_slots/pallas_call | solution.py:217
  47.9 0.0 collective-permute-done.3.left.before
  47.9 0.0 collective-permute-done.4.right.after
  47.9 7.7 %collective-permute-done.1.above = f32[40,512]{1,0:T(8,128)S(1)} collective-permute-done((f32[40,512]{1,0:T(8,128)S(1)}, f32[40,512]{1,0:T(8,128)S(1)}, u32[]{:S(2)}, u32[]{:S(2)}) %collective-permute-start.1) | collective-permute-done | bytes 81952 | tf_op jit(solution)/shard_map/ppermute | solution.py:725
  55.7 5.4 %all-to-all-done = f32[16,65,4,128]{3,2,1,0:T(4,128)} async-done(((f32[16,65,4,128]{3,2,1,0:T(4,128)}), f32[16,65,4,128]{3,2,1,0:T(4,128)}, u32[]{:S(2)}, u32[]{:S(2)}) %all-to-all-start) | async-done | bytes 2129952 | tf_op jit(solution)/shard_map/all_to_all | solution.py:708
  61.1 12.3 %all-to-all-start.1 = ((f32[16,64,4,128]{3,2,1,0:T(4,128)}), f32[16,64,4,128]{3,2,1,0:T(4,128)}, u32[]{:S(2)}, u32[]{:S(2)}) async-start(f32[16,64,4,128]{3,2,1,0:T(4,128)} %bitcast.7), calls=%async_computation.1 | async-start | bytes 4194304 | tf_op jit(solution)/shard_map/all_to_all | solution.py:708
  73.4 0.1 fusion
  73.5 0.8 slice.20
  74.2 0.1 broadcast_in_dim.27.odd_ref.rest_0_.rest_5_
  74.3 3.0 %sum_by_block.2 = (f32[4,128,512]{2,1,0:T(8,128)S(1)}, f32[4,512]{1,0:T(4,128)S(1)}, f32[4,512]{1,0:T(4,128)S(1)}, f32[4,128]{1,0:T(4,128)S(1)}, f32[4,128]{1,0:T(4,128)S(1)}) custom-call(f32[2,128]{1,0:T(2,128)S(1)} %broadcast_in_dim.27.odd_ref.rest_0_.rest_5_, f32[16,128]{1,0:T(8,128)S(1)} %bitcast.14, f32[4160,128]{1,0:T(8,128)} %bitcast.8.rows_ref), custom_call_target="tpu_custom_call" | custom-call | flops 1073741824 | bytes 3145728 | tf_op jit(solution)/shard_map/sum_by_block/pallas_call | solution.py:306
  77.4 1.3 collective-permute-start.8
  78.7 3.8 %collective-permute-start.5 = (f32[80,128]{1,0:T(8,128)S(1)}, f32[80,128]{1,0:T(8,128)S(1)}, u32[]{:S(2)}, u32[]{:S(2)}) collective-permute-start(f32[80,128]{1,0:T(8,128)S(1)} %pad_maximum_fusion), channel_id=1, source_target_pairs={{0,1},{1,2},{2,3},{4,5},{5,6},{6,7},{8,9},{9,10},{10,11},{12,13},{... | collective-permute-start | bytes 122888 | tf_op jit(solution)/shard_map/ppermute | solution.py:735
  82.5 1.9 %collective-permute-start.6 = (f32[80,128]{1,0:T(8,128)S(1)}, f32[80,128]{1,0:T(8,128)S(1)}, u32[]{:S(2)}, u32[]{:S(2)}) collective-permute-start(f32[80,128]{1,0:T(8,128)S(1)} %pad_maximum_fusion.1), channel_id=1, source_target_pairs={{1,0},{2,1},{3,2},{5,4},{6,5},{7,6},{9,8},{10,9},{11,10},{13,12},{... | collective-permute-start | bytes 122888 | tf_op jit(solution)/shard_map/ppermute | solution.py:736
  84.4 0.3 collective-permute-start.7
  84.8 4.8 %collective-permute-start.9 = (f32[4,128]{1,0:T(4,128)S(1)}, f32[4,128]{1,0:T(4,128)S(1)}, u32[]{:S(2)}, u32[]{:S(2)}) collective-permute-start(f32[4,128]{1,0:T(4,128)S(1)} %get-tuple-element.48), channel_id=1, source_target_pairs={{1,18},{2,17},{17,2},{18,1},{5,22},{6,21},{21,6},{22,5},{9,26},{10... | collective-permute-start | bytes 6152 | tf_op jit(solution)/shard_map/ppermute | solution.py:753
  89.6 0.0 collective-permute-done.5.corners_left
  89.6 0.1 collective-permute-start.10
  89.7 0.3 collective-permute-done.6.corners_right
  90.0 0.1 broadcast_in_dim.11.rates_ref
  90.0 12.1 %base.1 = (f32[1,16,128,512]{3,2,1,0:T(8,128)}, f32[4,128,512]{2,1,0:T(8,128)S(1)}, f32[6,128,512]{2,1,0:T(8,128)S(1)}) custom-call(f32[1,16]{1,0:T(1,128)S(1)} %get-tuple-element.70.rate_ref, f32[1,2]{1,0:T(1,128)S(1)} %get-tuple-element.72.mix_ref, f32[16,128]{1,0:T(8,128)S(1)} %broadcast_in_dim.11.rates_ref, f32[1,3,128,512]{3,2,1,0:T(8,128)S(1)} %copy-done, ...), custom_call_target="tpu_custom_call" | custom-call | flops 41943040 | bytes 8388608 | tf_op jit(solution)/shard_map/base/pallas_call | solution.py:513
  102.1 1.0 copy-done.2
  103.1 0.6 collective-permute-start.15
  103.7 4.3 %collective-permute-start.16 = (f32[4,512]{1,0:T(4,128)S(1)}, f32[4,512]{1,0:T(4,128)S(1)}, u32[]{:S(2)}, u32[]{:S(2)}) collective-permute-start(f32[4,512]{1,0:T(4,128)S(1)} %get-tuple-element.59), channel_id=1, source_target_pairs={{0,20},{8,28},{4,16},{12,24},{16,4},{24,12},{20,0},{28,8},{1,21},{... | collective-permute-start | bytes 24584 | tf_op jit(solution)/shard_map/ppermute | solution.py:750
  108.1 0.1 broadcast_in_dim.26.mix_ref
  108.1 3.5 %finish.2 = (f32[1,16,128,512]{3,2,1,0:T(8,128)}, f32[1,8,128,512]{3,2,1,0:T(8,128)}, f32[8,128]{1,0:T(8,128)S(1)}) custom-call(f32[16,128]{1,0:T(8,128)S(1)} %broadcast_in_dim.11.rates_ref, f32[2,128]{1,0:T(2,128)S(1)} %broadcast_in_dim.26.mix_ref, f32[40,512]{1,0:T(8,128)S(1)} %collective-permute-done.1.above, ...), custom_call_target="tpu_custom_call", output_to_operand_aliasing={{0}: (11, {})} | custom-call | flops 5242880 | bytes 5242880 | tf_op jit(solution)/shard_map/finish/pallas_call | solution.py:665
  111.7 3.3 %all-to-all-done.1 = f32[16,64,4,128]{3,2,1,0:T(4,128)} async-done(((f32[16,64,4,128]{3,2,1,0:T(4,128)}), f32[16,64,4,128]{3,2,1,0:T(4,128)}, u32[]{:S(2)}, u32[]{:S(2)}) %all-to-all-start.1) | async-done | bytes 2097184 | tf_op jit(solution)/shard_map/all_to_all | solution.py:708
  115.0 0.0 collective-permute-done.7.ids_ref
  115.0 3.0 %sum_by_block.3 = (f32[4,128,512]{2,1,0:T(8,128)S(1)}, f32[4,512]{1,0:T(4,128)S(1)}, f32[4,512]{1,0:T(4,128)S(1)}, f32[4,128]{1,0:T(4,128)S(1)}, f32[4,128]{1,0:T(4,128)S(1)}) custom-call(f32[2,128]{1,0:T(2,128)S(1)} %broadcast_in_dim.27.odd_ref.rest_0_.rest_5_, f32[16,128]{1,0:T(8,128)S(1)} %collective-permute-done.7.ids_ref, f32[4096,128]{1,0:T(8,128)} %bitcast.9.rows_ref), custom_call_target="tpu_custom_call" | custom-call | flops 1073741824 | bytes 3145728 | tf_op jit(solution)/shard_map/sum_by_block/pallas_call | solution.py:306
  118.0 0.7 collective-permute-start.13
  118.7 9.6 %collective-permute-start.14 = (f32[4,512]{1,0:T(4,128)S(1)}, f32[4,512]{1,0:T(4,128)S(1)}, u32[]{:S(2)}, u32[]{:S(2)}) collective-permute-start(f32[4,512]{1,0:T(4,128)S(1)} %get-tuple-element.57), channel_id=1, source_target_pairs={{0,4},{8,12},{4,0},{12,8},{1,5},{9,13},{5,1},{13,9},{2,6},{10,14},... | collective-permute-start | bytes 24584 | tf_op jit(solution)/shard_map/ppermute | solution.py:765
  128.2 2.7 %collective-permute-start.11 = (f32[4,128]{1,0:T(4,128)S(1)}, f32[4,128]{1,0:T(4,128)S(1)}, u32[]{:S(2)}, u32[]{:S(2)}) collective-permute-start(f32[4,128]{1,0:T(4,128)S(1)} %get-tuple-element.54), channel_id=1, source_target_pairs={{1,2},{2,1},{5,6},{6,5},{9,10},{10,9},{13,14},{14,13},{17,18},{18,... | collective-permute-start | bytes 6152 | tf_op jit(solution)/shard_map/ppermute | solution.py:768
  130.9 0.0 collective-permute-done.15.rest_2_
  130.9 0.1 collective-permute-start.12
  131.0 2.1 %collective-permute-done.11.left = f32[4,128]{1,0:T(4,128)S(1)} collective-permute-done((f32[4,128]{1,0:T(4,128)S(1)}, f32[4,128]{1,0:T(4,128)S(1)}, u32[]{:S(2)}, u32[]{:S(2)}) %collective-permute-start.11) | collective-permute-done | bytes 2080 | tf_op jit(solution)/shard_map/ppermute | solution.py:768
  133.1 0.0 collective-permute-done.14.rest_1_
  133.2 3.6 %finish.3 = (f32[1,16,128,512]{3,2,1,0:T(8,128)}, f32[1,8,128,512]{3,2,1,0:T(8,128)}, f32[8,128]{1,0:T(8,128)}) custom-call(f32[16,128]{1,0:T(8,128)S(1)} %broadcast_in_dim.11.rates_ref, f32[2,128]{1,0:T(2,128)S(1)} %broadcast_in_dim.26.mix_ref, f32[40,512]{1,0:T(8,128)S(1)} %collective-permute-done.1.above, ...), custom_call_target="tpu_custom_call", output_to_operand_aliasing={{0}: (16, {}), {1}: (17, {})} | custom-call | flops 5242880 | bytes 5242880 | tf_op jit(solution)/shard_map/finish/pallas_call | solution.py:665
  (20 shorter events, 0.1 us)
Async XLA Ops:
  11.4 8.7 %copy-start.4 = (f32[1,2]{1,0:T(1,128)S(1)}, f32[1,2]{1,0:T(1,128)}, u32[]{:S(2)}) copy-start(f32[1,2]{1,0:T(1,128)} %constant.23.clone) | copy-start | bytes 28
  11.5 8.7 %copy-start = (f32[1,3,128,512]{3,2,1,0:T(8,128)S(1)}, f32[1,3,128,512]{3,2,1,0:T(8,128)}, u32[]{:S(2)}) copy-start(f32[1,3,128,512]{3,2,1,0:T(8,128)} %coefs_ref.1) | copy-start | bytes 2359300
  11.5 8.7 %copy-start.1 = (s32[128,512]{1,0:T(8,128)S(1)}, s32[128,512]{1,0:T(8,128)}, u32[]{:S(2)}) copy-start(s32[128,512]{1,0:T(8,128)} %land_ref) | copy-start | bytes 786436
  11.5 49.6 %all-to-all-start = ((f32[16,65,4,128]{3,2,1,0:T(4,128)}), f32[16,65,4,128]{3,2,1,0:T(4,128)}, u32[]{:S(2)}, u32[]{:S(2)}) async-start(f32[16,65,4,128]{3,2,1,0:T(4,128)} %bitcast.5), calls=%async_computation | async-start | bytes 4259840 | tf_op jit(solution)/shard_map/all_to_all | solution.py:708
  19.0 24.9 %collective-permute-start = (f32[513,4,128]{2,1,0:T(4,128)}, f32[513,4,128]{2,1,0:T(4,128)S(1)}, u32[]{:S(2)}, u32[]{:S(2)}) collective-permute-start(f32[513,4,128]{2,1,0:T(4,128)} %get-tuple-element.34), channel_id=1, source_target_pairs={{0,16},{16,0},{1,17},{17,1},{2,18},{18,2},{3,19},{19,3},{4,20},{20... | collective-permute-start | bytes 3151880 | tf_op jit(solution)/shard_map/ppermute | solution.py:714
  23.4 32.2 %collective-permute-start.1 = (f32[40,512]{1,0:T(8,128)S(1)}, f32[40,512]{1,0:T(8,128)S(1)}, u32[]{:S(2)}, u32[]{:S(2)}) collective-permute-start(f32[40,512]{1,0:T(8,128)S(1)} %get-tuple-element.37.x_high), channel_id=1, source_target_pairs={{0,4},{4,8},{8,12},{1,5},{5,9},{9,13},{2,6},{6,10},{10,14},{3,7},{... | collective-permute-start | bytes 245768 | tf_op jit(solution)/shard_map/ppermute | solution.py:725
  26.7 28.9 %collective-permute-start.2 = (f32[40,512]{1,0:T(8,128)S(1)}, f32[40,512]{1,0:T(8,128)S(1)}, u32[]{:S(2)}, u32[]{:S(2)}) collective-permute-start(f32[40,512]{1,0:T(8,128)S(1)} %get-tuple-element.38.x_low), channel_id=1, source_target_pairs={{4,0},{8,4},{12,8},{5,1},{9,5},{13,9},{6,2},{10,6},{14,10},{7,3},{... | collective-permute-start | bytes 245768 | tf_op jit(solution)/shard_map/ppermute | solution.py:726
  28.0 19.9 %collective-permute-start.3 = (f32[40,128]{1,0:T(8,128)S(1)}, f32[40,128]{1,0:T(8,128)S(1)}, u32[]{:S(2)}, u32[]{:S(2)}) collective-permute-start(f32[40,128]{1,0:T(8,128)S(1)} %get-tuple-element.39.y_high), channel_id=1, source_target_pairs={{0,1},{1,2},{2,3},{4,5},{5,6},{6,7},{8,9},{9,10},{10,11},{12,13},{... | collective-permute-start | bytes 61448 | tf_op jit(solution)/shard_map/ppermute | solution.py:723
  31.9 16.0 %collective-permute-start.4 = (f32[40,128]{1,0:T(8,128)S(1)}, f32[40,128]{1,0:T(8,128)S(1)}, u32[]{:S(2)}, u32[]{:S(2)}) collective-permute-start(f32[40,128]{1,0:T(8,128)S(1)} %get-tuple-element.40.y_low), channel_id=1, source_target_pairs={{1,0},{2,1},{3,2},{5,4},{6,5},{7,6},{9,8},{10,9},{11,10},{13,12},{... | collective-permute-start | bytes 61448 | tf_op jit(solution)/shard_map/ppermute | solution.py:724
  61.1 53.9 %all-to-all-start.1 = ((f32[16,64,4,128]{3,2,1,0:T(4,128)}), f32[16,64,4,128]{3,2,1,0:T(4,128)}, u32[]{:S(2)}, u32[]{:S(2)}) async-start(f32[16,64,4,128]{3,2,1,0:T(4,128)} %bitcast.7), calls=%async_computation.1 | async-start | bytes 4194304 | tf_op jit(solution)/shard_map/all_to_all | solution.py:708
  74.3 10.4 %copy-start.5 = (f32[1,8]{1,0:T(1,128)S(1)}, f32[1,8]{1,0:T(1,128)}, u32[]{:S(2)}) copy-start(f32[1,8]{1,0:T(1,128)} %param.13) | copy-start | bytes 100
  77.4 30.7 %collective-permute-start.8 = (f32[4,128,512]{2,1,0:T(8,128)S(1)}, f32[4,128,512]{2,1,0:T(8,128)S(1)}, u32[]{:S(2)}, u32[]{:S(2)}) collective-permute-start(f32[4,128,512]{2,1,0:T(8,128)S(1)} %get-tuple-element.47), channel_id=1, source_target_pairs={{0,16},{16,0},{1,17},{17,1},{2,18},{18,2},{3,19},{19,3},{4,20},{20... | collective-permute-start | bytes 3145736 | tf_op jit(solution)/shard_map/ppermute | solution.py:747
  78.7 10.9 %collective-permute-start.5 = (f32[80,128]{1,0:T(8,128)S(1)}, f32[80,128]{1,0:T(8,128)S(1)}, u32[]{:S(2)}, u32[]{:S(2)}) collective-permute-start(f32[80,128]{1,0:T(8,128)S(1)} %pad_maximum_fusion), channel_id=1, source_target_pairs={{0,1},{1,2},{2,3},{4,5},{5,6},{6,7},{8,9},{9,10},{10,11},{12,13},{... | collective-permute-start | bytes 122888 | tf_op jit(solution)/shard_map/ppermute | solution.py:735
  82.5 7.5 %collective-permute-start.6 = (f32[80,128]{1,0:T(8,128)S(1)}, f32[80,128]{1,0:T(8,128)S(1)}, u32[]{:S(2)}, u32[]{:S(2)}) collective-permute-start(f32[80,128]{1,0:T(8,128)S(1)} %pad_maximum_fusion.1), channel_id=1, source_target_pairs={{1,0},{2,1},{3,2},{5,4},{6,5},{7,6},{9,8},{10,9},{11,10},{13,12},{... | collective-permute-start | bytes 122888 | tf_op jit(solution)/shard_map/ppermute | solution.py:736
  84.4 30.5 %collective-permute-start.7 = (f32[16,128]{1,0:T(8,128)S(1)}, f32[16,128]{1,0:T(8,128)S(1)}, u32[]{:S(2)}, u32[]{:S(2)}) collective-permute-start(f32[16,128]{1,0:T(8,128)S(1)} %bitcast.15), channel_id=1, source_target_pairs={{0,16},{16,0},{1,17},{17,1},{2,18},{18,2},{3,19},{19,3},{4,20},{20... | collective-permute-start | bytes 24584 | tf_op jit(solution)/shard_map/ppermute | solution.py:743
  84.8 19.0 %collective-permute-start.9 = (f32[4,128]{1,0:T(4,128)S(1)}, f32[4,128]{1,0:T(4,128)S(1)}, u32[]{:S(2)}, u32[]{:S(2)}) collective-permute-start(f32[4,128]{1,0:T(4,128)S(1)} %get-tuple-element.48), channel_id=1, source_target_pairs={{1,18},{2,17},{17,2},{18,1},{5,22},{6,21},{21,6},{22,5},{9,26},{10... | collective-permute-start | bytes 6152 | tf_op jit(solution)/shard_map/ppermute | solution.py:753
  89.6 18.4 %collective-permute-start.10 = (f32[4,128]{1,0:T(4,128)S(1)}, f32[4,128]{1,0:T(4,128)S(1)}, u32[]{:S(2)}, u32[]{:S(2)}) collective-permute-start(f32[4,128]{1,0:T(4,128)S(1)} %get-tuple-element.49), channel_id=1, source_target_pairs={{0,17},{2,19},{1,16},{3,18},{16,1},{18,3},{17,0},{19,2},{4,21},{6,... | collective-permute-start | bytes 6152 | tf_op jit(solution)/shard_map/ppermute | solution.py:754
  102.1 1.0 copy-start.2
  103.1 27.8 %collective-permute-start.15 = (f32[4,512]{1,0:T(4,128)S(1)}, f32[4,512]{1,0:T(4,128)S(1)}, u32[]{:S(2)}, u32[]{:S(2)}) collective-permute-start(f32[4,512]{1,0:T(4,128)S(1)} %get-tuple-element.58), channel_id=1, source_target_pairs={{4,24},{8,20},{20,8},{24,4},{5,25},{9,21},{21,9},{25,5},{6,26},{10... | collective-permute-start | bytes 24584 | tf_op jit(solution)/shard_map/ppermute | solution.py:749
  103.7 27.3 %collective-permute-start.16 = (f32[4,512]{1,0:T(4,128)S(1)}, f32[4,512]{1,0:T(4,128)S(1)}, u32[]{:S(2)}, u32[]{:S(2)}) collective-permute-start(f32[4,512]{1,0:T(4,128)S(1)} %get-tuple-element.59), channel_id=1, source_target_pairs={{0,20},{8,28},{4,16},{12,24},{16,4},{24,12},{20,0},{28,8},{1,21},{... | collective-permute-start | bytes 24584 | tf_op jit(solution)/shard_map/ppermute | solution.py:750
  111.6 21.5 %copy-start.3 = (f32[4,128,512]{2,1,0:T(8,128)S(1)}, f32[4,128,512]{2,1,0:T(8,128)}, u32[]{:S(2)}) copy-start(f32[4,128,512]{2,1,0:T(8,128)} %copy-done.2) | copy-start | bytes 3145732
  118.0 15.1 %collective-permute-start.13 = (f32[4,512]{1,0:T(4,128)S(1)}, f32[4,512]{1,0:T(4,128)S(1)}, u32[]{:S(2)}, u32[]{:S(2)}) collective-permute-start(f32[4,512]{1,0:T(4,128)S(1)} %get-tuple-element.56), channel_id=1, source_target_pairs={{4,8},{8,4},{5,9},{9,5},{6,10},{10,6},{7,11},{11,7},{20,24},{24,20... | collective-permute-start | bytes 24584 | tf_op jit(solution)/shard_map/ppermute | solution.py:764
  118.7 14.5 %collective-permute-start.14 = (f32[4,512]{1,0:T(4,128)S(1)}, f32[4,512]{1,0:T(4,128)S(1)}, u32[]{:S(2)}, u32[]{:S(2)}) collective-permute-start(f32[4,512]{1,0:T(4,128)S(1)} %get-tuple-element.57), channel_id=1, source_target_pairs={{0,4},{8,12},{4,0},{12,8},{1,5},{9,13},{5,1},{13,9},{2,6},{10,14},... | collective-permute-start | bytes 24584 | tf_op jit(solution)/shard_map/ppermute | solution.py:765
  128.2 4.9 %collective-permute-start.11 = (f32[4,128]{1,0:T(4,128)S(1)}, f32[4,128]{1,0:T(4,128)S(1)}, u32[]{:S(2)}, u32[]{:S(2)}) collective-permute-start(f32[4,128]{1,0:T(4,128)S(1)} %get-tuple-element.54), channel_id=1, source_target_pairs={{1,2},{2,1},{5,6},{6,5},{9,10},{10,9},{13,14},{14,13},{17,18},{18,... | collective-permute-start | bytes 6152 | tf_op jit(solution)/shard_map/ppermute | solution.py:768
  130.9 2.2 %collective-permute-start.12 = (f32[4,128]{1,0:T(4,128)S(1)}, f32[4,128]{1,0:T(4,128)S(1)}, u32[]{:S(2)}, u32[]{:S(2)}) collective-permute-start(f32[4,128]{1,0:T(4,128)S(1)} %get-tuple-element.55), channel_id=1, source_target_pairs={{0,1},{2,3},{1,0},{3,2},{4,5},{6,7},{5,4},{7,6},{8,9},{10,11},{9,8... | collective-permute-start | bytes 6152 | tf_op jit(solution)/shard_map/ppermute | solution.py:769

commit v15 on v14

--- a/solution.py
+++ b/solution.py
@@ -235,7 +235,7 @@
     tiles, capacity, fields, cells_x, cells_y, width = dims
     parts = cells_y // width
     group = LANES // capacity
-    stride = in_ref.shape[0] // tiles
+    stride = rows_ref.shape[0] // tiles
 
     def rows_copy(k):
         some = pl.ds(k * group * stride, group * stride)
@@ -312,7 +312,7 @@
             pltpu.VMEM((blocks, slots), jnp.bfloat16),
             pltpu.VMEM((slots, fields * width), jnp.bfloat16),
             pltpu.VMEM((slots, fields * width), jnp.bfloat16),
-            pltpu.VMEM(rows.shape, jnp.float32),
+            pltpu.VMEM((rows.shape[0] + 8, width), jnp.float32),
             pltpu.SemaphoreType.DMA((tiles * capacity // LANES,)),
         ],
         compiler_params=pltpu.CompilerParams(vmem_limit_bytes=24 * 1024 * 1024),

time: 138 us -> 138 us (level)
  no operation moved by 1% of the time
where the time goes in v15:
time: 138 us; the launch traced here: 137 us
  starting transfers between devices  61.5 us (45%)
  Pallas kernels  43.3 us (31%)
  waiting for transfers between devices  29 us (21%)
  local copies, waits for them, and re-layouts  1.99 us (1%)
    all_to_all x2, starting transfers between devices, exchanged(): lax.all_to_all(rows, ('tx', 'ty'), split_axis=0, concat_axis=0, tiled=True)  19.8 us
    pallas_call x1, Pallas kernels, base_of(): pl.pallas_call(functools.partial(base_kernel, half), grid=(nfield // PER_...  12.1 us
    pallas_call x1, Pallas kernels, contributions(): pl.pallas_call(functools.partial(contribution_kernel, dims), in_specs=[pl...  10.8 us
    ppermute x1, waiting for transfers between devices, body(): early = lax.ppermute(early, 'comp', swap)  10 us
    ppermute x1, starting transfers between devices, body(): lax.ppermute(x_even, 'tx', neighbour_pairs(tx, 0))  9.55 us
    all_to_all x2, waiting for transfers between devices, exchanged(): lax.all_to_all(rows, ('tx', 'ty'), split_axis=0, concat_axis=0, tiled=True)  8.77 us
    ppermute x1, waiting for transfers between devices, body(): above = lax.ppermute(x_high, 'tx', shift_pairs(tx, 1))  7.72 us
    pallas_call x2, Pallas kernels, finished(): pl.pallas_call(functools.partial(finish_kernel, first, with_x), in_specs=...  7.12 us
  transfers between devices with their start and end apart: 19, of which 6 were waited for; matrix products, arithmetic and copies ran while one was open for 1% of the time, Pallas kernels for 21%

profile of v15, /device:TPU:1, one launch (start us, length us, event | category | flops | bytes accessed | tf_op | source)
XLA Modules:
  0.0 136.8 jit_solution(10059743724483025066)
XLA Ops:
  0.6 10.8 %contributions.1 = (f32[513,4,128]{2,1,0:T(4,128)}, f32[1040,4,128]{2,1,0:T(4,128)}) custom-call(s32[1,512]{1,0:T(1,128)} %src_ref.1, s32[1,512]{1,0:T(1,128)} %bitcast.16, s32[1,512]{1,0:T(1,128)} %blk_ref.1, f32[1,16,128,512]{3,2,1,0:T(8,128)} %state_ref.3, bf16[1,512,128,128]{3,2,1,0:T(8,128)(2,1)} %weights_ref.1), custom_call_target="tpu_custom_call" | custom-call | flops 134217728 | bytes 25296896 | tf_op jit(solution)/shard_map/contributions/pallas_call | solution.py:166
  11.4 0.0 copy-start.4
  11.5 0.0 copy-start
  11.5 0.0 copy-start.1
  11.5 7.5 %all-to-all-start = ((f32[16,65,4,128]{3,2,1,0:T(4,128)}), f32[16,65,4,128]{3,2,1,0:T(4,128)}, u32[]{:S(2)}, u32[]{:S(2)}) async-start(f32[16,65,4,128]{3,2,1,0:T(4,128)} %bitcast.5), calls=%async_computation | async-start | bytes 4259840 | tf_op jit(solution)/shard_map/all_to_all | solution.py:708
  19.0 1.2 collective-permute-start
  20.2 3.2 %edges.1 = (f32[40,512]{1,0:T(8,128)S(1)}, f32[40,512]{1,0:T(8,128)S(1)}, f32[40,128]{1,0:T(8,128)S(1)}, f32[40,128]{1,0:T(8,128)S(1)}) custom-call(f32[1,2]{1,0:T(1,128)S(1)} %get-tuple-element.72.mix_ref, f32[1,16,128,512]{3,2,1,0:T(8,128)} %state_ref.3, f32[1,16,128,512]{3,2,1,0:T(8,128)} %state_ref.3, f32[1,16,128,512]{3,2,1,0:T(8,128)} %state_ref.3, ...), custom_call_target="tpu_custom_call" | custom-call | flops 1048576 | bytes 4194304 | tf_op jit(solution)/shard_map/edges/pallas_call | solution.py:422
  23.4 3.3 %collective-permute-start.1 = (f32[40,512]{1,0:T(8,128)S(1)}, f32[40,512]{1,0:T(8,128)S(1)}, u32[]{:S(2)}, u32[]{:S(2)}) collective-permute-start(f32[40,512]{1,0:T(8,128)S(1)} %get-tuple-element.37.x_high), channel_id=1, source_target_pairs={{0,4},{4,8},{8,12},{1,5},{5,9},{9,13},{2,6},{6,10},{10,14},{3,7},{... | collective-permute-start | bytes 245768 | tf_op jit(solution)/shard_map/ppermute | solution.py:725
  26.7 1.3 collective-permute-start.2
  28.0 3.9 %collective-permute-start.3 = (f32[40,128]{1,0:T(8,128)S(1)}, f32[40,128]{1,0:T(8,128)S(1)}, u32[]{:S(2)}, u32[]{:S(2)}) collective-permute-start(f32[40,128]{1,0:T(8,128)S(1)} %get-tuple-element.39.y_high), channel_id=1, source_target_pairs={{0,1},{1,2},{2,3},{4,5},{5,6},{6,7},{8,9},{9,10},{10,11},{12,13},{... | collective-permute-start | bytes 61448 | tf_op jit(solution)/shard_map/ppermute | solution.py:723
  31.9 1.9 %collective-permute-start.4 = (f32[40,128]{1,0:T(8,128)S(1)}, f32[40,128]{1,0:T(8,128)S(1)}, u32[]{:S(2)}, u32[]{:S(2)}) collective-permute-start(f32[40,128]{1,0:T(8,128)S(1)} %get-tuple-element.40.y_low), channel_id=1, source_target_pairs={{1,0},{2,1},{3,2},{5,4},{6,5},{7,6},{9,8},{10,9},{11,10},{13,12},{... | collective-permute-start | bytes 61448 | tf_op jit(solution)/shard_map/ppermute | solution.py:724
  33.9 10.0 %collective-permute-done.in_ref = f32[513,4,128]{2,1,0:T(4,128)S(1)} collective-permute-done((f32[513,4,128]{2,1,0:T(4,128)}, f32[513,4,128]{2,1,0:T(4,128)S(1)}, u32[]{:S(2)}, u32[]{:S(2)}) %collective-permute-start) | collective-permute-done | bytes 1050656 | tf_op jit(solution)/shard_map/ppermute | solution.py:714
  43.9 4.0 %place_in_slots.1 = f32[1024,4,128]{2,1,0:T(4,128)} custom-call(f32[513,4,128]{2,1,0:T(4,128)S(1)} %collective-permute-done.in_ref), custom_call_target="tpu_custom_call" | custom-call | flops 1050624 | bytes 3151872 | tf_op jit(solution)/shard_map/place_in_slots/pallas_call | solution.py:217
  47.9 0.0 collective-permute-done.3.left.before
  47.9 7.7 %collective-permute-done.1.above = f32[40,512]{1,0:T(8,128)S(1)} collective-permute-done((f32[40,512]{1,0:T(8,128)S(1)}, f32[40,512]{1,0:T(8,128)S(1)}, u32[]{:S(2)}, u32[]{:S(2)}) %collective-permute-start.1) | collective-permute-done | bytes 81952 | tf_op jit(solution)/shard_map/ppermute | solution.py:725
  55.7 5.4 %all-to-all-done = f32[16,65,4,128]{3,2,1,0:T(4,128)} async-done(((f32[16,65,4,128]{3,2,1,0:T(4,128)}), f32[16,65,4,128]{3,2,1,0:T(4,128)}, u32[]{:S(2)}, u32[]{:S(2)}) %all-to-all-start) | async-done | bytes 2129952 | tf_op jit(solution)/shard_map/all_to_all | solution.py:708
  61.1 12.3 %all-to-all-start.1 = ((f32[16,64,4,128]{3,2,1,0:T(4,128)}), f32[16,64,4,128]{3,2,1,0:T(4,128)}, u32[]{:S(2)}, u32[]{:S(2)}) async-start(f32[16,64,4,128]{3,2,1,0:T(4,128)} %bitcast.7), calls=%async_computation.1 | async-start | bytes 4194304 | tf_op jit(solution)/shard_map/all_to_all | solution.py:708
  73.4 0.1 fusion
  73.5 0.8 slice.20
  74.2 0.1 broadcast_in_dim.27.odd_ref.rest_0_.rest_5_
  74.3 3.0 %sum_by_block.2 = (f32[4,128,512]{2,1,0:T(8,128)S(1)}, f32[4,512]{1,0:T(4,128)S(1)}, f32[4,512]{1,0:T(4,128)S(1)}, f32[4,128]{1,0:T(4,128)S(1)}, f32[4,128]{1,0:T(4,128)S(1)}) custom-call(f32[2,128]{1,0:T(2,128)S(1)} %broadcast_in_dim.27.odd_ref.rest_0_.rest_5_, f32[16,128]{1,0:T(8,128)S(1)} %bitcast.14, f32[4160,128]{1,0:T(8,128)} %bitcast.8.rows_ref), custom_call_target="tpu_custom_call" | custom-call | flops 1073741824 | bytes 3145728 | tf_op jit(solution)/shard_map/sum_by_block/pallas_call | solution.py:306
  77.4 1.3 collective-permute-start.8
  78.7 3.8 %collective-permute-start.5 = (f32[80,128]{1,0:T(8,128)S(1)}, f32[80,128]{1,0:T(8,128)S(1)}, u32[]{:S(2)}, u32[]{:S(2)}) collective-permute-start(f32[80,128]{1,0:T(8,128)S(1)} %pad_maximum_fusion), channel_id=1, source_target_pairs={{0,1},{1,2},{2,3},{4,5},{5,6},{6,7},{8,9},{9,10},{10,11},{12,13},{... | collective-permute-start | bytes 122888 | tf_op jit(solution)/shard_map/ppermute | solution.py:735
  82.5 1.9 %collective-permute-start.6 = (f32[80,128]{1,0:T(8,128)S(1)}, f32[80,128]{1,0:T(8,128)S(1)}, u32[]{:S(2)}, u32[]{:S(2)}) collective-permute-start(f32[80,128]{1,0:T(8,128)S(1)} %pad_maximum_fusion.1), channel_id=1, source_target_pairs={{1,0},{2,1},{3,2},{5,4},{6,5},{7,6},{9,8},{10,9},{11,10},{13,12},{... | collective-permute-start | bytes 122888 | tf_op jit(solution)/shard_map/ppermute | solution.py:736
  84.4 0.3 collective-permute-start.7
  84.8 4.8 %collective-permute-start.9 = (f32[4,128]{1,0:T(4,128)S(1)}, f32[4,128]{1,0:T(4,128)S(1)}, u32[]{:S(2)}, u32[]{:S(2)}) collective-permute-start(f32[4,128]{1,0:T(4,128)S(1)} %get-tuple-element.48), channel_id=1, source_target_pairs={{1,18},{2,17},{17,2},{18,1},{5,22},{6,21},{21,6},{22,5},{9,26},{10... | collective-permute-start | bytes 6152 | tf_op jit(solution)/shard_map/ppermute | solution.py:753
  89.6 0.0 collective-permute-done.5.corners_left
  89.6 0.1 collective-permute-start.10
  89.7 0.3 collective-permute-done.6.corners_right
  90.0 0.1 broadcast_in_dim.11.rates_ref
  90.0 12.1 %base.1 = (f32[1,16,128,512]{3,2,1,0:T(8,128)}, f32[4,128,512]{2,1,0:T(8,128)S(1)}, f32[6,128,512]{2,1,0:T(8,128)S(1)}) custom-call(f32[1,16]{1,0:T(1,128)S(1)} %get-tuple-element.70.rate_ref, f32[1,2]{1,0:T(1,128)S(1)} %get-tuple-element.72.mix_ref, f32[16,128]{1,0:T(8,128)S(1)} %broadcast_in_dim.11.rates_ref, f32[1,3,128,512]{3,2,1,0:T(8,128)S(1)} %copy-done, ...), custom_call_target="tpu_custom_call" | custom-call | flops 41943040 | bytes 8388608 | tf_op jit(solution)/shard_map/base/pallas_call | solution.py:513
  102.1 1.0 copy-done.2
  103.1 0.6 collective-permute-start.15
  103.7 4.3 %collective-permute-start.16 = (f32[4,512]{1,0:T(4,128)S(1)}, f32[4,512]{1,0:T(4,128)S(1)}, u32[]{:S(2)}, u32[]{:S(2)}) collective-permute-start(f32[4,512]{1,0:T(4,128)S(1)} %get-tuple-element.59), channel_id=1, source_target_pairs={{0,20},{8,28},{4,16},{12,24},{16,4},{24,12},{20,0},{28,8},{1,21},{... | collective-permute-start | bytes 24584 | tf_op jit(solution)/shard_map/ppermute | solution.py:750
  108.1 0.0 collective-permute-done.10.right
  108.1 0.0 collective-permute-done.8.recv
  108.1 0.1 broadcast_in_dim.26.mix_ref
  108.1 3.5 %finish.2 = (f32[1,16,128,512]{3,2,1,0:T(8,128)}, f32[1,8,128,512]{3,2,1,0:T(8,128)}, f32[8,128]{1,0:T(8,128)S(1)}) custom-call(f32[16,128]{1,0:T(8,128)S(1)} %broadcast_in_dim.11.rates_ref, f32[2,128]{1,0:T(2,128)S(1)} %broadcast_in_dim.26.mix_ref, f32[40,512]{1,0:T(8,128)S(1)} %collective-permute-done.1.above, ...), custom_call_target="tpu_custom_call", output_to_operand_aliasing={{0}: (11, {})} | custom-call | flops 5242880 | bytes 5242880 | tf_op jit(solution)/shard_map/finish/pallas_call | solution.py:665
  111.6 3.3 %all-to-all-done.1 = f32[16,64,4,128]{3,2,1,0:T(4,128)} async-done(((f32[16,64,4,128]{3,2,1,0:T(4,128)}), f32[16,64,4,128]{3,2,1,0:T(4,128)}, u32[]{:S(2)}, u32[]{:S(2)}) %all-to-all-start.1) | async-done | bytes 2097184 | tf_op jit(solution)/shard_map/all_to_all | solution.py:708
  115.0 0.0 collective-permute-done.7.ids_ref
  115.0 3.0 %sum_by_block.3 = (f32[4,128,512]{2,1,0:T(8,128)S(1)}, f32[4,512]{1,0:T(4,128)S(1)}, f32[4,512]{1,0:T(4,128)S(1)}, f32[4,128]{1,0:T(4,128)S(1)}, f32[4,128]{1,0:T(4,128)S(1)}) custom-call(f32[2,128]{1,0:T(2,128)S(1)} %broadcast_in_dim.27.odd_ref.rest_0_.rest_5_, f32[16,128]{1,0:T(8,128)S(1)} %collective-permute-done.7.ids_ref, f32[4096,128]{1,0:T(8,128)} %bitcast.9.rows_ref), custom_call_target="tpu_custom_call" | custom-call | flops 1073741824 | bytes 3145728 | tf_op jit(solution)/shard_map/sum_by_block/pallas_call | solution.py:306
  118.0 0.7 collective-permute-start.13
  118.7 9.6 %collective-permute-start.14 = (f32[4,512]{1,0:T(4,128)S(1)}, f32[4,512]{1,0:T(4,128)S(1)}, u32[]{:S(2)}, u32[]{:S(2)}) collective-permute-start(f32[4,512]{1,0:T(4,128)S(1)} %get-tuple-element.57), channel_id=1, source_target_pairs={{0,4},{8,12},{4,0},{12,8},{1,5},{9,13},{5,1},{13,9},{2,6},{10,14},... | collective-permute-start | bytes 24584 | tf_op jit(solution)/shard_map/ppermute | solution.py:765
  128.2 2.7 %collective-permute-start.11 = (f32[4,128]{1,0:T(4,128)S(1)}, f32[4,128]{1,0:T(4,128)S(1)}, u32[]{:S(2)}, u32[]{:S(2)}) collective-permute-start(f32[4,128]{1,0:T(4,128)S(1)} %get-tuple-element.54), channel_id=1, source_target_pairs={{1,2},{2,1},{5,6},{6,5},{9,10},{10,9},{13,14},{14,13},{17,18},{18,... | collective-permute-start | bytes 6152 | tf_op jit(solution)/shard_map/ppermute | solution.py:768
  130.9 0.0 collective-permute-done.15.rest_2_
  130.9 0.1 collective-permute-start.12
  131.0 2.1 %collective-permute-done.11.left = f32[4,128]{1,0:T(4,128)S(1)} collective-permute-done((f32[4,128]{1,0:T(4,128)S(1)}, f32[4,128]{1,0:T(4,128)S(1)}, u32[]{:S(2)}, u32[]{:S(2)}) %collective-permute-start.11) | collective-permute-done | bytes 2080 | tf_op jit(solution)/shard_map/ppermute | solution.py:768
  133.2 3.6 %finish.3 = (f32[1,16,128,512]{3,2,1,0:T(8,128)}, f32[1,8,128,512]{3,2,1,0:T(8,128)}, f32[8,128]{1,0:T(8,128)}) custom-call(f32[16,128]{1,0:T(8,128)S(1)} %broadcast_in_dim.11.rates_ref, f32[2,128]{1,0:T(2,128)S(1)} %broadcast_in_dim.26.mix_ref, f32[40,512]{1,0:T(8,128)S(1)} %collective-permute-done.1.above, ...), custom_call_target="tpu_custom_call", output_to_operand_aliasing={{0}: (16, {}), {1}: (17, {})} | custom-call | flops 5242880 | bytes 5242880 | tf_op jit(solution)/shard_map/finish/pallas_call | solution.py:665
  (20 shorter events, 0.1 us)
Async XLA Ops:
  11.4 8.7 %copy-start.4 = (f32[1,2]{1,0:T(1,128)S(1)}, f32[1,2]{1,0:T(1,128)}, u32[]{:S(2)}) copy-start(f32[1,2]{1,0:T(1,128)} %constant.23.clone) | copy-start | bytes 28
  11.5 8.7 %copy-start = (f32[1,3,128,512]{3,2,1,0:T(8,128)S(1)}, f32[1,3,128,512]{3,2,1,0:T(8,128)}, u32[]{:S(2)}) copy-start(f32[1,3,128,512]{3,2,1,0:T(8,128)} %coefs_ref.1) | copy-start | bytes 2359300
  11.5 8.7 %copy-start.1 = (s32[128,512]{1,0:T(8,128)S(1)}, s32[128,512]{1,0:T(8,128)}, u32[]{:S(2)}) copy-start(s32[128,512]{1,0:T(8,128)} %land_ref) | copy-start | bytes 786436
  11.5 49.6 %all-to-all-start = ((f32[16,65,4,128]{3,2,1,0:T(4,128)}), f32[16,65,4,128]{3,2,1,0:T(4,128)}, u32[]{:S(2)}, u32[]{:S(2)}) async-start(f32[16,65,4,128]{3,2,1,0:T(4,128)} %bitcast.5), calls=%async_computation | async-start | bytes 4259840 | tf_op jit(solution)/shard_map/all_to_all | solution.py:708
  19.0 24.9 %collective-permute-start = (f32[513,4,128]{2,1,0:T(4,128)}, f32[513,4,128]{2,1,0:T(4,128)S(1)}, u32[]{:S(2)}, u32[]{:S(2)}) collective-permute-start(f32[513,4,128]{2,1,0:T(4,128)} %get-tuple-element.34), channel_id=1, source_target_pairs={{0,16},{16,0},{1,17},{17,1},{2,18},{18,2},{3,19},{19,3},{4,20},{20... | collective-permute-start | bytes 3151880 | tf_op jit(solution)/shard_map/ppermute | solution.py:714
  23.4 32.2 %collective-permute-start.1 = (f32[40,512]{1,0:T(8,128)S(1)}, f32[40,512]{1,0:T(8,128)S(1)}, u32[]{:S(2)}, u32[]{:S(2)}) collective-permute-start(f32[40,512]{1,0:T(8,128)S(1)} %get-tuple-element.37.x_high), channel_id=1, source_target_pairs={{0,4},{4,8},{8,12},{1,5},{5,9},{9,13},{2,6},{6,10},{10,14},{3,7},{... | collective-permute-start | bytes 245768 | tf_op jit(solution)/shard_map/ppermute | solution.py:725
  26.7 28.9 %collective-permute-start.2 = (f32[40,512]{1,0:T(8,128)S(1)}, f32[40,512]{1,0:T(8,128)S(1)}, u32[]{:S(2)}, u32[]{:S(2)}) collective-permute-start(f32[40,512]{1,0:T(8,128)S(1)} %get-tuple-element.38.x_low), channel_id=1, source_target_pairs={{4,0},{8,4},{12,8},{5,1},{9,5},{13,9},{6,2},{10,6},{14,10},{7,3},{... | collective-permute-start | bytes 245768 | tf_op jit(solution)/shard_map/ppermute | solution.py:726
  28.0 19.9 %collective-permute-start.3 = (f32[40,128]{1,0:T(8,128)S(1)}, f32[40,128]{1,0:T(8,128)S(1)}, u32[]{:S(2)}, u32[]{:S(2)}) collective-permute-start(f32[40,128]{1,0:T(8,128)S(1)} %get-tuple-element.39.y_high), channel_id=1, source_target_pairs={{0,1},{1,2},{2,3},{4,5},{5,6},{6,7},{8,9},{9,10},{10,11},{12,13},{... | collective-permute-start | bytes 61448 | tf_op jit(solution)/shard_map/ppermute | solution.py:723
  31.9 16.0 %collective-permute-start.4 = (f32[40,128]{1,0:T(8,128)S(1)}, f32[40,128]{1,0:T(8,128)S(1)}, u32[]{:S(2)}, u32[]{:S(2)}) collective-permute-start(f32[40,128]{1,0:T(8,128)S(1)} %get-tuple-element.40.y_low), channel_id=1, source_target_pairs={{1,0},{2,1},{3,2},{5,4},{6,5},{7,6},{9,8},{10,9},{11,10},{13,12},{... | collective-permute-start | bytes 61448 | tf_op jit(solution)/shard_map/ppermute | solution.py:724
  61.1 53.9 %all-to-all-start.1 = ((f32[16,64,4,128]{3,2,1,0:T(4,128)}), f32[16,64,4,128]{3,2,1,0:T(4,128)}, u32[]{:S(2)}, u32[]{:S(2)}) async-start(f32[16,64,4,128]{3,2,1,0:T(4,128)} %bitcast.7), calls=%async_computation.1 | async-start | bytes 4194304 | tf_op jit(solution)/shard_map/all_to_all | solution.py:708
  74.3 10.4 %copy-start.5 = (f32[1,8]{1,0:T(1,128)S(1)}, f32[1,8]{1,0:T(1,128)}, u32[]{:S(2)}) copy-start(f32[1,8]{1,0:T(1,128)} %param.13) | copy-start | bytes 100
  77.4 30.7 %collective-permute-start.8 = (f32[4,128,512]{2,1,0:T(8,128)S(1)}, f32[4,128,512]{2,1,0:T(8,128)S(1)}, u32[]{:S(2)}, u32[]{:S(2)}) collective-permute-start(f32[4,128,512]{2,1,0:T(8,128)S(1)} %get-tuple-element.47), channel_id=1, source_target_pairs={{0,16},{16,0},{1,17},{17,1},{2,18},{18,2},{3,19},{19,3},{4,20},{20... | collective-permute-start | bytes 3145736 | tf_op jit(solution)/shard_map/ppermute | solution.py:747
  78.7 10.9 %collective-permute-start.5 = (f32[80,128]{1,0:T(8,128)S(1)}, f32[80,128]{1,0:T(8,128)S(1)}, u32[]{:S(2)}, u32[]{:S(2)}) collective-permute-start(f32[80,128]{1,0:T(8,128)S(1)} %pad_maximum_fusion), channel_id=1, source_target_pairs={{0,1},{1,2},{2,3},{4,5},{5,6},{6,7},{8,9},{9,10},{10,11},{12,13},{... | collective-permute-start | bytes 122888 | tf_op jit(solution)/shard_map/ppermute | solution.py:735
  82.5 7.5 %collective-permute-start.6 = (f32[80,128]{1,0:T(8,128)S(1)}, f32[80,128]{1,0:T(8,128)S(1)}, u32[]{:S(2)}, u32[]{:S(2)}) collective-permute-start(f32[80,128]{1,0:T(8,128)S(1)} %pad_maximum_fusion.1), channel_id=1, source_target_pairs={{1,0},{2,1},{3,2},{5,4},{6,5},{7,6},{9,8},{10,9},{11,10},{13,12},{... | collective-permute-start | bytes 122888 | tf_op jit(solution)/shard_map/ppermute | solution.py:736
  84.4 30.5 %collective-permute-start.7 = (f32[16,128]{1,0:T(8,128)S(1)}, f32[16,128]{1,0:T(8,128)S(1)}, u32[]{:S(2)}, u32[]{:S(2)}) collective-permute-start(f32[16,128]{1,0:T(8,128)S(1)} %bitcast.15), channel_id=1, source_target_pairs={{0,16},{16,0},{1,17},{17,1},{2,18},{18,2},{3,19},{19,3},{4,20},{20... | collective-permute-start | bytes 24584 | tf_op jit(solution)/shard_map/ppermute | solution.py:743
  84.8 19.0 %collective-permute-start.9 = (f32[4,128]{1,0:T(4,128)S(1)}, f32[4,128]{1,0:T(4,128)S(1)}, u32[]{:S(2)}, u32[]{:S(2)}) collective-permute-start(f32[4,128]{1,0:T(4,128)S(1)} %get-tuple-element.48), channel_id=1, source_target_pairs={{1,18},{2,17},{17,2},{18,1},{5,22},{6,21},{21,6},{22,5},{9,26},{10... | collective-permute-start | bytes 6152 | tf_op jit(solution)/shard_map/ppermute | solution.py:753
  89.6 18.4 %collective-permute-start.10 = (f32[4,128]{1,0:T(4,128)S(1)}, f32[4,128]{1,0:T(4,128)S(1)}, u32[]{:S(2)}, u32[]{:S(2)}) collective-permute-start(f32[4,128]{1,0:T(4,128)S(1)} %get-tuple-element.49), channel_id=1, source_target_pairs={{0,17},{2,19},{1,16},{3,18},{16,1},{18,3},{17,0},{19,2},{4,21},{6,... | collective-permute-start | bytes 6152 | tf_op jit(solution)/shard_map/ppermute | solution.py:754
  102.1 1.0 copy-start.2
  103.1 27.8 %collective-permute-start.15 = (f32[4,512]{1,0:T(4,128)S(1)}, f32[4,512]{1,0:T(4,128)S(1)}, u32[]{:S(2)}, u32[]{:S(2)}) collective-permute-start(f32[4,512]{1,0:T(4,128)S(1)} %get-tuple-element.58), channel_id=1, source_target_pairs={{4,24},{8,20},{20,8},{24,4},{5,25},{9,21},{21,9},{25,5},{6,26},{10... | collective-permute-start | bytes 24584 | tf_op jit(solution)/shard_map/ppermute | solution.py:749
  103.7 27.3 %collective-permute-start.16 = (f32[4,512]{1,0:T(4,128)S(1)}, f32[4,512]{1,0:T(4,128)S(1)}, u32[]{:S(2)}, u32[]{:S(2)}) collective-permute-start(f32[4,512]{1,0:T(4,128)S(1)} %get-tuple-element.59), channel_id=1, source_target_pairs={{0,20},{8,28},{4,16},{12,24},{16,4},{24,12},{20,0},{28,8},{1,21},{... | collective-permute-start | bytes 24584 | tf_op jit(solution)/shard_map/ppermute | solution.py:750
  111.6 21.5 %copy-start.3 = (f32[4,128,512]{2,1,0:T(8,128)S(1)}, f32[4,128,512]{2,1,0:T(8,128)}, u32[]{:S(2)}) copy-start(f32[4,128,512]{2,1,0:T(8,128)} %copy-done.2) | copy-start | bytes 3145732
  118.0 15.1 %collective-permute-start.13 = (f32[4,512]{1,0:T(4,128)S(1)}, f32[4,512]{1,0:T(4,128)S(1)}, u32[]{:S(2)}, u32[]{:S(2)}) collective-permute-start(f32[4,512]{1,0:T(4,128)S(1)} %get-tuple-element.56), channel_id=1, source_target_pairs={{4,8},{8,4},{5,9},{9,5},{6,10},{10,6},{7,11},{11,7},{20,24},{24,20... | collective-permute-start | bytes 24584 | tf_op jit(solution)/shard_map/ppermute | solution.py:764
  118.7 14.5 %collective-permute-start.14 = (f32[4,512]{1,0:T(4,128)S(1)}, f32[4,512]{1,0:T(4,128)S(1)}, u32[]{:S(2)}, u32[]{:S(2)}) collective-permute-start(f32[4,512]{1,0:T(4,128)S(1)} %get-tuple-element.57), channel_id=1, source_target_pairs={{0,4},{8,12},{4,0},{12,8},{1,5},{9,13},{5,1},{13,9},{2,6},{10,14},... | collective-permute-start | bytes 24584 | tf_op jit(solution)/shard_map/ppermute | solution.py:765
  128.2 4.9 %collective-permute-start.11 = (f32[4,128]{1,0:T(4,128)S(1)}, f32[4,128]{1,0:T(4,128)S(1)}, u32[]{:S(2)}, u32[]{:S(2)}) collective-permute-start(f32[4,128]{1,0:T(4,128)S(1)} %get-tuple-element.54), channel_id=1, source_target_pairs={{1,2},{2,1},{5,6},{6,5},{9,10},{10,9},{13,14},{14,13},{17,18},{18,... | collective-permute-start | bytes 6152 | tf_op jit(solution)/shard_map/ppermute | solution.py:768
  130.9 2.2 %collective-permute-start.12 = (f32[4,128]{1,0:T(4,128)S(1)}, f32[4,128]{1,0:T(4,128)S(1)}, u32[]{:S(2)}, u32[]{:S(2)}) collective-permute-start(f32[4,128]{1,0:T(4,128)S(1)} %get-tuple-element.55), channel_id=1, source_target_pairs={{0,1},{2,3},{1,0},{3,2},{4,5},{6,7},{5,4},{7,6},{8,9},{10,11},{9,8... | collective-permute-start | bytes 6152 | tf_op jit(solution)/shard_map/ppermute | solution.py:769

commit v16 on v15

--- a/solution.py
+++ b/solution.py
@@ -633,7 +633,7 @@
             outer[f, i, row : row + 1, :] = outer[f, i, row : row + 1, :] + more
             outer_copy(f, i, True).start()
 
-    lax.fori_loop(0, count - 1, one_field, 0)
+    lax.fori_loop(0, count - 1, one_field, 0, unroll=True)
     add_lines()
     one_field(count - 1, 0)
     for f in range(count):

time: 138 us -> 138 us (level)
  no operation moved by 1% of the time
where the time goes in v16:
time: 138 us; the launch traced here: 137 us
  starting transfers between devices  61.5 us (45%)
  Pallas kernels  43.1 us (31%)
  waiting for transfers between devices  29.4 us (21%)
  local copies, waits for them, and re-layouts  1.99 us (1%)
    all_to_all x2, starting transfers between devices, exchanged(): lax.all_to_all(rows, ('tx', 'ty'), split_axis=0, concat_axis=0, tiled=True)  19.8 us
    pallas_call x1, Pallas kernels, base_of(): pl.pallas_call(functools.partial(base_kernel, half), grid=(nfield // PER_...  12.1 us
    pallas_call x1, Pallas kernels, contributions(): pl.pallas_call(functools.partial(contribution_kernel, dims), in_specs=[pl...  10.8 us
    ppermute x1, waiting for transfers between devices, body(): early = lax.ppermute(early, 'comp', swap)  10 us
    ppermute x1, starting transfers between devices, body(): lax.ppermute(x_even, 'tx', neighbour_pairs(tx, 0))  9.55 us
    all_to_all x2, waiting for transfers between devices, exchanged(): lax.all_to_all(rows, ('tx', 'ty'), split_axis=0, concat_axis=0, tiled=True)  9.19 us
    ppermute x1, waiting for transfers between devices, body(): above = lax.ppermute(x_high, 'tx', shift_pairs(tx, 1))  7.72 us
    pallas_call x2, Pallas kernels, finished(): pl.pallas_call(functools.partial(finish_kernel, first, with_x), in_specs=...  6.86 us
  transfers between devices with their start and end apart: 19, of which 6 were waited for; matrix products, arithmetic and copies ran while one was open for 1% of the time, Pallas kernels for 21%

profile of v16, /device:TPU:1, one launch (start us, length us, event | category | flops | bytes accessed | tf_op | source)
XLA Modules:
  0.0 136.9 jit_solution(8003649809372829780)
XLA Ops:
  0.6 10.8 %contributions.1 = (f32[513,4,128]{2,1,0:T(4,128)}, f32[1040,4,128]{2,1,0:T(4,128)}) custom-call(s32[1,512]{1,0:T(1,128)} %src_ref.1, s32[1,512]{1,0:T(1,128)} %bitcast.16, s32[1,512]{1,0:T(1,128)} %blk_ref.1, f32[1,16,128,512]{3,2,1,0:T(8,128)} %state_ref.3, bf16[1,512,128,128]{3,2,1,0:T(8,128)(2,1)} %weights_ref.1), custom_call_target="tpu_custom_call" | custom-call | flops 134217728 | bytes 25296896 | tf_op jit(solution)/shard_map/contributions/pallas_call | solution.py:166
  11.4 0.0 copy-start.4
  11.5 0.0 copy-start
  11.5 0.0 copy-start.1
  11.5 7.5 %all-to-all-start = ((f32[16,65,4,128]{3,2,1,0:T(4,128)}), f32[16,65,4,128]{3,2,1,0:T(4,128)}, u32[]{:S(2)}, u32[]{:S(2)}) async-start(f32[16,65,4,128]{3,2,1,0:T(4,128)} %bitcast.5), calls=%async_computation | async-start | bytes 4259840 | tf_op jit(solution)/shard_map/all_to_all | solution.py:708
  19.0 1.2 collective-permute-start
  20.2 3.2 %edges.1 = (f32[40,512]{1,0:T(8,128)S(1)}, f32[40,512]{1,0:T(8,128)S(1)}, f32[40,128]{1,0:T(8,128)S(1)}, f32[40,128]{1,0:T(8,128)S(1)}) custom-call(f32[1,2]{1,0:T(1,128)S(1)} %get-tuple-element.72.mix_ref, f32[1,16,128,512]{3,2,1,0:T(8,128)} %state_ref.3, f32[1,16,128,512]{3,2,1,0:T(8,128)} %state_ref.3, f32[1,16,128,512]{3,2,1,0:T(8,128)} %state_ref.3, ...), custom_call_target="tpu_custom_call" | custom-call | flops 1048576 | bytes 4194304 | tf_op jit(solution)/shard_map/edges/pallas_call | solution.py:422
  23.4 3.3 %collective-permute-start.1 = (f32[40,512]{1,0:T(8,128)S(1)}, f32[40,512]{1,0:T(8,128)S(1)}, u32[]{:S(2)}, u32[]{:S(2)}) collective-permute-start(f32[40,512]{1,0:T(8,128)S(1)} %get-tuple-element.37.x_high), channel_id=1, source_target_pairs={{0,4},{4,8},{8,12},{1,5},{5,9},{9,13},{2,6},{6,10},{10,14},{3,7},{... | collective-permute-start | bytes 245768 | tf_op jit(solution)/shard_map/ppermute | solution.py:725
  26.7 1.3 collective-permute-start.2
  28.0 3.9 %collective-permute-start.3 = (f32[40,128]{1,0:T(8,128)S(1)}, f32[40,128]{1,0:T(8,128)S(1)}, u32[]{:S(2)}, u32[]{:S(2)}) collective-permute-start(f32[40,128]{1,0:T(8,128)S(1)} %get-tuple-element.39.y_high), channel_id=1, source_target_pairs={{0,1},{1,2},{2,3},{4,5},{5,6},{6,7},{8,9},{9,10},{10,11},{12,13},{... | collective-permute-start | bytes 61448 | tf_op jit(solution)/shard_map/ppermute | solution.py:723
  31.9 1.9 %collective-permute-start.4 = (f32[40,128]{1,0:T(8,128)S(1)}, f32[40,128]{1,0:T(8,128)S(1)}, u32[]{:S(2)}, u32[]{:S(2)}) collective-permute-start(f32[40,128]{1,0:T(8,128)S(1)} %get-tuple-element.40.y_low), channel_id=1, source_target_pairs={{1,0},{2,1},{3,2},{5,4},{6,5},{7,6},{9,8},{10,9},{11,10},{13,12},{... | collective-permute-start | bytes 61448 | tf_op jit(solution)/shard_map/ppermute | solution.py:724
  33.9 10.0 %collective-permute-done.in_ref = f32[513,4,128]{2,1,0:T(4,128)S(1)} collective-permute-done((f32[513,4,128]{2,1,0:T(4,128)}, f32[513,4,128]{2,1,0:T(4,128)S(1)}, u32[]{:S(2)}, u32[]{:S(2)}) %collective-permute-start) | collective-permute-done | bytes 1050656 | tf_op jit(solution)/shard_map/ppermute | solution.py:714
  43.9 4.0 %place_in_slots.1 = f32[1024,4,128]{2,1,0:T(4,128)} custom-call(f32[513,4,128]{2,1,0:T(4,128)S(1)} %collective-permute-done.in_ref), custom_call_target="tpu_custom_call" | custom-call | flops 1050624 | bytes 3151872 | tf_op jit(solution)/shard_map/place_in_slots/pallas_call | solution.py:217
  47.9 7.7 %collective-permute-done.1.above = f32[40,512]{1,0:T(8,128)S(1)} collective-permute-done((f32[40,512]{1,0:T(8,128)S(1)}, f32[40,512]{1,0:T(8,128)S(1)}, u32[]{:S(2)}, u32[]{:S(2)}) %collective-permute-start.1) | collective-permute-done | bytes 81952 | tf_op jit(solution)/shard_map/ppermute | solution.py:725
  55.7 0.0 collective-permute-done.2.below
  55.7 5.4 %all-to-all-done = f32[16,65,4,128]{3,2,1,0:T(4,128)} async-done(((f32[16,65,4,128]{3,2,1,0:T(4,128)}), f32[16,65,4,128]{3,2,1,0:T(4,128)}, u32[]{:S(2)}, u32[]{:S(2)}) %all-to-all-start) | async-done | bytes 2129952 | tf_op jit(solution)/shard_map/all_to_all | solution.py:708
  61.1 12.3 %all-to-all-start.1 = ((f32[16,64,4,128]{3,2,1,0:T(4,128)}), f32[16,64,4,128]{3,2,1,0:T(4,128)}, u32[]{:S(2)}, u32[]{:S(2)}) async-start(f32[16,64,4,128]{3,2,1,0:T(4,128)} %bitcast.7), calls=%async_computation.1 | async-start | bytes 4194304 | tf_op jit(solution)/shard_map/all_to_all | solution.py:708
  73.4 0.1 fusion
  73.5 0.8 slice.20
  74.2 0.1 broadcast_in_dim.27.odd_ref.rest_0_.rest_5_
  74.3 3.0 %sum_by_block.2 = (f32[4,128,512]{2,1,0:T(8,128)S(1)}, f32[4,512]{1,0:T(4,128)S(1)}, f32[4,512]{1,0:T(4,128)S(1)}, f32[4,128]{1,0:T(4,128)S(1)}, f32[4,128]{1,0:T(4,128)S(1)}) custom-call(f32[2,128]{1,0:T(2,128)S(1)} %broadcast_in_dim.27.odd_ref.rest_0_.rest_5_, f32[16,128]{1,0:T(8,128)S(1)} %bitcast.14, f32[4160,128]{1,0:T(8,128)} %bitcast.8.rows_ref), custom_call_target="tpu_custom_call" | custom-call | flops 1073741824 | bytes 3145728 | tf_op jit(solution)/shard_map/sum_by_block/pallas_call | solution.py:306
  77.4 1.3 collective-permute-start.8
  78.7 3.8 %collective-permute-start.5 = (f32[80,128]{1,0:T(8,128)S(1)}, f32[80,128]{1,0:T(8,128)S(1)}, u32[]{:S(2)}, u32[]{:S(2)}) collective-permute-start(f32[80,128]{1,0:T(8,128)S(1)} %pad_maximum_fusion), channel_id=1, source_target_pairs={{0,1},{1,2},{2,3},{4,5},{5,6},{6,7},{8,9},{9,10},{10,11},{12,13},{... | collective-permute-start | bytes 122888 | tf_op jit(solution)/shard_map/ppermute | solution.py:735
  82.5 1.9 %collective-permute-start.6 = (f32[80,128]{1,0:T(8,128)S(1)}, f32[80,128]{1,0:T(8,128)S(1)}, u32[]{:S(2)}, u32[]{:S(2)}) collective-permute-start(f32[80,128]{1,0:T(8,128)S(1)} %pad_maximum_fusion.1), channel_id=1, source_target_pairs={{1,0},{2,1},{3,2},{5,4},{6,5},{7,6},{9,8},{10,9},{11,10},{13,12},{... | collective-permute-start | bytes 122888 | tf_op jit(solution)/shard_map/ppermute | solution.py:736
  84.4 0.3 collective-permute-start.7
  84.8 4.8 %collective-permute-start.9 = (f32[4,128]{1,0:T(4,128)S(1)}, f32[4,128]{1,0:T(4,128)S(1)}, u32[]{:S(2)}, u32[]{:S(2)}) collective-permute-start(f32[4,128]{1,0:T(4,128)S(1)} %get-tuple-element.48), channel_id=1, source_target_pairs={{1,18},{2,17},{17,2},{18,1},{5,22},{6,21},{21,6},{22,5},{9,26},{10... | collective-permute-start | bytes 6152 | tf_op jit(solution)/shard_map/ppermute | solution.py:753
  89.6 0.0 collective-permute-done.5.corners_left
  89.6 0.1 collective-permute-start.10
  89.7 0.3 collective-permute-done.6.corners_right
  90.0 0.1 broadcast_in_dim.11.rates_ref
  90.0 12.1 %base.1 = (f32[1,16,128,512]{3,2,1,0:T(8,128)}, f32[4,128,512]{2,1,0:T(8,128)S(1)}, f32[6,128,512]{2,1,0:T(8,128)S(1)}) custom-call(f32[1,16]{1,0:T(1,128)S(1)} %get-tuple-element.70.rate_ref, f32[1,2]{1,0:T(1,128)S(1)} %get-tuple-element.72.mix_ref, f32[16,128]{1,0:T(8,128)S(1)} %broadcast_in_dim.11.rates_ref, f32[1,3,128,512]{3,2,1,0:T(8,128)S(1)} %copy-done, ...), custom_call_target="tpu_custom_call" | custom-call | flops 41943040 | bytes 8388608 | tf_op jit(solution)/shard_map/base/pallas_call | solution.py:513
  102.1 1.0 copy-done.2
  103.1 0.6 collective-permute-start.15
  103.7 0.0 collective-permute-done.9.left
  103.7 4.3 %collective-permute-start.16 = (f32[4,512]{1,0:T(4,128)S(1)}, f32[4,512]{1,0:T(4,128)S(1)}, u32[]{:S(2)}, u32[]{:S(2)}) collective-permute-start(f32[4,512]{1,0:T(4,128)S(1)} %get-tuple-element.59), channel_id=1, source_target_pairs={{0,20},{8,28},{4,16},{12,24},{16,4},{24,12},{20,0},{28,8},{1,21},{... | collective-permute-start | bytes 24584 | tf_op jit(solution)/shard_map/ppermute | solution.py:750
  108.1 0.0 collective-permute-done.10.right
  108.1 0.0 collective-permute-done.8.recv
  108.1 0.1 broadcast_in_dim.26.mix_ref
  108.1 3.1 %finish.2 = (f32[1,16,128,512]{3,2,1,0:T(8,128)}, f32[1,8,128,512]{3,2,1,0:T(8,128)}, f32[8,128]{1,0:T(8,128)S(1)}) custom-call(f32[16,128]{1,0:T(8,128)S(1)} %broadcast_in_dim.11.rates_ref, f32[2,128]{1,0:T(2,128)S(1)} %broadcast_in_dim.26.mix_ref, f32[40,512]{1,0:T(8,128)S(1)} %collective-permute-done.1.above, ...), custom_call_target="tpu_custom_call", output_to_operand_aliasing={{0}: (11, {})} | custom-call | flops 5242880 | bytes 5242880 | tf_op jit(solution)/shard_map/finish/pallas_call | solution.py:665
  111.2 3.7 %all-to-all-done.1 = f32[16,64,4,128]{3,2,1,0:T(4,128)} async-done(((f32[16,64,4,128]{3,2,1,0:T(4,128)}), f32[16,64,4,128]{3,2,1,0:T(4,128)}, u32[]{:S(2)}, u32[]{:S(2)}) %all-to-all-start.1) | async-done | bytes 2097184 | tf_op jit(solution)/shard_map/all_to_all | solution.py:708
  115.0 3.0 %sum_by_block.3 = (f32[4,128,512]{2,1,0:T(8,128)S(1)}, f32[4,512]{1,0:T(4,128)S(1)}, f32[4,512]{1,0:T(4,128)S(1)}, f32[4,128]{1,0:T(4,128)S(1)}, f32[4,128]{1,0:T(4,128)S(1)}) custom-call(f32[2,128]{1,0:T(2,128)S(1)} %broadcast_in_dim.27.odd_ref.rest_0_.rest_5_, f32[16,128]{1,0:T(8,128)S(1)} %collective-permute-done.7.ids_ref, f32[4096,128]{1,0:T(8,128)} %bitcast.9.rows_ref), custom_call_target="tpu_custom_call" | custom-call | flops 1073741824 | bytes 3145728 | tf_op jit(solution)/shard_map/sum_by_block/pallas_call | solution.py:306
  118.0 0.7 collective-permute-start.13
  118.7 9.6 %collective-permute-start.14 = (f32[4,512]{1,0:T(4,128)S(1)}, f32[4,512]{1,0:T(4,128)S(1)}, u32[]{:S(2)}, u32[]{:S(2)}) collective-permute-start(f32[4,512]{1,0:T(4,128)S(1)} %get-tuple-element.57), channel_id=1, source_target_pairs={{0,4},{8,12},{4,0},{12,8},{1,5},{9,13},{5,1},{13,9},{2,6},{10,14},... | collective-permute-start | bytes 24584 | tf_op jit(solution)/shard_map/ppermute | solution.py:765
  128.2 2.7 %collective-permute-start.11 = (f32[4,128]{1,0:T(4,128)S(1)}, f32[4,128]{1,0:T(4,128)S(1)}, u32[]{:S(2)}, u32[]{:S(2)}) collective-permute-start(f32[4,128]{1,0:T(4,128)S(1)} %get-tuple-element.54), channel_id=1, source_target_pairs={{1,2},{2,1},{5,6},{6,5},{9,10},{10,9},{13,14},{14,13},{17,18},{18,... | collective-permute-start | bytes 6152 | tf_op jit(solution)/shard_map/ppermute | solution.py:768
  130.9 0.1 collective-permute-start.12
  131.0 0.0 collective-permute-done.16.rest_3_
  131.0 2.1 %collective-permute-done.11.left = f32[4,128]{1,0:T(4,128)S(1)} collective-permute-done((f32[4,128]{1,0:T(4,128)S(1)}, f32[4,128]{1,0:T(4,128)S(1)}, u32[]{:S(2)}, u32[]{:S(2)}) %collective-permute-start.11) | collective-permute-done | bytes 2080 | tf_op jit(solution)/shard_map/ppermute | solution.py:768
  133.2 3.8 %finish.3 = (f32[1,16,128,512]{3,2,1,0:T(8,128)}, f32[1,8,128,512]{3,2,1,0:T(8,128)}, f32[8,128]{1,0:T(8,128)}) custom-call(f32[16,128]{1,0:T(8,128)S(1)} %broadcast_in_dim.11.rates_ref, f32[2,128]{1,0:T(2,128)S(1)} %broadcast_in_dim.26.mix_ref, f32[40,512]{1,0:T(8,128)S(1)} %collective-permute-done.1.above, ...), custom_call_target="tpu_custom_call", output_to_operand_aliasing={{0}: (16, {}), {1}: (17, {})} | custom-call | flops 5242880 | bytes 5242880 | tf_op jit(solution)/shard_map/finish/pallas_call | solution.py:665
  (20 shorter events, 0.1 us)
Async XLA Ops:
  11.4 8.7 %copy-start.4 = (f32[1,2]{1,0:T(1,128)S(1)}, f32[1,2]{1,0:T(1,128)}, u32[]{:S(2)}) copy-start(f32[1,2]{1,0:T(1,128)} %constant.23.clone) | copy-start | bytes 28
  11.5 8.7 %copy-start = (f32[1,3,128,512]{3,2,1,0:T(8,128)S(1)}, f32[1,3,128,512]{3,2,1,0:T(8,128)}, u32[]{:S(2)}) copy-start(f32[1,3,128,512]{3,2,1,0:T(8,128)} %coefs_ref.1) | copy-start | bytes 2359300
  11.5 8.7 %copy-start.1 = (s32[128,512]{1,0:T(8,128)S(1)}, s32[128,512]{1,0:T(8,128)}, u32[]{:S(2)}) copy-start(s32[128,512]{1,0:T(8,128)} %land_ref) | copy-start | bytes 786436
  11.5 49.6 %all-to-all-start = ((f32[16,65,4,128]{3,2,1,0:T(4,128)}), f32[16,65,4,128]{3,2,1,0:T(4,128)}, u32[]{:S(2)}, u32[]{:S(2)}) async-start(f32[16,65,4,128]{3,2,1,0:T(4,128)} %bitcast.5), calls=%async_computation | async-start | bytes 4259840 | tf_op jit(solution)/shard_map/all_to_all | solution.py:708
  19.0 24.9 %collective-permute-start = (f32[513,4,128]{2,1,0:T(4,128)}, f32[513,4,128]{2,1,0:T(4,128)S(1)}, u32[]{:S(2)}, u32[]{:S(2)}) collective-permute-start(f32[513,4,128]{2,1,0:T(4,128)} %get-tuple-element.34), channel_id=1, source_target_pairs={{0,16},{16,0},{1,17},{17,1},{2,18},{18,2},{3,19},{19,3},{4,20},{20... | collective-permute-start | bytes 3151880 | tf_op jit(solution)/shard_map/ppermute | solution.py:714
  23.4 32.2 %collective-permute-start.1 = (f32[40,512]{1,0:T(8,128)S(1)}, f32[40,512]{1,0:T(8,128)S(1)}, u32[]{:S(2)}, u32[]{:S(2)}) collective-permute-start(f32[40,512]{1,0:T(8,128)S(1)} %get-tuple-element.37.x_high), channel_id=1, source_target_pairs={{0,4},{4,8},{8,12},{1,5},{5,9},{9,13},{2,6},{6,10},{10,14},{3,7},{... | collective-permute-start | bytes 245768 | tf_op jit(solution)/shard_map/ppermute | solution.py:725
  26.7 28.9 %collective-permute-start.2 = (f32[40,512]{1,0:T(8,128)S(1)}, f32[40,512]{1,0:T(8,128)S(1)}, u32[]{:S(2)}, u32[]{:S(2)}) collective-permute-start(f32[40,512]{1,0:T(8,128)S(1)} %get-tuple-element.38.x_low), channel_id=1, source_target_pairs={{4,0},{8,4},{12,8},{5,1},{9,5},{13,9},{6,2},{10,6},{14,10},{7,3},{... | collective-permute-start | bytes 245768 | tf_op jit(solution)/shard_map/ppermute | solution.py:726
  28.0 19.9 %collective-permute-start.3 = (f32[40,128]{1,0:T(8,128)S(1)}, f32[40,128]{1,0:T(8,128)S(1)}, u32[]{:S(2)}, u32[]{:S(2)}) collective-permute-start(f32[40,128]{1,0:T(8,128)S(1)} %get-tuple-element.39.y_high), channel_id=1, source_target_pairs={{0,1},{1,2},{2,3},{4,5},{5,6},{6,7},{8,9},{9,10},{10,11},{12,13},{... | collective-permute-start | bytes 61448 | tf_op jit(solution)/shard_map/ppermute | solution.py:723
  31.9 16.0 %collective-permute-start.4 = (f32[40,128]{1,0:T(8,128)S(1)}, f32[40,128]{1,0:T(8,128)S(1)}, u32[]{:S(2)}, u32[]{:S(2)}) collective-permute-start(f32[40,128]{1,0:T(8,128)S(1)} %get-tuple-element.40.y_low), channel_id=1, source_target_pairs={{1,0},{2,1},{3,2},{5,4},{6,5},{7,6},{9,8},{10,9},{11,10},{13,12},{... | collective-permute-start | bytes 61448 | tf_op jit(solution)/shard_map/ppermute | solution.py:724
  61.1 53.9 %all-to-all-start.1 = ((f32[16,64,4,128]{3,2,1,0:T(4,128)}), f32[16,64,4,128]{3,2,1,0:T(4,128)}, u32[]{:S(2)}, u32[]{:S(2)}) async-start(f32[16,64,4,128]{3,2,1,0:T(4,128)} %bitcast.7), calls=%async_computation.1 | async-start | bytes 4194304 | tf_op jit(solution)/shard_map/all_to_all | solution.py:708
  74.3 10.4 %copy-start.5 = (f32[1,8]{1,0:T(1,128)S(1)}, f32[1,8]{1,0:T(1,128)}, u32[]{:S(2)}) copy-start(f32[1,8]{1,0:T(1,128)} %param.13) | copy-start | bytes 100
  77.4 30.7 %collective-permute-start.8 = (f32[4,128,512]{2,1,0:T(8,128)S(1)}, f32[4,128,512]{2,1,0:T(8,128)S(1)}, u32[]{:S(2)}, u32[]{:S(2)}) collective-permute-start(f32[4,128,512]{2,1,0:T(8,128)S(1)} %get-tuple-element.47), channel_id=1, source_target_pairs={{0,16},{16,0},{1,17},{17,1},{2,18},{18,2},{3,19},{19,3},{4,20},{20... | collective-permute-start | bytes 3145736 | tf_op jit(solution)/shard_map/ppermute | solution.py:747
  78.7 10.9 %collective-permute-start.5 = (f32[80,128]{1,0:T(8,128)S(1)}, f32[80,128]{1,0:T(8,128)S(1)}, u32[]{:S(2)}, u32[]{:S(2)}) collective-permute-start(f32[80,128]{1,0:T(8,128)S(1)} %pad_maximum_fusion), channel_id=1, source_target_pairs={{0,1},{1,2},{2,3},{4,5},{5,6},{6,7},{8,9},{9,10},{10,11},{12,13},{... | collective-permute-start | bytes 122888 | tf_op jit(solution)/shard_map/ppermute | solution.py:735
  82.5 7.5 %collective-permute-start.6 = (f32[80,128]{1,0:T(8,128)S(1)}, f32[80,128]{1,0:T(8,128)S(1)}, u32[]{:S(2)}, u32[]{:S(2)}) collective-permute-start(f32[80,128]{1,0:T(8,128)S(1)} %pad_maximum_fusion.1), channel_id=1, source_target_pairs={{1,0},{2,1},{3,2},{5,4},{6,5},{7,6},{9,8},{10,9},{11,10},{13,12},{... | collective-permute-start | bytes 122888 | tf_op jit(solution)/shard_map/ppermute | solution.py:736
  84.4 30.6 %collective-permute-start.7 = (f32[16,128]{1,0:T(8,128)S(1)}, f32[16,128]{1,0:T(8,128)S(1)}, u32[]{:S(2)}, u32[]{:S(2)}) collective-permute-start(f32[16,128]{1,0:T(8,128)S(1)} %bitcast.15), channel_id=1, source_target_pairs={{0,16},{16,0},{1,17},{17,1},{2,18},{18,2},{3,19},{19,3},{4,20},{20... | collective-permute-start | bytes 24584 | tf_op jit(solution)/shard_map/ppermute | solution.py:743
  84.8 19.0 %collective-permute-start.9 = (f32[4,128]{1,0:T(4,128)S(1)}, f32[4,128]{1,0:T(4,128)S(1)}, u32[]{:S(2)}, u32[]{:S(2)}) collective-permute-start(f32[4,128]{1,0:T(4,128)S(1)} %get-tuple-element.48), channel_id=1, source_target_pairs={{1,18},{2,17},{17,2},{18,1},{5,22},{6,21},{21,6},{22,5},{9,26},{10... | collective-permute-start | bytes 6152 | tf_op jit(solution)/shard_map/ppermute | solution.py:753
  89.6 18.4 %collective-permute-start.10 = (f32[4,128]{1,0:T(4,128)S(1)}, f32[4,128]{1,0:T(4,128)S(1)}, u32[]{:S(2)}, u32[]{:S(2)}) collective-permute-start(f32[4,128]{1,0:T(4,128)S(1)} %get-tuple-element.49), channel_id=1, source_target_pairs={{0,17},{2,19},{1,16},{3,18},{16,1},{18,3},{17,0},{19,2},{4,21},{6,... | collective-permute-start | bytes 6152 | tf_op jit(solution)/shard_map/ppermute | solution.py:754
  102.1 1.0 copy-start.2
  103.1 27.8 %collective-permute-start.15 = (f32[4,512]{1,0:T(4,128)S(1)}, f32[4,512]{1,0:T(4,128)S(1)}, u32[]{:S(2)}, u32[]{:S(2)}) collective-permute-start(f32[4,512]{1,0:T(4,128)S(1)} %get-tuple-element.58), channel_id=1, source_target_pairs={{4,24},{8,20},{20,8},{24,4},{5,25},{9,21},{21,9},{25,5},{6,26},{10... | collective-permute-start | bytes 24584 | tf_op jit(solution)/shard_map/ppermute | solution.py:749
  103.7 27.3 %collective-permute-start.16 = (f32[4,512]{1,0:T(4,128)S(1)}, f32[4,512]{1,0:T(4,128)S(1)}, u32[]{:S(2)}, u32[]{:S(2)}) collective-permute-start(f32[4,512]{1,0:T(4,128)S(1)} %get-tuple-element.59), channel_id=1, source_target_pairs={{0,20},{8,28},{4,16},{12,24},{16,4},{24,12},{20,0},{28,8},{1,21},{... | collective-permute-start | bytes 24584 | tf_op jit(solution)/shard_map/ppermute | solution.py:750
  111.2 21.9 %copy-start.3 = (f32[4,128,512]{2,1,0:T(8,128)S(1)}, f32[4,128,512]{2,1,0:T(8,128)}, u32[]{:S(2)}) copy-start(f32[4,128,512]{2,1,0:T(8,128)} %copy-done.2) | copy-start | bytes 3145732
  118.0 15.1 %collective-permute-start.13 = (f32[4,512]{1,0:T(4,128)S(1)}, f32[4,512]{1,0:T(4,128)S(1)}, u32[]{:S(2)}, u32[]{:S(2)}) collective-permute-start(f32[4,512]{1,0:T(4,128)S(1)} %get-tuple-element.56), channel_id=1, source_target_pairs={{4,8},{8,4},{5,9},{9,5},{6,10},{10,6},{7,11},{11,7},{20,24},{24,20... | collective-permute-start | bytes 24584 | tf_op jit(solution)/shard_map/ppermute | solution.py:764
  118.7 14.5 %collective-permute-start.14 = (f32[4,512]{1,0:T(4,128)S(1)}, f32[4,512]{1,0:T(4,128)S(1)}, u32[]{:S(2)}, u32[]{:S(2)}) collective-permute-start(f32[4,512]{1,0:T(4,128)S(1)} %get-tuple-element.57), channel_id=1, source_target_pairs={{0,4},{8,12},{4,0},{12,8},{1,5},{9,13},{5,1},{13,9},{2,6},{10,14},... | collective-permute-start | bytes 24584 | tf_op jit(solution)/shard_map/ppermute | solution.py:765
  128.2 4.9 %collective-permute-start.11 = (f32[4,128]{1,0:T(4,128)S(1)}, f32[4,128]{1,0:T(4,128)S(1)}, u32[]{:S(2)}, u32[]{:S(2)}) collective-permute-start(f32[4,128]{1,0:T(4,128)S(1)} %get-tuple-element.54), channel_id=1, source_target_pairs={{1,2},{2,1},{5,6},{6,5},{9,10},{10,9},{13,14},{14,13},{17,18},{18,... | collective-permute-start | bytes 6152 | tf_op jit(solution)/shard_map/ppermute | solution.py:768
  130.9 2.2 %collective-permute-start.12 = (f32[4,128]{1,0:T(4,128)S(1)}, f32[4,128]{1,0:T(4,128)S(1)}, u32[]{:S(2)}, u32[]{:S(2)}) collective-permute-start(f32[4,128]{1,0:T(4,128)S(1)} %get-tuple-element.55), channel_id=1, source_target_pairs={{0,1},{2,3},{1,0},{3,2},{4,5},{6,7},{5,4},{7,6},{8,9},{10,11},{9,8... | collective-permute-start | bytes 6152 | tf_op jit(solution)/shard_map/ppermute | solution.py:769
